TPU v7x, 32 devices: a whole 2x2x4 slice. The times are simulated.
32 devices in a mesh: groups: 2 (over x), dom: 16 (over z, y, core).
Axes of the slice: x: 2, y: 2, z: 4, core: 2. Of those that a mesh axis runs over, the one named last changes fastest.
Arguments:
- grid: bfloat16 [32768, 1024], P(('groups', 'dom')), parts along dimension 0, may hold values from -6 to 6
- latent_in: bfloat16 [512, 1024], P(('groups', 'dom')), parts along dimension 0, may hold values from -3 to 3
- grid_gain: float32 [1024], replicated, may hold values from 0.5 to 1.5
- node_gain: float32 [1024], replicated, may hold values from 0.5 to 1.5
- dec_gain: float32 [1024], replicated, may hold values from 0.5 to 1.5
- w_q_enc: bfloat16 [1024, 512], replicated
- w_kv_enc: bfloat16 [1024, 1024], replicated, may hold values from -0.1875 to 0.1875
- w_o_enc: bfloat16 [512, 1024], replicated, may hold values from -0.25 to 0.25
- w_q_dec: bfloat16 [1024, 512], replicated
- w_kv_dec: bfloat16 [1024, 1024], replicated, may hold values from -0.1875 to 0.1875
- w_o_dec: bfloat16 [512, 1024], replicated, may hold values from -0.25 to 0.25
- enc_need: int32 [16, 512], P('dom'), may hold values from 0 to 1023
- enc_slot: int32 [32, 256], P(None, 'dom'), may hold values from 0 to 511
- enc_count: int32 [256], P('dom'), may hold values from 1 to 32
- dec_need: int32 [16, 4096], P('dom'), may hold values from 0 to 15
- dec_slot: int32 [4, 16384], P(None, 'dom'), may hold values from 0 to 4095
Outputs:
- latent_out: bfloat16 [512, 1024], P(('groups', 'dom')), parts along dimension 0
- grid_out: bfloat16 [32768, 1024], P(('groups', 'dom')), parts along dimension 0
There are 2 independent parts, one for each index of `groups`. A program takes and returns all parts, laid end to end along the dimension named above; an argument that names none is the same for every part. Nothing has to cross between parts.
Inputs may be any that keep to these rules, and one draw needn't show every extreme that they name: `enc_need`: a grid point's index within its band; entries may repeat. Edges of node n are enc_slot[0..enc_count[n]-1, n]; entries may repeat. `dec_need`: a latent node's index within its window; entries may repeat. `dec_slot`: entries may repeat.
All inputs are finite; a program needn't handle non-finite values.
Results may differ from a plain program's by a relative error of at most 0.02.
The roundings to bfloat16 on the way count: a program that leaves them out, or rounds other values in their place, can miss the bound.
Values may be sent and summed in bfloat16 or wider, within the bound.
No kernel may reach another device: no remote copies, remote signals or barrier semaphores. Data moves between devices by JAX's collectives and lax.ppermute only.
A program may use at most 128 MiB of HBM per device.

v0:
```python
import math

import jax
import jax.numpy as jnp
from jax import lax
from jax.sharding import PartitionSpec as P

HEADS = 8


norm_eps = 1e-06


def rms_norm(values, weight_gain):
    widened = values.astype(jnp.float32)
    spread = jnp.mean(widened * widened, axis=-1, keepdims=True)
    return (widened * lax.rsqrt(spread + norm_eps) * weight_gain).astype(jnp.bfloat16)


def attend_keys(queries, key_rows, keep_mask):
    rows_here = queries.shape[0]
    inner_width = queries.shape[1]
    head_size = inner_width // HEADS
    edge_count = key_rows.shape[0]
    query_heads = queries.reshape(rows_here, HEADS, head_size)
    key_heads = key_rows[..., :inner_width].reshape(edge_count, rows_here, HEADS, head_size)
    value_heads = key_rows[..., inner_width:].reshape(edge_count, rows_here, HEADS, head_size)
    scores = jnp.einsum(
        "rhd,krhd->krh", query_heads, key_heads, preferred_element_type=jnp.float32
    ) * (1.0 / math.sqrt(head_size))
    if keep_mask is not None:
        scores = jnp.where(keep_mask[:, :, None], scores, -1e30)
    highest = jnp.max(scores, axis=0, keepdims=True)
    raised = jnp.exp(scores - highest)
    weights = (raised / jnp.sum(raised, axis=0, keepdims=True)).astype(jnp.bfloat16)
    mixed = jnp.einsum("krh,krhd->rhd", weights, value_heads, preferred_element_type=jnp.float32)
    return mixed.reshape(rows_here, inner_width).astype(jnp.bfloat16)


def on_device(
    grid,
    latent_in,
    grid_gain,
    node_gain,
    dec_gain,
    w_q_enc,
    w_kv_enc,
    w_o_enc,
    w_q_dec,
    w_kv_dec,
    w_o_dec,
    enc_need,
    enc_slot,
    enc_count,
    dec_need,
    dec_slot,
):
    peer_count = lax.axis_size("dom")
    normed_grid = rms_norm(grid, grid_gain)
    requests = enc_need.reshape(peer_count, -1)
    wanted = lax.all_to_all(requests, "dom", split_axis=0, concat_axis=0, tiled=True)
    source_rows = jnp.dot(normed_grid, w_kv_enc, preferred_element_type=jnp.float32).astype(
        jnp.bfloat16
    )
    arrived = lax.all_to_all(source_rows[wanted], "dom", split_axis=0, concat_axis=0, tiled=True)
    arrived = arrived.reshape(-1, arrived.shape[-1])
    enc_queries = jnp.dot(
        rms_norm(latent_in, node_gain), w_q_enc, preferred_element_type=jnp.float32
    ).astype(jnp.bfloat16)
    keep_mask = jnp.arange(enc_slot.shape[0], dtype=jnp.int32)[:, None] < enc_count[None, :]
    enc_mixed = attend_keys(enc_queries, arrived[enc_slot], keep_mask)
    enc_update = jnp.dot(enc_mixed, w_o_enc, preferred_element_type=jnp.float32)
    latent_out = (latent_in.astype(jnp.float32) + enc_update).astype(jnp.bfloat16)
    latent_pairs = jnp.dot(
        rms_norm(latent_out, dec_gain), w_kv_dec, preferred_element_type=jnp.float32
    ).astype(jnp.bfloat16)
    dec_queries = jnp.dot(normed_grid, w_q_dec, preferred_element_type=jnp.float32).astype(
        jnp.bfloat16
    )
    everyone = lax.all_gather(latent_pairs, "dom", axis=0, tiled=True)
    slot_total = dec_need.shape[1]
    dec_cap = slot_total // peer_count
    owner_rows = jnp.arange(slot_total, dtype=jnp.int32) // dec_cap
    global_rows = owner_rows * latent_pairs.shape[0] + dec_need[0]
    dec_keys = everyone[global_rows[dec_slot]]
    dec_mixed = attend_keys(dec_queries, dec_keys, None)
    dec_update = jnp.dot(dec_mixed, w_o_dec, preferred_element_type=jnp.float32)
    grid_out = (grid.astype(jnp.float32) + dec_update).astype(jnp.bfloat16)
    return (latent_out, grid_out)


def solution(mesh):
    return jax.shard_map(
        on_device,
        mesh=mesh,
        in_specs=(
            P(("groups", "dom"), None),
            P(("groups", "dom"), None),
            P(),
            P(),
            P(),
            P(),
            P(),
            P(),
            P(),
            P(),
            P(),
            P("dom", None),
            P(None, "dom"),
            P("dom"),
            P("dom", None),
            P(None, "dom"),
        ),
        out_specs=(P(("groups", "dom"), None), P(("groups", "dom"), None)),
        check_vma=False,
    )
```

profile of v0, /device:TPU:0, one launch (start us, length us, event | category | flops | bytes accessed | tf_op | source)
XLA Modules:
  0.0 145.5 jit_solution(9233177008498145265)
XLA Ops:
  0.6 0.0 copy-start
  0.6 0.5 broadcast.131
  1.2 1.5 reduce.7
  2.6 0.7 all_to_all.11
  3.3 7.4 %all-to-all-start = ((s32[16,1,32]{2,1,0:T(1,128)}), s32[16,1,32]{2,1,0:T(1,128)S(1)}, u32[]{:S(2)}, u32[]{:S(2)}) async-start(s32[16,1,32]{2,1,0:T(1,128)} %all_to_all.11), calls=%async_computation | async-start | bytes 16384 | tf_op jit(solution)/shard_map/all_to_all | solution.py:61
  10.7 2.1 %fusion.2 = f32[1024]{0:T(1024)S(1)} fusion(bf16[1024,1024]{1,0:T(8,128)(2,1)} %param.16), kind=kLoop, calls=%fused_computation.11 | loop fusion | flops 3144704 | bytes 2101248 | tf_op jit(solution)/shard_map/reduce_sum | solution.py:16
  12.8 0.7 compare_select_fusion.2
  13.5 0.0 copy-done
  13.5 5.3 %convolution_convert_fusion = bf16[1024,1024]{1,0:T(8,128)(2,1)} fusion(bf16[1024,1024]{1,0:T(8,128)(2,1)S(1)} %copy-done, bf16[1024,1024]{1,0:T(8,128)(2,1)} %param.16, f32[1024]{0:T(1024)} %param.18, f32[1024]{0:T(1024)S(1)} %add_rsqrt_fusion), kind=kOutput, calls=%fused_computation.15 | convolution fusion | flops 2152726528 | bytes 6299648 | tf_op jit(solution)/shard_map/dot_general | solution.py:62
  18.8 0.1 fusion.23
  18.9 0.0 all-to-all-done
  18.9 0.1 reshape.132
  19.0 0.0 copy-start.4
  19.0 0.0 copy-start.5
  19.0 5.4 %gather_fusion = bf16[512,1024]{1,0:T(8,128)(2,1)} fusion(bf16[1024,1024]{1,0:T(8,128)(2,1)} %convolution_convert_fusion, s32[1024]{0:T(1024)S(1)} %pad_clamp_fusion.1), kind=kCustom, calls=%fused_computation | custom fusion | bytes 2099200 | tf_op jit(solution)/shard_map/gather | solution.py:65
  24.4 6.0 %all-to-all-start.1 = ((bf16[16,32,1024]{2,1,0:T(8,128)(2,1)}), bf16[16,32,1024]{2,1,0:T(8,128)(2,1)S(1)}, u32[]{:S(2)}, u32[]{:S(2)}) async-start(bf16[16,32,1024]{2,1,0:T(8,128)(2,1)} %bitcast.66), calls=%async_computation.1 | async-start | bytes 2097152 | tf_op jit(solution)/shard_map/all_to_all | solution.py:65
  30.4 0.1 copy.24
  30.5 0.1 reshape.140
  30.6 1.5 %convolution_convert_fusion.3 = bf16[16,512]{1,0:T(8,128)(2,1)S(1)} fusion(bf16[1024,512]{1,0:T(8,128)(2,1)} %param.21, bf16[16,1024]{1,0:T(8,128)(2,1)S(1)} %copy-done.2, f32[1024]{0:T(1024)S(1)} %copy-done.6, f32[16]{0:T(128)S(1)} %add_rsqrt_fusion.2), kind=kOutput, calls=%fused_computation.25 | convolution fusion | flops 16850944 | bytes 1101888 | tf_op jit(solution)/shard_map/dot_general | solution.py:67
  32.1 0.1 reshape.178
  32.3 0.0 copy-start.8
  32.3 0.0 copy-start.10
  32.3 23.0 %gather_fusion.2 = s32[4096]{0:T(1024)S(1)} fusion(s32[4096]{0:T(1024)S(1)} %get-tuple-element.8, s32[4096]{0:T(1024)S(1)} %get-tuple-element.9), kind=kCustom, calls=%fused_computation.2 | custom fusion | bytes 49152 | tf_op jit(solution)/shard_map/gather | solution.py:85
  55.4 0.1 iota_compare_fusion
  55.5 0.0 copy-done.10
  55.5 4.6 %bitcast_convert_fusion.1 = f32[1024,8,64]{0,2,1:T(8,128)} fusion(bf16[1024,512]{1,0:T(8,128)(2,1)} %param.24, bf16[1024,1024]{1,0:T(8,128)(2,1)} %param.16, f32[1024]{0:T(1024)S(1)} %copy-done.10, f32[1024]{0:T(1024)S(1)} %add_rsqrt_fusion), kind=kOutput, calls=%fused_computation.79 | convolution fusion | flops 1078984704 | bytes 5251072 | tf_op jit(solution)/shard_map/dot_general | solution.py:77
  60.1 0.0 all-to-all-done.1
  60.1 2.8 %gather_fusion.1 = bf16[512,1024]{1,0:T(8,128)(2,1)} fusion(bf16[512,1024]{1,0:T(8,128)(2,1)S(1)} %bitcast.62, s32[1024]{0:T(1024)S(1)} %pad_clamp_fusion), kind=kCustom, calls=%fused_computation.1 | custom fusion | bytes 2099200 | tf_op jit(solution)/shard_map/gather | solution.py:71
  62.9 1.3 fusion.47
  64.1 0.0 copy-start.7
  64.1 1.6 %reshape.124 = bf16[32,16,8,64]{3,2,1,0:T(8,128)(2,1)} reshape(bf16[32,16,512]{2,1,0:T(8,128)(2,1)S(1)} %get-tuple-element.4) | data formatting | bytes 1048576 | tf_op jit(solution)/shard_map/reshape | solution.py:26
  65.7 1.5 %reshape.126 = bf16[32,16,8,64]{3,2,1,0:T(8,128)(2,1)} reshape(bf16[32,16,512]{2,1,0:T(8,128)(2,1)S(1)} %get-tuple-element.5) | data formatting | bytes 1048576 | tf_op jit(solution)/shard_map/reshape | solution.py:27
  67.3 2.0 %fusion.14 = f32[16,8,1,32]{3,2,1,0:T(1,128)S(1)} fusion(bf16[16,8,64,1]{2,3,1,0:T(2,128)(2,1)S(1)} %reshape.178, bf16[32,16,8,64]{3,2,1,0:T(8,128)(2,1)} %reshape.124), kind=kOutput, calls=%fused_computation.28 | convolution fusion | flops 524288 | bytes 557056 | tf_op jit(solution)/shard_map/rhd,krhd->krh/dot_general | solution.py:28
  69.2 0.2 fusion.11
  69.4 1.9 %fusion.12 = f32[16,8,1,64]{3,2,1,0:T(1,128)S(1)} fusion(bf16[32,16,8,64]{3,2,1,0:T(8,128)(2,1)} %reshape.126, bf16[32,16,8,1]{0,2,1,3:T(8,128)(2,1)S(1)} %fusion.11), kind=kOutput, calls=%fused_computation.26 | convolution fusion | flops 524288 | bytes 565248 | tf_op jit(solution)/shard_map/krh,krhd->rhd/dot_general | solution.py:36
  71.4 0.1 convert_element_type.64
  71.5 1.6 %fusion.20 = (f32[16]{0:T(128)S(1)}, bf16[16,1024]{1,0:T(8,128)(2,1)S(1)}) fusion(bf16[16,512]{1,0:T(8,128)(2,1)S(1)} %convert_element_type.64, bf16[512,1024]{1,0:T(8,128)(2,1)} %param.23, bf16[16,1024]{1,0:T(8,128)(2,1)S(1)} %copy-done.2), kind=kOutput, calls=%fused_computation.39 | convolution fusion | flops 16875504 | bytes 1130560 | tf_op jit(solution)/shard_map/dot_general | solution.py:72
  73.1 0.0 copy-done.7
  73.1 2.0 %convolution_convert_fusion.2 = bf16[16,1024]{1,0:T(8,128)(2,1)S(1)} fusion(bf16[1024,1024]{1,0:T(8,128)(2,1)} %param.25, bf16[16,1024]{1,0:T(8,128)(2,1)S(1)} %get-tuple-element.7, f32[1024]{0:T(1024)S(1)} %copy-done.7, f32[16]{0:T(128)S(1)} %add_rsqrt_fusion.1), kind=kOutput, calls=%fused_computation.23 | convolution fusion | flops 33636352 | bytes 2166848 | tf_op jit(solution)/shard_map/dot_general | solution.py:74
  75.1 23.4 %all_gather.3 = bf16[256,1024]{1,0:T(8,128)(2,1)S(1)} all-gather(bf16[16,1024]{1,0:T(8,128)(2,1)S(1)} %convolution_convert_fusion.2), channel_id=1, replica_groups=mesh['groups'=2,'dom'=16] {'dom'}, dimensions={0}, use_global_device_ids=true | all-gather | bytes 557056 | tf_op jit(solution)/shard_map/all_gather | solution.py:80
  98.5 18.3 %gather_fusion.3 = bf16[4096,1024]{1,0:T(8,128)(2,1)} fusion(bf16[256,1024]{1,0:T(8,128)(2,1)S(1)} %all_gather.3, s32[4096]{0:T(1024)S(1)} %bitcast_clamp_fusion), kind=kCustom, calls=%fused_computation.3 | custom fusion | bytes 16793600 | tf_op jit(solution)/shard_map/gather | solution.py:85
  116.8 0.0 copy-done.3
  116.8 5.7 %fusion.46 = (bf16[4,1024,512]{2,1,0:T(8,128)(2,1)}, bf16[4,1024,512]{2,1,0:T(8,128)(2,1)}) fusion(bf16[4,1024,1024]{2,1,0:T(8,128)(2,1)} %bitcast.63), kind=kLoop, calls=%fused_computation.82 | loop fusion | bytes 16777216 | tf_op jit(solution)/shard_map/slice | solution.py:26
  122.5 6.3 %copy.45 = bf16[4,1024,512]{1,2,0:T(8,128)(2,1)} copy(bf16[4,1024,512]{2,1,0:T(8,128)(2,1)} %get-tuple-element.2) | data formatting | bytes 8388608
  128.8 4.1 %multiply_reduce_fusion.1 = f32[1024,8,4]{0,1,2:T(8,128)S(1)} fusion(f32[1024,8,64]{0,2,1:T(8,128)} %bitcast_convert_fusion.1, bf16[4,1024,512]{1,2,0:T(8,128)(2,1)} %copy.45), kind=kLoop, calls=%fused_computation.7 | loop fusion | flops 6258688 | bytes 6422528 | tf_op jit(solution)/shard_map/rhd,krhd->krh/dot_general | solution.py:28
  133.0 6.3 %copy.46 = bf16[4,1024,512]{1,2,0:T(8,128)(2,1)} copy(bf16[4,1024,512]{2,1,0:T(8,128)(2,1)} %get-tuple-element.3) | data formatting | bytes 8388608
  139.4 3.5 %multiply_reduce_fusion = bf16[1024,8,64]{0,2,1:T(8,128)(2,1)S(1)} fusion(bf16[1024,8,4,64]{0,3,1,2:T(8,128)(2,1)} %bitcast.64, f32[1024,8,4]{0,1,2:T(8,128)S(1)} %bitcast_convert_fusion), kind=kLoop, calls=%fused_computation.6 | loop fusion | flops 5767168 | bytes 5373952 | tf_op jit(solution)/shard_map/krh,krhd->rhd/dot_general | solution.py:36
  142.9 2.6 %fusion.5 = bf16[1024,1024]{1,0:T(8,128)(2,1)} fusion(bf16[1024,1024]{1,0:T(8,128)(2,1)S(1)} %copy-done.1, bf16[1024,512]{0,1:T(8,128)(2,1)S(1)} %bitcast.67, bf16[512,1024]{1,0:T(8,128)(2,1)S(1)} %copy-done.9), kind=kOutput, calls=%fused_computation.14 | convolution fusion | flops 1076887552 | bytes 6291456 | tf_op jit(solution)/shard_map/dot_general | solution.py:87
  (27 shorter events, 0.2 us)
Async XLA Ops:
  0.6 12.9 %copy-start = (bf16[1024,1024]{1,0:T(8,128)(2,1)S(1)}, bf16[1024,1024]{1,0:T(8,128)(2,1)}, u32[]{:S(2)}) copy-start(bf16[1024,1024]{1,0:T(8,128)(2,1)} %param.22) | copy-start | bytes 6291460
  3.3 15.6 %all-to-all-start = ((s32[16,1,32]{2,1,0:T(1,128)}), s32[16,1,32]{2,1,0:T(1,128)S(1)}, u32[]{:S(2)}, u32[]{:S(2)}) async-start(s32[16,1,32]{2,1,0:T(1,128)} %all_to_all.11), calls=%async_computation | async-start | bytes 16384 | tf_op jit(solution)/shard_map/all_to_all | solution.py:61
  13.5 5.3 %copy-start.2 = (bf16[16,1024]{1,0:T(8,128)(2,1)S(1)}, bf16[16,1024]{1,0:T(8,128)(2,1)}, u32[]{:S(2)}) copy-start(bf16[16,1024]{1,0:T(8,128)(2,1)} %param.17) | copy-start | bytes 98308
  19.0 11.6 %copy-start.6 = (f32[1024]{0:T(1024)S(1)}, f32[1024]{0:T(1024)}, u32[]{:S(2)}) copy-start(f32[1024]{0:T(1024)} %param.19) | copy-start | bytes 12292
  19.0 13.2 %copy-start.4 = (s32[4,1024]{1,0:T(4,128)S(1)}, s32[4,1024]{1,0:T(4,128)}, u32[]{:S(2)}) copy-start(s32[4,1024]{1,0:T(4,128)} %param.31) | copy-start | bytes 49156
  19.0 13.2 %copy-start.5 = (s32[1,4096]{1,0:T(1,128)S(1)}, s32[1,4096]{1,0:T(1,128)}, u32[]{:S(2)}) copy-start(s32[1,4096]{1,0:T(1,128)} %param.30) | copy-start | bytes 49156
  24.4 35.7 %all-to-all-start.1 = ((bf16[16,32,1024]{2,1,0:T(8,128)(2,1)}), bf16[16,32,1024]{2,1,0:T(8,128)(2,1)S(1)}, u32[]{:S(2)}, u32[]{:S(2)}) async-start(bf16[16,32,1024]{2,1,0:T(8,128)(2,1)} %bitcast.66), calls=%async_computation.1 | async-start | bytes 2097152 | tf_op jit(solution)/shard_map/all_to_all | solution.py:65
  32.3 23.1 %copy-start.8 = (s32[16]{0:T(128)S(1)}, s32[16]{0:T(128)}, u32[]{:S(2)}) copy-start(s32[16]{0:T(128)} %param.29) | copy-start | bytes 196
  32.3 23.2 %copy-start.10 = (f32[1024]{0:T(1024)S(1)}, f32[1024]{0:T(1024)}, u32[]{:S(2)}) copy-start(f32[1024]{0:T(1024)} %param.18) | copy-start | bytes 12292
  64.1 8.9 %copy-start.7 = (f32[1024]{0:T(1024)S(1)}, f32[1024]{0:T(1024)}, u32[]{:S(2)}) copy-start(f32[1024]{0:T(1024)} %param.20) | copy-start | bytes 12292
  73.1 43.7 %copy-start.3 = (bf16[16,1024]{1,0:T(8,128)(2,1)}, bf16[16,1024]{1,0:T(8,128)(2,1)S(1)}, u32[]{:S(2)}) copy-start(bf16[16,1024]{1,0:T(8,128)(2,1)S(1)} %get-tuple-element.7) | copy-start | bytes 98308
  139.4 3.5 %copy-start.1 = (bf16[1024,1024]{1,0:T(8,128)(2,1)S(1)}, bf16[1024,1024]{1,0:T(8,128)(2,1)}, u32[]{:S(2)}) copy-start(bf16[1024,1024]{1,0:T(8,128)(2,1)} %param.16) | copy-start | bytes 6291460
  139.4 3.5 %copy-start.9 = (bf16[512,1024]{1,0:T(8,128)(2,1)S(1)}, bf16[512,1024]{1,0:T(8,128)(2,1)}, u32[]{:S(2)}) copy-start(bf16[512,1024]{1,0:T(8,128)(2,1)} %param.26) | copy-start | bytes 3145732
where the time goes:
time: 146 us
  local copies, waits for them, and re-layouts  73.9 us (51%)
  blocking collectives  23.4 us (16%)
  matrix products  21.5 us (15%)
  starting transfers between devices  13.4 us (9%)
  other arithmetic  12.3 us (8%)
    gather x3, local copies, waits for them, and re-layouts, on_device(): dec_keys = everyone[global_rows[dec_slot]]  41.3 us
    all_gather x1, blocking collectives, on_device(): everyone = lax.all_gather(latent_pairs, 'dom', axis=0, tiled=True)  23.4 us
    unnamed x25, local copies, waits for them, and re-layouts  13.2 us
    all_to_all x1, starting transfers between devices, on_device(): lax.all_to_all(requests, 'dom', split_axis=0, concat_axis=0, tiled=True)  7.39 us
    slice x2, local copies, waits for them, and re-layouts, attend_keys(): key_rows[..., :inner_width].reshape(edge_count, rows_here, HEADS, head_size)  7.01 us
    all_to_all x1, starting transfers between devices, on_device(): lax.all_to_all(source_rows[wanted], 'dom', split_axis=0, concat_axis=0, t...  6.01 us
    gather x1, local copies, waits for them, and re-layouts, on_device(): source_rows[wanted]  5.36 us
    dot_general x1, matrix products, on_device(): jnp.dot(normed_grid, w_kv_enc, preferred_element_type=jnp.float32)  5.3 us
  transfers between devices with their start and end apart: 2, of which 0 were waited for; matrix products, arithmetic and copies ran while one was open for 26% of the time, Pallas kernels for 0%

commit v1 on v0

v1 whole, which is shorter than its diff:
```python
import functools
import math

import jax
import jax.numpy as jnp
from jax import lax
from jax.experimental import pallas as pl
from jax.experimental.pallas import tpu as pltpu
from jax.sharding import PartitionSpec as P

HEADS = 8
LANES = 128
NEG = -1e30
norm_eps = 1e-06
f32 = jnp.float32
bf16 = jnp.bfloat16


def iota(shape, dim):
    return lax.broadcasted_iota(jnp.int32, shape, dim)


def div(values, by):
    if by & (by - 1) == 0:
        return values >> (by.bit_length() - 1)
    return values // by


def mod(values, by):
    if by & (by - 1) == 0:
        return values & (by - 1)
    return values % by


def dot(a, b):
    return jnp.dot(a, b, preferred_element_type=f32)


def dot_t(a, b):
    return lax.dot_general(a, b, (((1,), (1,)), ((), ())), preferred_element_type=f32)


def normed(values, gain):
    widened = values.astype(f32)
    spread = jnp.mean(widened * widened, axis=-1, keepdims=True)
    return (widened * lax.rsqrt(spread + norm_eps) * gain).astype(bf16)


def params(mib, grid_dims=0):
    return pltpu.CompilerParams(
        vmem_limit_bytes=mib * 2**20,
        dimension_semantics=("arbitrary",) * grid_dims if grid_dims else None,
    )


def cost(flops, read, exps=0):
    return pl.CostEstimate(flops=int(flops), bytes_accessed=int(read), transcendentals=int(exps))


def ask_kernel(cap, latent_ref, gain_ref, w_ref, slot_ref, count_ref, need_ref, out_ref):
    peers, rows, _ = out_ref.shape
    width = w_ref.shape[1]
    entries = need_ref.shape[1]
    edges = slot_ref.shape[1]
    queries = dot(normed(latent_ref[...], gain_ref[...]), w_ref[...]).astype(bf16)
    eye = iota((rows, rows), 0) == iota((rows, rows), 1)
    counts = jnp.sum(jnp.where(eye, count_ref[...], 0), axis=1, keepdims=True)
    slots = jnp.where(iota((rows, edges), 1) < counts, slot_ref[...], -1)
    place = iota((rows, entries), 1)
    uses = jnp.zeros((rows, entries), f32)
    for j in range(edges):
        uses += jnp.where(slots[:, j : j + 1] == place, 1.0, 0.0)
    need = need_ref[...]
    low = jnp.broadcast_to((need & 255).astype(f32), (rows, entries))
    high = jnp.broadcast_to((need >> 8).astype(f32), (rows, entries))
    lane = iota((rows, LANES), 1)
    for p in range(peers):
        at = p * cap
        block, start = at // LANES * LANES, at % LANES

        def moved(values, to):
            piece = values[:, block : block + LANES]
            shift = (to - start) % LANES
            return pltpu.roll(piece, shift, 1) if shift else piece

        extra = jnp.where(
            lane < cap,
            moved(uses, 0),
            jnp.where(
                lane < 2 * cap,
                moved(low, cap),
                jnp.where(lane < 3 * cap, moved(high, 2 * cap), 0.0),
            ),
        )
        out_ref[p, :, :width] = queries
        out_ref[p, :, width:] = extra.astype(bf16)


def front_kernel(x_ref, gain_ref, w_ref, normed_ref, pairs_ref):
    rows = normed(x_ref[...], gain_ref[...])
    normed_ref[...] = rows
    pairs_ref[...] = dot(rows, w_ref[...]).astype(bf16)


def head_scores(keys, queries, h, size, scale):
    per = LANES // size
    at = h // per * LANES
    key_part = keys[:, at : at + LANES]
    lane = iota(key_part.shape, 1)
    own = div(lane, size) == h % per
    key_part = jnp.where(own, key_part, jnp.zeros_like(key_part))
    return dot_t(key_part, queries[:, at : at + LANES]) * scale


def partial_kernel(cap, rows, asked_ref, pairs_ref, out_ref, mixed_ref):
    nodes = asked_ref.shape[0]
    points, both = pairs_ref.shape
    width = both // 2
    size = width // HEADS
    entries = nodes // rows * cap
    scale = math.log2(math.e) / math.sqrt(size)
    extra = asked_ref[:, width:]
    pick = iota((entries, nodes), 1) == div(iota((entries, nodes), 0), cap) * rows
    lists = dot(pick.astype(bf16), extra)
    lane = iota((entries, LANES), 1)
    within = mod(iota((entries, LANES), 0), cap)
    weights = jnp.where(lane == within + cap, 1.0, jnp.where(lane == within + 2 * cap, 256.0, 0.0))
    index = jnp.sum(lists * weights, axis=1, keepdims=True).astype(jnp.int32)
    chosen = (index == iota((entries, points), 1)).astype(bf16)
    keys = dot(chosen, pairs_ref[:, :width]).astype(bf16)
    values = dot(chosen, pairs_ref[:, width:]).astype(bf16)
    values_t = values.T
    uses = dot_t((lane == within).astype(bf16), extra)
    here = div(iota((entries, nodes), 0), cap) == div(iota((entries, nodes), 1), rows)
    live = here & (uses > 0.5)
    bias = jnp.where(live, jnp.log2(jnp.where(live, uses, 1.0)), NEG)
    queries = asked_ref[:, :width]
    tops, totals = [], []
    for h in range(HEADS):
        scores = head_scores(keys, queries, h, size, scale) + bias
        top = jnp.max(scores, axis=0, keepdims=True)
        raised = jnp.exp2(scores - top)
        tops.append(top)
        totals.append(jnp.sum(raised, axis=0, keepdims=True))
        mixed_ref[h * size : (h + 1) * size, :] = dot(
            values_t[h * size : (h + 1) * size, :], raised.astype(bf16)
        )
    top = jnp.concatenate(tops, axis=0)
    total = jnp.concatenate(totals, axis=0)
    top_1 = top.astype(bf16).astype(f32)
    top_2 = (top - top_1).astype(bf16).astype(f32)
    top_3 = top - top_1 - top_2
    total_1 = total.astype(bf16).astype(f32)
    for i, part in enumerate((top_1, top_2, top_3, total_1, total - total_1)):
        mixed_ref[width + i * HEADS : width + (i + 1) * HEADS, :] = part
    mixed_ref[width + 5 * HEADS :, :] = jnp.zeros_like(mixed_ref[width + 5 * HEADS :, :])
    out_ref[...] = mixed_ref[...].T.astype(bf16)


def combine_kernel(parts_ref, latent_ref, gain_ref, w_o_ref, w_kv_ref, latent_out_ref, out_ref):
    peers, rows, total_width = parts_ref.shape
    width = w_o_ref.shape[0]
    size = width // HEADS
    parts = parts_ref[...].reshape(peers * rows, total_width)
    stats = parts[:, width:]
    col, head = iota((LANES, LANES), 0), iota((LANES, LANES), 1)
    head_of = mod(col, HEADS) == head
    take_top = head_of & (col < 3 * HEADS)
    take_sum = head_of & (col >= 3 * HEADS) & (col < 5 * HEADS)
    top = dot(stats, take_top.astype(bf16)).reshape(peers, rows, LANES)
    total = dot(stats, take_sum.astype(bf16)).reshape(peers, rows, LANES)
    highest = jnp.max(top, axis=0, keepdims=True)
    factor = jnp.exp2(top - highest)
    whole = jnp.sum(total * factor, axis=0, keepdims=True)
    used = iota((1, rows, LANES), 2) < HEADS
    factor = factor * jnp.where(used, 1.0 / jnp.where(used, whole, 1.0), 0.0)
    factor = factor.reshape(peers * rows, LANES)
    spread = (div(iota((LANES, width), 1), size) == iota((LANES, width), 0)).astype(bf16)
    factor_1 = factor.astype(bf16)
    factor_2 = (factor - factor_1.astype(f32)).astype(bf16)
    wide = dot(factor_1, spread) + dot(factor_2, spread)
    mixed = jnp.sum((parts[:, :width].astype(f32) * wide).reshape(peers, rows, width), axis=0)
    update = dot(mixed.astype(bf16), w_o_ref[...])
    latent_out = (latent_ref[...].astype(f32) + update).astype(bf16)
    latent_out_ref[...] = latent_out
    pairs = dot(normed(latent_out, gain_ref[...]), w_kv_ref[...]).astype(bf16)
    for p in range(peers):
        out_ref[p] = pairs


def middle_kernel(cap, rows, x_ref, w_ref, need_ref, slot_ref, query_ref, bias_ref):
    query_ref[...] = dot(x_ref[...], w_ref[...]).astype(bf16)
    nodes, points = bias_ref.shape
    high_count = need_ref.shape[0]
    need = need_ref[...].astype(f32).astype(bf16)
    uses = jnp.zeros((nodes, points), f32)
    for j in range(slot_ref.shape[0]):
        slots = slot_ref[j : j + 1, :]
        row_of = (div(slots, LANES) == iota((high_count, points), 0)).astype(bf16)
        listed = lax.dot_general(need, row_of, (((0,), (0,)), ((), ())), preferred_element_type=f32)
        own = mod(slots, LANES) == iota((LANES, points), 0)
        found = jnp.sum(jnp.where(own, listed, 0.0), axis=0, keepdims=True).astype(jnp.int32)
        node = div(slots, cap) * rows + found
        uses += jnp.where(node == iota((nodes, points), 0), 1.0, 0.0)
    live = uses > 0.5
    bias_ref[...] = jnp.where(live, jnp.log2(jnp.where(live, uses, 1.0)), NEG)


def decode_kernel(x_ref, query_ref, bias_ref, pairs_ref, w_ref, out_ref, mixed_ref):
    width = w_ref.shape[0]
    size = width // HEADS
    scale = math.log2(math.e) / math.sqrt(size)
    keys = pairs_ref[:, :width]
    values_t = pairs_ref[:, width:].T
    queries = query_ref[...]
    bias = bias_ref[...]
    for h in range(HEADS):
        scores = head_scores(keys, queries, h, size, scale) + bias
        raised = jnp.exp2(scores - jnp.max(scores, axis=0, keepdims=True))
        total = jnp.sum(raised, axis=0, keepdims=True)
        mixed = dot(values_t[h * size : (h + 1) * size, :], raised.astype(bf16))
        mixed_ref[h * size : (h + 1) * size, :] = mixed * (1.0 / total)
    update = dot(mixed_ref[...].T.astype(bf16), w_ref[...])
    out_ref[...] = (x_ref[...].astype(f32) + update).astype(bf16)


def whole(*shape):
    return pl.BlockSpec(shape, lambda *_: (0,) * len(shape))


def on_device(
    grid,
    latent_in,
    grid_gain,
    node_gain,
    dec_gain,
    w_q_enc,
    w_kv_enc,
    w_o_enc,
    w_q_dec,
    w_kv_dec,
    w_o_dec,
    enc_need,
    enc_slot,
    enc_count,
    dec_need,
    dec_slot,
):
    peers = lax.axis_size("dom")
    points, depth = grid.shape
    rows = latent_in.shape[0]
    width = w_q_enc.shape[1]
    nodes = peers * rows
    entries = enc_need.shape[1]
    cap = entries // peers
    sent = width + LANES
    block = math.gcd(points, 256)

    asked = pl.pallas_call(
        functools.partial(ask_kernel, cap),
        out_shape=jax.ShapeDtypeStruct((peers, rows, sent), bf16),
        compiler_params=params(16),
        cost_estimate=cost(2 * rows * depth * width, 2 * depth * width),
        name="ask",
    )(
        latent_in,
        node_gain.reshape(1, -1),
        w_q_enc,
        enc_slot.T,
        enc_count.reshape(1, -1),
        enc_need,
    )
    asked = lax.all_to_all(asked, "dom", split_axis=0, concat_axis=0, tiled=True)

    normed_grid, pairs = pl.pallas_call(
        front_kernel,
        grid=(points // block,),
        in_specs=[
            pl.BlockSpec((block, depth), lambda i: (i, 0)),
            whole(1, depth),
            whole(depth, 2 * width),
        ],
        out_specs=[
            pl.BlockSpec((block, depth), lambda i: (i, 0)),
            pl.BlockSpec((block, 2 * width), lambda i: (i, 0)),
        ],
        out_shape=[
            jax.ShapeDtypeStruct((points, depth), bf16),
            jax.ShapeDtypeStruct((points, 2 * width), bf16),
        ],
        compiler_params=params(20, 1),
        cost_estimate=cost(4 * points * depth * width, 8 * points * depth),
        name="front",
    )(grid, grid_gain.reshape(1, -1), w_kv_enc)

    parts = pl.pallas_call(
        functools.partial(partial_kernel, cap, rows),
        out_shape=jax.ShapeDtypeStruct((nodes, sent), bf16),
        scratch_shapes=[pltpu.VMEM((sent, nodes), f32)],
        compiler_params=params(32),
        cost_estimate=cost(4 * entries * points * width, 4 * points * width),
        name="partial",
    )(asked.reshape(nodes, sent), pairs)
    parts = lax.all_to_all(
        parts.reshape(peers, rows, sent), "dom", split_axis=0, concat_axis=0, tiled=True
    )

    slot_total = dec_need.shape[1]
    queries, bias = pl.pallas_call(
        functools.partial(middle_kernel, slot_total // peers, rows),
        out_shape=[
            jax.ShapeDtypeStruct((points, width), bf16),
            jax.ShapeDtypeStruct((nodes, points), f32),
        ],
        compiler_params=params(32),
        cost_estimate=cost(2 * points * depth * width, 8 * points * depth),
        name="middle",
    )(normed_grid, w_q_dec, dec_need.reshape(slot_total // LANES, LANES), dec_slot)

    latent_out, everyone = pl.pallas_call(
        combine_kernel,
        out_shape=[
            jax.ShapeDtypeStruct((rows, depth), bf16),
            jax.ShapeDtypeStruct((peers, rows, 2 * width), bf16),
        ],
        compiler_params=params(24),
        cost_estimate=cost(6 * rows * depth * width, 6 * depth * width),
        name="combine",
    )(parts, latent_in, dec_gain.reshape(1, -1), w_o_enc, w_kv_dec)
    everyone = lax.all_to_all(everyone, "dom", split_axis=0, concat_axis=0, tiled=True)

    grid_out = pl.pallas_call(
        decode_kernel,
        grid=(points // block,),
        in_specs=[
            pl.BlockSpec((block, depth), lambda i: (i, 0)),
            pl.BlockSpec((block, width), lambda i: (i, 0)),
            pl.BlockSpec((nodes, block), lambda i: (0, i)),
            whole(nodes, 2 * width),
            whole(width, depth),
        ],
        out_specs=pl.BlockSpec((block, depth), lambda i: (i, 0)),
        out_shape=jax.ShapeDtypeStruct((points, depth), bf16),
        scratch_shapes=[pltpu.VMEM((width, block), f32)],
        compiler_params=params(32, 1),
        cost_estimate=cost(8 * points * depth * width, 8 * points * depth),
        name="decode",
    )(grid, queries, bias, everyone.reshape(nodes, 2 * width), w_o_dec)
    return (latent_out, grid_out)


def solution(mesh):
    return jax.shard_map(
        on_device,
        mesh=mesh,
        in_specs=(
            P(("groups", "dom"), None),
            P(("groups", "dom"), None),
            P(),
            P(),
            P(),
            P(),
            P(),
            P(),
            P(),
            P(),
            P(),
            P("dom", None),
            P(None, "dom"),
            P("dom"),
            P("dom", None),
            P(None, "dom"),
        ),
        out_specs=(P(("groups", "dom"), None), P(("groups", "dom"), None)),
        check_vma=False,
    )
```

time: 146 us -> 81.1 us (0.56)
  local copies, waits for them, and re-layouts: 73.9 us -> 18.5 us
  Pallas kernels: 0 us -> 26.5 us
  matrix products: 21.5 us -> 0 us
  other arithmetic: 12.3 us -> 0 us
  waiting for transfers between devices: 0.01 us -> 9.09 us
  blocking collectives: 23.4 us -> 14.4 us
  starting transfers between devices: 13.4 us -> 11 us
    gather x5 -> x0, local copies, waits for them, and re-layouts: 49.5 us -> none  [the longest x3 41.3 us: on_device(): dec_keys = everyone[global_rows[dec_slot]]]
    pallas_call x0 -> x6, Pallas kernels: none -> 26.5 us  [the longest x1 12.2 us: on_device(): pl.pallas_call(decode_kernel, grid=(points // block,), in_specs=[pl.Block...]
    all_gather x1 -> x0, blocking collectives: 23.4 us -> none  [on_device(): everyone = lax.all_gather(latent_pairs, 'dom', axis=0, tiled=True)]
    dot_general x8 -> x0, matrix products: 21.5 us -> none  [the longest x1 5.3 us: on_device(): jnp.dot(normed_grid, w_kv_enc, preferred_element_type=jnp.float32)]
    all_to_all x0 -> x1, blocking collectives: none -> 14.4 us  [on_device(): lax.all_to_all(parts.reshape(peers, rows, sent), 'dom', split_axis=0, con...]
    all_to_all x2, waiting for transfers between devices: 0.01 us -> 9.09 us  [the longest x1 6.6 us: on_device(): lax.all_to_all(everyone, 'dom', split_axis=0, concat_axis=0, tiled=True)]
    dot_general x2 -> x0, other arithmetic: 7.57 us -> none  [the longest x1 4.1 us: attend_keys(): jnp.einsum('rhd,krhd->krh', query_heads, key_heads, preferred_element_typ...]
    slice x2 -> x0, local copies, waits for them, and re-layouts: 7.01 us -> none  [attend_keys(): key_rows[..., :inner_width].reshape(edge_count, rows_here, HEADS, head_size)]
  transfers between devices with their start and end apart: 2 -> 2, of which waited for: 0 -> 2; matrix products, arithmetic and copies ran while one was open for 26% -> 0% of each run, Pallas kernels for 0% -> 8%
where the time goes in v1:
time: 81.1 us; the launch traced here: 80.3 us
  Pallas kernels  26.5 us (33%)
  local copies, waits for them, and re-layouts  18.5 us (23%)
  blocking collectives  14.4 us (18%)
  starting transfers between devices  11 us (14%)
  waiting for transfers between devices  9.09 us (11%)
    unnamed x48, local copies, waits for them, and re-layouts  18.5 us
    all_to_all x1, blocking collectives, on_device(): lax.all_to_all(parts.reshape(peers, rows, sent), 'dom', split_axis=0, con...  14.4 us
    pallas_call x1, Pallas kernels, on_device(): pl.pallas_call(decode_kernel, grid=(points // block,), in_specs=[pl.Block...  12.2 us
    all_to_all x1, starting transfers between devices, on_device(): lax.all_to_all(asked, 'dom', split_axis=0, concat_axis=0, tiled=True)  7.39 us
    all_to_all x1, waiting for transfers between devices, on_device(): lax.all_to_all(everyone, 'dom', split_axis=0, concat_axis=0, tiled=True)  6.6 us
    pallas_call x1, Pallas kernels, on_device(): pl.pallas_call(functools.partial(partial_kernel, cap, rows), out_shape=ja...  4.88 us
    all_to_all x1, starting transfers between devices, on_device(): lax.all_to_all(everyone, 'dom', split_axis=0, concat_axis=0, tiled=True)  3.57 us
    pallas_call x1, Pallas kernels, on_device(): pl.pallas_call(front_kernel, grid=(points // block,), in_specs=[pl.BlockS...  3.41 us
  transfers between devices with their start and end apart: 2, of which 2 were waited for; matrix products, arithmetic and copies ran while one was open for 0% of the time, Pallas kernels for 8%

profile of v1, /device:TPU:0, one launch (start us, length us, event | category | flops | bytes accessed | tf_op | source)
XLA Modules:
  0.0 80.3 jit_solution(708772815526074013)
XLA Ops:
  0.6 0.0 copy-start.1
  0.6 1.2 %copy-done.1 = bf16[1024,512]{1,0:T(8,128)(2,1)S(1)} copy-done((bf16[1024,512]{1,0:T(8,128)(2,1)S(1)}, bf16[1024,512]{1,0:T(8,128)(2,1)}, u32[]{:S(2)}) %copy-start.1) | copy-done | bytes 1048600
  1.9 0.0 copy-start.3
  1.9 0.8 copy-done.3
  2.6 0.0 copy-start.5
  2.6 0.7 copy-done.5
  3.3 0.0 copy-start.6
  3.3 0.7 copy-done.6
  4.0 0.0 copy-start.8
  4.0 0.7 copy-done.8
  4.7 0.0 copy-start.9
  4.7 0.7 copy-done.9
  5.3 1.1 %ask.1 = bf16[16,16,640]{2,1,0:T(8,128)(2,1)} custom-call(bf16[16,1024]{1,0:T(8,128)(2,1)S(1)} %copy-done.3, f32[1,1024]{1,0:T(1,128)S(1)} %bitcast.13, bf16[1024,512]{1,0:T(8,128)(2,1)S(1)} %copy-done.1, s32[16,32]{1,0:T(8,128)S(1)} %bitcast.12, s32[1,16]{1,0:T(1,128)S(1)} %bitcast.15, s32[1,512]{1,0:T(1,128)S(1)} %copy-done.8), custom_call_target="tpu_custom_call" | custom-call | flops 16777216 | bytes 1048576 | tf_op jit(solution)/shard_map/ask/pallas_call | solution.py:259
  6.5 7.4 %all-to-all-start = ((bf16[16,16,640]{2,1,0:T(8,128)(2,1)}), bf16[16,16,640]{2,1,0:T(8,128)(2,1)S(1)}, u32[]{:S(2)}, u32[]{:S(2)}) async-start(bf16[16,16,640]{2,1,0:T(8,128)(2,1)} %ask.1), calls=%async_computation | async-start | bytes 655360 | tf_op jit(solution)/shard_map/all_to_all | solution.py:273
  13.9 0.0 copy-start.10
  13.9 1.6 %copy-done.10 = bf16[1024,1024]{1,0:T(8,128)(2,1)S(1)} copy-done((bf16[1024,1024]{1,0:T(8,128)(2,1)S(1)}, bf16[1024,1024]{1,0:T(8,128)(2,1)}, u32[]{:S(2)}) %copy-start.10) | copy-done | bytes 2097176
  15.5 1.6 %copy-done.11 = bf16[1024,1024]{1,0:T(8,128)(2,1)S(1)} copy-done((bf16[1024,1024]{1,0:T(8,128)(2,1)S(1)}, bf16[1024,1024]{1,0:T(8,128)(2,1)}, u32[]{:S(2)}) %copy-start.11) | copy-done | bytes 2097176
  17.1 0.7 copy-done.17
  17.7 3.4 %front.1 = (bf16[1024,1024]{1,0:T(8,128)(2,1)S(1)}, bf16[1024,1024]{1,0:T(8,128)(2,1)S(1)}) custom-call(bf16[1024,1024]{1,0:T(8,128)(2,1)S(1)} %copy-done.11, f32[1,1024]{1,0:T(1,128)S(1)} %bitcast.17, bf16[1024,1024]{1,0:T(8,128)(2,1)S(1)} %copy-done.10), custom_call_target="tpu_custom_call" | custom-call | flops 2147483648 | bytes 8388608 | tf_op jit(solution)/shard_map/front/pallas_call | solution.py:275
  21.2 0.0 copy-start.18
  21.2 1.3 %copy-done.18 = bf16[1024,1024]{1,0:T(8,128)(2,1)} copy-done((bf16[1024,1024]{1,0:T(8,128)(2,1)}, bf16[1024,1024]{1,0:T(8,128)(2,1)S(1)}, u32[]{:S(2)}) %copy-start.18) | copy-done | bytes 2097176
  22.5 2.5 %all-to-all-done = bf16[16,16,640]{2,1,0:T(8,128)(2,1)S(1)} async-done(((bf16[16,16,640]{2,1,0:T(8,128)(2,1)}), bf16[16,16,640]{2,1,0:T(8,128)(2,1)S(1)}, u32[]{:S(2)}, u32[]{:S(2)}) %all-to-all-start) | async-done | bytes 327712 | tf_op jit(solution)/shard_map/all_to_all | solution.py:273
  25.0 4.9 %partial.1 = bf16[256,640]{1,0:T(8,128)(2,1)S(1)} custom-call(bf16[256,640]{1,0:T(8,128)(2,1)S(1)} %bitcast.10, bf16[1024,1024]{1,0:T(8,128)(2,1)S(1)} %get-tuple-element.8.pairs_ref), custom_call_target="tpu_custom_call" | custom-call | flops 1073741824 | bytes 2097152 | tf_op jit(solution)/shard_map/partial/pallas_call | solution.py:296
  29.9 14.4 %all_to_all.15.parts_ref = bf16[16,16,640]{2,1,0:T(8,128)(2,1)S(1)} all-to-all(bf16[16,16,640]{2,1,0:T(8,128)(2,1)S(1)} %bitcast.11), channel_id=1, replica_groups=mesh['groups'=2,'dom'=16] {'dom'}, dimensions={0} | all-to-all | bytes 655360 | tf_op jit(solution)/shard_map/all_to_all | solution.py:304
  44.3 0.0 copy-done
  44.3 0.0 copy-done.2
  44.3 0.0 copy-done.4
  44.3 0.0 copy-done.7
  44.3 0.0 copy-start.15
  44.3 0.0 copy-start.16
  44.3 2.0 %combine.1 = (bf16[16,1024]{1,0:T(8,128)(2,1)}, bf16[16,16,1024]{2,1,0:T(8,128)(2,1)}) custom-call(bf16[16,16,640]{2,1,0:T(8,128)(2,1)S(1)} %all_to_all.15.parts_ref, bf16[16,1024]{1,0:T(8,128)(2,1)S(1)} %copy-done.4, f32[1,1024]{1,0:T(1,128)S(1)} %bitcast.14, bf16[512,1024]{1,0:T(8,128)(2,1)S(1)} %copy-done.2, bf16[1024,1024]{1,0:T(8,128)(2,1)S(1)} %copy-done), custom_call_target="tpu_custom_call" | custom-call | flops 50331648 | bytes 3145728 | tf_op jit(solution)/shard_map/combine/pallas_call | solution.py:320
  46.3 3.6 %all-to-all-start.2 = ((bf16[16,16,1024]{2,1,0:T(8,128)(2,1)}), bf16[16,16,1024]{2,1,0:T(8,128)(2,1)S(1)}, u32[]{:S(2)}, u32[]{:S(2)}) async-start(bf16[16,16,1024]{2,1,0:T(8,128)(2,1)} %get-tuple-element.13), calls=%async_computation.2 | async-start | bytes 1048576 | tf_op jit(solution)/shard_map/all_to_all | solution.py:330
  49.9 0.0 copy-start.12
  49.9 0.0 copy-done.15
  49.9 0.0 copy-done.16
  50.0 0.0 copy-start.13
  50.0 1.4 %copy-done.13 = bf16[1024,512]{1,0:T(8,128)(2,1)S(1)} copy-done((bf16[1024,512]{1,0:T(8,128)(2,1)S(1)}, bf16[1024,512]{1,0:T(8,128)(2,1)}, u32[]{:S(2)}) %copy-start.13) | copy-done | bytes 1048600
  51.3 1.6 %copy-done.19 = bf16[1024,1024]{1,0:T(8,128)(2,1)S(1)} copy-done((bf16[1024,1024]{1,0:T(8,128)(2,1)S(1)}, bf16[1024,1024]{1,0:T(8,128)(2,1)}, u32[]{:S(2)}) %copy-start.19) | copy-done | bytes 2097176
  52.9 2.9 %middle.1 = (bf16[1024,512]{1,0:T(8,128)(2,1)S(1)}, f32[256,1024]{1,0:T(8,128)S(1)}) custom-call(bf16[1024,1024]{1,0:T(8,128)(2,1)S(1)} %copy-done.19, bf16[1024,512]{1,0:T(8,128)(2,1)S(1)} %copy-done.13, s32[32,128]{1,0:T(8,128)S(1)} %bitcast.16, s32[4,1024]{1,0:T(4,128)S(1)} %copy-done.16), custom_call_target="tpu_custom_call" | custom-call | flops 1073741824 | bytes 8388608 | tf_op jit(solution)/shard_map/middle/pallas_call | solution.py:309
  55.8 0.0 copy-start.20
  55.8 1.0 %copy-done.20 = bf16[1024,512]{1,0:T(8,128)(2,1)} copy-done((bf16[1024,512]{1,0:T(8,128)(2,1)}, bf16[1024,512]{1,0:T(8,128)(2,1)S(1)}, u32[]{:S(2)}) %copy-start.20) | copy-done | bytes 1048600
  56.8 1.0 %copy-done.22 = f32[256,1024]{1,0:T(8,128)} copy-done((f32[256,1024]{1,0:T(8,128)}, f32[256,1024]{1,0:T(8,128)S(1)}, u32[]{:S(2)}) %copy-start.22) | copy-done | bytes 1048600
  57.7 6.6 %all-to-all-done.2 = bf16[16,16,1024]{2,1,0:T(8,128)(2,1)S(1)} async-done(((bf16[16,16,1024]{2,1,0:T(8,128)(2,1)}), bf16[16,16,1024]{2,1,0:T(8,128)(2,1)S(1)}, u32[]{:S(2)}, u32[]{:S(2)}) %all-to-all-start.2) | async-done | bytes 524320 | tf_op jit(solution)/shard_map/all_to_all | solution.py:330
  64.3 0.0 copy-done.12
  64.4 1.2 %copy-done.14 = bf16[512,1024]{1,0:T(8,128)(2,1)S(1)} copy-done((bf16[512,1024]{1,0:T(8,128)(2,1)S(1)}, bf16[512,1024]{1,0:T(8,128)(2,1)}, u32[]{:S(2)}) %copy-start.14) | copy-done | bytes 1048600
  65.6 1.2 %copy-done.21 = bf16[1024,512]{1,0:T(8,128)(2,1)S(1)} copy-done((bf16[1024,512]{1,0:T(8,128)(2,1)S(1)}, bf16[1024,512]{1,0:T(8,128)(2,1)}, u32[]{:S(2)}) %copy-start.21) | copy-done | bytes 1048600
  66.8 1.2 %copy-done.23 = f32[256,1024]{1,0:T(8,128)S(1)} copy-done((f32[256,1024]{1,0:T(8,128)S(1)}, f32[256,1024]{1,0:T(8,128)}, u32[]{:S(2)}) %copy-start.23) | copy-done | bytes 1048600
  68.0 12.2 %decode.1 = bf16[1024,1024]{1,0:T(8,128)(2,1)} custom-call(bf16[1024,1024]{1,0:T(8,128)(2,1)S(1)} %copy-done.12, bf16[1024,512]{1,0:T(8,128)(2,1)S(1)} %copy-done.21, f32[256,1024]{1,0:T(8,128)S(1)} %copy-done.23, bf16[256,1024]{1,0:T(8,128)(2,1)S(1)} %bitcast.9, bf16[512,1024]{1,0:T(8,128)(2,1)S(1)} %copy-done.14), custom_call_target="tpu_custom_call" | custom-call | flops 4294967296 | bytes 8388608 | tf_op jit(solution)/shard_map/decode/pallas_call | solution.py:332
  (11 shorter events, 0.0 us)
Async XLA Ops:
  0.6 1.2 %copy-start.1 = (bf16[1024,512]{1,0:T(8,128)(2,1)S(1)}, bf16[1024,512]{1,0:T(8,128)(2,1)}, u32[]{:S(2)}) copy-start(bf16[1024,512]{1,0:T(8,128)(2,1)} %w_ref.4) | copy-start | bytes 3145732
  1.9 0.8 copy-start.3
  2.6 0.7 copy-start.5
  3.3 0.7 copy-start.6
  4.0 0.7 copy-start.8
  4.7 0.7 copy-start.9
  6.5 18.5 %all-to-all-start = ((bf16[16,16,640]{2,1,0:T(8,128)(2,1)}), bf16[16,16,640]{2,1,0:T(8,128)(2,1)S(1)}, u32[]{:S(2)}, u32[]{:S(2)}) async-start(bf16[16,16,640]{2,1,0:T(8,128)(2,1)} %ask.1), calls=%async_computation | async-start | bytes 655360 | tf_op jit(solution)/shard_map/all_to_all | solution.py:273
  13.9 1.6 %copy-start.10 = (bf16[1024,1024]{1,0:T(8,128)(2,1)S(1)}, bf16[1024,1024]{1,0:T(8,128)(2,1)}, u32[]{:S(2)}) copy-start(bf16[1024,1024]{1,0:T(8,128)(2,1)} %w_ref.5) | copy-start | bytes 6291460
  15.5 1.6 %copy-start.11 = (bf16[1024,1024]{1,0:T(8,128)(2,1)S(1)}, bf16[1024,1024]{1,0:T(8,128)(2,1)}, u32[]{:S(2)}) copy-start(bf16[1024,1024]{1,0:T(8,128)(2,1)} %x_ref.3) | copy-start | bytes 6291460
  17.1 0.7 copy-start.17
  21.2 1.3 %copy-start.18 = (bf16[1024,1024]{1,0:T(8,128)(2,1)}, bf16[1024,1024]{1,0:T(8,128)(2,1)S(1)}, u32[]{:S(2)}) copy-start(bf16[1024,1024]{1,0:T(8,128)(2,1)S(1)} %get-tuple-element.10.x_ref) | copy-start | bytes 6291460
  25.0 19.3 %copy-start = (bf16[1024,1024]{1,0:T(8,128)(2,1)S(1)}, bf16[1024,1024]{1,0:T(8,128)(2,1)}, u32[]{:S(2)}) copy-start(bf16[1024,1024]{1,0:T(8,128)(2,1)} %w_kv_ref.1) | copy-start | bytes 6291460
  25.0 19.3 %copy-start.2 = (bf16[512,1024]{1,0:T(8,128)(2,1)S(1)}, bf16[512,1024]{1,0:T(8,128)(2,1)}, u32[]{:S(2)}) copy-start(bf16[512,1024]{1,0:T(8,128)(2,1)} %w_o_ref.1) | copy-start | bytes 3145732
  25.0 19.3 %copy-start.4 = (bf16[16,1024]{1,0:T(8,128)(2,1)S(1)}, bf16[16,1024]{1,0:T(8,128)(2,1)}, u32[]{:S(2)}) copy-start(bf16[16,1024]{1,0:T(8,128)(2,1)} %latent_ref.3) | copy-start | bytes 98308
  25.0 19.3 %copy-start.7 = (f32[1024]{0:T(1024)S(1)}, f32[1024]{0:T(1024)}, u32[]{:S(2)}) copy-start(f32[1024]{0:T(1024)} %param.20) | copy-start | bytes 12292
  44.3 5.6 %copy-start.15 = (s32[1,4096]{1,0:T(1,128)S(1)}, s32[1,4096]{1,0:T(1,128)}, u32[]{:S(2)}) copy-start(s32[1,4096]{1,0:T(1,128)} %param.30) | copy-start | bytes 49156
  44.3 5.6 %copy-start.16 = (s32[4,1024]{1,0:T(4,128)S(1)}, s32[4,1024]{1,0:T(4,128)}, u32[]{:S(2)}) copy-start(s32[4,1024]{1,0:T(4,128)} %slot_ref.1) | copy-start | bytes 49156
  46.3 18.0 %all-to-all-start.2 = ((bf16[16,16,1024]{2,1,0:T(8,128)(2,1)}), bf16[16,16,1024]{2,1,0:T(8,128)(2,1)S(1)}, u32[]{:S(2)}, u32[]{:S(2)}) async-start(bf16[16,16,1024]{2,1,0:T(8,128)(2,1)} %get-tuple-element.13), calls=%async_computation.2 | async-start | bytes 1048576 | tf_op jit(solution)/shard_map/all_to_all | solution.py:330
  49.9 14.4 %copy-start.12 = (bf16[1024,1024]{1,0:T(8,128)(2,1)S(1)}, bf16[1024,1024]{1,0:T(8,128)(2,1)}, u32[]{:S(2)}) copy-start(bf16[1024,1024]{1,0:T(8,128)(2,1)} %x_ref.3) | copy-start | bytes 6291460
  50.0 1.4 %copy-start.13 = (bf16[1024,512]{1,0:T(8,128)(2,1)S(1)}, bf16[1024,512]{1,0:T(8,128)(2,1)}, u32[]{:S(2)}) copy-start(bf16[1024,512]{1,0:T(8,128)(2,1)} %w_ref.6) | copy-start | bytes 3145732
  51.3 1.6 %copy-start.19 = (bf16[1024,1024]{1,0:T(8,128)(2,1)S(1)}, bf16[1024,1024]{1,0:T(8,128)(2,1)}, u32[]{:S(2)}) copy-start(bf16[1024,1024]{1,0:T(8,128)(2,1)} %copy-done.18) | copy-start | bytes 6291460
  55.8 1.0 %copy-start.20 = (bf16[1024,512]{1,0:T(8,128)(2,1)}, bf16[1024,512]{1,0:T(8,128)(2,1)S(1)}, u32[]{:S(2)}) copy-start(bf16[1024,512]{1,0:T(8,128)(2,1)S(1)} %get-tuple-element.11.query_ref) | copy-start | bytes 3145732
  56.8 1.0 %copy-start.22 = (f32[256,1024]{1,0:T(8,128)}, f32[256,1024]{1,0:T(8,128)S(1)}, u32[]{:S(2)}) copy-start(f32[256,1024]{1,0:T(8,128)S(1)} %get-tuple-element.12.bias_ref) | copy-start | bytes 3145732
  64.4 1.2 %copy-start.14 = (bf16[512,1024]{1,0:T(8,128)(2,1)S(1)}, bf16[512,1024]{1,0:T(8,128)(2,1)}, u32[]{:S(2)}) copy-start(bf16[512,1024]{1,0:T(8,128)(2,1)} %w_ref.7) | copy-start | bytes 3145732
  65.6 1.2 %copy-start.21 = (bf16[1024,512]{1,0:T(8,128)(2,1)S(1)}, bf16[1024,512]{1,0:T(8,128)(2,1)}, u32[]{:S(2)}) copy-start(bf16[1024,512]{1,0:T(8,128)(2,1)} %copy-done.20) | copy-start | bytes 3145732
  66.8 1.2 %copy-start.23 = (f32[256,1024]{1,0:T(8,128)S(1)}, f32[256,1024]{1,0:T(8,128)}, u32[]{:S(2)}) copy-start(f32[256,1024]{1,0:T(8,128)} %copy-done.22) | copy-start | bytes 3145732

commit v2 on v1

v2 whole, which is shorter than its diff:
```python
import functools
import math

import jax
import jax.numpy as jnp
from jax import lax
from jax.experimental import pallas as pl
from jax.experimental.pallas import tpu as pltpu
from jax.sharding import PartitionSpec as P

HEADS = 8
LANES = 128
NEG = -1e30
norm_eps = 1e-06
f32 = jnp.float32
bf16 = jnp.bfloat16


def iota(shape, dim):
    return lax.broadcasted_iota(jnp.int32, shape, dim)


def div(values, by):
    if by & (by - 1) == 0:
        return values >> (by.bit_length() - 1)
    return values // by


def mod(values, by):
    if by & (by - 1) == 0:
        return values & (by - 1)
    return values % by


def dot(a, b):
    return jnp.dot(a, b, preferred_element_type=f32)


def dot_t(a, b):
    return lax.dot_general(a, b, (((1,), (1,)), ((), ())), preferred_element_type=f32)


def normed(values, gain):
    widened = values.astype(f32)
    spread = jnp.mean(widened * widened, axis=-1, keepdims=True)
    return (widened * lax.rsqrt(spread + norm_eps) * gain).astype(bf16)


def params(mib, grid_dims=0):
    return pltpu.CompilerParams(
        vmem_limit_bytes=mib * 2**20,
        dimension_semantics=("arbitrary",) * grid_dims if grid_dims else None,
    )


def cost(flops, read, exps=0):
    return pl.CostEstimate(flops=int(flops), bytes_accessed=int(read), transcendentals=int(exps))


def digits(index):
    return div(index, 4), div(index, 2) & 1, index & 1


def place_of(index, me, far):
    there, here = digits(index), digits(me)
    step = mod(there[0] - here[0] + far, far)
    return ((there[2] ^ here[2]) * 2 + (there[1] ^ here[1])) * far + step


def far_perm(far, step):
    return [(i, (i // 4 + step) % far * 4 + i % 4) for i in range(4 * far)]


def flip_perm(count, bits):
    return [(i, i ^ bits) for i in range(count)]


def gather_half(block, far):
    blocks = [block] + [lax.ppermute(block, "dom", far_perm(far, -s)) for s in range(1, far)]
    column = jnp.concatenate(blocks, axis=0)
    other = lax.ppermute(column, "dom", flip_perm(4 * far, 2))
    half = jnp.concatenate([column, other], axis=0)
    return half, lax.ppermute(half, "dom", flip_perm(4 * far, 1))


def ask_kernel(latent_ref, gain_ref, w_ref, slot_ref, count_ref, need_ref, out_ref):
    rows = latent_ref.shape[0]
    width = w_ref.shape[1]
    entries = need_ref.shape[1]
    edges = slot_ref.shape[1]
    per = entries // rows
    out_ref[:, :width] = dot(normed(latent_ref[...], gain_ref[...]), w_ref[...]).astype(bf16)
    eye = iota((rows, rows), 0) == iota((rows, rows), 1)
    counts = jnp.sum(jnp.where(eye, count_ref[...], 0), axis=1, keepdims=True)
    slots = jnp.where(iota((rows, edges), 1) < counts, slot_ref[...], 65535)
    need = need_ref[...]
    own = div(iota((rows, entries), 1), per) == iota((rows, entries), 0)
    extra = jnp.zeros((rows, LANES), f32)
    for i, part in enumerate((slots & 255, slots >> 8)):
        to = iota((edges, LANES), 1) == iota((edges, LANES), 0) + i * edges
        extra += dot(part.astype(f32).astype(bf16), to.astype(bf16))
    for i, part in enumerate((need & 255, need >> 8)):
        to = iota((entries, LANES), 1) == mod(iota((entries, LANES), 0), per) + 2 * edges + i * per
        spread = jnp.where(own, part.astype(f32), 0.0).astype(bf16)
        extra += dot(spread, to.astype(bf16))
    out_ref[:, width:] = extra.astype(bf16)


def front_kernel(x_ref, gain_ref, w_ref, normed_ref, pairs_ref):
    rows = normed(x_ref[...], gain_ref[...])
    normed_ref[...] = rows
    pairs_ref[...] = dot(rows, w_ref[...]).astype(bf16)


def head_keys(keys, h, size):
    per = LANES // size
    part = keys[:, h // per * LANES : (h // per + 1) * LANES]
    return jnp.where(div(iota(part.shape, 1), size) == h % per, part, jnp.zeros_like(part))


def stat_parts(top, total):
    top_1 = top.astype(bf16).astype(f32)
    top_2 = (top - top_1).astype(bf16).astype(f32)
    total_1 = total.astype(bf16).astype(f32)
    return top_1, top_2, top - top_1 - top_2, total_1, total - total_1


def partial_kernel(cap, rows, edges, near_ref, far_ref, pairs_ref, *refs):
    out_refs, mixed_ref = refs[:-1], refs[-1]
    me = lax.axis_index("dom")
    points, both = pairs_ref.shape
    width = both // 2
    size = width // HEADS
    per = rows * edges // rows
    scale = math.log2(math.e) / math.sqrt(size)
    nodes = near_ref.shape[0]
    entries = nodes // rows * cap
    list_row, list_lane = div(me * cap, per), mod(me * cap, per)
    pick = iota((entries, nodes), 1) == div(iota((entries, nodes), 0), cap) * rows + list_row
    pick = pick.astype(bf16)
    lane = iota((entries, LANES), 1)
    within = mod(iota((entries, LANES), 0), cap)
    low_lane = within + (2 * edges + list_lane)
    weights = jnp.where(lane == low_lane, 1.0, jnp.where(lane == low_lane + per, 256.0, 0.0))
    here = div(iota((entries, nodes), 0), cap) == div(iota((entries, nodes), 1), rows)
    listed = -(-cap // 8) * 8
    repeat = iota((entries, listed), 1) == mod(iota((entries, listed), 0), cap)
    for half, asked_ref in enumerate((near_ref, far_ref)):
        extra = asked_ref[:, width:]
        index = jnp.sum(dot(pick, extra) * weights, axis=1, keepdims=True).astype(jnp.int32)
        chosen = (index == iota((entries, points), 1)).astype(bf16)
        keys = dot(chosen, pairs_ref[:, :width]).astype(bf16)
        values_t = dot(chosen, pairs_ref[:, width:]).T.astype(bf16)
        extra_t = extra.astype(f32).T
        slots = (extra_t[:edges] + 256.0 * extra_t[edges : 2 * edges]).astype(jnp.int32) - me * cap
        uses = jnp.zeros((listed, nodes), f32)
        for j in range(edges):
            uses += jnp.where(slots[j : j + 1] == iota((listed, nodes), 0), 1.0, 0.0)
        uses = dot(repeat.astype(bf16), uses.astype(bf16))
        live = here & (uses > 0.5)
        bias = jnp.where(live, jnp.log2(jnp.where(live, uses, 1.0)), NEG)
        tops, totals = [], []
        for h in range(HEADS):
            at = h * size // LANES * LANES
            queries = asked_ref[:, at : at + LANES]
            scores = dot_t(head_keys(keys, h, size), queries) * scale + bias
            top = jnp.max(scores, axis=0, keepdims=True)
            raised = jnp.exp2(scores - top)
            tops.append(top)
            totals.append(jnp.sum(raised, axis=0, keepdims=True))
            mixed_ref[h * size : (h + 1) * size, :] = dot(
                values_t[h * size : (h + 1) * size, :], raised.astype(bf16)
            )
        stats = stat_parts(jnp.concatenate(tops, axis=0), jnp.concatenate(totals, axis=0))
        for i, part in enumerate(stats):
            mixed_ref[width + i * HEADS : width + (i + 1) * HEADS, :] = part
        rest = mixed_ref.shape[0] - width - len(stats) * HEADS
        mixed_ref[width + len(stats) * HEADS :, :] = jnp.zeros((rest, nodes), f32)
        result = mixed_ref[...].T.astype(bf16)
        out_refs[2 * half][...] = result[: nodes // 2]
        out_refs[2 * half + 1][...] = result[nodes // 2 :]


def read_stats(stats):
    col, head = iota((LANES, LANES), 0), iota((LANES, LANES), 1)
    head_of = mod(col, HEADS) == head
    take_top = head_of & (col < 3 * HEADS)
    take_sum = head_of & (col >= 3 * HEADS) & (col < 5 * HEADS)
    return dot(stats, take_top.astype(bf16)), dot(stats, take_sum.astype(bf16))


def spread_heads(factor, width):
    size = width // HEADS
    spread = (div(iota((LANES, width), 1), size) == iota((LANES, width), 0)).astype(bf16)
    factor_1 = factor.astype(bf16)
    factor_2 = (factor - factor_1.astype(f32)).astype(bf16)
    return dot(factor_1, spread) + dot(factor_2, spread)


def merged(part_refs, width):
    tops, totals = zip(*[read_stats(ref[:, width:]) for ref in part_refs])
    highest = functools.reduce(jnp.maximum, tops)
    factors = [jnp.exp2(top - highest) for top in tops]
    total = sum(total * factor for total, factor in zip(totals, factors))
    return highest, total, factors


def merge_kernel(own_ref, *refs):
    part_refs, out_refs = (own_ref,) + refs[:3], refs[3:]
    width = own_ref.shape[1] - LANES
    highest, total, factors = merged(part_refs, width)
    mixed = sum(
        ref[:, :width].astype(f32) * spread_heads(factor, width)
        for ref, factor in zip(part_refs, factors)
    )
    used = iota(total.shape, 1) < HEADS
    stats = jnp.zeros_like(total)
    for i, part in enumerate(stat_parts(highest, total)):
        part = jnp.where(used, part, 0.0)
        stats += pltpu.roll(part, i * HEADS, 1) if i else part
    mixed, stats = mixed.astype(bf16), stats.astype(bf16)
    rows = out_refs[0].shape[0]
    for i, out_ref in enumerate(out_refs):
        out_ref[:, :width] = mixed[i * rows : (i + 1) * rows]
        out_ref[:, width:] = stats[i * rows : (i + 1) * rows]


def combine_kernel(part_count, *refs):
    part_refs, refs = refs[:part_count], refs[part_count:]
    latent_ref, gain_ref, w_o_ref, w_kv_ref, latent_out_ref, out_ref = refs
    width = w_o_ref.shape[0]
    _, total, factors = merged(part_refs, width)
    used = iota(total.shape, 1) < HEADS
    inverse = jnp.where(used, 1.0 / jnp.where(used, total, 1.0), 0.0)
    mixed = sum(
        ref[:, :width].astype(f32) * spread_heads(factor * inverse, width)
        for ref, factor in zip(part_refs, factors)
    )
    update = dot(mixed.astype(bf16), w_o_ref[...])
    latent_out = (latent_ref[...].astype(f32) + update).astype(bf16)
    latent_out_ref[...] = latent_out
    out_ref[...] = dot(normed(latent_out, gain_ref[...]), w_kv_ref[...]).astype(bf16)


def middle_kernel(cap, rows, far, x_ref, w_ref, need_ref, slot_ref, query_ref, pick_ref):
    query_ref[...] = dot(x_ref[...], w_ref[...]).T.astype(bf16)
    me = lax.axis_index("dom")
    edges, nodes, points = pick_ref.shape
    high_count = need_ref.shape[0]
    need = need_ref[...].astype(f32).astype(bf16)
    for j in range(edges):
        slots = slot_ref[j : j + 1, :]
        row_of = (div(slots, LANES) == iota((high_count, points), 0)).astype(bf16)
        listed = lax.dot_general(need, row_of, (((0,), (0,)), ((), ())), preferred_element_type=f32)
        own = mod(slots, LANES) == iota((LANES, points), 0)
        found = jnp.sum(jnp.where(own, listed, 0.0), axis=0, keepdims=True).astype(jnp.int32)
        node = place_of(div(slots, cap), me, far) * rows + found
        pick_ref[j] = (node == iota((nodes, points), 0)).astype(bf16)


def decode_kernel(x_ref, query_ref, pick_ref, near_ref, far_ref, w_ref, out_ref, pairs_ref):
    width, points = query_ref.shape
    edges = pick_ref.shape[0]
    size = width // HEADS
    half = width // 2

    @pl.when(pl.program_id(0) == 0)
    def _():
        nodes = near_ref.shape[0]
        pairs_ref[:, :nodes] = near_ref[...].T
        pairs_ref[:, nodes:] = far_ref[...].T

    scores = []
    for j in range(edges):
        parts = []
        for start in (0, half):
            keys = dot(pairs_ref[start : start + half, :], pick_ref[j])
            products = keys * query_ref[start : start + half, :].astype(f32)
            parts.append(jnp.sum(products.reshape(HEADS // 2, size, points), axis=1))
        scores.append(jnp.concatenate(parts, axis=0) * (1.0 / math.sqrt(size)))
    highest = functools.reduce(jnp.maximum, scores)
    raised = [jnp.exp(score - highest) for score in scores]
    inverse = 1.0 / sum(raised)
    weights = [(one * inverse).astype(bf16).astype(f32) for one in raised]
    mixed = []
    for start in (0, half):
        total = jnp.zeros((HEADS // 2, size, points), f32)
        for j in range(edges):
            values = dot(pairs_ref[width + start : width + start + half, :], pick_ref[j])
            first = start // size
            weight = weights[j][first : first + HEADS // 2].reshape(HEADS // 2, 1, points)
            total += values.reshape(HEADS // 2, size, points) * weight
        mixed.append(total.reshape(half, points).T.astype(bf16))
    update = dot(jnp.concatenate(mixed, axis=1), w_ref[...])
    out_ref[...] = (x_ref[...].astype(f32) + update).astype(bf16)


def whole(*shape):
    return pl.BlockSpec(shape, lambda *_: (0,) * len(shape))


def on_device(
    grid,
    latent_in,
    grid_gain,
    node_gain,
    dec_gain,
    w_q_enc,
    w_kv_enc,
    w_o_enc,
    w_q_dec,
    w_kv_dec,
    w_o_dec,
    enc_need,
    enc_slot,
    enc_count,
    dec_need,
    dec_slot,
):
    peers = lax.axis_size("dom")
    far = peers // 4
    points, depth = grid.shape
    rows = latent_in.shape[0]
    width = w_q_enc.shape[1]
    nodes = peers * rows
    entries = enc_need.shape[1]
    edges = enc_slot.shape[0]
    cap = entries // peers
    sent = width + LANES
    block = math.gcd(points, 256)

    asked = pl.pallas_call(
        ask_kernel,
        out_shape=jax.ShapeDtypeStruct((rows, sent), bf16),
        compiler_params=params(58),
        cost_estimate=cost(2 * rows * depth * width, 2 * depth * width),
        name="ask",
    )(
        latent_in,
        node_gain.reshape(1, -1),
        w_q_enc,
        enc_slot.T,
        enc_count.reshape(1, -1),
        enc_need,
    )
    asked = gather_half(asked, far)

    normed_grid, pairs = pl.pallas_call(
        front_kernel,
        grid=(points // block,),
        in_specs=[
            pl.BlockSpec((block, depth), lambda i: (i, 0)),
            whole(1, depth),
            whole(depth, 2 * width),
        ],
        out_specs=[
            pl.BlockSpec((block, depth), lambda i: (i, 0)),
            pl.BlockSpec((block, 2 * width), lambda i: (i, 0)),
        ],
        out_shape=[
            jax.ShapeDtypeStruct((points, depth), bf16),
            jax.ShapeDtypeStruct((points, 2 * width), bf16),
        ],
        compiler_params=params(58, 1),
        cost_estimate=cost(4 * points * depth * width, 8 * points * depth),
        name="front",
    )(grid, grid_gain.reshape(1, -1), w_kv_enc)

    parts = pl.pallas_call(
        functools.partial(partial_kernel, cap, rows, edges),
        out_shape=[jax.ShapeDtypeStruct((far * rows, sent), bf16)] * 4,
        scratch_shapes=[pltpu.VMEM((sent, nodes // 2), f32)],
        compiler_params=params(58),
        cost_estimate=cost(4 * entries * points * width, 4 * points * width),
        name="partial",
    )(*asked, pairs)
    parts = [parts[0]] + [
        lax.ppermute(parts[i], "dom", flip_perm(peers, (i & 1) * 2 + (i >> 1))) for i in (1, 2, 3)
    ]
    parts = pl.pallas_call(
        merge_kernel,
        out_shape=[jax.ShapeDtypeStruct((rows, sent), bf16)] * far,
        compiler_params=params(58),
        cost_estimate=cost(2 * nodes * LANES * width, 4 * nodes * width),
        name="merge",
    )(*parts)
    parts = [parts[0]] + [
        lax.ppermute(parts[s], "dom", far_perm(far, s)) for s in range(1, far)
    ]

    slot_total = dec_need.shape[1]
    queries, picks = pl.pallas_call(
        functools.partial(middle_kernel, slot_total // peers, rows, far),
        out_shape=[
            jax.ShapeDtypeStruct((width, points), bf16),
            jax.ShapeDtypeStruct((dec_slot.shape[0], nodes, points), bf16),
        ],
        compiler_params=params(58),
        cost_estimate=cost(2 * points * depth * width, 8 * points * depth),
        name="middle",
    )(normed_grid, w_q_dec, dec_need.reshape(slot_total // LANES, LANES), dec_slot)

    latent_out, own_pairs = pl.pallas_call(
        functools.partial(combine_kernel, far),
        out_shape=[
            jax.ShapeDtypeStruct((rows, depth), bf16),
            jax.ShapeDtypeStruct((rows, 2 * width), bf16),
        ],
        compiler_params=params(58),
        cost_estimate=cost(6 * rows * depth * width, 6 * depth * width),
        name="combine",
    )(*parts, latent_in, dec_gain.reshape(1, -1), w_o_enc, w_kv_dec)
    near, other = gather_half(own_pairs, far)

    grid_out = pl.pallas_call(
        decode_kernel,
        grid=(points // block,),
        in_specs=[
            pl.BlockSpec((block, depth), lambda i: (i, 0)),
            pl.BlockSpec((width, block), lambda i: (0, i)),
            pl.BlockSpec((dec_slot.shape[0], nodes, block), lambda i: (0, 0, i)),
            whole(nodes // 2, 2 * width),
            whole(nodes // 2, 2 * width),
            whole(width, depth),
        ],
        out_specs=pl.BlockSpec((block, depth), lambda i: (i, 0)),
        out_shape=jax.ShapeDtypeStruct((points, depth), bf16),
        scratch_shapes=[pltpu.VMEM((2 * width, nodes), bf16)],
        compiler_params=params(58, 1),
        cost_estimate=cost(8 * points * depth * width, 8 * points * depth),
        name="decode",
    )(grid, queries, picks, near, other, w_o_dec)
    return (latent_out, grid_out)


def solution(mesh):
    return jax.shard_map(
        on_device,
        mesh=mesh,
        in_specs=(
            P(("groups", "dom"), None),
            P(("groups", "dom"), None),
            P(),
            P(),
            P(),
            P(),
            P(),
            P(),
            P(),
            P(),
            P(),
            P("dom", None),
            P(None, "dom"),
            P("dom"),
            P("dom", None),
            P(None, "dom"),
        ),
        out_specs=(P(("groups", "dom"), None), P(("groups", "dom"), None)),
        check_vma=False,
    )
```

time: 81.1 us -> 82.8 us (1.021)
  blocking collectives: 14.4 us -> 0 us
  local copies, waits for them, and re-layouts: 18.5 us -> 4.25 us
  waiting for transfers between devices: 9.09 us -> 21.7 us
  starting transfers between devices: 11 us -> 19.4 us
  Pallas kernels: 26.5 us -> 34.6 us
  other arithmetic: 0 us -> 1.5 us
    ppermute x0 -> x16, waiting for transfers between devices: none -> 21.7 us  [the longest x6 8.58 us: gather_half(): lax.ppermute(block, 'dom', far_perm(far, -s))]
    ppermute x0 -> x16, starting transfers between devices: none -> 19.4 us  [the longest x6 10.1 us: gather_half(): lax.ppermute(block, 'dom', far_perm(far, -s))]
    all_to_all x1 -> x0, blocking collectives: 14.4 us -> none  [on_device(): lax.all_to_all(parts.reshape(peers, rows, sent), 'dom', split_axis=0, con...]
    unnamed x48 -> x28, local copies, waits for them, and re-layouts: 18.5 us -> 4.22 us
    all_to_all x2 -> x0, starting transfers between devices: 11 us -> none  [the longest x1 7.39 us: on_device(): lax.all_to_all(asked, 'dom', split_axis=0, concat_axis=0, tiled=True)]
    all_to_all x2 -> x0, waiting for transfers between devices: 9.09 us -> none  [the longest x1 6.6 us: on_device(): lax.all_to_all(everyone, 'dom', split_axis=0, concat_axis=0, tiled=True)]
    pallas_call x3 -> x4, Pallas kernels: 8.01 us -> 14.4 us  [the longest x1 6.39 us: on_device(): pl.pallas_call(functools.partial(partial_kernel, cap, rows, edges), out_s...]
    pallas_call x1, Pallas kernels: 12.2 us -> 7.87 us  [on_device(): pl.pallas_call(decode_kernel, grid=(points // block,), in_specs=[pl.Block...]
  transfers between devices with their start and end apart: 2 -> 16, of which waited for: 2 -> 11; matrix products, arithmetic and copies ran while one was open for 0% -> 2% of each run, Pallas kernels for 8% -> 15%
where the time goes in v2:
time: 82.8 us; the launch traced here: 82.1 us
  Pallas kernels  34.6 us (42%)
  waiting for transfers between devices  21.7 us (26%)
  starting transfers between devices  19.4 us (23%)
  local copies, waits for them, and re-layouts  4.25 us (5%)
  other arithmetic  1.5 us (2%)
    ppermute x6, starting transfers between devices, gather_half(): lax.ppermute(block, 'dom', far_perm(far, -s))  10.1 us
    ppermute x6, waiting for transfers between devices, gather_half(): lax.ppermute(block, 'dom', far_perm(far, -s))  8.58 us
    pallas_call x1, Pallas kernels, on_device(): pl.pallas_call(decode_kernel, grid=(points // block,), in_specs=[pl.Block...  7.87 us
    ppermute x2, waiting for transfers between devices, gather_half(): other = lax.ppermute(column, 'dom', flip_perm(4 * far, 2))  6.45 us
    pallas_call x1, Pallas kernels, on_device(): pl.pallas_call(front_kernel, grid=(points // block,), in_specs=[pl.BlockS...  6.42 us
    pallas_call x1, Pallas kernels, on_device(): pl.pallas_call(functools.partial(partial_kernel, cap, rows, edges), out_s...  6.39 us
    pallas_call x1, Pallas kernels, on_device(): pl.pallas_call(functools.partial(middle_kernel, slot_total // peers, rows...  5.83 us
    ppermute x3, waiting for transfers between devices, on_device(): lax.ppermute(parts[i], 'dom', flip_perm(peers, (i & 1) * 2 + (i >> 1)))  4.35 us
  transfers between devices with their start and end apart: 16, of which 11 were waited for; matrix products, arithmetic and copies ran while one was open for 2% of the time, Pallas kernels for 15%

profile of v2, /device:TPU:0, one launch (start us, length us, event | category | flops | bytes accessed | tf_op | source)
XLA Modules:
  0.0 82.1 jit_solution(14386851991944305959)
XLA Ops:
  0.6 2.3 %ask.1 = bf16[16,640]{1,0:T(8,128)(2,1)} custom-call(bf16[16,1024]{1,0:T(8,128)(2,1)} %refs_4_.1, f32[1,1024]{1,0:T(1,128)} %bitcast.7, bf16[1024,512]{1,0:T(8,128)(2,1)} %w_ref.4, s32[16,32]{1,0:T(8,128)} %bitcast.6, s32[1,16]{1,0:T(1,128)} %bitcast.9, s32[1,512]{1,0:T(1,128)} %need_ref.1), custom_call_target="tpu_custom_call" | custom-call | flops 16777216 | bytes 1048576 | tf_op jit(solution)/shard_map/ask/pallas_call | solution.py:332
  2.9 5.0 %collective-permute-start = (bf16[16,640]{1,0:T(8,128)(2,1)}, bf16[16,640]{1,0:T(8,128)(2,1)S(1)}, u32[]{:S(2)}, u32[]{:S(2)}) collective-permute-start(bf16[16,640]{1,0:T(8,128)(2,1)} %ask.1), channel_id=1, source_target_pairs={{0,12},{1,13},{2,14},{3,15},{4,0},{5,1},{6,2},{7,3},{8,4},{9,5},{1... | collective-permute-start | bytes 61448 | tf_op jit(solution)/shard_map/ppermute | solution.py:79
  8.0 0.0 collective-permute-start.1
  8.0 1.0 %collective-permute-start.2 = (bf16[16,640]{1,0:T(8,128)(2,1)}, bf16[16,640]{1,0:T(8,128)(2,1)S(1)}, u32[]{:S(2)}, u32[]{:S(2)}) collective-permute-start(bf16[16,640]{1,0:T(8,128)(2,1)} %ask.1), channel_id=1, source_target_pairs={{0,4},{1,5},{2,6},{3,7},{4,8},{5,9},{6,10},{7,11},{8,12},{9,13},{1... | collective-permute-start | bytes 61448 | tf_op jit(solution)/shard_map/ppermute | solution.py:79
  9.0 0.8 constant_dynamic-update-slice_fusion.4
  9.7 0.0 collective-permute-done
  9.7 3.1 %collective-permute-done.1 = bf16[16,640]{1,0:T(8,128)(2,1)S(1)} collective-permute-done((bf16[16,640]{1,0:T(8,128)(2,1)}, bf16[16,640]{1,0:T(8,128)(2,1)S(1)}, u32[]{:S(2)}, u32[]{:S(2)}) %collective-permute-start.1) | collective-permute-done | bytes 20512 | tf_op jit(solution)/shard_map/ppermute | solution.py:79
  12.9 0.9 %collective-permute-done.2 = bf16[16,640]{1,0:T(8,128)(2,1)S(1)} collective-permute-done((bf16[16,640]{1,0:T(8,128)(2,1)}, bf16[16,640]{1,0:T(8,128)(2,1)S(1)}, u32[]{:S(2)}, u32[]{:S(2)}) %collective-permute-start.2) | collective-permute-done | bytes 20512 | tf_op jit(solution)/shard_map/ppermute | solution.py:79
  13.8 0.7 pad_maximum_fusion.1
  14.5 1.5 %collective-permute-start.3 = (bf16[64,640]{1,0:T(8,128)(2,1)S(1)}, bf16[64,640]{1,0:T(8,128)(2,1)S(1)}, u32[]{:S(2)}, u32[]{:S(2)}) collective-permute-start(bf16[64,640]{1,0:T(8,128)(2,1)S(1)} %pad_maximum_fusion.1), channel_id=1, source_target_pairs={{0,2},{1,3},{2,0},{3,1},{4,6},{5,7},{6,4},{7,5},{8,10},{9,11},{10,... | collective-permute-start | bytes 245768 | tf_op jit(solution)/shard_map/ppermute | solution.py:81
  16.0 2.9 %collective-permute-done.3 = bf16[64,640]{1,0:T(8,128)(2,1)S(1)} collective-permute-done((bf16[64,640]{1,0:T(8,128)(2,1)S(1)}, bf16[64,640]{1,0:T(8,128)(2,1)S(1)}, u32[]{:S(2)}, u32[]{:S(2)}) %collective-permute-start.3) | collective-permute-done | bytes 81952 | tf_op jit(solution)/shard_map/ppermute | solution.py:81
  19.0 0.1 collective-permute-start.4
  19.0 6.4 %front.1 = (bf16[1024,1024]{1,0:T(8,128)(2,1)}, bf16[1024,1024]{1,0:T(8,128)(2,1)}) custom-call(bf16[1024,1024]{1,0:T(8,128)(2,1)} %x_ref.3, f32[1,1024]{1,0:T(1,128)} %bitcast.11, bf16[1024,1024]{1,0:T(8,128)(2,1)} %w_ref.5), custom_call_target="tpu_custom_call" | custom-call | flops 2147483648 | bytes 8388608 | tf_op jit(solution)/shard_map/front/pallas_call | solution.py:348
  25.5 0.0 collective-permute-done.4.far_ref
  25.5 0.7 copy-done.9
  26.1 6.4 %partial.1 = (bf16[64,640]{1,0:T(8,128)(2,1)}, bf16[64,640]{1,0:T(8,128)(2,1)}, bf16[64,640]{1,0:T(8,128)(2,1)}, bf16[64,640]{1,0:T(8,128)(2,1)}) custom-call(bf16[128,640]{1,0:T(8,128)(2,1)} %copy-done.7, bf16[128,640]{1,0:T(8,128)(2,1)} %copy-done.9, bf16[1024,1024]{1,0:T(8,128)(2,1)} %get-tuple-element.16.pairs_ref), custom_call_target="tpu_custom_call" | custom-call | flops 1073741824 | bytes 2097152 | tf_op jit(solution)/shard_map/partial/pallas_call | solution.py:369
  32.5 1.5 %collective-permute-start.5 = (bf16[64,640]{1,0:T(8,128)(2,1)}, bf16[64,640]{1,0:T(8,128)(2,1)S(1)}, u32[]{:S(2)}, u32[]{:S(2)}) collective-permute-start(bf16[64,640]{1,0:T(8,128)(2,1)} %get-tuple-element.18), channel_id=1, source_target_pairs={{0,2},{1,3},{2,0},{3,1},{4,6},{5,7},{6,4},{7,5},{8,10},{9,11},{10,... | collective-permute-start | bytes 245768 | tf_op jit(solution)/shard_map/ppermute | solution.py:378
  34.1 0.2 collective-permute-start.6
  34.3 0.4 collective-permute-start.7
  34.7 3.0 %collective-permute-done.5.refs_0_ = bf16[64,640]{1,0:T(8,128)(2,1)S(1)} collective-permute-done((bf16[64,640]{1,0:T(8,128)(2,1)}, bf16[64,640]{1,0:T(8,128)(2,1)S(1)}, u32[]{:S(2)}, u32[]{:S(2)}) %collective-permute-start.5) | collective-permute-done | bytes 81952 | tf_op jit(solution)/shard_map/ppermute | solution.py:378
  37.7 0.0 collective-permute-done.6.refs_1_
  37.7 1.3 %collective-permute-done.7.refs_2_ = bf16[64,640]{1,0:T(8,128)(2,1)S(1)} collective-permute-done((bf16[64,640]{1,0:T(8,128)(2,1)}, bf16[64,640]{1,0:T(8,128)(2,1)S(1)}, u32[]{:S(2)}, u32[]{:S(2)}) %collective-permute-start.7) | collective-permute-done | bytes 81952 | tf_op jit(solution)/shard_map/ppermute | solution.py:378
  39.0 0.6 copy-done.2
  39.7 2.1 %merge.1 = (bf16[16,640]{1,0:T(8,128)(2,1)}, bf16[16,640]{1,0:T(8,128)(2,1)}, bf16[16,640]{1,0:T(8,128)(2,1)}, bf16[16,640]{1,0:T(8,128)(2,1)}) custom-call(bf16[64,640]{1,0:T(8,128)(2,1)} %get-tuple-element.17.own_ref, bf16[64,640]{1,0:T(8,128)(2,1)} %copy-done, bf16[64,640]{1,0:T(8,128)(2,1)} %copy-done.1, bf16[64,640]{1,0:T(8,128)(2,1)} %copy-done.2), custom_call_target="tpu_custom_call" | custom-call | flops 33554432 | bytes 524288 | tf_op jit(solution)/shard_map/merge/pallas_call | solution.py:380
  41.7 0.0 collective-permute-start.8
  41.7 1.2 %collective-permute-start.9 = (bf16[16,640]{1,0:T(8,128)(2,1)}, bf16[16,640]{1,0:T(8,128)(2,1)S(1)}, u32[]{:S(2)}, u32[]{:S(2)}) collective-permute-start(bf16[16,640]{1,0:T(8,128)(2,1)} %get-tuple-element.23), channel_id=1, source_target_pairs={{0,8},{1,9},{2,10},{3,11},{4,12},{5,13},{6,14},{7,15},{8,0},{9,1},... | collective-permute-start | bytes 61448 | tf_op jit(solution)/shard_map/ppermute | solution.py:388
  42.9 2.9 %collective-permute-start.10 = (bf16[16,640]{1,0:T(8,128)(2,1)}, bf16[16,640]{1,0:T(8,128)(2,1)S(1)}, u32[]{:S(2)}, u32[]{:S(2)}) collective-permute-start(bf16[16,640]{1,0:T(8,128)(2,1)} %get-tuple-element.24), channel_id=1, source_target_pairs={{0,12},{1,13},{2,14},{3,15},{4,0},{5,1},{6,2},{7,3},{8,4},{9,5},{1... | collective-permute-start | bytes 61448 | tf_op jit(solution)/shard_map/ppermute | solution.py:388
  45.8 1.7 %collective-permute-done.8.refs_1_ = bf16[16,640]{1,0:T(8,128)(2,1)S(1)} collective-permute-done((bf16[16,640]{1,0:T(8,128)(2,1)}, bf16[16,640]{1,0:T(8,128)(2,1)S(1)}, u32[]{:S(2)}, u32[]{:S(2)}) %collective-permute-start.8) | collective-permute-done | bytes 20512 | tf_op jit(solution)/shard_map/ppermute | solution.py:388
  47.5 0.0 collective-permute-done.9.refs_2_
  47.5 0.6 collective-permute-done.10.refs_3_
  48.1 0.0 copy-done.3
  48.1 0.0 copy-done.4
  48.2 0.5 copy-done.5
  48.7 3.7 %combine.1 = (bf16[16,1024]{1,0:T(8,128)(2,1)}, bf16[16,1024]{1,0:T(8,128)(2,1)}) custom-call(bf16[16,640]{1,0:T(8,128)(2,1)} %get-tuple-element.21.refs_0_, bf16[16,640]{1,0:T(8,128)(2,1)} %copy-done.3, bf16[16,640]{1,0:T(8,128)(2,1)} %copy-done.4, bf16[16,640]{1,0:T(8,128)(2,1)} %copy-done.5, bf16[16,1024]{1,0:T(8,128)(2,1)} %refs_4_.1, ...), custom_call_target="tpu_custom_call" | custom-call | flops 50331648 | bytes 3145728 | tf_op jit(solution)/shard_map/combine/pallas_call | solution.py:403
  52.4 3.5 %collective-permute-start.11 = (bf16[16,1024]{1,0:T(8,128)(2,1)}, bf16[16,1024]{1,0:T(8,128)(2,1)S(1)}, u32[]{:S(2)}, u32[]{:S(2)}) collective-permute-start(bf16[16,1024]{1,0:T(8,128)(2,1)} %get-tuple-element.29), channel_id=1, source_target_pairs={{0,12},{1,13},{2,14},{3,15},{4,0},{5,1},{6,2},{7,3},{8,4},{9,5},{1... | collective-permute-start | bytes 98312 | tf_op jit(solution)/shard_map/ppermute | solution.py:79
  55.9 0.0 collective-permute-start.12
  55.9 0.6 collective-permute-start.13
  56.4 0.8 constant_dynamic-update-slice_fusion.9
  57.2 0.6 collective-permute-done.11
  57.8 3.1 %collective-permute-done.12 = bf16[16,1024]{1,0:T(8,128)(2,1)S(1)} collective-permute-done((bf16[16,1024]{1,0:T(8,128)(2,1)}, bf16[16,1024]{1,0:T(8,128)(2,1)S(1)}, u32[]{:S(2)}, u32[]{:S(2)}) %collective-permute-start.12) | collective-permute-done | bytes 32800 | tf_op jit(solution)/shard_map/ppermute | solution.py:79
  60.9 0.9 %collective-permute-done.13 = bf16[16,1024]{1,0:T(8,128)(2,1)S(1)} collective-permute-done((bf16[16,1024]{1,0:T(8,128)(2,1)}, bf16[16,1024]{1,0:T(8,128)(2,1)S(1)}, u32[]{:S(2)}, u32[]{:S(2)}) %collective-permute-start.13) | collective-permute-done | bytes 32800 | tf_op jit(solution)/shard_map/ppermute | solution.py:79
  61.8 0.8 pad_maximum_fusion
  62.6 1.5 %collective-permute-start.14 = (bf16[64,1024]{1,0:T(8,128)(2,1)S(1)}, bf16[64,1024]{1,0:T(8,128)(2,1)S(1)}, u32[]{:S(2)}, u32[]{:S(2)}) collective-permute-start(bf16[64,1024]{1,0:T(8,128)(2,1)S(1)} %pad_maximum_fusion), channel_id=1, source_target_pairs={{0,2},{1,3},{2,0},{3,1},{4,6},{5,7},{6,4},{7,5},{8,10},{9,11},{10,... | collective-permute-start | bytes 393224 | tf_op jit(solution)/shard_map/ppermute | solution.py:81
  64.0 3.6 %collective-permute-done.14 = bf16[64,1024]{1,0:T(8,128)(2,1)S(1)} collective-permute-done((bf16[64,1024]{1,0:T(8,128)(2,1)S(1)}, bf16[64,1024]{1,0:T(8,128)(2,1)S(1)}, u32[]{:S(2)}, u32[]{:S(2)}) %collective-permute-start.14) | collective-permute-done | bytes 131104 | tf_op jit(solution)/shard_map/ppermute | solution.py:81
  67.6 0.1 collective-permute-start.15
  67.7 5.8 %middle.1 = (bf16[512,1024]{1,0:T(8,128)(2,1)}, bf16[4,256,1024]{2,1,0:T(8,128)(2,1)}) custom-call(bf16[1024,1024]{1,0:T(8,128)(2,1)} %get-tuple-element.26.x_ref, bf16[1024,512]{1,0:T(8,128)(2,1)} %w_ref.6, s32[32,128]{1,0:T(8,128)} %bitcast.10, s32[4,1024]{1,0:T(4,128)} %slot_ref.1), custom_call_target="tpu_custom_call" | custom-call | flops 1073741824 | bytes 8388608 | tf_op jit(solution)/shard_map/middle/pallas_call | solution.py:392
  73.5 0.7 copy-done.8
  74.3 7.9 %decode.1 = bf16[1024,1024]{1,0:T(8,128)(2,1)} custom-call(bf16[1024,1024]{1,0:T(8,128)(2,1)} %x_ref.3, bf16[512,1024]{1,0:T(8,128)(2,1)} %get-tuple-element.27.query_ref, bf16[4,256,1024]{2,1,0:T(8,128)(2,1)} %get-tuple-element.28.pick_ref, bf16[128,1024]{1,0:T(8,128)(2,1)} %copy-done.6, bf16[128,1024]{1,0:T(8,128)(2,1)} %copy-done.8, bf16[512,1024]{1,0:T(8,128)(2,1)} %w_ref.7), custom_call_target="tpu_custom_call" | custom-call | flops 4294967296 | bytes 8388608 | tf_op jit(solution)/shard_map/decode/pallas_call | solution.py:415
  (23 shorter events, 0.1 us)
Async XLA Ops:
  2.9 6.8 %collective-permute-start = (bf16[16,640]{1,0:T(8,128)(2,1)}, bf16[16,640]{1,0:T(8,128)(2,1)S(1)}, u32[]{:S(2)}, u32[]{:S(2)}) collective-permute-start(bf16[16,640]{1,0:T(8,128)(2,1)} %ask.1), channel_id=1, source_target_pairs={{0,12},{1,13},{2,14},{3,15},{4,0},{5,1},{6,2},{7,3},{8,4},{9,5},{1... | collective-permute-start | bytes 61448 | tf_op jit(solution)/shard_map/ppermute | solution.py:79
  8.0 4.9 %collective-permute-start.1 = (bf16[16,640]{1,0:T(8,128)(2,1)}, bf16[16,640]{1,0:T(8,128)(2,1)S(1)}, u32[]{:S(2)}, u32[]{:S(2)}) collective-permute-start(bf16[16,640]{1,0:T(8,128)(2,1)} %ask.1), channel_id=1, source_target_pairs={{0,8},{1,9},{2,10},{3,11},{4,12},{5,13},{6,14},{7,15},{8,0},{9,1},... | collective-permute-start | bytes 61448 | tf_op jit(solution)/shard_map/ppermute | solution.py:79
  8.0 5.8 %collective-permute-start.2 = (bf16[16,640]{1,0:T(8,128)(2,1)}, bf16[16,640]{1,0:T(8,128)(2,1)S(1)}, u32[]{:S(2)}, u32[]{:S(2)}) collective-permute-start(bf16[16,640]{1,0:T(8,128)(2,1)} %ask.1), channel_id=1, source_target_pairs={{0,4},{1,5},{2,6},{3,7},{4,8},{5,9},{6,10},{7,11},{8,12},{9,13},{1... | collective-permute-start | bytes 61448 | tf_op jit(solution)/shard_map/ppermute | solution.py:79
  14.5 4.4 %collective-permute-start.3 = (bf16[64,640]{1,0:T(8,128)(2,1)S(1)}, bf16[64,640]{1,0:T(8,128)(2,1)S(1)}, u32[]{:S(2)}, u32[]{:S(2)}) collective-permute-start(bf16[64,640]{1,0:T(8,128)(2,1)S(1)} %pad_maximum_fusion.1), channel_id=1, source_target_pairs={{0,2},{1,3},{2,0},{3,1},{4,6},{5,7},{6,4},{7,5},{8,10},{9,11},{10,... | collective-permute-start | bytes 245768 | tf_op jit(solution)/shard_map/ppermute | solution.py:81
  18.9 6.5 %copy-start.7 = (bf16[128,640]{1,0:T(8,128)(2,1)}, bf16[128,640]{1,0:T(8,128)(2,1)S(1)}, u32[]{:S(2)}) copy-start(bf16[128,640]{1,0:T(8,128)(2,1)S(1)} %constant_dynamic-update-slice_fusion.near_ref) | copy-start | bytes 491524
  19.0 6.5 %collective-permute-start.4 = (bf16[128,640]{1,0:T(8,128)(2,1)S(1)}, bf16[128,640]{1,0:T(8,128)(2,1)S(1)}, u32[]{:S(2)}, u32[]{:S(2)}) collective-permute-start(bf16[128,640]{1,0:T(8,128)(2,1)S(1)} %constant_dynamic-update-slice_fusion.near_ref), channel_id=1, source_target_pairs={{0,1},{1,0},{2,3},{3,2},{4,5},{5,4},{6,7},{7,6},{8,9},{9,8},{10,11... | collective-permute-start | bytes 491528 | tf_op jit(solution)/shard_map/ppermute | solution.py:83
  25.5 0.7 copy-start.9
  32.5 5.1 %collective-permute-start.5 = (bf16[64,640]{1,0:T(8,128)(2,1)}, bf16[64,640]{1,0:T(8,128)(2,1)S(1)}, u32[]{:S(2)}, u32[]{:S(2)}) collective-permute-start(bf16[64,640]{1,0:T(8,128)(2,1)} %get-tuple-element.18), channel_id=1, source_target_pairs={{0,2},{1,3},{2,0},{3,1},{4,6},{5,7},{6,4},{7,5},{8,10},{9,11},{10,... | collective-permute-start | bytes 245768 | tf_op jit(solution)/shard_map/ppermute | solution.py:378
  34.1 3.6 %collective-permute-start.6 = (bf16[64,640]{1,0:T(8,128)(2,1)}, bf16[64,640]{1,0:T(8,128)(2,1)S(1)}, u32[]{:S(2)}, u32[]{:S(2)}) collective-permute-start(bf16[64,640]{1,0:T(8,128)(2,1)} %get-tuple-element.19), channel_id=1, source_target_pairs={{0,1},{1,0},{2,3},{3,2},{4,5},{5,4},{6,7},{7,6},{8,9},{9,8},{10,11... | collective-permute-start | bytes 245768 | tf_op jit(solution)/shard_map/ppermute | solution.py:378
  34.3 4.8 %collective-permute-start.7 = (bf16[64,640]{1,0:T(8,128)(2,1)}, bf16[64,640]{1,0:T(8,128)(2,1)S(1)}, u32[]{:S(2)}, u32[]{:S(2)}) collective-permute-start(bf16[64,640]{1,0:T(8,128)(2,1)} %get-tuple-element.20), channel_id=1, source_target_pairs={{0,3},{1,2},{2,1},{3,0},{4,7},{5,6},{6,5},{7,4},{8,11},{9,10},{10,... | collective-permute-start | bytes 245768 | tf_op jit(solution)/shard_map/ppermute | solution.py:378
  37.7 1.4 %copy-start = (bf16[64,640]{1,0:T(8,128)(2,1)}, bf16[64,640]{1,0:T(8,128)(2,1)S(1)}, u32[]{:S(2)}) copy-start(bf16[64,640]{1,0:T(8,128)(2,1)S(1)} %collective-permute-done.5.refs_0_) | copy-start | bytes 245764
  37.7 1.4 %copy-start.1 = (bf16[64,640]{1,0:T(8,128)(2,1)}, bf16[64,640]{1,0:T(8,128)(2,1)S(1)}, u32[]{:S(2)}) copy-start(bf16[64,640]{1,0:T(8,128)(2,1)S(1)} %collective-permute-done.6.refs_1_) | copy-start | bytes 245764
  39.0 0.6 copy-start.2
  41.7 5.8 %collective-permute-start.8 = (bf16[16,640]{1,0:T(8,128)(2,1)}, bf16[16,640]{1,0:T(8,128)(2,1)S(1)}, u32[]{:S(2)}, u32[]{:S(2)}) collective-permute-start(bf16[16,640]{1,0:T(8,128)(2,1)} %get-tuple-element.22), channel_id=1, source_target_pairs={{0,4},{1,5},{2,6},{3,7},{4,8},{5,9},{6,10},{7,11},{8,12},{9,13},{1... | collective-permute-start | bytes 61448 | tf_op jit(solution)/shard_map/ppermute | solution.py:388
  41.7 5.8 %collective-permute-start.9 = (bf16[16,640]{1,0:T(8,128)(2,1)}, bf16[16,640]{1,0:T(8,128)(2,1)S(1)}, u32[]{:S(2)}, u32[]{:S(2)}) collective-permute-start(bf16[16,640]{1,0:T(8,128)(2,1)} %get-tuple-element.23), channel_id=1, source_target_pairs={{0,8},{1,9},{2,10},{3,11},{4,12},{5,13},{6,14},{7,15},{8,0},{9,1},... | collective-permute-start | bytes 61448 | tf_op jit(solution)/shard_map/ppermute | solution.py:388
  42.9 5.2 %collective-permute-start.10 = (bf16[16,640]{1,0:T(8,128)(2,1)}, bf16[16,640]{1,0:T(8,128)(2,1)S(1)}, u32[]{:S(2)}, u32[]{:S(2)}) collective-permute-start(bf16[16,640]{1,0:T(8,128)(2,1)} %get-tuple-element.24), channel_id=1, source_target_pairs={{0,12},{1,13},{2,14},{3,15},{4,0},{5,1},{6,2},{7,3},{8,4},{9,5},{1... | collective-permute-start | bytes 61448 | tf_op jit(solution)/shard_map/ppermute | solution.py:388
  47.5 0.6 copy-start.3
  47.5 0.6 copy-start.4
  48.1 0.6 copy-start.5
  52.4 5.4 %collective-permute-start.11 = (bf16[16,1024]{1,0:T(8,128)(2,1)}, bf16[16,1024]{1,0:T(8,128)(2,1)S(1)}, u32[]{:S(2)}, u32[]{:S(2)}) collective-permute-start(bf16[16,1024]{1,0:T(8,128)(2,1)} %get-tuple-element.29), channel_id=1, source_target_pairs={{0,12},{1,13},{2,14},{3,15},{4,0},{5,1},{6,2},{7,3},{8,4},{9,5},{1... | collective-permute-start | bytes 98312 | tf_op jit(solution)/shard_map/ppermute | solution.py:79
  55.9 5.0 %collective-permute-start.12 = (bf16[16,1024]{1,0:T(8,128)(2,1)}, bf16[16,1024]{1,0:T(8,128)(2,1)S(1)}, u32[]{:S(2)}, u32[]{:S(2)}) collective-permute-start(bf16[16,1024]{1,0:T(8,128)(2,1)} %get-tuple-element.29), channel_id=1, source_target_pairs={{0,8},{1,9},{2,10},{3,11},{4,12},{5,13},{6,14},{7,15},{8,0},{9,1},... | collective-permute-start | bytes 98312 | tf_op jit(solution)/shard_map/ppermute | solution.py:79
  55.9 5.9 %collective-permute-start.13 = (bf16[16,1024]{1,0:T(8,128)(2,1)}, bf16[16,1024]{1,0:T(8,128)(2,1)S(1)}, u32[]{:S(2)}, u32[]{:S(2)}) collective-permute-start(bf16[16,1024]{1,0:T(8,128)(2,1)} %get-tuple-element.29), channel_id=1, source_target_pairs={{0,4},{1,5},{2,6},{3,7},{4,8},{5,9},{6,10},{7,11},{8,12},{9,13},{1... | collective-permute-start | bytes 98312 | tf_op jit(solution)/shard_map/ppermute | solution.py:79
  62.6 5.0 %collective-permute-start.14 = (bf16[64,1024]{1,0:T(8,128)(2,1)S(1)}, bf16[64,1024]{1,0:T(8,128)(2,1)S(1)}, u32[]{:S(2)}, u32[]{:S(2)}) collective-permute-start(bf16[64,1024]{1,0:T(8,128)(2,1)S(1)} %pad_maximum_fusion), channel_id=1, source_target_pairs={{0,2},{1,3},{2,0},{3,1},{4,6},{5,7},{6,4},{7,5},{8,10},{9,11},{10,... | collective-permute-start | bytes 393224 | tf_op jit(solution)/shard_map/ppermute | solution.py:81
  67.6 5.9 %copy-start.6 = (bf16[128,1024]{1,0:T(8,128)(2,1)}, bf16[128,1024]{1,0:T(8,128)(2,1)S(1)}, u32[]{:S(2)}) copy-start(bf16[128,1024]{1,0:T(8,128)(2,1)S(1)} %constant_dynamic-update-slice_fusion.5.near_ref) | copy-start | bytes 786436
  67.6 5.9 %collective-permute-start.15 = (bf16[128,1024]{1,0:T(8,128)(2,1)S(1)}, bf16[128,1024]{1,0:T(8,128)(2,1)S(1)}, u32[]{:S(2)}, u32[]{:S(2)}) collective-permute-start(bf16[128,1024]{1,0:T(8,128)(2,1)S(1)} %constant_dynamic-update-slice_fusion.5.near_ref), channel_id=1, source_target_pairs={{0,1},{1,0},{2,3},{3,2},{4,5},{5,4},{6,7},{7,6},{8,9},{9,8},{10,11... | collective-permute-start | bytes 786440 | tf_op jit(solution)/shard_map/ppermute | solution.py:83
  73.5 0.7 copy-start.8

commit v3 on v2

v3 whole, which is shorter than its diff:
```python
import functools
import math

import jax
import jax.numpy as jnp
from jax import lax
from jax.experimental import pallas as pl
from jax.experimental.pallas import tpu as pltpu
from jax.sharding import PartitionSpec as P

HEADS = 8
LANES = 128
NEG = -1e30
norm_eps = 1e-06
f32 = jnp.float32
bf16 = jnp.bfloat16


def iota(shape, dim):
    return lax.broadcasted_iota(jnp.int32, shape, dim)


def div(values, by):
    if by & (by - 1) == 0:
        return values >> (by.bit_length() - 1)
    return values // by


def mod(values, by):
    if by & (by - 1) == 0:
        return values & (by - 1)
    return values % by


def dot(a, b):
    return jnp.dot(a, b, preferred_element_type=f32)


def dot_t(a, b):
    return lax.dot_general(a, b, (((1,), (1,)), ((), ())), preferred_element_type=f32)


def normed(values, gain):
    widened = values.astype(f32)
    spread = jnp.mean(widened * widened, axis=-1, keepdims=True)
    return (widened * lax.rsqrt(spread + norm_eps) * gain).astype(bf16)


def params(mib, grid_dims=0):
    return pltpu.CompilerParams(
        vmem_limit_bytes=mib * 2**20,
        dimension_semantics=("arbitrary",) * grid_dims if grid_dims else None,
    )


def cost(flops, read, exps=0):
    return pl.CostEstimate(flops=int(flops), bytes_accessed=int(read), transcendentals=int(exps))


def column_groups(far):
    return [[z * 4 + p for z in range(far)] for p in range(4)]


def plane_groups(far):
    return [[z * 4 + p for p in range(4)] for z in range(far)]


def ask_kernel(latent_ref, gain_ref, w_ref, slot_ref, count_ref, need_ref, out_ref):
    rows = latent_ref.shape[0]
    width = w_ref.shape[1]
    entries = need_ref.shape[1]
    edges = slot_ref.shape[1]
    per = entries // rows
    queries = dot(normed(latent_ref[...], gain_ref[...]), w_ref[...]).astype(bf16)
    eye = iota((rows, rows), 0) == iota((rows, rows), 1)
    counts = jnp.sum(jnp.where(eye, count_ref[...], 0), axis=1, keepdims=True)
    slots = jnp.where(iota((rows, edges), 1) < counts, slot_ref[...], 65535)
    need = need_ref[...]
    own = div(iota((rows, entries), 1), per) == iota((rows, entries), 0)
    extra = jnp.zeros((rows, LANES), f32)
    for i, part in enumerate((slots & 255, slots >> 8)):
        to = iota((edges, LANES), 1) == iota((edges, LANES), 0) + i * edges
        extra += dot(part.astype(f32).astype(bf16), to.astype(bf16))
    for i, part in enumerate((need & 255, need >> 8)):
        to = iota((entries, LANES), 1) == mod(iota((entries, LANES), 0), per) + 2 * edges + i * per
        spread = jnp.where(own, part.astype(f32), 0.0).astype(bf16)
        extra += dot(spread, to.astype(bf16))
    for i in range(out_ref.shape[0]):
        out_ref[i, :, :width] = queries
        out_ref[i, :, width:] = extra.astype(bf16)


def front_kernel(x_ref, gain_ref, w_kv_ref, w_q_ref, pairs_ref, query_ref):
    rows = normed(x_ref[...], gain_ref[...])
    pairs_ref[...] = dot(rows, w_kv_ref[...]).astype(bf16)
    query_ref[...] = dot(rows, w_q_ref[...]).T.astype(bf16)


def head_keys(keys, h, size):
    per = LANES // size
    part = keys[:, h // per * LANES : (h // per + 1) * LANES]
    return jnp.where(div(iota(part.shape, 1), size) == h % per, part, jnp.zeros_like(part))


def stat_parts(top, total):
    top_1 = top.astype(bf16).astype(f32)
    top_2 = (top - top_1).astype(bf16).astype(f32)
    total_1 = total.astype(bf16).astype(f32)
    return top_1, top_2, top - top_1 - top_2, total_1, total - total_1


def partial_kernel(cap, rows, edges, asked_ref, pairs_ref, out_ref, mixed_ref):
    me = lax.axis_index("dom")
    points, both = pairs_ref.shape
    peers = out_ref.shape[0]
    far = peers // 4
    width = both // 2
    size = width // HEADS
    per = cap * peers // rows
    scale = math.log2(math.e) / math.sqrt(size)
    all_nodes = asked_ref.shape[0]
    all_entries = peers * cap
    list_row, list_lane = div(me * cap, per), mod(me * cap, per)
    pick_shape = (all_entries, all_nodes)
    pick = iota(pick_shape, 1) == div(iota(pick_shape, 0), cap) * rows + list_row
    lane = iota((all_entries, LANES), 1)
    within = mod(iota((all_entries, LANES), 0), cap)
    low_lane = within + (2 * edges + list_lane)
    weights = jnp.where(lane == low_lane, 1.0, jnp.where(lane == low_lane + per, 256.0, 0.0))
    lists = dot(pick.astype(bf16), asked_ref[:, width:])
    index = jnp.sum(lists * weights, axis=1, keepdims=True).astype(jnp.int32)
    chosen = (index == iota((all_entries, points), 1)).astype(bf16)
    all_keys = dot(chosen, pairs_ref[:, :width]).astype(bf16)
    all_values = dot(chosen, pairs_ref[:, width:]).astype(bf16)

    nodes, entries = all_nodes // 2, all_entries // 2
    here = div(iota((entries, nodes), 0), cap) == div(iota((entries, nodes), 1), rows)
    listed = -(-cap // 8) * 8
    repeat = iota((entries, listed), 1) == mod(iota((entries, listed), 0), cap)
    for half in range(2):
        own = slice(half * nodes, (half + 1) * nodes)
        keys = all_keys[half * entries : (half + 1) * entries]
        values_t = all_values[half * entries : (half + 1) * entries].T
        extra_t = asked_ref[own, width:].astype(f32).T
        slots = (extra_t[:edges] + 256.0 * extra_t[edges : 2 * edges]).astype(jnp.int32) - me * cap
        uses = jnp.zeros((listed, nodes), f32)
        for j in range(edges):
            uses += jnp.where(slots[j : j + 1] == iota((listed, nodes), 0), 1.0, 0.0)
        uses = dot(repeat.astype(bf16), uses.astype(bf16))
        live = here & (uses > 0.5)
        bias = jnp.where(live, jnp.log2(jnp.where(live, uses, 1.0)), NEG)
        tops, totals = [], []
        for h in range(HEADS):
            at = h * size // LANES * LANES
            queries = asked_ref[own, at : at + LANES]
            scores = dot_t(head_keys(keys, h, size), queries) * scale + bias
            top = jnp.max(scores, axis=0, keepdims=True)
            raised = jnp.exp2(scores - top)
            tops.append(top)
            totals.append(jnp.sum(raised, axis=0, keepdims=True))
            mixed_ref[h * size : (h + 1) * size, :] = dot(
                values_t[h * size : (h + 1) * size, :], raised.astype(bf16)
            )
        stats = stat_parts(jnp.concatenate(tops, axis=0), jnp.concatenate(totals, axis=0))
        for i, part in enumerate(stats):
            mixed_ref[width + i * HEADS : width + (i + 1) * HEADS, :] = part
        rest = mixed_ref.shape[0] - width - len(stats) * HEADS
        mixed_ref[width + len(stats) * HEADS :, :] = jnp.zeros((rest, nodes), f32)
        result = mixed_ref[...].T.astype(bf16)
        for i in range(peers // 2):
            place = half * (peers // 2) + i
            out_ref[place % far * 4 + place // far] = result[i * rows : (i + 1) * rows]


def read_stats(stats):
    col, head = iota((LANES, LANES), 0), iota((LANES, LANES), 1)
    head_of = mod(col, HEADS) == head
    take_top = head_of & (col < 3 * HEADS)
    take_sum = head_of & (col >= 3 * HEADS) & (col < 5 * HEADS)
    return dot(stats, take_top.astype(bf16)), dot(stats, take_sum.astype(bf16))


def spread_heads(factor, width):
    size = width // HEADS
    spread = (div(iota((LANES, width), 1), size) == iota((LANES, width), 0)).astype(bf16)
    factor_1 = factor.astype(bf16)
    factor_2 = (factor - factor_1.astype(f32)).astype(bf16)
    return dot(factor_1, spread) + dot(factor_2, spread)


def combine_kernel(parts_ref, latent_ref, gain_ref, w_o_ref, w_kv_ref, latent_out_ref, out_ref):
    peers, rows, sent = parts_ref.shape
    width = w_o_ref.shape[0]
    parts = parts_ref[...].reshape(peers * rows, sent)
    top, total = read_stats(parts[:, width:])
    top = top.reshape(peers, rows, LANES)
    factor = jnp.exp2(top - jnp.max(top, axis=0, keepdims=True))
    total = jnp.sum(total.reshape(peers, rows, LANES) * factor, axis=0, keepdims=True)
    used = iota((1, rows, LANES), 2) < HEADS
    factor = factor * jnp.where(used, 1.0 / jnp.where(used, total, 1.0), 0.0)
    wide = spread_heads(factor.reshape(peers * rows, LANES), width)
    mixed = jnp.sum((parts[:, :width].astype(f32) * wide).reshape(peers, rows, width), axis=0)
    update = dot(mixed.astype(bf16), w_o_ref[...])
    latent_out = (latent_ref[...].astype(f32) + update).astype(bf16)
    latent_out_ref[...] = latent_out
    out_ref[...] = dot(normed(latent_out, gain_ref[...]), w_kv_ref[...]).astype(bf16)


def picks_kernel(cap, rows, far, need_ref, slot_ref, pick_ref):
    edges, nodes, points = pick_ref.shape
    high_count = need_ref.shape[0]
    need = need_ref[...].astype(f32).astype(bf16)
    for j in range(edges):
        slots = slot_ref[j : j + 1, :]
        row_of = (div(slots, LANES) == iota((high_count, points), 0)).astype(bf16)
        listed = lax.dot_general(need, row_of, (((0,), (0,)), ((), ())), preferred_element_type=f32)
        own = mod(slots, LANES) == iota((LANES, points), 0)
        found = jnp.sum(jnp.where(own, listed, 0.0), axis=0, keepdims=True).astype(jnp.int32)
        owner = div(slots, cap)
        node = (mod(owner, 4) * far + div(owner, 4)) * rows + found
        pick_ref[j] = (node == iota((nodes, points), 0)).astype(bf16)


def decode_kernel(x_ref, query_ref, pick_ref, nodes_ref, w_ref, out_ref, pairs_ref):
    width, points = query_ref.shape
    edges = pick_ref.shape[0]
    size = width // HEADS
    half = width // 2

    @pl.when(pl.program_id(0) == 0)
    def _():
        pairs_ref[...] = nodes_ref[...].T

    scores = []
    for j in range(edges):
        parts = []
        for start in (0, half):
            keys = dot(pairs_ref[start : start + half, :], pick_ref[j])
            products = keys * query_ref[start : start + half, :].astype(f32)
            parts.append(jnp.sum(products.reshape(HEADS // 2, size, points), axis=1))
        scores.append(jnp.concatenate(parts, axis=0) * (1.0 / math.sqrt(size)))
    highest = functools.reduce(jnp.maximum, scores)
    raised = [jnp.exp(score - highest) for score in scores]
    inverse = 1.0 / sum(raised)
    weights = [(one * inverse).astype(bf16).astype(f32) for one in raised]
    mixed = []
    for start in (0, half):
        total = jnp.zeros((HEADS // 2, size, points), f32)
        for j in range(edges):
            values = dot(pairs_ref[width + start : width + start + half, :], pick_ref[j])
            first = start // size
            weight = weights[j][first : first + HEADS // 2].reshape(HEADS // 2, 1, points)
            total += values.reshape(HEADS // 2, size, points) * weight
        mixed.append(total.reshape(half, points).T.astype(bf16))
    update = dot(jnp.concatenate(mixed, axis=1), w_ref[...])
    out_ref[...] = (x_ref[...].astype(f32) + update).astype(bf16)


def whole(*shape):
    return pl.BlockSpec(shape, lambda *_: (0,) * len(shape))


def on_device(
    grid,
    latent_in,
    grid_gain,
    node_gain,
    dec_gain,
    w_q_enc,
    w_kv_enc,
    w_o_enc,
    w_q_dec,
    w_kv_dec,
    w_o_dec,
    enc_need,
    enc_slot,
    enc_count,
    dec_need,
    dec_slot,
):
    peers = lax.axis_size("dom")
    far = peers // 4
    points, depth = grid.shape
    rows = latent_in.shape[0]
    width = w_q_enc.shape[1]
    nodes = peers * rows
    entries = enc_need.shape[1]
    edges = enc_slot.shape[0]
    cap = entries // peers
    sent = width + LANES
    block = math.gcd(points, 256)

    asked = pl.pallas_call(
        ask_kernel,
        out_shape=jax.ShapeDtypeStruct((far, rows, sent), bf16),
        compiler_params=params(58),
        cost_estimate=cost(2 * rows * depth * width, 2 * depth * width),
        name="ask",
    )(
        latent_in,
        node_gain.reshape(1, -1),
        w_q_enc,
        enc_slot.T,
        enc_count.reshape(1, -1),
        enc_need,
    )
    asked = lax.all_to_all(asked, "dom", 0, 0, tiled=True, axis_index_groups=column_groups(far))
    asked = jnp.broadcast_to(asked.reshape(1, far * rows, sent), (4, far * rows, sent))
    asked = lax.all_to_all(asked, "dom", 0, 0, tiled=True, axis_index_groups=plane_groups(far))

    pairs, queries = pl.pallas_call(
        front_kernel,
        grid=(points // block,),
        in_specs=[
            pl.BlockSpec((block, depth), lambda i: (i, 0)),
            whole(1, depth),
            whole(depth, 2 * width),
            whole(depth, width),
        ],
        out_specs=[
            pl.BlockSpec((block, 2 * width), lambda i: (i, 0)),
            pl.BlockSpec((width, block), lambda i: (0, i)),
        ],
        out_shape=[
            jax.ShapeDtypeStruct((points, 2 * width), bf16),
            jax.ShapeDtypeStruct((width, points), bf16),
        ],
        compiler_params=params(58, 1),
        cost_estimate=cost(6 * points * depth * width, 8 * points * depth),
        name="front",
    )(grid, grid_gain.reshape(1, -1), w_kv_enc, w_q_dec)

    parts = pl.pallas_call(
        functools.partial(partial_kernel, cap, rows, edges),
        out_shape=jax.ShapeDtypeStruct((peers, rows, sent), bf16),
        scratch_shapes=[pltpu.VMEM((sent, nodes // 2), f32)],
        compiler_params=params(58),
        cost_estimate=cost(4 * entries * points * width, 4 * points * width),
        name="partial",
    )(asked.reshape(nodes, sent), pairs)
    parts = lax.all_to_all(parts, "dom", split_axis=0, concat_axis=0, tiled=True)

    slot_total = dec_need.shape[1]
    picks = pl.pallas_call(
        functools.partial(picks_kernel, slot_total // peers, rows, far),
        out_shape=jax.ShapeDtypeStruct((dec_slot.shape[0], nodes, points), bf16),
        compiler_params=params(58),
        cost_estimate=cost(points * nodes * LANES, 8 * points * nodes),
        name="picks",
    )(dec_need.reshape(slot_total // LANES, LANES), dec_slot)

    latent_out, everyone = pl.pallas_call(
        combine_kernel,
        out_shape=[
            jax.ShapeDtypeStruct((rows, depth), bf16),
            jax.ShapeDtypeStruct((rows, 2 * width), bf16),
        ],
        compiler_params=params(24),
        cost_estimate=cost(6 * rows * depth * width, 6 * depth * width),
        name="combine",
    )(parts, latent_in, dec_gain.reshape(1, -1), w_o_enc, w_kv_dec)
    for groups in (column_groups(far), plane_groups(far)):
        everyone = lax.all_gather(everyone, "dom", tiled=True, axis_index_groups=groups)

    grid_out = pl.pallas_call(
        decode_kernel,
        grid=(points // block,),
        in_specs=[
            pl.BlockSpec((block, depth), lambda i: (i, 0)),
            pl.BlockSpec((width, block), lambda i: (0, i)),
            pl.BlockSpec((dec_slot.shape[0], nodes, block), lambda i: (0, 0, i)),
            whole(nodes, 2 * width),
            whole(width, depth),
        ],
        out_specs=pl.BlockSpec((block, depth), lambda i: (i, 0)),
        out_shape=jax.ShapeDtypeStruct((points, depth), bf16),
        scratch_shapes=[pltpu.VMEM((2 * width, nodes), bf16)],
        compiler_params=params(58, 1),
        cost_estimate=cost(8 * points * depth * width, 8 * points * depth),
        name="decode",
    )(grid, queries, picks, everyone, w_o_dec)
    return (latent_out, grid_out)


def solution(mesh):
    return jax.shard_map(
        on_device,
        mesh=mesh,
        in_specs=(
            P(("groups", "dom"), None),
            P(("groups", "dom"), None),
            P(),
            P(),
            P(),
            P(),
            P(),
            P(),
            P(),
            P(),
            P(),
            P("dom", None),
            P(None, "dom"),
            P("dom"),
            P("dom", None),
            P(None, "dom"),
        ),
        out_specs=(P(("groups", "dom"), None), P(("groups", "dom"), None)),
        check_vma=False,
    )
```

time: 82.8 us -> 79.4 us (0.959)
  blocking collectives: 0 us -> 32.4 us
  waiting for transfers between devices: 21.7 us -> 7.67 us
  starting transfers between devices: 19.4 us -> 7.39 us
  Pallas kernels: 34.6 us -> 29.2 us
  local copies, waits for them, and re-layouts: 4.25 us -> 1.5 us
  other arithmetic: 1.5 us -> 0 us
    ppermute x16 -> x0, waiting for transfers between devices: 21.7 us -> none  [the longest x6 8.58 us: gather_half(): lax.ppermute(block, 'dom', far_perm(far, -s))]
    all_gather x0 -> x2, blocking collectives: none -> 20.3 us  [on_device(): lax.all_gather(everyone, 'dom', tiled=True, axis_index_groups=groups)]
    ppermute x16 -> x0, starting transfers between devices: 19.4 us -> none  [the longest x6 10.1 us: gather_half(): lax.ppermute(block, 'dom', far_perm(far, -s))]
    all_to_all x0 -> x1, blocking collectives: none -> 12.1 us  [on_device(): lax.all_to_all(asked, 'dom', 0, 0, tiled=True, axis_index_groups=column_g...]
    all_to_all x0 -> x2, waiting for transfers between devices: none -> 7.67 us  [the longest x1 7.67 us: on_device(): lax.all_to_all(parts, 'dom', split_axis=0, concat_axis=0, tiled=True)]
    all_to_all x0 -> x2, starting transfers between devices: none -> 7.39 us  [the longest x1 3.93 us: on_device(): lax.all_to_all(parts, 'dom', split_axis=0, concat_axis=0, tiled=True)]
    pallas_call x4 -> x3, Pallas kernels: 13.9 us -> 7.36 us  [the longest x1 3.43 us: on_device(): pl.pallas_call(functools.partial(picks_kernel, slot_total // peers, rows,...]
    unnamed x28 -> x10, local copies, waits for them, and re-layouts: 4.22 us -> 0.74 us
  transfers between devices with their start and end apart: 16 -> 2, of which waited for: 11 -> 1; matrix products, arithmetic and copies ran while one was open for 2% -> 0% of each run, Pallas kernels for 15% -> 14%
where the time goes in v3:
time: 79.4 us; the launch traced here: 78.8 us
  blocking collectives  32.4 us (41%)
  Pallas kernels  29.2 us (37%)
  waiting for transfers between devices  7.67 us (10%)
  starting transfers between devices  7.39 us (9%)
  local copies, waits for them, and re-layouts  1.5 us (2%)
    all_gather x2, blocking collectives, on_device(): lax.all_gather(everyone, 'dom', tiled=True, axis_index_groups=groups)  20.3 us
    all_to_all x1, blocking collectives, on_device(): lax.all_to_all(asked, 'dom', 0, 0, tiled=True, axis_index_groups=column_g...  12.1 us
    pallas_call x1, Pallas kernels, on_device(): pl.pallas_call(decode_kernel, grid=(points // block,), in_specs=[pl.Block...  7.99 us
    all_to_all x1, waiting for transfers between devices, on_device(): lax.all_to_all(parts, 'dom', split_axis=0, concat_axis=0, tiled=True)  7.67 us
    pallas_call x1, Pallas kernels, on_device(): pl.pallas_call(front_kernel, grid=(points // block,), in_specs=[pl.BlockS...  7.58 us
    pallas_call x1, Pallas kernels, on_device(): pl.pallas_call(functools.partial(partial_kernel, cap, rows, edges), out_s...  6.27 us
    all_to_all x1, starting transfers between devices, on_device(): lax.all_to_all(parts, 'dom', split_axis=0, concat_axis=0, tiled=True)  3.93 us
    all_to_all x1, starting transfers between devices, on_device(): lax.all_to_all(asked, 'dom', 0, 0, tiled=True, axis_index_groups=plane_gr...  3.45 us
  transfers between devices with their start and end apart: 2, of which 1 were waited for; matrix products, arithmetic and copies ran while one was open for 0% of the time, Pallas kernels for 14%

profile of v3, /device:TPU:0, one launch (start us, length us, event | category | flops | bytes accessed | tf_op | source)
XLA Modules:
  0.0 78.8 jit_solution(6886011378030497739)
XLA Ops:
  0.6 2.3 %ask.1 = bf16[4,16,640]{2,1,0:T(8,128)(2,1)} custom-call(bf16[16,1024]{1,0:T(8,128)(2,1)} %latent_ref.3, f32[1,1024]{1,0:T(1,128)} %bitcast.13, bf16[1024,512]{1,0:T(8,128)(2,1)} %w_ref.2, s32[16,32]{1,0:T(8,128)} %bitcast.12, s32[1,16]{1,0:T(1,128)} %bitcast.14, s32[1,512]{1,0:T(1,128)} %need_ref.1), custom_call_target="tpu_custom_call" | custom-call | flops 16777216 | bytes 1048576 | tf_op jit(solution)/shard_map/ask/pallas_call | solution.py:293
  2.9 12.1 %all_to_all.15 = bf16[4,16,640]{2,1,0:T(8,128)(2,1)S(1)} all-to-all(bf16[4,16,640]{2,1,0:T(8,128)(2,1)} %ask.1), channel_id=1, replica_groups={{0,4,8,12},{1,5,9,13},{2,6,10,14},{3,7,11,15},{16,20,24,28},{17,21,25,2..., dimensions={0} | all-to-all | bytes 163840 | tf_op jit(solution)/shard_map/all_to_all | solution.py:307
  15.0 0.8 broadcast_in_dim.8
  15.8 3.5 %all-to-all-start.1 = ((bf16[4,64,640]{2,1,0:T(8,128)(2,1)}), bf16[4,64,640]{2,1,0:T(8,128)(2,1)S(1)}, u32[]{:S(2)}, u32[]{:S(2)}) async-start(bf16[4,64,640]{2,1,0:T(8,128)(2,1)} %broadcast_in_dim.8), calls=%async_computation.1 | async-start | bytes 655360 | tf_op jit(solution)/shard_map/all_to_all | solution.py:309
  19.3 7.6 %front.1 = (bf16[1024,1024]{1,0:T(8,128)(2,1)}, bf16[512,1024]{1,0:T(8,128)(2,1)}) custom-call(bf16[1024,1024]{1,0:T(8,128)(2,1)} %x_ref.3, f32[1,1024]{1,0:T(1,128)} %bitcast.15, bf16[1024,1024]{1,0:T(8,128)(2,1)} %w_kv_ref.2, bf16[1024,512]{1,0:T(8,128)(2,1)} %w_q_ref.1), custom_call_target="tpu_custom_call" | custom-call | flops 3221225472 | bytes 8388608 | tf_op jit(solution)/shard_map/front/pallas_call | solution.py:311
  26.8 0.0 all-to-all-done.1
  26.9 0.0 copy-start.4
  26.9 0.7 copy-done.4
  27.6 0.0 copy-start.1
  27.6 6.3 %partial.1 = bf16[16,16,640]{2,1,0:T(8,128)(2,1)} custom-call(bf16[256,640]{1,0:T(8,128)(2,1)} %bitcast.9, bf16[1024,1024]{1,0:T(8,128)(2,1)} %get-tuple-element.6.pairs_ref), custom_call_target="tpu_custom_call" | custom-call | flops 1073741824 | bytes 2097152 | tf_op jit(solution)/shard_map/partial/pallas_call | solution.py:333
  33.9 0.0 copy-start
  33.9 0.0 copy-start.2
  33.9 0.0 copy-start.3
  33.9 3.9 %all-to-all-start.2 = ((bf16[16,16,640]{2,1,0:T(8,128)(2,1)}), bf16[16,16,640]{2,1,0:T(8,128)(2,1)S(1)}, u32[]{:S(2)}, u32[]{:S(2)}) async-start(bf16[16,16,640]{2,1,0:T(8,128)(2,1)} %partial.1), calls=%async_computation.2 | async-start | bytes 655360 | tf_op jit(solution)/shard_map/all_to_all | solution.py:341
  37.8 3.4 %picks.1.pick_ref = bf16[4,256,1024]{2,1,0:T(8,128)(2,1)} custom-call(s32[32,128]{1,0:T(8,128)} %bitcast.11, s32[4,1024]{1,0:T(4,128)} %slot_ref.1), custom_call_target="tpu_custom_call" | custom-call | flops 33554432 | bytes 2097152 | tf_op jit(solution)/shard_map/picks/pallas_call | solution.py:344
  41.2 7.7 %all-to-all-done.2.parts_ref = bf16[16,16,640]{2,1,0:T(8,128)(2,1)S(1)} async-done(((bf16[16,16,640]{2,1,0:T(8,128)(2,1)}), bf16[16,16,640]{2,1,0:T(8,128)(2,1)S(1)}, u32[]{:S(2)}, u32[]{:S(2)}) %all-to-all-start.2) | async-done | bytes 327712 | tf_op jit(solution)/shard_map/all_to_all | solution.py:341
  48.9 0.0 copy-done.1
  48.9 0.0 copy-done
  48.9 0.0 copy-done.2
  48.9 0.0 copy-done.3
  48.9 1.6 %combine.1 = (bf16[16,1024]{1,0:T(8,128)(2,1)}, bf16[16,1024]{1,0:T(8,128)(2,1)S(1)}) custom-call(bf16[16,16,640]{2,1,0:T(8,128)(2,1)S(1)} %all-to-all-done.2.parts_ref, bf16[16,1024]{1,0:T(8,128)(2,1)S(1)} %copy-done.2, f32[1,1024]{1,0:T(1,128)S(1)} %bitcast.8, bf16[512,1024]{1,0:T(8,128)(2,1)S(1)} %copy-done.1, bf16[1024,1024]{1,0:T(8,128)(2,1)S(1)} %copy-done), custom_call_target="tpu_custom_call" | custom-call | flops 50331648 | bytes 3145728 | tf_op jit(solution)/shard_map/combine/pallas_call | solution.py:352
  50.5 13.3 %all_gather.6 = bf16[64,1024]{1,0:T(8,128)(2,1)S(1)} all-gather(bf16[16,1024]{1,0:T(8,128)(2,1)S(1)} %get-tuple-element.9), channel_id=1, replica_groups={{0,4,8,12},{1,5,9,13},{2,6,10,14},{3,7,11,15},{16,20,24,28},{17,21,25,2..., dimensions={0}, use_global_device_ids=true | all-gather | bytes 163840 | tf_op jit(solution)/shard_map/all_gather | solution.py:363
  63.9 6.9 %all_gather.7.nodes_ref = bf16[256,1024]{1,0:T(8,128)(2,1)} all-gather(bf16[64,1024]{1,0:T(8,128)(2,1)S(1)} %all_gather.6), channel_id=1, replica_groups={{0,1,2,3},{4,5,6,7},{8,9,10,11},{12,13,14,15},{16,17,18,19},{20,21,22,2..., dimensions={0}, use_global_device_ids=true | all-gather | bytes 655360 | tf_op jit(solution)/shard_map/all_gather | solution.py:363
  70.8 8.0 %decode.1 = bf16[1024,1024]{1,0:T(8,128)(2,1)} custom-call(bf16[1024,1024]{1,0:T(8,128)(2,1)} %x_ref.3, bf16[512,1024]{1,0:T(8,128)(2,1)} %get-tuple-element.8.query_ref, bf16[4,256,1024]{2,1,0:T(8,128)(2,1)} %picks.1.pick_ref, bf16[256,1024]{1,0:T(8,128)(2,1)} %all_gather.7.nodes_ref, bf16[512,1024]{1,0:T(8,128)(2,1)} %w_ref.3), custom_call_target="tpu_custom_call" | custom-call | flops 4294967296 | bytes 8388608 | tf_op jit(solution)/shard_map/decode/pallas_call | solution.py:365
Async XLA Ops:
  15.8 11.0 %all-to-all-start.1 = ((bf16[4,64,640]{2,1,0:T(8,128)(2,1)}), bf16[4,64,640]{2,1,0:T(8,128)(2,1)S(1)}, u32[]{:S(2)}, u32[]{:S(2)}) async-start(bf16[4,64,640]{2,1,0:T(8,128)(2,1)} %broadcast_in_dim.8), calls=%async_computation.1 | async-start | bytes 655360 | tf_op jit(solution)/shard_map/all_to_all | solution.py:309
  26.9 0.7 copy-start.4
  27.6 21.3 %copy-start.1 = (bf16[512,1024]{1,0:T(8,128)(2,1)S(1)}, bf16[512,1024]{1,0:T(8,128)(2,1)}, u32[]{:S(2)}) copy-start(bf16[512,1024]{1,0:T(8,128)(2,1)} %w_o_ref.1) | copy-start | bytes 3145732
  33.9 15.1 %copy-start = (bf16[1024,1024]{1,0:T(8,128)(2,1)S(1)}, bf16[1024,1024]{1,0:T(8,128)(2,1)}, u32[]{:S(2)}) copy-start(bf16[1024,1024]{1,0:T(8,128)(2,1)} %w_kv_ref.3) | copy-start | bytes 6291460
  33.9 15.1 %copy-start.2 = (bf16[16,1024]{1,0:T(8,128)(2,1)S(1)}, bf16[16,1024]{1,0:T(8,128)(2,1)}, u32[]{:S(2)}) copy-start(bf16[16,1024]{1,0:T(8,128)(2,1)} %latent_ref.3) | copy-start | bytes 98308
  33.9 15.1 %copy-start.3 = (f32[1024]{0:T(1024)S(1)}, f32[1024]{0:T(1024)}, u32[]{:S(2)}) copy-start(f32[1024]{0:T(1024)} %param.20) | copy-start | bytes 12292
  33.9 15.0 %all-to-all-start.2 = ((bf16[16,16,640]{2,1,0:T(8,128)(2,1)}), bf16[16,16,640]{2,1,0:T(8,128)(2,1)S(1)}, u32[]{:S(2)}, u32[]{:S(2)}) async-start(bf16[16,16,640]{2,1,0:T(8,128)(2,1)} %partial.1), calls=%async_computation.2 | async-start | bytes 655360 | tf_op jit(solution)/shard_map/all_to_all | solution.py:341

commit v4 on v3

--- a/solution.py
+++ b/solution.py
@@ -55,14 +55,6 @@
 
 def cost(flops, read, exps=0):
     return pl.CostEstimate(flops=int(flops), bytes_accessed=int(read), transcendentals=int(exps))
-
-
-def column_groups(far):
-    return [[z * 4 + p for z in range(far)] for p in range(4)]
-
-
-def plane_groups(far):
-    return [[z * 4 + p for p in range(4)] for z in range(far)]
 
 
 def ask_kernel(latent_ref, gain_ref, w_ref, slot_ref, count_ref, need_ref, out_ref):
@@ -96,12 +88,6 @@
     query_ref[...] = dot(rows, w_q_ref[...]).T.astype(bf16)
 
 
-def head_keys(keys, h, size):
-    per = LANES // size
-    part = keys[:, h // per * LANES : (h // per + 1) * LANES]
-    return jnp.where(div(iota(part.shape, 1), size) == h % per, part, jnp.zeros_like(part))
-
-
 def stat_parts(top, total):
     top_1 = top.astype(bf16).astype(f32)
     top_2 = (top - top_1).astype(bf16).astype(f32)
@@ -113,7 +99,6 @@
     me = lax.axis_index("dom")
     points, both = pairs_ref.shape
     peers = out_ref.shape[0]
-    far = peers // 4
     width = both // 2
     size = width // HEADS
     per = cap * peers // rows
@@ -149,27 +134,34 @@
         uses = dot(repeat.astype(bf16), uses.astype(bf16))
         live = here & (uses > 0.5)
         bias = jnp.where(live, jnp.log2(jnp.where(live, uses, 1.0)), NEG)
-        tops, totals = [], []
-        for h in range(HEADS):
-            at = h * size // LANES * LANES
-            queries = asked_ref[own, at : at + LANES]
-            scores = dot_t(head_keys(keys, h, size), queries) * scale + bias
-            top = jnp.max(scores, axis=0, keepdims=True)
-            raised = jnp.exp2(scores - top)
-            tops.append(top)
-            totals.append(jnp.sum(raised, axis=0, keepdims=True))
-            mixed_ref[h * size : (h + 1) * size, :] = dot(
-                values_t[h * size : (h + 1) * size, :], raised.astype(bf16)
+        queries = asked_ref[own, :width]
+        head = div(iota(queries.shape, 1), size)
+        queries = jnp.concatenate(
+            [jnp.where(head == h, queries, jnp.zeros_like(queries)) for h in range(HEADS)], axis=0
+        )
+        scores = dot_t(keys, queries) * scale + jnp.concatenate([bias] * HEADS, axis=1)
+        top = jnp.max(scores, axis=0, keepdims=True)
+        raised = jnp.exp2(scores - top)
+        total = jnp.sum(raised, axis=0, keepdims=True)
+        raised = raised.astype(bf16)
+        for h in range(0, HEADS, 2):
+            mixed = dot(
+                values_t[h * size : (h + 2) * size, :], raised[:, h * nodes : (h + 2) * nodes]
             )
-        stats = stat_parts(jnp.concatenate(tops, axis=0), jnp.concatenate(totals, axis=0))
+            mixed_ref[h * size : (h + 1) * size, :] = mixed[:size, :nodes]
+            mixed_ref[(h + 1) * size : (h + 2) * size, :] = mixed[size:, nodes:]
+        by_head = [
+            jnp.concatenate([one[:, h * nodes : (h + 1) * nodes] for h in range(HEADS)], axis=0)
+            for one in (top, total)
+        ]
+        stats = stat_parts(*by_head)
         for i, part in enumerate(stats):
             mixed_ref[width + i * HEADS : width + (i + 1) * HEADS, :] = part
         rest = mixed_ref.shape[0] - width - len(stats) * HEADS
         mixed_ref[width + len(stats) * HEADS :, :] = jnp.zeros((rest, nodes), f32)
         result = mixed_ref[...].T.astype(bf16)
         for i in range(peers // 2):
-            place = half * (peers // 2) + i
-            out_ref[place % far * 4 + place // far] = result[i * rows : (i + 1) * rows]
+            out_ref[half * (peers // 2) + i] = result[i * rows : (i + 1) * rows]
 
 
 def read_stats(stats):
@@ -203,10 +195,15 @@
     update = dot(mixed.astype(bf16), w_o_ref[...])
     latent_out = (latent_ref[...].astype(f32) + update).astype(bf16)
     latent_out_ref[...] = latent_out
-    out_ref[...] = dot(normed(latent_out, gain_ref[...]), w_kv_ref[...]).astype(bf16)
-
-
-def picks_kernel(cap, rows, far, need_ref, slot_ref, pick_ref):
+    pairs = dot(normed(latent_out, gain_ref[...]), w_kv_ref[...]).astype(bf16)
+    half = width // 2
+    for p in range(peers):
+        at = p % 2 * half
+        out_ref[p, :, :half] = pairs[:, at : at + half]
+        out_ref[p, :, half:] = pairs[:, width + at : width + at + half]
+
+
+def picks_kernel(cap, rows, need_ref, slot_ref, pick_ref):
     edges, nodes, points = pick_ref.shape
     high_count = need_ref.shape[0]
     need = need_ref[...].astype(f32).astype(bf16)
@@ -216,43 +213,56 @@
         listed = lax.dot_general(need, row_of, (((0,), (0,)), ((), ())), preferred_element_type=f32)
         own = mod(slots, LANES) == iota((LANES, points), 0)
         found = jnp.sum(jnp.where(own, listed, 0.0), axis=0, keepdims=True).astype(jnp.int32)
-        owner = div(slots, cap)
-        node = (mod(owner, 4) * far + div(owner, 4)) * rows + found
+        node = div(slots, cap) * rows + found
         pick_ref[j] = (node == iota((nodes, points), 0)).astype(bf16)
 
 
-def decode_kernel(x_ref, query_ref, pick_ref, nodes_ref, w_ref, out_ref, pairs_ref):
-    width, points = query_ref.shape
+def attend_half(pairs_ref, queries, pick_ref):
+    half, points = queries.shape
     edges = pick_ref.shape[0]
-    size = width // HEADS
-    half = width // 2
-
+    heads = HEADS // 2
+    size = half // heads
+    scores = []
+    for j in range(edges):
+        products = dot(pairs_ref[:half, :], pick_ref[j]) * queries.astype(f32)
+        score = jnp.sum(products.reshape(heads, size, points), axis=1)
+        scores.append(score * (1.0 / math.sqrt(size)))
+    highest = functools.reduce(jnp.maximum, scores)
+    raised = [jnp.exp(score - highest) for score in scores]
+    inverse = 1.0 / sum(raised)
+    mixed = jnp.zeros((heads, size, points), f32)
+    for j in range(edges):
+        weight = (raised[j] * inverse).astype(bf16).astype(f32).reshape(heads, 1, points)
+        mixed += dot(pairs_ref[half:, :], pick_ref[j]).reshape(heads, size, points) * weight
+    return mixed.reshape(half, points).T.astype(bf16)
+
+
+def half_of(ref, first, half):
+    return ref[pl.ds(pl.multiple_of(first, half), half), :]
+
+
+def own_kernel(query_ref, pick_ref, nodes_ref, out_ref, pairs_ref):
     @pl.when(pl.program_id(0) == 0)
     def _():
         pairs_ref[...] = nodes_ref[...].T
 
-    scores = []
-    for j in range(edges):
-        parts = []
-        for start in (0, half):
-            keys = dot(pairs_ref[start : start + half, :], pick_ref[j])
-            products = keys * query_ref[start : start + half, :].astype(f32)
-            parts.append(jnp.sum(products.reshape(HEADS // 2, size, points), axis=1))
-        scores.append(jnp.concatenate(parts, axis=0) * (1.0 / math.sqrt(size)))
-    highest = functools.reduce(jnp.maximum, scores)
-    raised = [jnp.exp(score - highest) for score in scores]
-    inverse = 1.0 / sum(raised)
-    weights = [(one * inverse).astype(bf16).astype(f32) for one in raised]
-    mixed = []
-    for start in (0, half):
-        total = jnp.zeros((HEADS // 2, size, points), f32)
-        for j in range(edges):
-            values = dot(pairs_ref[width + start : width + start + half, :], pick_ref[j])
-            first = start // size
-            weight = weights[j][first : first + HEADS // 2].reshape(HEADS // 2, 1, points)
-            total += values.reshape(HEADS // 2, size, points) * weight
-        mixed.append(total.reshape(half, points).T.astype(bf16))
-    update = dot(jnp.concatenate(mixed, axis=1), w_ref[...])
+    half = out_ref.shape[1]
+    queries = half_of(query_ref, (lax.axis_index("dom") & 1) * half, half)
+    out_ref[...] = attend_half(pairs_ref, queries, pick_ref)
+
+
+def other_kernel(x_ref, query_ref, pick_ref, nodes_ref, own_ref, w_ref, out_ref, pairs_ref):
+    @pl.when(pl.program_id(0) == 0)
+    def _():
+        pairs_ref[...] = nodes_ref[...].T
+
+    half = own_ref.shape[1]
+    core = lax.axis_index("dom") & 1
+    update = dot(own_ref[...], half_of(w_ref, core * half, half))
+    queries = half_of(query_ref, (1 - core) * half, half)
+    update += dot(
+        attend_half(pairs_ref, queries, pick_ref), half_of(w_ref, (1 - core) * half, half)
+    )
     out_ref[...] = (x_ref[...].astype(f32) + update).astype(bf16)
 
 
@@ -279,7 +289,6 @@
     dec_slot,
 ):
     peers = lax.axis_size("dom")
-    far = peers // 4
     points, depth = grid.shape
     rows = latent_in.shape[0]
     width = w_q_enc.shape[1]
@@ -292,7 +301,7 @@
 
     asked = pl.pallas_call(
         ask_kernel,
-        out_shape=jax.ShapeDtypeStruct((far, rows, sent), bf16),
+        out_shape=jax.ShapeDtypeStruct((peers, rows, sent), bf16),
         compiler_params=params(58),
         cost_estimate=cost(2 * rows * depth * width, 2 * depth * width),
         name="ask",
@@ -304,9 +313,7 @@
         enc_count.reshape(1, -1),
         enc_need,
     )
-    asked = lax.all_to_all(asked, "dom", 0, 0, tiled=True, axis_index_groups=column_groups(far))
-    asked = jnp.broadcast_to(asked.reshape(1, far * rows, sent), (4, far * rows, sent))
-    asked = lax.all_to_all(asked, "dom", 0, 0, tiled=True, axis_index_groups=plane_groups(far))
+    asked = lax.all_to_all(asked, "dom", split_axis=0, concat_axis=0, tiled=True)
 
     pairs, queries = pl.pallas_call(
         front_kernel,
@@ -342,7 +349,7 @@
 
     slot_total = dec_need.shape[1]
     picks = pl.pallas_call(
-        functools.partial(picks_kernel, slot_total // peers, rows, far),
+        functools.partial(picks_kernel, slot_total // peers, rows),
         out_shape=jax.ShapeDtypeStruct((dec_slot.shape[0], nodes, points), bf16),
         compiler_params=params(58),
         cost_estimate=cost(points * nodes * LANES, 8 * points * nodes),
@@ -353,32 +360,46 @@
         combine_kernel,
         out_shape=[
             jax.ShapeDtypeStruct((rows, depth), bf16),
-            jax.ShapeDtypeStruct((rows, 2 * width), bf16),
+            jax.ShapeDtypeStruct((peers, rows, width), bf16),
         ],
         compiler_params=params(24),
         cost_estimate=cost(6 * rows * depth * width, 6 * depth * width),
         name="combine",
     )(parts, latent_in, dec_gain.reshape(1, -1), w_o_enc, w_kv_dec)
-    for groups in (column_groups(far), plane_groups(far)):
-        everyone = lax.all_gather(everyone, "dom", tiled=True, axis_index_groups=groups)
-
+    own = lax.all_to_all(everyone, "dom", split_axis=0, concat_axis=0, tiled=True)
+    own = own.reshape(nodes, width)
+    other = lax.ppermute(own, "dom", [(i, i ^ 1) for i in range(peers)])
+
+    block = math.gcd(points, 512)
+    point_rows = lambda columns: pl.BlockSpec((block, columns), lambda i: (i, 0))
+    point_lanes = [
+        pl.BlockSpec((width, block), lambda i: (0, i)),
+        pl.BlockSpec((dec_slot.shape[0], nodes, block), lambda i: (0, 0, i)),
+    ]
+    own_mixed = pl.pallas_call(
+        own_kernel,
+        grid=(points // block,),
+        in_specs=point_lanes + [whole(nodes, width)],
+        out_specs=point_rows(width // 2),
+        out_shape=jax.ShapeDtypeStruct((points, width // 2), bf16),
+        scratch_shapes=[pltpu.VMEM((width, nodes), bf16)],
+        compiler_params=params(58, 1),
+        cost_estimate=cost(4 * points * nodes * width, 8 * points * nodes),
+        name="own",
+    )(queries, picks, own)
     grid_out = pl.pallas_call(
-        decode_kernel,
+        other_kernel,
         grid=(points // block,),
-        in_specs=[
-            pl.BlockSpec((block, depth), lambda i: (i, 0)),
-            pl.BlockSpec((width, block), lambda i: (0, i)),
-            pl.BlockSpec((dec_slot.shape[0], nodes, block), lambda i: (0, 0, i)),
-            whole(nodes, 2 * width),
-            whole(width, depth),
-        ],
-        out_specs=pl.BlockSpec((block, depth), lambda i: (i, 0)),
+        in_specs=[point_rows(depth)]
+        + point_lanes
+        + [whole(nodes, width), point_rows(width // 2), whole(width, depth)],
+        out_specs=point_rows(depth),
         out_shape=jax.ShapeDtypeStruct((points, depth), bf16),
-        scratch_shapes=[pltpu.VMEM((2 * width, nodes), bf16)],
+        scratch_shapes=[pltpu.VMEM((width, nodes), bf16)],
         compiler_params=params(58, 1),
-        cost_estimate=cost(8 * points * depth * width, 8 * points * depth),
-        name="decode",
-    )(grid, queries, picks, everyone, w_o_dec)
+        cost_estimate=cost(4 * points * depth * width, 8 * points * depth),
+        name="other",
+    )(grid, queries, picks, other, own_mixed, w_o_dec)
     return (latent_out, grid_out)
 
 

time: 79.4 us -> 72.1 us (0.908)
  blocking collectives: 32.4 us -> 27.7 us
  waiting for transfers between devices: 7.67 us -> 3.53 us
  Pallas kernels: 29.2 us -> 30.9 us
    all_gather x2 -> x0, blocking collectives: 20.3 us -> none  [on_device(): lax.all_gather(everyone, 'dom', tiled=True, axis_index_groups=groups)]
    all_to_all x1 -> x2, blocking collectives: 12.1 us -> 27.7 us  [the longest x1 14.6 us: on_device(): lax.all_to_all(parts, 'dom', split_axis=0, concat_axis=0, tiled=True)]
    all_to_all x2 -> x1, waiting for transfers between devices: 7.67 us -> 3.53 us  [on_device(): lax.all_to_all(asked, 'dom', split_axis=0, concat_axis=0, tiled=True)]
    pallas_call x3 -> x4, Pallas kernels: 13.7 us -> 16.3 us  [the longest x1 6.39 us: on_device(): pl.pallas_call(other_kernel, grid=(points // block,), in_specs=[point_row...]
    pallas_call x1, Pallas kernels: 6.27 us -> 5.39 us  [on_device(): pl.pallas_call(functools.partial(partial_kernel, cap, rows, edges), out_s...]
    all_to_all x2 -> x1, starting transfers between devices: 7.39 us -> 7.39 us  [on_device(): lax.all_to_all(asked, 'dom', split_axis=0, concat_axis=0, tiled=True)]
  transfers between devices with their start and end apart: 2 -> 2, of which waited for: 1 -> 1; matrix products, arithmetic and copies ran while one was open for 0% -> 0% of each run, Pallas kernels for 14% -> 21%
where the time goes in v4:
time: 72.1 us; the launch traced here: 71.6 us
  Pallas kernels  30.9 us (43%)
  blocking collectives  27.7 us (38%)
  starting transfers between devices  7.39 us (10%)
  waiting for transfers between devices  3.53 us (5%)
  local copies, waits for them, and re-layouts  1.45 us (2%)
    all_to_all x1, blocking collectives, on_device(): lax.all_to_all(parts, 'dom', split_axis=0, concat_axis=0, tiled=True)  14.6 us
    all_to_all x1, blocking collectives, on_device(): lax.all_to_all(everyone, 'dom', split_axis=0, concat_axis=0, tiled=True)  13.1 us
    pallas_call x1, Pallas kernels, on_device(): pl.pallas_call(front_kernel, grid=(points // block,), in_specs=[pl.BlockS...  7.57 us
    all_to_all x1, starting transfers between devices, on_device(): lax.all_to_all(asked, 'dom', split_axis=0, concat_axis=0, tiled=True)  7.39 us
    pallas_call x1, Pallas kernels, on_device(): pl.pallas_call(other_kernel, grid=(points // block,), in_specs=[point_row...  6.39 us
    pallas_call x1, Pallas kernels, on_device(): pl.pallas_call(functools.partial(partial_kernel, cap, rows, edges), out_s...  5.39 us
    pallas_call x1, Pallas kernels, on_device(): pl.pallas_call(own_kernel, grid=(points // block,), in_specs=point_lanes...  4.07 us
    all_to_all x1, waiting for transfers between devices, on_device(): lax.all_to_all(asked, 'dom', split_axis=0, concat_axis=0, tiled=True)  3.53 us
  transfers between devices with their start and end apart: 2, of which 1 were waited for; matrix products, arithmetic and copies ran while one was open for 0% of the time, Pallas kernels for 21%

profile of v4, /device:TPU:0, one launch (start us, length us, event | category | flops | bytes accessed | tf_op | source)
XLA Modules:
  0.0 71.6 jit_solution(17082244226510983855)
XLA Ops:
  0.6 2.4 %ask.1 = bf16[16,16,640]{2,1,0:T(8,128)(2,1)} custom-call(bf16[16,1024]{1,0:T(8,128)(2,1)} %latent_ref.3, f32[1,1024]{1,0:T(1,128)} %bitcast.14, bf16[1024,512]{1,0:T(8,128)(2,1)} %w_ref.2, s32[16,32]{1,0:T(8,128)} %bitcast.13, s32[1,16]{1,0:T(1,128)} %bitcast.15, s32[1,512]{1,0:T(1,128)} %need_ref.1), custom_call_target="tpu_custom_call" | custom-call | flops 16777216 | bytes 1048576 | tf_op jit(solution)/shard_map/ask/pallas_call | solution.py:302
  3.0 7.4 %all-to-all-start = ((bf16[16,16,640]{2,1,0:T(8,128)(2,1)}), bf16[16,16,640]{2,1,0:T(8,128)(2,1)S(1)}, u32[]{:S(2)}, u32[]{:S(2)}) async-start(bf16[16,16,640]{2,1,0:T(8,128)(2,1)} %ask.1), calls=%async_computation | async-start | bytes 655360 | tf_op jit(solution)/shard_map/all_to_all | solution.py:316
  10.4 7.6 %front.1 = (bf16[1024,1024]{1,0:T(8,128)(2,1)}, bf16[512,1024]{1,0:T(8,128)(2,1)}) custom-call(bf16[1024,1024]{1,0:T(8,128)(2,1)} %x_ref.3, f32[1,1024]{1,0:T(1,128)} %bitcast.16, bf16[1024,1024]{1,0:T(8,128)(2,1)} %w_kv_ref.2, bf16[1024,512]{1,0:T(8,128)(2,1)} %w_q_ref.1), custom_call_target="tpu_custom_call" | custom-call | flops 3221225472 | bytes 8388608 | tf_op jit(solution)/shard_map/front/pallas_call | solution.py:318
  18.0 3.5 %all-to-all-done = bf16[16,16,640]{2,1,0:T(8,128)(2,1)S(1)} async-done(((bf16[16,16,640]{2,1,0:T(8,128)(2,1)}), bf16[16,16,640]{2,1,0:T(8,128)(2,1)S(1)}, u32[]{:S(2)}, u32[]{:S(2)}) %all-to-all-start) | async-done | bytes 327712 | tf_op jit(solution)/shard_map/all_to_all | solution.py:316
  21.5 0.0 copy-start.5
  21.5 0.7 %copy-done.5 = bf16[16,16,640]{2,1,0:T(8,128)(2,1)} copy-done((bf16[16,16,640]{2,1,0:T(8,128)(2,1)}, bf16[16,16,640]{2,1,0:T(8,128)(2,1)S(1)}, u32[]{:S(2)}) %copy-start.5) | copy-done | bytes 327704
  22.3 0.0 copy-start
  22.3 0.0 copy-start.1
  22.3 0.0 copy-start.2
  22.3 0.0 copy-start.3
  22.3 5.4 %partial.1 = bf16[16,16,640]{2,1,0:T(8,128)(2,1)} custom-call(bf16[256,640]{1,0:T(8,128)(2,1)} %bitcast.11, bf16[1024,1024]{1,0:T(8,128)(2,1)} %get-tuple-element.6.pairs_ref), custom_call_target="tpu_custom_call" | custom-call | flops 1073741824 | bytes 2097152 | tf_op jit(solution)/shard_map/partial/pallas_call | solution.py:340
  27.7 14.6 %all_to_all.15.parts_ref = bf16[16,16,640]{2,1,0:T(8,128)(2,1)S(1)} all-to-all(bf16[16,16,640]{2,1,0:T(8,128)(2,1)} %partial.1), channel_id=1, replica_groups=mesh['groups'=2,'dom'=16] {'dom'}, dimensions={0} | all-to-all | bytes 655360 | tf_op jit(solution)/shard_map/all_to_all | solution.py:348
  42.2 0.0 copy-done
  42.2 0.0 copy-done.1
  42.3 0.0 copy-done.2
  42.3 0.0 copy-done.3
  42.3 1.6 %combine.1 = (bf16[16,1024]{1,0:T(8,128)(2,1)}, bf16[16,16,512]{2,1,0:T(8,128)(2,1)S(1)}) custom-call(bf16[16,16,640]{2,1,0:T(8,128)(2,1)S(1)} %all_to_all.15.parts_ref, bf16[16,1024]{1,0:T(8,128)(2,1)S(1)} %copy-done.2, f32[1,1024]{1,0:T(1,128)S(1)} %bitcast.8, bf16[512,1024]{1,0:T(8,128)(2,1)S(1)} %copy-done.1, bf16[1024,1024]{1,0:T(8,128)(2,1)S(1)} %copy-done), custom_call_target="tpu_custom_call" | custom-call | flops 50331648 | bytes 3145728 | tf_op jit(solution)/shard_map/combine/pallas_call | solution.py:359
  43.9 13.1 %all_to_all.16 = bf16[16,16,512]{2,1,0:T(8,128)(2,1)S(1)} all-to-all(bf16[16,16,512]{2,1,0:T(8,128)(2,1)S(1)} %get-tuple-element.9), channel_id=1, replica_groups=mesh['groups'=2,'dom'=16] {'dom'}, dimensions={0} | all-to-all | bytes 524288 | tf_op jit(solution)/shard_map/all_to_all | solution.py:369
  57.0 0.0 copy-start.4
  57.0 0.0 collective-permute-start
  57.0 3.5 %picks.1.pick_ref = bf16[4,256,1024]{2,1,0:T(8,128)(2,1)} custom-call(s32[32,128]{1,0:T(8,128)} %bitcast.12, s32[4,1024]{1,0:T(4,128)} %slot_ref.1), custom_call_target="tpu_custom_call" | custom-call | flops 33554432 | bytes 2097152 | tf_op jit(solution)/shard_map/picks/pallas_call | solution.py:351
  60.4 0.0 copy-done.4
  60.4 4.1 %own.1.own_ref = bf16[1024,256]{1,0:T(8,128)(2,1)} custom-call(bf16[512,1024]{1,0:T(8,128)(2,1)} %get-tuple-element.8.query_ref, bf16[4,256,1024]{2,1,0:T(8,128)(2,1)} %picks.1.pick_ref, bf16[256,512]{1,0:T(8,128)(2,1)} %bitcast.10), custom_call_target="tpu_custom_call" | custom-call | flops 536870912 | bytes 2097152 | tf_op jit(solution)/shard_map/own/pallas_call | solution.py:379
  64.5 0.0 collective-permute-done.nodes_ref
  64.5 0.0 copy-start.6
  64.5 0.7 copy-done.6
  65.2 6.4 %other.1 = bf16[1024,1024]{1,0:T(8,128)(2,1)} custom-call(bf16[1024,1024]{1,0:T(8,128)(2,1)} %x_ref.3, bf16[512,1024]{1,0:T(8,128)(2,1)} %get-tuple-element.8.query_ref, bf16[4,256,1024]{2,1,0:T(8,128)(2,1)} %picks.1.pick_ref, bf16[256,512]{1,0:T(8,128)(2,1)} %copy-done.6, bf16[1024,256]{1,0:T(8,128)(2,1)} %own.1.own_ref, bf16[512,1024]{1,0:T(8,128)(2,1)} %w_ref.3), custom_call_target="tpu_custom_call" | custom-call | flops 2147483648 | bytes 8388608 | tf_op jit(solution)/shard_map/other/pallas_call | solution.py:390
Async XLA Ops:
  3.0 18.5 %all-to-all-start = ((bf16[16,16,640]{2,1,0:T(8,128)(2,1)}), bf16[16,16,640]{2,1,0:T(8,128)(2,1)S(1)}, u32[]{:S(2)}, u32[]{:S(2)}) async-start(bf16[16,16,640]{2,1,0:T(8,128)(2,1)} %ask.1), calls=%async_computation | async-start | bytes 655360 | tf_op jit(solution)/shard_map/all_to_all | solution.py:316
  21.5 0.7 %copy-start.5 = (bf16[16,16,640]{2,1,0:T(8,128)(2,1)}, bf16[16,16,640]{2,1,0:T(8,128)(2,1)S(1)}, u32[]{:S(2)}) copy-start(bf16[16,16,640]{2,1,0:T(8,128)(2,1)S(1)} %all-to-all-done) | copy-start | bytes 983044
  22.3 20.0 %copy-start = (bf16[1024,1024]{1,0:T(8,128)(2,1)S(1)}, bf16[1024,1024]{1,0:T(8,128)(2,1)}, u32[]{:S(2)}) copy-start(bf16[1024,1024]{1,0:T(8,128)(2,1)} %w_kv_ref.3) | copy-start | bytes 6291460
  22.3 20.0 %copy-start.1 = (bf16[512,1024]{1,0:T(8,128)(2,1)S(1)}, bf16[512,1024]{1,0:T(8,128)(2,1)}, u32[]{:S(2)}) copy-start(bf16[512,1024]{1,0:T(8,128)(2,1)} %w_o_ref.1) | copy-start | bytes 3145732
  22.3 20.0 %copy-start.2 = (bf16[16,1024]{1,0:T(8,128)(2,1)S(1)}, bf16[16,1024]{1,0:T(8,128)(2,1)}, u32[]{:S(2)}) copy-start(bf16[16,1024]{1,0:T(8,128)(2,1)} %latent_ref.3) | copy-start | bytes 98308
  22.3 20.0 %copy-start.3 = (f32[1024]{0:T(1024)S(1)}, f32[1024]{0:T(1024)}, u32[]{:S(2)}) copy-start(f32[1024]{0:T(1024)} %param.20) | copy-start | bytes 12292
  57.0 3.5 %copy-start.4 = (bf16[16,16,512]{2,1,0:T(8,128)(2,1)}, bf16[16,16,512]{2,1,0:T(8,128)(2,1)S(1)}, u32[]{:S(2)}) copy-start(bf16[16,16,512]{2,1,0:T(8,128)(2,1)S(1)} %all_to_all.16) | copy-start | bytes 786436
  57.0 7.5 %collective-permute-start = (bf16[256,512]{1,0:T(8,128)(2,1)S(1)}, bf16[256,512]{1,0:T(8,128)(2,1)S(1)}, u32[]{:S(2)}, u32[]{:S(2)}) collective-permute-start(bf16[256,512]{1,0:T(8,128)(2,1)S(1)} %bitcast.9), channel_id=1, source_target_pairs={{0,1},{1,0},{2,3},{3,2},{4,5},{5,4},{6,7},{7,6},{8,9},{9,8},{10,11... | collective-permute-start | bytes 786440 | tf_op jit(solution)/shard_map/ppermute | solution.py:371
  64.5 0.7 copy-start.6

commit v5 on v4

--- a/solution.py
+++ b/solution.py
@@ -77,15 +77,32 @@
         to = iota((entries, LANES), 1) == mod(iota((entries, LANES), 0), per) + 2 * edges + i * per
         spread = jnp.where(own, part.astype(f32), 0.0).astype(bf16)
         extra += dot(spread, to.astype(bf16))
-    for i in range(out_ref.shape[0]):
-        out_ref[i, :, :width] = queries
-        out_ref[i, :, width:] = extra.astype(bf16)
-
-
-def front_kernel(x_ref, gain_ref, w_kv_ref, w_q_ref, pairs_ref, query_ref):
-    rows = normed(x_ref[...], gain_ref[...])
-    pairs_ref[...] = dot(rows, w_kv_ref[...]).astype(bf16)
-    query_ref[...] = dot(rows, w_q_ref[...]).T.astype(bf16)
+    half = width // 2
+    for p in range(out_ref.shape[0]):
+        out_ref[p, :, :half] = queries[:, p % 2 * half : (p % 2 + 1) * half]
+        out_ref[p, :, half:] = extra.astype(bf16)
+
+
+def half_columns(ref, core, half):
+    return ref[:, pl.ds(pl.multiple_of(core * half, half), half)]
+
+
+def front_kernel(steps, own_ref, other_ref, gain_ref, w_ref, pairs_ref, rows_ref):
+    step = pl.program_id(0)
+
+    @pl.when(step < steps)
+    def _():
+        rows_ref[...] = normed(own_ref[...], gain_ref[...])
+
+    @pl.when(step >= steps)
+    def _():
+        rows_ref[...] = normed(other_ref[...], gain_ref[...])
+
+    core = lax.axis_index("dom") & 1
+    half = pairs_ref.shape[1] // 2
+    rows = rows_ref[...]
+    pairs_ref[:, :half] = dot(rows, half_columns(w_ref, core, half)).astype(bf16)
+    pairs_ref[:, half:] = dot(rows, half_columns(w_ref, core + 2, half)).astype(bf16)
 
 
 def stat_parts(top, total):
@@ -95,85 +112,100 @@
     return top_1, top_2, top - top_1 - top_2, total_1, total - total_1
 
 
-def partial_kernel(cap, rows, edges, asked_ref, pairs_ref, out_ref, mixed_ref):
+def partial_kernel(cap, edges, asked_hbm, pairs_hbm, out_ref, asked_ref, pairs_ref, mixed_ref, sems):
+    copies = [
+        pltpu.make_async_copy(asked_hbm, asked_ref, sems.at[0]),
+        pltpu.make_async_copy(pairs_hbm, pairs_ref, sems.at[1]),
+    ]
+    for copy in copies:
+        copy.start()
     me = lax.axis_index("dom")
     points, both = pairs_ref.shape
-    peers = out_ref.shape[0]
+    points = points // 2
+    peers, rows, _ = out_ref.shape
     width = both // 2
-    size = width // HEADS
+    heads = HEADS // 2
+    size = width // heads
     per = cap * peers // rows
     scale = math.log2(math.e) / math.sqrt(size)
     all_nodes = asked_ref.shape[0]
     all_entries = peers * cap
-    list_row, list_lane = div(me * cap, per), mod(me * cap, per)
+    nodes, entries = all_nodes // 2, all_entries // 2
     pick_shape = (all_entries, all_nodes)
-    pick = iota(pick_shape, 1) == div(iota(pick_shape, 0), cap) * rows + list_row
-    lane = iota((all_entries, LANES), 1)
-    within = mod(iota((all_entries, LANES), 0), cap)
-    low_lane = within + (2 * edges + list_lane)
-    weights = jnp.where(lane == low_lane, 1.0, jnp.where(lane == low_lane + per, 256.0, 0.0))
-    lists = dot(pick.astype(bf16), asked_ref[:, width:])
-    index = jnp.sum(lists * weights, axis=1, keepdims=True).astype(jnp.int32)
-    chosen = (index == iota((all_entries, points), 1)).astype(bf16)
-    all_keys = dot(chosen, pairs_ref[:, :width]).astype(bf16)
-    all_values = dot(chosen, pairs_ref[:, width:]).astype(bf16)
-
-    nodes, entries = all_nodes // 2, all_entries // 2
+    pick_row = iota(pick_shape, 1) - div(iota(pick_shape, 0), cap) * rows
+    lane = iota((all_entries, LANES), 1) - mod(iota((all_entries, LANES), 0), cap)
     here = div(iota((entries, nodes), 0), cap) == div(iota((entries, nodes), 1), rows)
     listed = -(-cap // 8) * 8
     repeat = iota((entries, listed), 1) == mod(iota((entries, listed), 0), cap)
+    repeat = repeat.astype(bf16)
+    copies[0].wait()
+    extra = asked_ref[:, width:]
+    extra_t = extra.astype(f32).T
+    all_slots = (extra_t[:edges] + 256.0 * extra_t[edges : 2 * edges]).astype(jnp.int32)
+    chosen, biases = [], []
+    for other in range(2):
+        first = (me ^ other) * cap
+        list_row, low_lane = div(first, per), mod(first, per) + 2 * edges
+        weights = jnp.where(lane == low_lane, 1.0, jnp.where(lane == low_lane + per, 256.0, 0.0))
+        lists = dot((pick_row == list_row).astype(bf16), extra)
+        index = jnp.sum(lists * weights, axis=1, keepdims=True).astype(jnp.int32)
+        chosen.append((index == iota((all_entries, points), 1)).astype(bf16))
+        slots = all_slots - first
+        uses = jnp.zeros((listed, all_nodes), f32)
+        for j in range(edges):
+            uses += jnp.where(slots[j : j + 1] == iota((listed, all_nodes), 0), 1.0, 0.0)
+        for half in range(2):
+            used = dot(repeat, uses[:, half * nodes : (half + 1) * nodes].astype(bf16))
+            live = here & (used > 0.5)
+            biases.append(jnp.where(live, jnp.log2(jnp.where(live, used, 1.0)), NEG))
+    copies[1].wait()
+    gathered = [
+        dot(chosen[other], pairs_ref[other * points : (other + 1) * points, :]).astype(bf16)
+        for other in range(2)
+    ]
     for half in range(2):
-        own = slice(half * nodes, (half + 1) * nodes)
-        keys = all_keys[half * entries : (half + 1) * entries]
-        values_t = all_values[half * entries : (half + 1) * entries].T
-        extra_t = asked_ref[own, width:].astype(f32).T
-        slots = (extra_t[:edges] + 256.0 * extra_t[edges : 2 * edges]).astype(jnp.int32) - me * cap
-        uses = jnp.zeros((listed, nodes), f32)
-        for j in range(edges):
-            uses += jnp.where(slots[j : j + 1] == iota((listed, nodes), 0), 1.0, 0.0)
-        uses = dot(repeat.astype(bf16), uses.astype(bf16))
-        live = here & (uses > 0.5)
-        bias = jnp.where(live, jnp.log2(jnp.where(live, uses, 1.0)), NEG)
-        queries = asked_ref[own, :width]
+        part = slice(half * entries, (half + 1) * entries)
+        pairs = jnp.concatenate([gathered[0][part], gathered[1][part]], axis=0)
+        bias = jnp.concatenate([biases[half], biases[2 + half]], axis=0)
+        keys, values_t = pairs[:, :width], pairs[:, width:].T
+        queries = asked_ref[half * nodes : (half + 1) * nodes, :width]
         head = div(iota(queries.shape, 1), size)
         queries = jnp.concatenate(
-            [jnp.where(head == h, queries, jnp.zeros_like(queries)) for h in range(HEADS)], axis=0
+            [jnp.where(head == h, queries, jnp.zeros_like(queries)) for h in range(heads)], axis=0
         )
-        scores = dot_t(keys, queries) * scale + jnp.concatenate([bias] * HEADS, axis=1)
+        scores = dot_t(keys, queries) * scale + jnp.concatenate([bias] * heads, axis=1)
         top = jnp.max(scores, axis=0, keepdims=True)
         raised = jnp.exp2(scores - top)
         total = jnp.sum(raised, axis=0, keepdims=True)
         raised = raised.astype(bf16)
-        for h in range(0, HEADS, 2):
+        for h in range(0, heads, 2):
             mixed = dot(
                 values_t[h * size : (h + 2) * size, :], raised[:, h * nodes : (h + 2) * nodes]
             )
             mixed_ref[h * size : (h + 1) * size, :] = mixed[:size, :nodes]
             mixed_ref[(h + 1) * size : (h + 2) * size, :] = mixed[size:, nodes:]
         by_head = [
-            jnp.concatenate([one[:, h * nodes : (h + 1) * nodes] for h in range(HEADS)], axis=0)
+            jnp.concatenate([one[:, h * nodes : (h + 1) * nodes] for h in range(heads)], axis=0)
             for one in (top, total)
         ]
-        stats = stat_parts(*by_head)
-        for i, part in enumerate(stats):
-            mixed_ref[width + i * HEADS : width + (i + 1) * HEADS, :] = part
-        rest = mixed_ref.shape[0] - width - len(stats) * HEADS
-        mixed_ref[width + len(stats) * HEADS :, :] = jnp.zeros((rest, nodes), f32)
+        stats = jnp.concatenate(stat_parts(*by_head), axis=0)
+        rest = mixed_ref.shape[0] - width - stats.shape[0]
+        mixed_ref[width:, :] = jnp.concatenate([stats, jnp.zeros((rest, nodes), f32)], axis=0)
         result = mixed_ref[...].T.astype(bf16)
         for i in range(peers // 2):
             out_ref[half * (peers // 2) + i] = result[i * rows : (i + 1) * rows]
 
 
 def read_stats(stats):
+    heads = HEADS // 2
     col, head = iota((LANES, LANES), 0), iota((LANES, LANES), 1)
-    head_of = mod(col, HEADS) == head
-    take_top = head_of & (col < 3 * HEADS)
-    take_sum = head_of & (col >= 3 * HEADS) & (col < 5 * HEADS)
+    head_of = mod(col, heads) == head
+    take_top = head_of & (col < 3 * heads)
+    take_sum = head_of & (col >= 3 * heads) & (col < 5 * heads)
     return dot(stats, take_top.astype(bf16)), dot(stats, take_sum.astype(bf16))
 
 
-def spread_heads(factor, width):
-    size = width // HEADS
+def spread_heads(factor, width, size):
     spread = (div(iota((LANES, width), 1), size) == iota((LANES, width), 0)).astype(bf16)
     factor_1 = factor.astype(bf16)
     factor_2 = (factor - factor_1.astype(f32)).astype(bf16)
@@ -183,27 +215,30 @@
 def combine_kernel(parts_ref, latent_ref, gain_ref, w_o_ref, w_kv_ref, latent_out_ref, out_ref):
     peers, rows, sent = parts_ref.shape
     width = w_o_ref.shape[0]
+    half = width // 2
+    chips = (peers // 2, 2, rows)
     parts = parts_ref[...].reshape(peers * rows, sent)
-    top, total = read_stats(parts[:, width:])
-    top = top.reshape(peers, rows, LANES)
+    top, total = read_stats(parts[:, half:])
+    top = top.reshape(*chips, LANES)
     factor = jnp.exp2(top - jnp.max(top, axis=0, keepdims=True))
-    total = jnp.sum(total.reshape(peers, rows, LANES) * factor, axis=0, keepdims=True)
-    used = iota((1, rows, LANES), 2) < HEADS
+    total = jnp.sum(total.reshape(*chips, LANES) * factor, axis=0, keepdims=True)
+    used = iota((1, 2, rows, LANES), 3) < HEADS // 2
     factor = factor * jnp.where(used, 1.0 / jnp.where(used, total, 1.0), 0.0)
-    wide = spread_heads(factor.reshape(peers * rows, LANES), width)
-    mixed = jnp.sum((parts[:, :width].astype(f32) * wide).reshape(peers, rows, width), axis=0)
+    wide = spread_heads(factor.reshape(peers * rows, LANES), half, width // HEADS)
+    mixed = jnp.sum((parts[:, :half].astype(f32) * wide).reshape(*chips, half), axis=0)
+    mixed = jnp.concatenate([mixed[0], mixed[1]], axis=1)
     update = dot(mixed.astype(bf16), w_o_ref[...])
     latent_out = (latent_ref[...].astype(f32) + update).astype(bf16)
     latent_out_ref[...] = latent_out
     pairs = dot(normed(latent_out, gain_ref[...]), w_kv_ref[...]).astype(bf16)
-    half = width // 2
     for p in range(peers):
         at = p % 2 * half
         out_ref[p, :, :half] = pairs[:, at : at + half]
         out_ref[p, :, half:] = pairs[:, width + at : width + at + half]
 
 
-def picks_kernel(cap, rows, need_ref, slot_ref, pick_ref):
+def middle_kernel(cap, rows, x_ref, gain_ref, w_ref, need_ref, slot_ref, query_ref, pick_ref):
+    query_ref[...] = dot(normed(x_ref[...], gain_ref[...]), w_ref[...]).T.astype(bf16)
     edges, nodes, points = pick_ref.shape
     high_count = need_ref.shape[0]
     need = need_ref[...].astype(f32).astype(bf16)
@@ -241,9 +276,12 @@
     return ref[pl.ds(pl.multiple_of(first, half), half), :]
 
 
-def own_kernel(query_ref, pick_ref, nodes_ref, out_ref, pairs_ref):
+def own_kernel(query_ref, pick_ref, nodes_hbm, out_ref, nodes_ref, pairs_ref, sem):
     @pl.when(pl.program_id(0) == 0)
     def _():
+        copy = pltpu.make_async_copy(nodes_hbm, nodes_ref, sem)
+        copy.start()
+        copy.wait()
         pairs_ref[...] = nodes_ref[...].T
 
     half = out_ref.shape[1]
@@ -251,9 +289,14 @@
     out_ref[...] = attend_half(pairs_ref, queries, pick_ref)
 
 
-def other_kernel(x_ref, query_ref, pick_ref, nodes_ref, own_ref, w_ref, out_ref, pairs_ref):
+def other_kernel(
+    x_ref, query_ref, pick_ref, nodes_hbm, own_ref, w_ref, out_ref, nodes_ref, pairs_ref, sem
+):
     @pl.when(pl.program_id(0) == 0)
     def _():
+        copy = pltpu.make_async_copy(nodes_hbm, nodes_ref, sem)
+        copy.start()
+        copy.wait()
         pairs_ref[...] = nodes_ref[...].T
 
     half = own_ref.shape[1]
@@ -296,9 +339,12 @@
     entries = enc_need.shape[1]
     edges = enc_slot.shape[0]
     cap = entries // peers
-    sent = width + LANES
-    block = math.gcd(points, 256)
-
+    half = width // 2
+    sent = half + LANES
+    swap = [(i, i ^ 1) for i in range(peers)]
+    anywhere = pl.BlockSpec(memory_space=pl.ANY)
+
+    other_grid = lax.ppermute(grid, "dom", swap)
     asked = pl.pallas_call(
         ask_kernel,
         out_shape=jax.ShapeDtypeStruct((peers, rows, sent), bf16),
@@ -315,32 +361,35 @@
     )
     asked = lax.all_to_all(asked, "dom", split_axis=0, concat_axis=0, tiled=True)
 
-    pairs, queries = pl.pallas_call(
-        front_kernel,
-        grid=(points // block,),
+    block = math.gcd(points, 256)
+    steps = points // block
+    pairs = pl.pallas_call(
+        functools.partial(front_kernel, steps),
+        grid=(2 * steps,),
         in_specs=[
-            pl.BlockSpec((block, depth), lambda i: (i, 0)),
+            pl.BlockSpec((block, depth), lambda i: (jnp.minimum(i, steps - 1), 0)),
+            pl.BlockSpec((block, depth), lambda i: (jnp.maximum(i - steps, 0), 0)),
             whole(1, depth),
             whole(depth, 2 * width),
-            whole(depth, width),
-        ],
-        out_specs=[
-            pl.BlockSpec((block, 2 * width), lambda i: (i, 0)),
-            pl.BlockSpec((width, block), lambda i: (0, i)),
-        ],
-        out_shape=[
-            jax.ShapeDtypeStruct((points, 2 * width), bf16),
-            jax.ShapeDtypeStruct((width, points), bf16),
-        ],
+        ],
+        out_specs=pl.BlockSpec((block, width), lambda i: (i, 0)),
+        out_shape=jax.ShapeDtypeStruct((2 * points, width), bf16),
+        scratch_shapes=[pltpu.VMEM((block, depth), bf16)],
         compiler_params=params(58, 1),
-        cost_estimate=cost(6 * points * depth * width, 8 * points * depth),
+        cost_estimate=cost(4 * points * depth * width, 8 * points * depth),
         name="front",
-    )(grid, grid_gain.reshape(1, -1), w_kv_enc, w_q_dec)
+    )(grid, other_grid, grid_gain.reshape(1, -1), w_kv_enc)
 
     parts = pl.pallas_call(
-        functools.partial(partial_kernel, cap, rows, edges),
+        functools.partial(partial_kernel, cap, edges),
+        in_specs=[anywhere, anywhere],
         out_shape=jax.ShapeDtypeStruct((peers, rows, sent), bf16),
-        scratch_shapes=[pltpu.VMEM((sent, nodes // 2), f32)],
+        scratch_shapes=[
+            pltpu.VMEM((nodes, sent), bf16),
+            pltpu.VMEM((2 * points, width), bf16),
+            pltpu.VMEM((sent, nodes // 2), f32),
+            pltpu.SemaphoreType.DMA((2,)),
+        ],
         compiler_params=params(58),
         cost_estimate=cost(4 * entries * points * width, 4 * points * width),
         name="partial",
@@ -348,13 +397,23 @@
     parts = lax.all_to_all(parts, "dom", split_axis=0, concat_axis=0, tiled=True)
 
     slot_total = dec_need.shape[1]
-    picks = pl.pallas_call(
-        functools.partial(picks_kernel, slot_total // peers, rows),
-        out_shape=jax.ShapeDtypeStruct((dec_slot.shape[0], nodes, points), bf16),
+    queries, picks = pl.pallas_call(
+        functools.partial(middle_kernel, slot_total // peers, rows),
+        out_shape=[
+            jax.ShapeDtypeStruct((width, points), bf16),
+            jax.ShapeDtypeStruct((dec_slot.shape[0], nodes, points), bf16),
+        ],
         compiler_params=params(58),
-        cost_estimate=cost(points * nodes * LANES, 8 * points * nodes),
-        name="picks",
-    )(dec_need.reshape(slot_total // LANES, LANES), dec_slot)
+        cost_estimate=cost(2 * points * depth * width, 8 * points * depth),
+        name="middle",
+    )(
+        grid,
+        grid_gain.reshape(1, -1),
+        w_q_dec,
+        dec_need.reshape(slot_total // LANES, LANES),
+        dec_slot,
+    )
+    parts, queries, picks = lax.optimization_barrier((parts, queries, picks))
 
     latent_out, everyone = pl.pallas_call(
         combine_kernel,
@@ -368,7 +427,7 @@
     )(parts, latent_in, dec_gain.reshape(1, -1), w_o_enc, w_kv_dec)
     own = lax.all_to_all(everyone, "dom", split_axis=0, concat_axis=0, tiled=True)
     own = own.reshape(nodes, width)
-    other = lax.ppermute(own, "dom", [(i, i ^ 1) for i in range(peers)])
+    other = lax.ppermute(own, "dom", swap)
 
     block = math.gcd(points, 512)
     point_rows = lambda columns: pl.BlockSpec((block, columns), lambda i: (i, 0))
@@ -379,10 +438,14 @@
     own_mixed = pl.pallas_call(
         own_kernel,
         grid=(points // block,),
-        in_specs=point_lanes + [whole(nodes, width)],
-        out_specs=point_rows(width // 2),
-        out_shape=jax.ShapeDtypeStruct((points, width // 2), bf16),
-        scratch_shapes=[pltpu.VMEM((width, nodes), bf16)],
+        in_specs=point_lanes + [anywhere],
+        out_specs=point_rows(half),
+        out_shape=jax.ShapeDtypeStruct((points, half), bf16),
+        scratch_shapes=[
+            pltpu.VMEM((nodes, width), bf16),
+            pltpu.VMEM((width, nodes), bf16),
+            pltpu.SemaphoreType.DMA,
+        ],
         compiler_params=params(58, 1),
         cost_estimate=cost(4 * points * nodes * width, 8 * points * nodes),
         name="own",
@@ -392,10 +455,14 @@
         grid=(points // block,),
         in_specs=[point_rows(depth)]
         + point_lanes
-        + [whole(nodes, width), point_rows(width // 2), whole(width, depth)],
+        + [anywhere, point_rows(half), whole(width, depth)],
         out_specs=point_rows(depth),
         out_shape=jax.ShapeDtypeStruct((points, depth), bf16),
-        scratch_shapes=[pltpu.VMEM((width, nodes), bf16)],
+        scratch_shapes=[
+            pltpu.VMEM((nodes, width), bf16),
+            pltpu.VMEM((width, nodes), bf16),
+            pltpu.SemaphoreType.DMA,
+        ],
         compiler_params=params(58, 1),
         cost_estimate=cost(4 * points * depth * width, 8 * points * depth),
         name="other",

time: 72.1 us -> 72 us (level)
  blocking collectives: 27.7 us -> 12.9 us
  Pallas kernels: 30.9 us -> 37.6 us
  starting transfers between devices: 7.39 us -> 13.9 us
  local copies, waits for them, and re-layouts: 1.45 us -> 3.41 us
    all_to_all x1 -> x0, blocking collectives: 14.6 us -> none  [on_device(): lax.all_to_all(parts, 'dom', split_axis=0, concat_axis=0, tiled=True)]
    all_to_all x0 -> x1, starting transfers between devices: none -> 6.29 us  [on_device(): lax.all_to_all(parts, 'dom', split_axis=0, concat_axis=0, tiled=True)]
    pallas_call x3, Pallas kernels: 16.4 us -> 20.8 us  [the longest x1 9.67 us: on_device(): pl.pallas_call(functools.partial(front_kernel, steps), grid=(2 * steps,),...]
    all_to_all x1, waiting for transfers between devices: 3.53 us -> 0.01 us  [on_device(): lax.all_to_all(asked, 'dom', split_axis=0, concat_axis=0, tiled=True)]
    all_to_all x0 -> x1, waiting for transfers between devices: none -> 2.93 us  [on_device(): lax.all_to_all(parts, 'dom', split_axis=0, concat_axis=0, tiled=True)]
    unnamed x14 -> x16, local copies, waits for them, and re-layouts: 1.45 us -> 3.41 us
    pallas_call x1, Pallas kernels: 6.39 us -> 7.91 us  [on_device(): pl.pallas_call(other_kernel, grid=(points // block,), in_specs=[point_row...]
    pallas_call x1, Pallas kernels: 4.07 us -> 4.91 us  [on_device(): pl.pallas_call(own_kernel, grid=(points // block,), in_specs=point_lanes...]
  transfers between devices with their start and end apart: 2 -> 4, of which waited for: 1 -> 1; matrix products, arithmetic and copies ran while one was open for 0% -> 0% of each run, Pallas kernels for 21% -> 32%
where the time goes in v5:
time: 72 us; the launch traced here: 71.5 us
  Pallas kernels  37.6 us (52%)
  starting transfers between devices  13.9 us (19%)
  blocking collectives  12.9 us (18%)
  local copies, waits for them, and re-layouts  3.41 us (5%)
  waiting for transfers between devices  2.93 us (4%)
  between operations  0.75 us (1%)
    all_to_all x1, blocking collectives, on_device(): lax.all_to_all(everyone, 'dom', split_axis=0, concat_axis=0, tiled=True)  12.9 us
    pallas_call x1, Pallas kernels, on_device(): pl.pallas_call(functools.partial(front_kernel, steps), grid=(2 * steps,),...  9.67 us
    pallas_call x1, Pallas kernels, on_device(): pl.pallas_call(other_kernel, grid=(points // block,), in_specs=[point_row...  7.91 us
    all_to_all x1, starting transfers between devices, on_device(): lax.all_to_all(asked, 'dom', split_axis=0, concat_axis=0, tiled=True)  7.05 us
    all_to_all x1, starting transfers between devices, on_device(): lax.all_to_all(parts, 'dom', split_axis=0, concat_axis=0, tiled=True)  6.29 us
    pallas_call x1, Pallas kernels, on_device(): pl.pallas_call(functools.partial(middle_kernel, slot_total // peers, rows...  6.07 us
    pallas_call x1, Pallas kernels, on_device(): pl.pallas_call(functools.partial(partial_kernel, cap, edges), in_specs=[a...  5.05 us
    pallas_call x1, Pallas kernels, on_device(): pl.pallas_call(own_kernel, grid=(points // block,), in_specs=point_lanes...  4.91 us
  transfers between devices with their start and end apart: 4, of which 1 were waited for; matrix products, arithmetic and copies ran while one was open for 0% of the time, Pallas kernels for 32%

profile of v5, /device:TPU:0, one launch (start us, length us, event | category | flops | bytes accessed | tf_op | source)
XLA Modules:
  0.0 71.5 jit_solution(8716495613936766929)
XLA Ops:
  0.6 0.5 collective-permute-start
  1.1 2.3 %ask.1 = bf16[16,16,384]{2,1,0:T(8,128)(2,1)} custom-call(bf16[16,1024]{1,0:T(8,128)(2,1)} %latent_ref.3, f32[1,1024]{1,0:T(1,128)} %bitcast.13, bf16[1024,512]{1,0:T(8,128)(2,1)} %w_ref.4, s32[16,32]{1,0:T(8,128)} %bitcast.12, s32[1,16]{1,0:T(1,128)} %bitcast.16, s32[1,512]{1,0:T(1,128)} %need_ref.1), custom_call_target="tpu_custom_call" | custom-call | flops 16777216 | bytes 1048576 | tf_op jit(solution)/shard_map/ask/pallas_call | solution.py:348
  3.5 7.0 %all-to-all-start = ((bf16[16,16,384]{2,1,0:T(8,128)(2,1)}), bf16[16,16,384]{2,1,0:T(8,128)(2,1)S(1)}, u32[]{:S(2)}, u32[]{:S(2)}) async-start(bf16[16,16,384]{2,1,0:T(8,128)(2,1)} %ask.1), calls=%async_computation | async-start | bytes 393216 | tf_op jit(solution)/shard_map/all_to_all | solution.py:362
  10.5 0.0 collective-permute-done.other_ref
  10.6 0.0 copy-start.4
  10.6 1.3 %copy-done.4 = bf16[1024,1024]{1,0:T(8,128)(2,1)} copy-done((bf16[1024,1024]{1,0:T(8,128)(2,1)}, bf16[1024,1024]{1,0:T(8,128)(2,1)S(1)}, u32[]{:S(2)}) %copy-start.4) | copy-done | bytes 2097176
  11.9 9.7 %front.1.pairs_hbm = bf16[2048,512]{1,0:T(8,128)(2,1)} custom-call(bf16[1024,1024]{1,0:T(8,128)(2,1)} %x_ref.3, bf16[1024,1024]{1,0:T(8,128)(2,1)} %copy-done.4, f32[1,1024]{1,0:T(1,128)} %bitcast.14, bf16[1024,1024]{1,0:T(8,128)(2,1)} %w_ref.5), custom_call_target="tpu_custom_call" | custom-call | flops 2147483648 | bytes 8388608 | tf_op jit(solution)/shard_map/front/pallas_call | solution.py:366
  21.6 0.0 all-to-all-done
  21.6 0.0 copy-start.7
  21.6 0.7 copy-done.7
  22.2 5.1 %partial.1 = bf16[16,16,384]{2,1,0:T(8,128)(2,1)} custom-call(bf16[256,384]{1,0:T(8,128)(2,1)} %bitcast.11, bf16[2048,512]{1,0:T(8,128)(2,1)} %front.1.pairs_hbm), custom_call_target="tpu_custom_call" | custom-call | flops 1073741824 | bytes 2097152 | tf_op jit(solution)/shard_map/partial/pallas_call | solution.py:383
  27.3 0.0 copy-start
  27.3 0.0 copy-start.1
  27.3 0.0 copy-start.2
  27.3 0.0 copy-start.3
  27.3 6.3 %all-to-all-start.1 = ((bf16[16,16,384]{2,1,0:T(8,128)(2,1)}), bf16[16,16,384]{2,1,0:T(8,128)(2,1)S(1)}, u32[]{:S(2)}, u32[]{:S(2)}) async-start(bf16[16,16,384]{2,1,0:T(8,128)(2,1)} %partial.1), calls=%async_computation.1 | async-start | bytes 393216 | tf_op jit(solution)/shard_map/all_to_all | solution.py:397
  33.6 6.1 %middle.1 = (bf16[512,1024]{1,0:T(8,128)(2,1)}, bf16[4,256,1024]{2,1,0:T(8,128)(2,1)}) custom-call(bf16[1024,1024]{1,0:T(8,128)(2,1)} %x_ref.3, f32[1,1024]{1,0:T(1,128)} %bitcast.15, bf16[1024,512]{1,0:T(8,128)(2,1)} %w_ref.6, s32[32,128]{1,0:T(8,128)} %bitcast.17, s32[4,1024]{1,0:T(4,128)} %slot_ref.1), custom_call_target="tpu_custom_call" | custom-call | flops 1073741824 | bytes 8388608 | tf_op jit(solution)/shard_map/middle/pallas_call | solution.py:400
  39.7 2.9 %all-to-all-done.1.parts_ref = bf16[16,16,384]{2,1,0:T(8,128)(2,1)S(1)} async-done(((bf16[16,16,384]{2,1,0:T(8,128)(2,1)}), bf16[16,16,384]{2,1,0:T(8,128)(2,1)S(1)}, u32[]{:S(2)}, u32[]{:S(2)}) %all-to-all-start.1) | async-done | bytes 196640 | tf_op jit(solution)/shard_map/all_to_all | solution.py:397
  42.6 0.0 copy-done
  42.6 0.0 copy-done.1
  42.6 0.0 copy-done.2
  42.6 0.0 copy-done.3
  42.6 1.7 %combine.1 = (bf16[16,1024]{1,0:T(8,128)(2,1)}, bf16[16,16,512]{2,1,0:T(8,128)(2,1)S(1)}) custom-call(bf16[16,16,384]{2,1,0:T(8,128)(2,1)S(1)} %all-to-all-done.1.parts_ref, bf16[16,1024]{1,0:T(8,128)(2,1)S(1)} %copy-done.2, f32[1,1024]{1,0:T(1,128)S(1)} %bitcast.8, bf16[512,1024]{1,0:T(8,128)(2,1)S(1)} %copy-done.1, bf16[1024,1024]{1,0:T(8,128)(2,1)S(1)} %copy-done), custom_call_target="tpu_custom_call" | custom-call | flops 50331648 | bytes 3145728 | tf_op jit(solution)/shard_map/combine/pallas_call | solution.py:418
  44.3 12.9 %all_to_all.15 = bf16[16,16,512]{2,1,0:T(8,128)(2,1)S(1)} all-to-all(bf16[16,16,512]{2,1,0:T(8,128)(2,1)S(1)} %get-tuple-element.15), channel_id=1, replica_groups=mesh['groups'=2,'dom'=16] {'dom'}, dimensions={0} | all-to-all | bytes 524288 | tf_op jit(solution)/shard_map/all_to_all | solution.py:428
  57.2 0.0 copy-start.5
  57.3 0.0 collective-permute-start.1
  57.3 0.7 copy-done.5
  58.0 4.9 %own.1.own_ref = bf16[1024,256]{1,0:T(8,128)(2,1)} custom-call(bf16[512,1024]{1,0:T(8,128)(2,1)} %get-tuple-element.13.query_ref, bf16[4,256,1024]{2,1,0:T(8,128)(2,1)} %get-tuple-element.14.pick_ref, bf16[256,512]{1,0:T(8,128)(2,1)} %bitcast.10), custom_call_target="tpu_custom_call" | custom-call | flops 536870912 | bytes 2097152 | tf_op jit(solution)/shard_map/own/pallas_call | solution.py:438
  62.9 0.0 collective-permute-done.1.nodes_hbm
  62.9 0.0 copy-start.6
  62.9 0.7 copy-done.6
  63.6 7.9 %other.1 = bf16[1024,1024]{1,0:T(8,128)(2,1)} custom-call(bf16[1024,1024]{1,0:T(8,128)(2,1)} %x_ref.3, bf16[512,1024]{1,0:T(8,128)(2,1)} %get-tuple-element.13.query_ref, bf16[4,256,1024]{2,1,0:T(8,128)(2,1)} %get-tuple-element.14.pick_ref, bf16[256,512]{1,0:T(8,128)(2,1)} %copy-done.6, bf16[1024,256]{1,0:T(8,128)(2,1)} %own.1.own_ref, bf16[512,1024]{1,0:T(8,128)(2,1)} %w_ref.7), custom_call_target="tpu_custom_call" | custom-call | flops 2147483648 | bytes 8388608 | tf_op jit(solution)/shard_map/other/pallas_call | solution.py:453
Async XLA Ops:
  0.6 9.9 %collective-permute-start = (bf16[1024,1024]{1,0:T(8,128)(2,1)}, bf16[1024,1024]{1,0:T(8,128)(2,1)S(1)}, u32[]{:S(2)}, u32[]{:S(2)}) collective-permute-start(bf16[1024,1024]{1,0:T(8,128)(2,1)} %x_ref.3), channel_id=1, source_target_pairs={{0,1},{1,0},{2,3},{3,2},{4,5},{5,4},{6,7},{7,6},{8,9},{9,8},{10,11... | collective-permute-start | bytes 6291464 | tf_op jit(solution)/shard_map/ppermute | solution.py:347
  3.5 18.1 %all-to-all-start = ((bf16[16,16,384]{2,1,0:T(8,128)(2,1)}), bf16[16,16,384]{2,1,0:T(8,128)(2,1)S(1)}, u32[]{:S(2)}, u32[]{:S(2)}) async-start(bf16[16,16,384]{2,1,0:T(8,128)(2,1)} %ask.1), calls=%async_computation | async-start | bytes 393216 | tf_op jit(solution)/shard_map/all_to_all | solution.py:362
  10.6 1.3 %copy-start.4 = (bf16[1024,1024]{1,0:T(8,128)(2,1)}, bf16[1024,1024]{1,0:T(8,128)(2,1)S(1)}, u32[]{:S(2)}) copy-start(bf16[1024,1024]{1,0:T(8,128)(2,1)S(1)} %collective-permute-done.other_ref) | copy-start | bytes 6291460
  21.6 0.7 copy-start.7
  27.3 15.3 %copy-start = (bf16[1024,1024]{1,0:T(8,128)(2,1)S(1)}, bf16[1024,1024]{1,0:T(8,128)(2,1)}, u32[]{:S(2)}) copy-start(bf16[1024,1024]{1,0:T(8,128)(2,1)} %w_kv_ref.1) | copy-start | bytes 6291460
  27.3 15.3 %copy-start.1 = (bf16[512,1024]{1,0:T(8,128)(2,1)S(1)}, bf16[512,1024]{1,0:T(8,128)(2,1)}, u32[]{:S(2)}) copy-start(bf16[512,1024]{1,0:T(8,128)(2,1)} %w_o_ref.1) | copy-start | bytes 3145732
  27.3 15.3 %copy-start.2 = (bf16[16,1024]{1,0:T(8,128)(2,1)S(1)}, bf16[16,1024]{1,0:T(8,128)(2,1)}, u32[]{:S(2)}) copy-start(bf16[16,1024]{1,0:T(8,128)(2,1)} %latent_ref.3) | copy-start | bytes 98308
  27.3 15.3 %copy-start.3 = (f32[1024]{0:T(1024)S(1)}, f32[1024]{0:T(1024)}, u32[]{:S(2)}) copy-start(f32[1024]{0:T(1024)} %param.20) | copy-start | bytes 12292
  27.3 15.3 %all-to-all-start.1 = ((bf16[16,16,384]{2,1,0:T(8,128)(2,1)}), bf16[16,16,384]{2,1,0:T(8,128)(2,1)S(1)}, u32[]{:S(2)}, u32[]{:S(2)}) async-start(bf16[16,16,384]{2,1,0:T(8,128)(2,1)} %partial.1), calls=%async_computation.1 | async-start | bytes 393216 | tf_op jit(solution)/shard_map/all_to_all | solution.py:397
  57.2 0.7 copy-start.5
  57.3 5.6 %collective-permute-start.1 = (bf16[256,512]{1,0:T(8,128)(2,1)S(1)}, bf16[256,512]{1,0:T(8,128)(2,1)S(1)}, u32[]{:S(2)}, u32[]{:S(2)}) collective-permute-start(bf16[256,512]{1,0:T(8,128)(2,1)S(1)} %bitcast.9), channel_id=1, source_target_pairs={{0,1},{1,0},{2,3},{3,2},{4,5},{5,4},{6,7},{7,6},{8,9},{9,8},{10,11... | collective-permute-start | bytes 786440 | tf_op jit(solution)/shard_map/ppermute | solution.py:430
  62.9 0.7 copy-start.6

commit v6 on v5

--- a/solution.py
+++ b/solution.py
@@ -46,24 +46,25 @@
     return (widened * lax.rsqrt(spread + norm_eps) * gain).astype(bf16)
 
 
-def params(mib, grid_dims=0):
-    return pltpu.CompilerParams(
-        vmem_limit_bytes=mib * 2**20,
-        dimension_semantics=("arbitrary",) * grid_dims if grid_dims else None,
-    )
+def params(mib):
+    return pltpu.CompilerParams(vmem_limit_bytes=mib * 2**20)
 
 
 def cost(flops, read, exps=0):
     return pl.CostEstimate(flops=int(flops), bytes_accessed=int(read), transcendentals=int(exps))
 
 
-def ask_kernel(latent_ref, gain_ref, w_ref, slot_ref, count_ref, need_ref, out_ref):
+def ask_kernel(
+    latent_ref, gain_ref, slot_ref, count_ref, need_ref, w_hbm, out_ref, w_ref, sem
+):
+    copy = pltpu.make_async_copy(w_hbm, w_ref, sem)
+    copy.start()
     rows = latent_ref.shape[0]
     width = w_ref.shape[1]
     entries = need_ref.shape[1]
     edges = slot_ref.shape[1]
     per = entries // rows
-    queries = dot(normed(latent_ref[...], gain_ref[...]), w_ref[...]).astype(bf16)
+    rows_normed = normed(latent_ref[...], gain_ref[...])
     eye = iota((rows, rows), 0) == iota((rows, rows), 1)
     counts = jnp.sum(jnp.where(eye, count_ref[...], 0), axis=1, keepdims=True)
     slots = jnp.where(iota((rows, edges), 1) < counts, slot_ref[...], 65535)
@@ -77,32 +78,50 @@
         to = iota((entries, LANES), 1) == mod(iota((entries, LANES), 0), per) + 2 * edges + i * per
         spread = jnp.where(own, part.astype(f32), 0.0).astype(bf16)
         extra += dot(spread, to.astype(bf16))
+    copy.wait()
+    queries = dot(rows_normed, w_ref[...]).astype(bf16)
     half = width // 2
     for p in range(out_ref.shape[0]):
         out_ref[p, :, :half] = queries[:, p % 2 * half : (p % 2 + 1) * half]
         out_ref[p, :, half:] = extra.astype(bf16)
 
 
-def half_columns(ref, core, half):
-    return ref[:, pl.ds(pl.multiple_of(core * half, half), half)]
-
-
-def front_kernel(steps, own_ref, other_ref, gain_ref, w_ref, pairs_ref, rows_ref):
-    step = pl.program_id(0)
-
-    @pl.when(step < steps)
-    def _():
-        rows_ref[...] = normed(own_ref[...], gain_ref[...])
-
-    @pl.when(step >= steps)
-    def _():
-        rows_ref[...] = normed(other_ref[...], gain_ref[...])
-
+def started(*copies):
+    for copy in copies:
+        copy.start()
+    return copies
+
+
+def front_kernel(steps, own_hbm, other_ref, gain_ref, w_hbm, pairs_ref, own_ref, w_ref, sems):
+    points = own_ref.shape[0]
+    block = points // steps
+    half = pairs_ref.shape[1] // 2
     core = lax.axis_index("dom") & 1
-    half = pairs_ref.shape[1] // 2
-    rows = rows_ref[...]
-    pairs_ref[:, :half] = dot(rows, half_columns(w_ref, core, half)).astype(bf16)
-    pairs_ref[:, half:] = dot(rows, half_columns(w_ref, core + 2, half)).astype(bf16)
+    parts = [pl.ds(i * block, block) for i in range(steps)]
+    weights = started(
+        *[
+            pltpu.make_async_copy(
+                w_hbm.at[:, pl.ds(pl.multiple_of((core + 2 * i) * half, half), half)],
+                w_ref.at[:, pl.ds(i * half, half)],
+                sems.at[steps + i],
+            )
+            for i in range(2)
+        ]
+    )
+    rows = started(
+        *[
+            pltpu.make_async_copy(own_hbm.at[part], own_ref.at[part], sems.at[i])
+            for i, part in enumerate(parts)
+        ]
+    )
+    gain = gain_ref[...]
+    for copy in weights + rows:
+        copy.wait()
+    for start, ref in ((0, own_ref), (points, other_ref)):
+        for i, part in enumerate(parts):
+            pairs_ref[pl.ds(start + i * block, block), :] = dot(
+                normed(ref[part, :], gain), w_ref[...]
+            ).astype(bf16)
 
 
 def stat_parts(top, total):
@@ -112,13 +131,7 @@
     return top_1, top_2, top - top_1 - top_2, total_1, total - total_1
 
 
-def partial_kernel(cap, edges, asked_hbm, pairs_hbm, out_ref, asked_ref, pairs_ref, mixed_ref, sems):
-    copies = [
-        pltpu.make_async_copy(asked_hbm, asked_ref, sems.at[0]),
-        pltpu.make_async_copy(pairs_hbm, pairs_ref, sems.at[1]),
-    ]
-    for copy in copies:
-        copy.start()
+def partial_kernel(cap, edges, asked_ref, pairs_ref, out_ref, mixed_ref):
     me = lax.axis_index("dom")
     points, both = pairs_ref.shape
     points = points // 2
@@ -137,8 +150,7 @@
     here = div(iota((entries, nodes), 0), cap) == div(iota((entries, nodes), 1), rows)
     listed = -(-cap // 8) * 8
     repeat = iota((entries, listed), 1) == mod(iota((entries, listed), 0), cap)
-    repeat = repeat.astype(bf16)
-    copies[0].wait()
+    repeat = repeat.astype(f32)
     extra = asked_ref[:, width:]
     extra_t = extra.astype(f32).T
     all_slots = (extra_t[:edges] + 256.0 * extra_t[edges : 2 * edges]).astype(jnp.int32)
@@ -154,11 +166,17 @@
         uses = jnp.zeros((listed, all_nodes), f32)
         for j in range(edges):
             uses += jnp.where(slots[j : j + 1] == iota((listed, all_nodes), 0), 1.0, 0.0)
+        live = uses > 0.5
+        bias = jnp.where(live, jnp.log2(jnp.where(live, uses, 1.0)), NEG)
         for half in range(2):
-            used = dot(repeat, uses[:, half * nodes : (half + 1) * nodes].astype(bf16))
-            live = here & (used > 0.5)
-            biases.append(jnp.where(live, jnp.log2(jnp.where(live, used, 1.0)), NEG))
-    copies[1].wait()
+            part = bias[:, half * nodes : (half + 1) * nodes]
+            if cap == listed:
+                repeated = jnp.concatenate([part] * (entries // cap), axis=0)
+            else:
+                repeated = lax.dot_general(
+                    repeat, part, (((1,), (0,)), ((), ())), precision=lax.Precision.HIGHEST
+                )
+            biases.append(jnp.where(here, repeated, NEG))
     gathered = [
         dot(chosen[other], pairs_ref[other * points : (other + 1) * points, :]).astype(bf16)
         for other in range(2)
@@ -252,14 +270,14 @@
         pick_ref[j] = (node == iota((nodes, points), 0)).astype(bf16)
 
 
-def attend_half(pairs_ref, queries, pick_ref):
+def attend_half(pairs, queries, pick_ref, part):
     half, points = queries.shape
     edges = pick_ref.shape[0]
     heads = HEADS // 2
     size = half // heads
     scores = []
     for j in range(edges):
-        products = dot(pairs_ref[:half, :], pick_ref[j]) * queries.astype(f32)
+        products = dot(pairs[:half], pick_ref[j, :, part]) * queries.astype(f32)
         score = jnp.sum(products.reshape(heads, size, points), axis=1)
         scores.append(score * (1.0 / math.sqrt(size)))
     highest = functools.reduce(jnp.maximum, scores)
@@ -268,49 +286,58 @@
     mixed = jnp.zeros((heads, size, points), f32)
     for j in range(edges):
         weight = (raised[j] * inverse).astype(bf16).astype(f32).reshape(heads, 1, points)
-        mixed += dot(pairs_ref[half:, :], pick_ref[j]).reshape(heads, size, points) * weight
+        mixed += dot(pairs[half:], pick_ref[j, :, part]).reshape(heads, size, points) * weight
     return mixed.reshape(half, points).T.astype(bf16)
 
 
 def half_of(ref, first, half):
-    return ref[pl.ds(pl.multiple_of(first, half), half), :]
-
-
-def own_kernel(query_ref, pick_ref, nodes_hbm, out_ref, nodes_ref, pairs_ref, sem):
-    @pl.when(pl.program_id(0) == 0)
-    def _():
-        copy = pltpu.make_async_copy(nodes_hbm, nodes_ref, sem)
-        copy.start()
+    return ref.at[pl.ds(pl.multiple_of(first, half), half)]
+
+
+def own_kernel(steps, nodes_ref, query_hbm, pick_hbm, out_ref, query_ref, pick_ref, sems):
+    points, half = out_ref.shape
+    block = points // steps
+    core = lax.axis_index("dom") & 1
+    copies = started(
+        pltpu.make_async_copy(half_of(query_hbm, core * half, half), query_ref, sems.at[0]),
+        pltpu.make_async_copy(pick_hbm, pick_ref, sems.at[1]),
+    )
+    pairs = nodes_ref[...].T
+    for copy in copies:
         copy.wait()
-        pairs_ref[...] = nodes_ref[...].T
-
-    half = out_ref.shape[1]
-    queries = half_of(query_ref, (lax.axis_index("dom") & 1) * half, half)
-    out_ref[...] = attend_half(pairs_ref, queries, pick_ref)
+    for i in range(steps):
+        part = pl.ds(i * block, block)
+        out_ref[part, :] = attend_half(pairs, query_ref[:, part], pick_ref, part)
 
 
 def other_kernel(
-    x_ref, query_ref, pick_ref, nodes_hbm, own_ref, w_ref, out_ref, nodes_ref, pairs_ref, sem
+    steps, nodes_ref, own_ref, x_hbm, query_hbm, pick_hbm, w_hbm, out_hbm,
+    x_ref, query_ref, pick_ref, w_ref, out_ref, sems, out_sems,
 ):
-    @pl.when(pl.program_id(0) == 0)
-    def _():
-        copy = pltpu.make_async_copy(nodes_hbm, nodes_ref, sem)
-        copy.start()
+    points, half = own_ref.shape
+    block = points // steps
+    core = lax.axis_index("dom") & 1
+    copies = started(
+        pltpu.make_async_copy(half_of(w_hbm, core * half, half), w_ref.at[0], sems.at[0]),
+        pltpu.make_async_copy(half_of(w_hbm, (1 - core) * half, half), w_ref.at[1], sems.at[1]),
+        pltpu.make_async_copy(half_of(query_hbm, (1 - core) * half, half), query_ref, sems.at[2]),
+        pltpu.make_async_copy(pick_hbm, pick_ref, sems.at[3]),
+        pltpu.make_async_copy(x_hbm, x_ref, sems.at[4]),
+    )
+    pairs = nodes_ref[...].T
+    for copy in copies:
         copy.wait()
-        pairs_ref[...] = nodes_ref[...].T
-
-    half = own_ref.shape[1]
-    core = lax.axis_index("dom") & 1
-    update = dot(own_ref[...], half_of(w_ref, core * half, half))
-    queries = half_of(query_ref, (1 - core) * half, half)
-    update += dot(
-        attend_half(pairs_ref, queries, pick_ref), half_of(w_ref, (1 - core) * half, half)
-    )
-    out_ref[...] = (x_ref[...].astype(f32) + update).astype(bf16)
-
-
-def whole(*shape):
-    return pl.BlockSpec(shape, lambda *_: (0,) * len(shape))
+    sends = []
+    for i in range(steps):
+        part = pl.ds(i * block, block)
+        mixed = attend_half(pairs, query_ref[:, part], pick_ref, part)
+        update = dot(own_ref[part, :], w_ref[0]) + dot(mixed, w_ref[1])
+        out_ref[part, :] = (x_ref[part, :].astype(f32) + update).astype(bf16)
+        sends += started(
+            pltpu.make_async_copy(out_ref.at[part], out_hbm.at[part], out_sems.at[i])
+        )
+    for send in sends:
+        send.wait()
 
 
 def on_device(
@@ -342,22 +369,25 @@
     half = width // 2
     sent = half + LANES
     swap = [(i, i ^ 1) for i in range(peers)]
-    anywhere = pl.BlockSpec(memory_space=pl.ANY)
+    vmem = pl.BlockSpec(memory_space=pltpu.VMEM)
+    hbm = pl.BlockSpec(memory_space=pltpu.HBM)
 
     other_grid = lax.ppermute(grid, "dom", swap)
     asked = pl.pallas_call(
         ask_kernel,
+        in_specs=[vmem] * 5 + [hbm],
         out_shape=jax.ShapeDtypeStruct((peers, rows, sent), bf16),
+        scratch_shapes=[pltpu.VMEM((depth, width), bf16), pltpu.SemaphoreType.DMA],
         compiler_params=params(58),
         cost_estimate=cost(2 * rows * depth * width, 2 * depth * width),
         name="ask",
     )(
         latent_in,
         node_gain.reshape(1, -1),
-        w_q_enc,
         enc_slot.T,
         enc_count.reshape(1, -1),
         enc_need,
+        w_q_enc,
     )
     asked = lax.all_to_all(asked, "dom", split_axis=0, concat_axis=0, tiled=True)
 
@@ -365,32 +395,23 @@
     steps = points // block
     pairs = pl.pallas_call(
         functools.partial(front_kernel, steps),
-        grid=(2 * steps,),
-        in_specs=[
-            pl.BlockSpec((block, depth), lambda i: (jnp.minimum(i, steps - 1), 0)),
-            pl.BlockSpec((block, depth), lambda i: (jnp.maximum(i - steps, 0), 0)),
-            whole(1, depth),
-            whole(depth, 2 * width),
+        in_specs=[hbm, vmem, vmem, hbm],
+        out_shape=jax.ShapeDtypeStruct((2 * points, width), bf16),
+        scratch_shapes=[
+            pltpu.VMEM((points, depth), bf16),
+            pltpu.VMEM((depth, width), bf16),
+            pltpu.SemaphoreType.DMA((steps + 2,)),
         ],
-        out_specs=pl.BlockSpec((block, width), lambda i: (i, 0)),
-        out_shape=jax.ShapeDtypeStruct((2 * points, width), bf16),
-        scratch_shapes=[pltpu.VMEM((block, depth), bf16)],
-        compiler_params=params(58, 1),
+        compiler_params=params(32),
         cost_estimate=cost(4 * points * depth * width, 8 * points * depth),
         name="front",
     )(grid, other_grid, grid_gain.reshape(1, -1), w_kv_enc)
 
     parts = pl.pallas_call(
         functools.partial(partial_kernel, cap, edges),
-        in_specs=[anywhere, anywhere],
         out_shape=jax.ShapeDtypeStruct((peers, rows, sent), bf16),
-        scratch_shapes=[
-            pltpu.VMEM((nodes, sent), bf16),
-            pltpu.VMEM((2 * points, width), bf16),
-            pltpu.VMEM((sent, nodes // 2), f32),
-            pltpu.SemaphoreType.DMA((2,)),
-        ],
-        compiler_params=params(58),
+        scratch_shapes=[pltpu.VMEM((sent, nodes // 2), f32)],
+        compiler_params=params(40),
         cost_estimate=cost(4 * entries * points * width, 4 * points * width),
         name="partial",
     )(asked.reshape(nodes, sent), pairs)
@@ -429,44 +450,39 @@
     own = own.reshape(nodes, width)
     other = lax.ppermute(own, "dom", swap)
 
-    block = math.gcd(points, 512)
-    point_rows = lambda columns: pl.BlockSpec((block, columns), lambda i: (i, 0))
-    point_lanes = [
-        pl.BlockSpec((width, block), lambda i: (0, i)),
-        pl.BlockSpec((dec_slot.shape[0], nodes, block), lambda i: (0, 0, i)),
-    ]
+    steps = points // math.gcd(points, 512)
+    edge_count = dec_slot.shape[0]
     own_mixed = pl.pallas_call(
-        own_kernel,
-        grid=(points // block,),
-        in_specs=point_lanes + [anywhere],
-        out_specs=point_rows(half),
+        functools.partial(own_kernel, steps),
+        in_specs=[vmem, hbm, hbm],
         out_shape=jax.ShapeDtypeStruct((points, half), bf16),
         scratch_shapes=[
-            pltpu.VMEM((nodes, width), bf16),
-            pltpu.VMEM((width, nodes), bf16),
-            pltpu.SemaphoreType.DMA,
+            pltpu.VMEM((half, points), bf16),
+            pltpu.VMEM((edge_count, nodes, points), bf16),
+            pltpu.SemaphoreType.DMA((2,)),
         ],
-        compiler_params=params(58, 1),
+        compiler_params=params(48),
         cost_estimate=cost(4 * points * nodes * width, 8 * points * nodes),
         name="own",
-    )(queries, picks, own)
+    )(own, queries, picks)
     grid_out = pl.pallas_call(
-        other_kernel,
-        grid=(points // block,),
-        in_specs=[point_rows(depth)]
-        + point_lanes
-        + [anywhere, point_rows(half), whole(width, depth)],
-        out_specs=point_rows(depth),
+        functools.partial(other_kernel, steps),
+        in_specs=[vmem, vmem] + [hbm] * 4,
+        out_specs=hbm,
         out_shape=jax.ShapeDtypeStruct((points, depth), bf16),
         scratch_shapes=[
-            pltpu.VMEM((nodes, width), bf16),
-            pltpu.VMEM((width, nodes), bf16),
-            pltpu.SemaphoreType.DMA,
+            pltpu.VMEM((points, depth), bf16),
+            pltpu.VMEM((half, points), bf16),
+            pltpu.VMEM((edge_count, nodes, points), bf16),
+            pltpu.VMEM((2, half, depth), bf16),
+            pltpu.VMEM((points, depth), bf16),
+            pltpu.SemaphoreType.DMA((5,)),
+            pltpu.SemaphoreType.DMA((steps,)),
         ],
-        compiler_params=params(58, 1),
+        compiler_params=params(48),
         cost_estimate=cost(4 * points * depth * width, 8 * points * depth),
         name="other",
-    )(grid, queries, picks, other, own_mixed, w_o_dec)
+    )(other, own_mixed, grid, queries, picks, w_o_dec)
     return (latent_out, grid_out)
 
 

time: 72 us -> 65.2 us (0.906)
  Pallas kernels: 37.6 us -> 24.1 us
  local copies, waits for them, and re-layouts: 3.41 us -> 9.72 us
  starting transfers between devices: 13.9 us -> 12.8 us
  waiting for transfers between devices: 2.93 us -> 3.88 us
    pallas_call x5, Pallas kernels: 29.9 us -> 16.4 us  [the longest x1 5.48 us: on_device(): pl.pallas_call(functools.partial(other_kernel, steps), in_specs=[vmem, vm...]
    unnamed x16 -> x26, local copies, waits for them, and re-layouts: 3.41 us -> 9.72 us
    all_to_all x1, starting transfers between devices: 6.29 us -> 5.19 us  [on_device(): lax.all_to_all(parts, 'dom', split_axis=0, concat_axis=0, tiled=True)]
    all_to_all x1, waiting for transfers between devices: 0.01 us -> 0.96 us  [on_device(): lax.all_to_all(asked, 'dom', split_axis=0, concat_axis=0, tiled=True)]
  transfers between devices with their start and end apart: 4 -> 4, of which waited for: 1 -> 2; matrix products, arithmetic and copies ran while one was open for 0% -> 0% of each run, Pallas kernels for 32% -> 21%
where the time goes in v6:
time: 65.2 us; the launch traced here: 64.5 us
  Pallas kernels  24.1 us (37%)
  blocking collectives  13.1 us (20%)
  starting transfers between devices  12.8 us (20%)
  local copies, waits for them, and re-layouts  9.72 us (15%)
  waiting for transfers between devices  3.88 us (6%)
  between operations  0.9 us (1%)
    all_to_all x1, blocking collectives, on_device(): lax.all_to_all(everyone, 'dom', split_axis=0, concat_axis=0, tiled=True)  13.1 us
    unnamed x26, local copies, waits for them, and re-layouts  9.72 us
    all_to_all x1, starting transfers between devices, on_device(): lax.all_to_all(asked, 'dom', split_axis=0, concat_axis=0, tiled=True)  7.06 us
    pallas_call x1, Pallas kernels, on_device(): pl.pallas_call(functools.partial(middle_kernel, slot_total // peers, rows...  6.07 us
    pallas_call x1, Pallas kernels, on_device(): pl.pallas_call(functools.partial(other_kernel, steps), in_specs=[vmem, vm...  5.48 us
    all_to_all x1, starting transfers between devices, on_device(): lax.all_to_all(parts, 'dom', split_axis=0, concat_axis=0, tiled=True)  5.19 us
    pallas_call x1, Pallas kernels, on_device(): pl.pallas_call(functools.partial(partial_kernel, cap, edges), out_shape=j...  3.4 us
    pallas_call x1, Pallas kernels, on_device(): pl.pallas_call(ask_kernel, in_specs=[vmem] * 5 + [hbm], out_shape=jax.Sha...  2.95 us
  transfers between devices with their start and end apart: 4, of which 2 were waited for; matrix products, arithmetic and copies ran while one was open for 0% of the time, Pallas kernels for 21%

profile of v6, /device:TPU:0, one launch (start us, length us, event | category | flops | bytes accessed | tf_op | source)
XLA Modules:
  0.0 64.5 jit_solution(8621244676698562931)
XLA Ops:
  0.6 0.5 collective-permute-start
  1.1 3.0 %ask.1 = bf16[16,16,384]{2,1,0:T(8,128)(2,1)} custom-call(bf16[16,1024]{1,0:T(8,128)(2,1)} %latent_ref.3, f32[1,1024]{1,0:T(1,128)} %bitcast.15, s32[16,32]{1,0:T(8,128)} %bitcast.14, s32[1,16]{1,0:T(1,128)} %bitcast.16, s32[1,512]{1,0:T(1,128)} %need_ref.1, bf16[1024,512]{1,0:T(8,128)(2,1)} %w_hbm.3), custom_call_target="tpu_custom_call" | custom-call | flops 16777216 | bytes 1048576 | tf_op jit(solution)/shard_map/ask/pallas_call | solution.py:376
  4.1 7.1 %all-to-all-start = ((bf16[16,16,384]{2,1,0:T(8,128)(2,1)}), bf16[16,16,384]{2,1,0:T(8,128)(2,1)S(1)}, u32[]{:S(2)}, u32[]{:S(2)}) async-start(bf16[16,16,384]{2,1,0:T(8,128)(2,1)} %ask.1), calls=%async_computation | async-start | bytes 393216 | tf_op jit(solution)/shard_map/all_to_all | solution.py:392
  11.2 0.0 collective-permute-done.other_ref
  11.2 0.0 copy-start
  11.2 1.6 %copy-done = bf16[1024,1024]{1,0:T(8,128)(2,1)S(1)} copy-done((bf16[1024,1024]{1,0:T(8,128)(2,1)S(1)}, bf16[1024,1024]{1,0:T(8,128)(2,1)}, u32[]{:S(2)}) %copy-start) | copy-done | bytes 2097176
  12.8 0.0 copy-start.5
  12.8 1.6 %copy-done.5 = bf16[1024,1024]{1,0:T(8,128)(2,1)S(1)} copy-done((bf16[1024,1024]{1,0:T(8,128)(2,1)S(1)}, bf16[1024,1024]{1,0:T(8,128)(2,1)}, u32[]{:S(2)}) %copy-start.5) | copy-done | bytes 2097176
  14.4 0.0 copy-start.11
  14.4 0.7 %copy-done.11 = f32[1024]{0:T(1024)S(1)} copy-done((f32[1024]{0:T(1024)S(1)}, f32[1024]{0:T(1024)}, u32[]{:S(2)}) %copy-start.11) | copy-done | bytes 4120
  15.1 2.8 %front.1.pairs_ref = bf16[2048,512]{1,0:T(8,128)(2,1)S(1)} custom-call(bf16[1024,1024]{1,0:T(8,128)(2,1)S(1)} %copy-done, bf16[1024,1024]{1,0:T(8,128)(2,1)S(1)} %collective-permute-done.other_ref, f32[1,1024]{1,0:T(1,128)S(1)} %bitcast.12, bf16[1024,1024]{1,0:T(8,128)(2,1)S(1)} %copy-done.5), custom_call_target="tpu_custom_call" | custom-call | flops 2147483648 | bytes 8388608 | tf_op jit(solution)/shard_map/front/pallas_call | solution.py:396
  17.9 0.0 copy-start.6
  17.9 1.3 %copy-done.6 = bf16[2048,512]{1,0:T(8,128)(2,1)} copy-done((bf16[2048,512]{1,0:T(8,128)(2,1)}, bf16[2048,512]{1,0:T(8,128)(2,1)S(1)}, u32[]{:S(2)}) %copy-start.6) | copy-done | bytes 2097176
  19.2 1.0 %all-to-all-done = bf16[16,16,384]{2,1,0:T(8,128)(2,1)S(1)} async-done(((bf16[16,16,384]{2,1,0:T(8,128)(2,1)}), bf16[16,16,384]{2,1,0:T(8,128)(2,1)S(1)}, u32[]{:S(2)}, u32[]{:S(2)}) %all-to-all-start) | async-done | bytes 196640 | tf_op jit(solution)/shard_map/all_to_all | solution.py:392
  20.2 0.0 copy-start.7
  20.2 1.6 %copy-done.7 = bf16[2048,512]{1,0:T(8,128)(2,1)S(1)} copy-done((bf16[2048,512]{1,0:T(8,128)(2,1)S(1)}, bf16[2048,512]{1,0:T(8,128)(2,1)}, u32[]{:S(2)}) %copy-start.7) | copy-done | bytes 2097176
  21.8 3.4 %partial.1 = bf16[16,16,384]{2,1,0:T(8,128)(2,1)} custom-call(bf16[256,384]{1,0:T(8,128)(2,1)S(1)} %bitcast.10, bf16[2048,512]{1,0:T(8,128)(2,1)S(1)} %copy-done.7), custom_call_target="tpu_custom_call" | custom-call | flops 1073741824 | bytes 2097152 | tf_op jit(solution)/shard_map/partial/pallas_call | solution.py:410
  25.2 0.0 copy-start.10
  25.2 0.0 copy-start.12
  25.2 5.2 %all-to-all-start.1 = ((bf16[16,16,384]{2,1,0:T(8,128)(2,1)}), bf16[16,16,384]{2,1,0:T(8,128)(2,1)S(1)}, u32[]{:S(2)}, u32[]{:S(2)}) async-start(bf16[16,16,384]{2,1,0:T(8,128)(2,1)} %partial.1), calls=%async_computation.1 | async-start | bytes 393216 | tf_op jit(solution)/shard_map/all_to_all | solution.py:418
  30.4 6.1 %middle.1 = (bf16[512,1024]{1,0:T(8,128)(2,1)}, bf16[4,256,1024]{2,1,0:T(8,128)(2,1)}) custom-call(bf16[1024,1024]{1,0:T(8,128)(2,1)} %x_hbm.1, f32[1,1024]{1,0:T(1,128)} %bitcast.11, bf16[1024,512]{1,0:T(8,128)(2,1)} %w_ref.1, s32[32,128]{1,0:T(8,128)} %bitcast.17, s32[4,1024]{1,0:T(4,128)} %slot_ref.1), custom_call_target="tpu_custom_call" | custom-call | flops 1073741824 | bytes 8388608 | tf_op jit(solution)/shard_map/middle/pallas_call | solution.py:421
  36.4 0.0 copy-start.2
  36.4 0.0 copy-start.3
  36.4 2.9 %all-to-all-done.1.parts_ref = bf16[16,16,384]{2,1,0:T(8,128)(2,1)S(1)} async-done(((bf16[16,16,384]{2,1,0:T(8,128)(2,1)}), bf16[16,16,384]{2,1,0:T(8,128)(2,1)S(1)}, u32[]{:S(2)}, u32[]{:S(2)}) %all-to-all-start.1) | async-done | bytes 196640 | tf_op jit(solution)/shard_map/all_to_all | solution.py:418
  39.4 0.0 copy-done.10
  39.4 0.0 copy-done.12
  39.4 0.0 copy-start.4
  39.4 1.6 %copy-done.4 = bf16[1024,1024]{1,0:T(8,128)(2,1)S(1)} copy-done((bf16[1024,1024]{1,0:T(8,128)(2,1)S(1)}, bf16[1024,1024]{1,0:T(8,128)(2,1)}, u32[]{:S(2)}) %copy-start.4) | copy-done | bytes 2097176
  41.0 0.0 copy-start.9
  41.0 1.2 %copy-done.9 = bf16[512,1024]{1,0:T(8,128)(2,1)S(1)} copy-done((bf16[512,1024]{1,0:T(8,128)(2,1)S(1)}, bf16[512,1024]{1,0:T(8,128)(2,1)}, u32[]{:S(2)}) %copy-start.9) | copy-done | bytes 1048600
  42.2 1.7 %combine.1 = (bf16[16,1024]{1,0:T(8,128)(2,1)}, bf16[16,16,512]{2,1,0:T(8,128)(2,1)S(1)}) custom-call(bf16[16,16,384]{2,1,0:T(8,128)(2,1)S(1)} %all-to-all-done.1.parts_ref, bf16[16,1024]{1,0:T(8,128)(2,1)S(1)} %copy-done.10, f32[1,1024]{1,0:T(1,128)S(1)} %bitcast.13, bf16[512,1024]{1,0:T(8,128)(2,1)S(1)} %copy-done.9, bf16[1024,1024]{1,0:T(8,128)(2,1)S(1)} %copy-done.4), custom_call_target="tpu_custom_call" | custom-call | flops 50331648 | bytes 3145728 | tf_op jit(solution)/shard_map/combine/pallas_call | solution.py:439
  43.9 13.1 %all_to_all.15 = bf16[16,16,512]{2,1,0:T(8,128)(2,1)S(1)} all-to-all(bf16[16,16,512]{2,1,0:T(8,128)(2,1)S(1)} %get-tuple-element.13), channel_id=1, replica_groups=mesh['groups'=2,'dom'=16] {'dom'}, dimensions={0} | all-to-all | bytes 524288 | tf_op jit(solution)/shard_map/all_to_all | solution.py:449
  57.0 0.0 copy-start.1
  57.0 0.0 copy-start.8
  57.0 0.0 collective-permute-start.1
  57.0 0.0 copy-done.2
  57.0 0.0 copy-done.3
  57.0 1.7 %own.1.own_ref = bf16[1024,256]{1,0:T(8,128)(2,1)S(1)} custom-call(bf16[256,512]{1,0:T(8,128)(2,1)S(1)} %bitcast.9, bf16[512,1024]{1,0:T(8,128)(2,1)S(1)} %copy-done.3, bf16[4,256,1024]{2,1,0:T(8,128)(2,1)S(1)} %copy-done.2), custom_call_target="tpu_custom_call" | custom-call | flops 536870912 | bytes 2097152 | tf_op jit(solution)/shard_map/own/pallas_call | solution.py:455
  58.7 0.0 collective-permute-done.1.nodes_ref
  58.7 0.0 copy-done.1
  58.7 0.1 copy-done.8
  58.8 5.5 %other.1 = bf16[1024,1024]{1,0:T(8,128)(2,1)} custom-call(bf16[256,512]{1,0:T(8,128)(2,1)S(1)} %collective-permute-done.1.nodes_ref, bf16[1024,256]{1,0:T(8,128)(2,1)S(1)} %own.1.own_ref, bf16[1024,1024]{1,0:T(8,128)(2,1)S(1)} %copy-done.1, bf16[512,1024]{1,0:T(8,128)(2,1)S(1)} %copy-done.3, bf16[4,256,1024]{2,1,0:T(8,128)(2,1)} %get-tuple-element.15.pick_hbm, ...), custom_call_target="tpu_custom_call" | custom-call | flops 2147483648 | bytes 8388608 | tf_op jit(solution)/shard_map/other/pallas_call | solution.py:468
Async XLA Ops:
  0.6 10.5 %collective-permute-start = (bf16[1024,1024]{1,0:T(8,128)(2,1)}, bf16[1024,1024]{1,0:T(8,128)(2,1)S(1)}, u32[]{:S(2)}, u32[]{:S(2)}) collective-permute-start(bf16[1024,1024]{1,0:T(8,128)(2,1)} %x_hbm.1), channel_id=1, source_target_pairs={{0,1},{1,0},{2,3},{3,2},{4,5},{5,4},{6,7},{7,6},{8,9},{9,8},{10,11... | collective-permute-start | bytes 6291464 | tf_op jit(solution)/shard_map/ppermute | solution.py:375
  4.1 16.1 %all-to-all-start = ((bf16[16,16,384]{2,1,0:T(8,128)(2,1)}), bf16[16,16,384]{2,1,0:T(8,128)(2,1)S(1)}, u32[]{:S(2)}, u32[]{:S(2)}) async-start(bf16[16,16,384]{2,1,0:T(8,128)(2,1)} %ask.1), calls=%async_computation | async-start | bytes 393216 | tf_op jit(solution)/shard_map/all_to_all | solution.py:392
  11.2 1.6 %copy-start = (bf16[1024,1024]{1,0:T(8,128)(2,1)S(1)}, bf16[1024,1024]{1,0:T(8,128)(2,1)}, u32[]{:S(2)}) copy-start(bf16[1024,1024]{1,0:T(8,128)(2,1)} %x_hbm.1) | copy-start | bytes 6291460
  12.8 1.6 %copy-start.5 = (bf16[1024,1024]{1,0:T(8,128)(2,1)S(1)}, bf16[1024,1024]{1,0:T(8,128)(2,1)}, u32[]{:S(2)}) copy-start(bf16[1024,1024]{1,0:T(8,128)(2,1)} %w_hbm.4) | copy-start | bytes 6291460
  14.4 0.7 %copy-start.11 = (f32[1024]{0:T(1024)S(1)}, f32[1024]{0:T(1024)}, u32[]{:S(2)}) copy-start(f32[1024]{0:T(1024)} %param.18) | copy-start | bytes 12292
  17.9 1.3 %copy-start.6 = (bf16[2048,512]{1,0:T(8,128)(2,1)}, bf16[2048,512]{1,0:T(8,128)(2,1)S(1)}, u32[]{:S(2)}) copy-start(bf16[2048,512]{1,0:T(8,128)(2,1)S(1)} %front.1.pairs_ref) | copy-start | bytes 6291460
  20.2 1.6 %copy-start.7 = (bf16[2048,512]{1,0:T(8,128)(2,1)S(1)}, bf16[2048,512]{1,0:T(8,128)(2,1)}, u32[]{:S(2)}) copy-start(bf16[2048,512]{1,0:T(8,128)(2,1)} %copy-done.6) | copy-start | bytes 6291460
  25.2 14.2 %copy-start.10 = (bf16[16,1024]{1,0:T(8,128)(2,1)S(1)}, bf16[16,1024]{1,0:T(8,128)(2,1)}, u32[]{:S(2)}) copy-start(bf16[16,1024]{1,0:T(8,128)(2,1)} %latent_ref.3) | copy-start | bytes 98308
  25.2 14.2 %copy-start.12 = (f32[1024]{0:T(1024)S(1)}, f32[1024]{0:T(1024)}, u32[]{:S(2)}) copy-start(f32[1024]{0:T(1024)} %param.20) | copy-start | bytes 12292
  25.2 14.2 %all-to-all-start.1 = ((bf16[16,16,384]{2,1,0:T(8,128)(2,1)}), bf16[16,16,384]{2,1,0:T(8,128)(2,1)S(1)}, u32[]{:S(2)}, u32[]{:S(2)}) async-start(bf16[16,16,384]{2,1,0:T(8,128)(2,1)} %partial.1), calls=%async_computation.1 | async-start | bytes 393216 | tf_op jit(solution)/shard_map/all_to_all | solution.py:418
  36.4 20.5 %copy-start.2 = (bf16[4,256,1024]{2,1,0:T(8,128)(2,1)S(1)}, bf16[4,256,1024]{2,1,0:T(8,128)(2,1)}, u32[]{:S(2)}) copy-start(bf16[4,256,1024]{2,1,0:T(8,128)(2,1)} %get-tuple-element.15.pick_hbm) | copy-start | bytes 6291460
  36.4 20.5 %copy-start.3 = (bf16[512,1024]{1,0:T(8,128)(2,1)S(1)}, bf16[512,1024]{1,0:T(8,128)(2,1)}, u32[]{:S(2)}) copy-start(bf16[512,1024]{1,0:T(8,128)(2,1)} %get-tuple-element.14.query_hbm) | copy-start | bytes 3145732
  39.4 1.6 %copy-start.4 = (bf16[1024,1024]{1,0:T(8,128)(2,1)S(1)}, bf16[1024,1024]{1,0:T(8,128)(2,1)}, u32[]{:S(2)}) copy-start(bf16[1024,1024]{1,0:T(8,128)(2,1)} %w_kv_ref.1) | copy-start | bytes 6291460
  41.0 1.2 %copy-start.9 = (bf16[512,1024]{1,0:T(8,128)(2,1)S(1)}, bf16[512,1024]{1,0:T(8,128)(2,1)}, u32[]{:S(2)}) copy-start(bf16[512,1024]{1,0:T(8,128)(2,1)} %w_o_ref.1) | copy-start | bytes 3145732
  57.0 1.7 %copy-start.1 = (bf16[1024,1024]{1,0:T(8,128)(2,1)S(1)}, bf16[1024,1024]{1,0:T(8,128)(2,1)}, u32[]{:S(2)}) copy-start(bf16[1024,1024]{1,0:T(8,128)(2,1)} %x_hbm.1) | copy-start | bytes 6291460
  57.0 1.9 %copy-start.8 = (bf16[512,1024]{1,0:T(8,128)(2,1)S(1)}, bf16[512,1024]{1,0:T(8,128)(2,1)}, u32[]{:S(2)}) copy-start(bf16[512,1024]{1,0:T(8,128)(2,1)} %w_hbm.5) | copy-start | bytes 3145732
  57.0 1.7 %collective-permute-start.1 = (bf16[256,512]{1,0:T(8,128)(2,1)S(1)}, bf16[256,512]{1,0:T(8,128)(2,1)S(1)}, u32[]{:S(2)}, u32[]{:S(2)}) collective-permute-start(bf16[256,512]{1,0:T(8,128)(2,1)S(1)} %bitcast.8), channel_id=1, source_target_pairs={{0,1},{1,0},{2,3},{3,2},{4,5},{5,4},{6,7},{7,6},{8,9},{9,8},{10,11... | collective-permute-start | bytes 786440 | tf_op jit(solution)/shard_map/ppermute | solution.py:451

commit v7 on v6

--- a/solution.py
+++ b/solution.py
@@ -48,6 +48,12 @@
 
 def params(mib):
     return pltpu.CompilerParams(vmem_limit_bytes=mib * 2**20)
+
+
+def started(*copies):
+    for copy in copies:
+        copy.start()
+    return copies
 
 
 def cost(flops, read, exps=0):
@@ -86,42 +92,41 @@
         out_ref[p, :, half:] = extra.astype(bf16)
 
 
-def started(*copies):
-    for copy in copies:
-        copy.start()
-    return copies
-
-
-def front_kernel(steps, own_hbm, other_ref, gain_ref, w_hbm, pairs_ref, own_ref, w_ref, sems):
+def front_kernel(
+    steps, other_ref, gain_ref, own_hbm, w_hbm, out_hbm, own_ref, w_ref, pairs_ref, sems, out_sems
+):
     points = own_ref.shape[0]
     block = points // steps
     half = pairs_ref.shape[1] // 2
     core = lax.axis_index("dom") & 1
-    parts = [pl.ds(i * block, block) for i in range(steps)]
-    weights = started(
+    copies = started(
         *[
             pltpu.make_async_copy(
                 w_hbm.at[:, pl.ds(pl.multiple_of((core + 2 * i) * half, half), half)],
                 w_ref.at[:, pl.ds(i * half, half)],
-                sems.at[steps + i],
+                sems.at[i],
             )
             for i in range(2)
-        ]
-    )
-    rows = started(
-        *[
-            pltpu.make_async_copy(own_hbm.at[part], own_ref.at[part], sems.at[i])
-            for i, part in enumerate(parts)
-        ]
+        ],
+        pltpu.make_async_copy(own_hbm, own_ref, sems.at[2]),
     )
     gain = gain_ref[...]
-    for copy in weights + rows:
-        copy.wait()
-    for start, ref in ((0, own_ref), (points, other_ref)):
-        for i, part in enumerate(parts):
-            pairs_ref[pl.ds(start + i * block, block), :] = dot(
-                normed(ref[part, :], gain), w_ref[...]
-            ).astype(bf16)
+    sends = []
+    for step in range(2 * steps):
+        rows_ref = other_ref if step < steps else own_ref
+        if step == 0:
+            copies[0].wait()
+            copies[1].wait()
+        if step == steps:
+            copies[2].wait()
+        part = pl.ds(step % steps * block, block)
+        place = pl.ds((step + steps) % (2 * steps) * block, block)
+        pairs_ref[place, :] = dot(normed(rows_ref[part, :], gain), w_ref[...]).astype(bf16)
+        sends += started(
+            pltpu.make_async_copy(pairs_ref.at[place], out_hbm.at[place], out_sems.at[step])
+        )
+    for send in sends:
+        send.wait()
 
 
 def stat_parts(top, total):
@@ -131,7 +136,9 @@
     return top_1, top_2, top - top_1 - top_2, total_1, total - total_1
 
 
-def partial_kernel(cap, edges, asked_ref, pairs_ref, out_ref, mixed_ref):
+def partial_kernel(cap, edges, asked_ref, pairs_hbm, out_ref, pairs_ref, mixed_ref, sem):
+    copy = pltpu.make_async_copy(pairs_hbm, pairs_ref, sem)
+    copy.start()
     me = lax.axis_index("dom")
     points, both = pairs_ref.shape
     points = points // 2
@@ -177,6 +184,7 @@
                     repeat, part, (((1,), (0,)), ((), ())), precision=lax.Precision.HIGHEST
                 )
             biases.append(jnp.where(here, repeated, NEG))
+    copy.wait()
     gathered = [
         dot(chosen[other], pairs_ref[other * points : (other + 1) * points, :]).astype(bf16)
         for other in range(2)
@@ -255,29 +263,49 @@
         out_ref[p, :, half:] = pairs[:, width + at : width + at + half]
 
 
-def middle_kernel(cap, rows, x_ref, gain_ref, w_ref, need_ref, slot_ref, query_ref, pick_ref):
-    query_ref[...] = dot(normed(x_ref[...], gain_ref[...]), w_ref[...]).T.astype(bf16)
-    edges, nodes, points = pick_ref.shape
+def middle_kernel(
+    steps, cap, rows, gain_ref, need_ref, slot_ref, x_hbm, w_hbm, out_hbm, node_ref,
+    x_ref, w_ref, query_ref, sems, out_sems,
+):
+    copies = started(
+        pltpu.make_async_copy(w_hbm, w_ref, sems.at[0]),
+        pltpu.make_async_copy(x_hbm, x_ref, sems.at[1]),
+    )
+    points = x_ref.shape[0]
+    block = points // steps
     high_count = need_ref.shape[0]
     need = need_ref[...].astype(f32).astype(bf16)
-    for j in range(edges):
+    for j in range(slot_ref.shape[0]):
         slots = slot_ref[j : j + 1, :]
         row_of = (div(slots, LANES) == iota((high_count, points), 0)).astype(bf16)
         listed = lax.dot_general(need, row_of, (((0,), (0,)), ((), ())), preferred_element_type=f32)
         own = mod(slots, LANES) == iota((LANES, points), 0)
         found = jnp.sum(jnp.where(own, listed, 0.0), axis=0, keepdims=True).astype(jnp.int32)
-        node = div(slots, cap) * rows + found
-        pick_ref[j] = (node == iota((nodes, points), 0)).astype(bf16)
-
-
-def attend_half(pairs, queries, pick_ref, part):
+        node_ref[j : j + 1, :] = div(slots, cap) * rows + found
+    for copy in copies:
+        copy.wait()
+    sends = []
+    for i in range(steps):
+        part = pl.ds(i * block, block)
+        queries = dot(normed(x_ref[part, :], gain_ref[...]), w_ref[...])
+        query_ref[:, part] = queries.T.astype(bf16)
+        sends += started(
+            pltpu.make_async_copy(query_ref.at[:, part], out_hbm.at[:, part], out_sems.at[i])
+        )
+    for send in sends:
+        send.wait()
+
+
+def attend_half(pairs, queries, nodes):
     half, points = queries.shape
-    edges = pick_ref.shape[0]
+    edges = nodes.shape[0]
     heads = HEADS // 2
     size = half // heads
+    node = iota((pairs.shape[1], points), 0)
+    picks = [(nodes[j : j + 1] == node).astype(bf16) for j in range(edges)]
     scores = []
     for j in range(edges):
-        products = dot(pairs[:half], pick_ref[j, :, part]) * queries.astype(f32)
+        products = dot(pairs[:half], picks[j]) * queries.astype(f32)
         score = jnp.sum(products.reshape(heads, size, points), axis=1)
         scores.append(score * (1.0 / math.sqrt(size)))
     highest = functools.reduce(jnp.maximum, scores)
@@ -286,7 +314,7 @@
     mixed = jnp.zeros((heads, size, points), f32)
     for j in range(edges):
         weight = (raised[j] * inverse).astype(bf16).astype(f32).reshape(heads, 1, points)
-        mixed += dot(pairs[half:], pick_ref[j, :, part]).reshape(heads, size, points) * weight
+        mixed += dot(pairs[half:], picks[j]).reshape(heads, size, points) * weight
     return mixed.reshape(half, points).T.astype(bf16)
 
 
@@ -294,50 +322,47 @@
     return ref.at[pl.ds(pl.multiple_of(first, half), half)]
 
 
-def own_kernel(steps, nodes_ref, query_hbm, pick_hbm, out_ref, query_ref, pick_ref, sems):
+def own_kernel(steps, pairs_ref, node_ref, query_hbm, out_ref, query_ref, sem):
     points, half = out_ref.shape
     block = points // steps
     core = lax.axis_index("dom") & 1
-    copies = started(
-        pltpu.make_async_copy(half_of(query_hbm, core * half, half), query_ref, sems.at[0]),
-        pltpu.make_async_copy(pick_hbm, pick_ref, sems.at[1]),
-    )
-    pairs = nodes_ref[...].T
-    for copy in copies:
-        copy.wait()
+    copy = pltpu.make_async_copy(half_of(query_hbm, core * half, half), query_ref, sem)
+    copy.start()
+    pairs = pairs_ref[...].T
+    copy.wait()
     for i in range(steps):
         part = pl.ds(i * block, block)
-        out_ref[part, :] = attend_half(pairs, query_ref[:, part], pick_ref, part)
+        out_ref[part, :] = attend_half(pairs, query_ref[:, part], node_ref[:, part])
 
 
 def other_kernel(
-    steps, nodes_ref, own_ref, x_hbm, query_hbm, pick_hbm, w_hbm, out_hbm,
-    x_ref, query_ref, pick_ref, w_ref, out_ref, sems, out_sems,
+    steps, pairs_ref, own_ref, node_ref, x_ref, w_ref, query_hbm, out_hbm,
+    query_ref, out_ref, sem, out_sems,
 ):
     points, half = own_ref.shape
     block = points // steps
     core = lax.axis_index("dom") & 1
-    copies = started(
-        pltpu.make_async_copy(half_of(w_hbm, core * half, half), w_ref.at[0], sems.at[0]),
-        pltpu.make_async_copy(half_of(w_hbm, (1 - core) * half, half), w_ref.at[1], sems.at[1]),
-        pltpu.make_async_copy(half_of(query_hbm, (1 - core) * half, half), query_ref, sems.at[2]),
-        pltpu.make_async_copy(pick_hbm, pick_ref, sems.at[3]),
-        pltpu.make_async_copy(x_hbm, x_ref, sems.at[4]),
-    )
-    pairs = nodes_ref[...].T
-    for copy in copies:
-        copy.wait()
+    copy = pltpu.make_async_copy(half_of(query_hbm, (1 - core) * half, half), query_ref, sem)
+    copy.start()
+    pairs = pairs_ref[...].T
+    own_w = half_of(w_ref, core * half, half)
+    other_w = half_of(w_ref, (1 - core) * half, half)
+    copy.wait()
     sends = []
     for i in range(steps):
         part = pl.ds(i * block, block)
-        mixed = attend_half(pairs, query_ref[:, part], pick_ref, part)
-        update = dot(own_ref[part, :], w_ref[0]) + dot(mixed, w_ref[1])
+        mixed = attend_half(pairs, query_ref[:, part], node_ref[:, part])
+        update = dot(own_ref[part, :], own_w[...]) + dot(mixed, other_w[...])
         out_ref[part, :] = (x_ref[part, :].astype(f32) + update).astype(bf16)
         sends += started(
             pltpu.make_async_copy(out_ref.at[part], out_hbm.at[part], out_sems.at[i])
         )
     for send in sends:
         send.wait()
+
+
+def in_hbm(array):
+    return pltpu.with_memory_space_constraint(array, pltpu.HBM)
 
 
 def on_device(
@@ -387,7 +412,7 @@
         enc_slot.T,
         enc_count.reshape(1, -1),
         enc_need,
-        w_q_enc,
+        in_hbm(w_q_enc),
     )
     asked = lax.all_to_all(asked, "dom", split_axis=0, concat_axis=0, tiled=True)
 
@@ -395,46 +420,65 @@
     steps = points // block
     pairs = pl.pallas_call(
         functools.partial(front_kernel, steps),
-        in_specs=[hbm, vmem, vmem, hbm],
-        out_shape=jax.ShapeDtypeStruct((2 * points, width), bf16),
+        in_specs=[vmem, vmem, hbm, hbm],
+        out_specs=hbm,
+        out_shape=pltpu.HBM((2 * points, width), bf16),
         scratch_shapes=[
             pltpu.VMEM((points, depth), bf16),
             pltpu.VMEM((depth, width), bf16),
-            pltpu.SemaphoreType.DMA((steps + 2,)),
-        ],
-        compiler_params=params(32),
+            pltpu.VMEM((2 * points, width), bf16),
+            pltpu.SemaphoreType.DMA((3,)),
+            pltpu.SemaphoreType.DMA((2 * steps,)),
+        ],
+        compiler_params=params(40),
         cost_estimate=cost(4 * points * depth * width, 8 * points * depth),
         name="front",
-    )(grid, other_grid, grid_gain.reshape(1, -1), w_kv_enc)
+    )(other_grid, grid_gain.reshape(1, -1), in_hbm(grid), in_hbm(w_kv_enc))
 
     parts = pl.pallas_call(
         functools.partial(partial_kernel, cap, edges),
+        in_specs=[vmem, hbm],
         out_shape=jax.ShapeDtypeStruct((peers, rows, sent), bf16),
-        scratch_shapes=[pltpu.VMEM((sent, nodes // 2), f32)],
+        scratch_shapes=[
+            pltpu.VMEM((2 * points, width), bf16),
+            pltpu.VMEM((sent, nodes // 2), f32),
+            pltpu.SemaphoreType.DMA,
+        ],
         compiler_params=params(40),
         cost_estimate=cost(4 * entries * points * width, 4 * points * width),
         name="partial",
-    )(asked.reshape(nodes, sent), pairs)
+    )(asked.reshape(nodes, sent), in_hbm(pairs))
+    parts, dec_need, dec_slot = lax.optimization_barrier((parts, dec_need, dec_slot))
     parts = lax.all_to_all(parts, "dom", split_axis=0, concat_axis=0, tiled=True)
 
     slot_total = dec_need.shape[1]
-    queries, picks = pl.pallas_call(
-        functools.partial(middle_kernel, slot_total // peers, rows),
+    edge_count = dec_slot.shape[0]
+    queries, node_of = pl.pallas_call(
+        functools.partial(middle_kernel, steps, slot_total // peers, rows),
+        in_specs=[vmem] * 3 + [hbm] * 2,
+        out_specs=[hbm, vmem],
         out_shape=[
-            jax.ShapeDtypeStruct((width, points), bf16),
-            jax.ShapeDtypeStruct((dec_slot.shape[0], nodes, points), bf16),
-        ],
-        compiler_params=params(58),
+            pltpu.HBM((width, points), bf16),
+            jax.ShapeDtypeStruct((edge_count, points), jnp.int32),
+        ],
+        scratch_shapes=[
+            pltpu.VMEM((points, depth), bf16),
+            pltpu.VMEM((depth, width), bf16),
+            pltpu.VMEM((width, points), bf16),
+            pltpu.SemaphoreType.DMA((2,)),
+            pltpu.SemaphoreType.DMA((steps,)),
+        ],
+        compiler_params=params(40),
         cost_estimate=cost(2 * points * depth * width, 8 * points * depth),
         name="middle",
     )(
-        grid,
         grid_gain.reshape(1, -1),
-        w_q_dec,
         dec_need.reshape(slot_total // LANES, LANES),
         dec_slot,
+        in_hbm(grid),
+        in_hbm(w_q_dec),
     )
-    parts, queries, picks = lax.optimization_barrier((parts, queries, picks))
+    parts, queries, node_of = lax.optimization_barrier((parts, queries, node_of))
 
     latent_out, everyone = pl.pallas_call(
         combine_kernel,
@@ -450,39 +494,30 @@
     own = own.reshape(nodes, width)
     other = lax.ppermute(own, "dom", swap)
 
-    steps = points // math.gcd(points, 512)
-    edge_count = dec_slot.shape[0]
     own_mixed = pl.pallas_call(
-        functools.partial(own_kernel, steps),
-        in_specs=[vmem, hbm, hbm],
+        functools.partial(own_kernel, max(steps // 2, 1)),
+        in_specs=[vmem, vmem, hbm],
         out_shape=jax.ShapeDtypeStruct((points, half), bf16),
-        scratch_shapes=[
-            pltpu.VMEM((half, points), bf16),
-            pltpu.VMEM((edge_count, nodes, points), bf16),
-            pltpu.SemaphoreType.DMA((2,)),
-        ],
+        scratch_shapes=[pltpu.VMEM((half, points), bf16), pltpu.SemaphoreType.DMA],
         compiler_params=params(48),
         cost_estimate=cost(4 * points * nodes * width, 8 * points * nodes),
         name="own",
-    )(own, queries, picks)
+    )(own, node_of, in_hbm(queries))
     grid_out = pl.pallas_call(
         functools.partial(other_kernel, steps),
-        in_specs=[vmem, vmem] + [hbm] * 4,
+        in_specs=[vmem] * 5 + [hbm],
         out_specs=hbm,
-        out_shape=jax.ShapeDtypeStruct((points, depth), bf16),
+        out_shape=pltpu.HBM((points, depth), bf16),
         scratch_shapes=[
+            pltpu.VMEM((half, points), bf16),
             pltpu.VMEM((points, depth), bf16),
-            pltpu.VMEM((half, points), bf16),
-            pltpu.VMEM((edge_count, nodes, points), bf16),
-            pltpu.VMEM((2, half, depth), bf16),
-            pltpu.VMEM((points, depth), bf16),
-            pltpu.SemaphoreType.DMA((5,)),
+            pltpu.SemaphoreType.DMA,
             pltpu.SemaphoreType.DMA((steps,)),
         ],
         compiler_params=params(48),
         cost_estimate=cost(4 * points * depth * width, 8 * points * depth),
         name="other",
-    )(other, own_mixed, grid, queries, picks, w_o_dec)
+    )(other, own_mixed, node_of, grid, w_o_dec, in_hbm(queries))
     return (latent_out, grid_out)
 
 

time: 65.2 us -> 61.2 us (0.939)
  local copies, waits for them, and re-layouts: 9.72 us -> 0.73 us
  waiting for transfers between devices: 3.88 us -> 8.17 us
  Pallas kernels: 24.1 us -> 26.6 us
  starting transfers between devices: 12.8 us -> 11.4 us
    unnamed x26 -> x20, local copies, waits for them, and re-layouts: 9.72 us -> 0.73 us
    all_to_all x1, waiting for transfers between devices: 0.96 us -> 3.55 us  [on_device(): lax.all_to_all(asked, 'dom', split_axis=0, concat_axis=0, tiled=True)]
    pallas_call x5, Pallas kernels: 19.5 us -> 21.9 us  [the longest x1 5.2 us: on_device(): pl.pallas_call(functools.partial(other_kernel, steps), in_specs=[vmem] *...]
    all_to_all x1, waiting for transfers between devices: 2.92 us -> 4.62 us  [on_device(): lax.all_to_all(parts, 'dom', split_axis=0, concat_axis=0, tiled=True)]
    all_to_all x1, starting transfers between devices: 5.19 us -> 3.8 us  [on_device(): lax.all_to_all(parts, 'dom', split_axis=0, concat_axis=0, tiled=True)]
  transfers between devices with their start and end apart: 4 -> 4, of which waited for: 2 -> 2; matrix products, arithmetic and copies ran while one was open for 0% -> 0% of each run, Pallas kernels for 21% -> 25%
where the time goes in v7:
time: 61.2 us; the launch traced here: 60.6 us
  Pallas kernels  26.6 us (43%)
  blocking collectives  12.8 us (21%)
  starting transfers between devices  11.4 us (19%)
  waiting for transfers between devices  8.17 us (13%)
  between operations  0.97 us (2%)
  local copies, waits for them, and re-layouts  0.73 us (1%)
    all_to_all x1, blocking collectives, on_device(): lax.all_to_all(everyone, 'dom', split_axis=0, concat_axis=0, tiled=True)  12.8 us
    all_to_all x1, starting transfers between devices, on_device(): lax.all_to_all(asked, 'dom', split_axis=0, concat_axis=0, tiled=True)  7.06 us
    pallas_call x1, Pallas kernels, on_device(): pl.pallas_call(functools.partial(other_kernel, steps), in_specs=[vmem] *...  5.2 us
    pallas_call x1, Pallas kernels, on_device(): pl.pallas_call(functools.partial(partial_kernel, cap, edges), in_specs=[v...  4.78 us
    pallas_call x1, Pallas kernels, on_device(): pl.pallas_call(functools.partial(front_kernel, steps), in_specs=[vmem, vm...  4.74 us
    all_to_all x1, waiting for transfers between devices, on_device(): lax.all_to_all(parts, 'dom', split_axis=0, concat_axis=0, tiled=True)  4.62 us
    pallas_call x1, Pallas kernels, on_device(): pl.pallas_call(functools.partial(middle_kernel, steps, slot_total // peer...  4.31 us
    all_to_all x1, starting transfers between devices, on_device(): lax.all_to_all(parts, 'dom', split_axis=0, concat_axis=0, tiled=True)  3.8 us
  transfers between devices with their start and end apart: 4, of which 2 were waited for; matrix products, arithmetic and copies ran while one was open for 0% of the time, Pallas kernels for 25%

profile of v7, /device:TPU:0, one launch (start us, length us, event | category | flops | bytes accessed | tf_op | source)
XLA Modules:
  0.0 60.6 jit_solution(17063861851450446754)
XLA Ops:
  0.6 0.5 collective-permute-start
  1.1 3.0 %ask.1 = bf16[16,16,384]{2,1,0:T(8,128)(2,1)} custom-call(bf16[16,1024]{1,0:T(8,128)(2,1)} %latent_ref.3, f32[1,1024]{1,0:T(1,128)} %bitcast.16, s32[16,32]{1,0:T(8,128)} %bitcast.15, s32[1,16]{1,0:T(1,128)} %bitcast.17, s32[1,512]{1,0:T(1,128)} %need_ref.1, bf16[1024,512]{1,0:T(8,128)(2,1)} %w_hbm.3), custom_call_target="tpu_custom_call" | custom-call | flops 16777216 | bytes 1048576 | tf_op jit(solution)/shard_map/ask/pallas_call | solution.py:401
  4.1 7.1 %all-to-all-start = ((bf16[16,16,384]{2,1,0:T(8,128)(2,1)}), bf16[16,16,384]{2,1,0:T(8,128)(2,1)S(1)}, u32[]{:S(2)}, u32[]{:S(2)}) async-start(bf16[16,16,384]{2,1,0:T(8,128)(2,1)} %ask.1), calls=%async_computation | async-start | bytes 393216 | tf_op jit(solution)/shard_map/all_to_all | solution.py:417
  11.2 0.0 collective-permute-done.other_ref
  11.2 0.0 copy-start.4
  11.2 0.7 %copy-done.4 = f32[1024]{0:T(1024)S(1)} copy-done((f32[1024]{0:T(1024)S(1)}, f32[1024]{0:T(1024)}, u32[]{:S(2)}) %copy-start.4) | copy-done | bytes 4120
  11.9 4.7 %front.1.pairs_hbm = bf16[2048,512]{1,0:T(8,128)(2,1)} custom-call(bf16[1024,1024]{1,0:T(8,128)(2,1)S(1)} %collective-permute-done.other_ref, f32[1,1024]{1,0:T(1,128)S(1)} %bitcast.11, bf16[1024,1024]{1,0:T(8,128)(2,1)} %x_ref.1, bf16[1024,1024]{1,0:T(8,128)(2,1)} %w_hbm.4), custom_call_target="tpu_custom_call" | custom-call | flops 2147483648 | bytes 8388608 | tf_op jit(solution)/shard_map/front/pallas_call | solution.py:421
  16.6 3.5 %all-to-all-done = bf16[16,16,384]{2,1,0:T(8,128)(2,1)S(1)} async-done(((bf16[16,16,384]{2,1,0:T(8,128)(2,1)}), bf16[16,16,384]{2,1,0:T(8,128)(2,1)S(1)}, u32[]{:S(2)}, u32[]{:S(2)}) %all-to-all-start) | async-done | bytes 196640 | tf_op jit(solution)/shard_map/all_to_all | solution.py:417
  20.2 0.0 copy-start.5
  20.2 0.0 copy-start.8
  20.2 0.0 copy-start.9
  20.2 4.8 %partial.1 = bf16[16,16,384]{2,1,0:T(8,128)(2,1)} custom-call(bf16[256,384]{1,0:T(8,128)(2,1)S(1)} %bitcast.10, bf16[2048,512]{1,0:T(8,128)(2,1)} %front.1.pairs_hbm), custom_call_target="tpu_custom_call" | custom-call | flops 1073741824 | bytes 2097152 | tf_op jit(solution)/shard_map/partial/pallas_call | solution.py:438
  25.0 0.0 copy-start
  25.0 0.0 copy-start.2
  25.0 0.0 copy-start.3
  25.0 0.0 copy-start.6
  25.0 3.8 %all-to-all-start.1 = ((bf16[16,16,384]{2,1,0:T(8,128)(2,1)}), bf16[16,16,384]{2,1,0:T(8,128)(2,1)S(1)}, u32[]{:S(2)}, u32[]{:S(2)}) async-start(bf16[16,16,384]{2,1,0:T(8,128)(2,1)} %partial.1), calls=%async_computation.1 | async-start | bytes 393216 | tf_op jit(solution)/shard_map/all_to_all | solution.py:452
  28.8 0.0 copy-done.5
  28.8 0.0 copy-done.8
  28.8 0.0 copy-done.9
  28.9 4.3 %middle.1 = (bf16[512,1024]{1,0:T(8,128)(2,1)}, s32[4,1024]{1,0:T(4,128)S(1)}) custom-call(f32[1,1024]{1,0:T(1,128)S(1)} %bitcast.12, s32[32,128]{1,0:T(8,128)S(1)} %bitcast.14, s32[4,1024]{1,0:T(4,128)S(1)} %copy-done.9, bf16[1024,1024]{1,0:T(8,128)(2,1)} %x_ref.1, bf16[1024,512]{1,0:T(8,128)(2,1)} %w_hbm.5), custom_call_target="tpu_custom_call" | custom-call | flops 1073741824 | bytes 8388608 | tf_op jit(solution)/shard_map/middle/pallas_call | solution.py:456
  33.2 4.6 %all-to-all-done.1.parts_ref = bf16[16,16,384]{2,1,0:T(8,128)(2,1)S(1)} async-done(((bf16[16,16,384]{2,1,0:T(8,128)(2,1)}), bf16[16,16,384]{2,1,0:T(8,128)(2,1)S(1)}, u32[]{:S(2)}, u32[]{:S(2)}) %all-to-all-start.1) | async-done | bytes 196640 | tf_op jit(solution)/shard_map/all_to_all | solution.py:452
  37.8 0.0 copy-done
  37.8 0.0 copy-done.2
  37.8 0.0 copy-done.3
  37.8 0.0 copy-done.6
  37.8 0.0 copy-start.7
  37.8 1.7 %combine.1 = (bf16[16,1024]{1,0:T(8,128)(2,1)}, bf16[16,16,512]{2,1,0:T(8,128)(2,1)S(1)}) custom-call(bf16[16,16,384]{2,1,0:T(8,128)(2,1)S(1)} %all-to-all-done.1.parts_ref, bf16[16,1024]{1,0:T(8,128)(2,1)S(1)} %copy-done.3, f32[1,1024]{1,0:T(1,128)S(1)} %bitcast.13, bf16[512,1024]{1,0:T(8,128)(2,1)S(1)} %copy-done.2, bf16[1024,1024]{1,0:T(8,128)(2,1)S(1)} %copy-done), custom_call_target="tpu_custom_call" | custom-call | flops 50331648 | bytes 3145728 | tf_op jit(solution)/shard_map/combine/pallas_call | solution.py:483
  39.5 0.0 copy-start.1
  39.5 12.8 %all_to_all.15 = bf16[16,16,512]{2,1,0:T(8,128)(2,1)S(1)} all-to-all(bf16[16,16,512]{2,1,0:T(8,128)(2,1)S(1)} %get-tuple-element.19), channel_id=1, replica_groups=mesh['groups'=2,'dom'=16] {'dom'}, dimensions={0} | all-to-all | bytes 524288 | tf_op jit(solution)/shard_map/all_to_all | solution.py:493
  52.3 0.0 collective-permute-start.1
  52.3 2.9 %own.1.own_ref = bf16[1024,256]{1,0:T(8,128)(2,1)S(1)} custom-call(bf16[256,512]{1,0:T(8,128)(2,1)S(1)} %bitcast.9, s32[4,1024]{1,0:T(4,128)S(1)} %get-tuple-element.20.node_ref, bf16[512,1024]{1,0:T(8,128)(2,1)} %get-tuple-element.21.query_hbm), custom_call_target="tpu_custom_call" | custom-call | flops 536870912 | bytes 2097152 | tf_op jit(solution)/shard_map/own/pallas_call | solution.py:497
  55.2 0.0 collective-permute-done.1.pairs_ref
  55.2 0.0 copy-done.7
  55.2 0.0 copy-done.1
  55.2 5.2 %other.1 = bf16[1024,1024]{1,0:T(8,128)(2,1)} custom-call(bf16[256,512]{1,0:T(8,128)(2,1)S(1)} %collective-permute-done.1.pairs_ref, bf16[1024,256]{1,0:T(8,128)(2,1)S(1)} %own.1.own_ref, s32[4,1024]{1,0:T(4,128)S(1)} %get-tuple-element.20.node_ref, bf16[1024,1024]{1,0:T(8,128)(2,1)S(1)} %copy-done.1, bf16[512,1024]{1,0:T(8,128)(2,1)S(1)} %copy-done.7, ...), custom_call_target="tpu_custom_call" | custom-call | flops 2147483648 | bytes 8388608 | tf_op jit(solution)/shard_map/other/pallas_call | solution.py:506
Async XLA Ops:
  0.6 10.6 %collective-permute-start = (bf16[1024,1024]{1,0:T(8,128)(2,1)}, bf16[1024,1024]{1,0:T(8,128)(2,1)S(1)}, u32[]{:S(2)}, u32[]{:S(2)}) collective-permute-start(bf16[1024,1024]{1,0:T(8,128)(2,1)} %x_ref.1), channel_id=1, source_target_pairs={{0,1},{1,0},{2,3},{3,2},{4,5},{5,4},{6,7},{7,6},{8,9},{9,8},{10,11... | collective-permute-start | bytes 6291464 | tf_op jit(solution)/shard_map/ppermute | solution.py:400
  4.1 16.1 %all-to-all-start = ((bf16[16,16,384]{2,1,0:T(8,128)(2,1)}), bf16[16,16,384]{2,1,0:T(8,128)(2,1)S(1)}, u32[]{:S(2)}, u32[]{:S(2)}) async-start(bf16[16,16,384]{2,1,0:T(8,128)(2,1)} %ask.1), calls=%async_computation | async-start | bytes 393216 | tf_op jit(solution)/shard_map/all_to_all | solution.py:417
  11.2 0.7 %copy-start.4 = (f32[1024]{0:T(1024)S(1)}, f32[1024]{0:T(1024)}, u32[]{:S(2)}) copy-start(f32[1024]{0:T(1024)} %param.18) | copy-start | bytes 12292
  20.2 8.7 %copy-start.5 = (f32[1024]{0:T(1024)S(1)}, f32[1024]{0:T(1024)}, u32[]{:S(2)}) copy-start(f32[1024]{0:T(1024)} %param.18) | copy-start | bytes 12292
  20.2 8.7 %copy-start.8 = (s32[1,4096]{1,0:T(1,128)S(1)}, s32[1,4096]{1,0:T(1,128)}, u32[]{:S(2)}) copy-start(s32[1,4096]{1,0:T(1,128)} %param.30) | copy-start | bytes 49156
  20.2 8.7 %copy-start.9 = (s32[4,1024]{1,0:T(4,128)S(1)}, s32[4,1024]{1,0:T(4,128)}, u32[]{:S(2)}) copy-start(s32[4,1024]{1,0:T(4,128)} %slot_ref) | copy-start | bytes 49156
  25.0 12.8 %copy-start = (bf16[1024,1024]{1,0:T(8,128)(2,1)S(1)}, bf16[1024,1024]{1,0:T(8,128)(2,1)}, u32[]{:S(2)}) copy-start(bf16[1024,1024]{1,0:T(8,128)(2,1)} %w_kv_ref.1) | copy-start | bytes 6291460
  25.0 12.8 %copy-start.2 = (bf16[512,1024]{1,0:T(8,128)(2,1)S(1)}, bf16[512,1024]{1,0:T(8,128)(2,1)}, u32[]{:S(2)}) copy-start(bf16[512,1024]{1,0:T(8,128)(2,1)} %w_o_ref.1) | copy-start | bytes 3145732
  25.0 12.8 %copy-start.3 = (bf16[16,1024]{1,0:T(8,128)(2,1)S(1)}, bf16[16,1024]{1,0:T(8,128)(2,1)}, u32[]{:S(2)}) copy-start(bf16[16,1024]{1,0:T(8,128)(2,1)} %latent_ref.3) | copy-start | bytes 98308
  25.0 12.8 %copy-start.6 = (f32[1024]{0:T(1024)S(1)}, f32[1024]{0:T(1024)}, u32[]{:S(2)}) copy-start(f32[1024]{0:T(1024)} %param.20) | copy-start | bytes 12292
  25.0 12.8 %all-to-all-start.1 = ((bf16[16,16,384]{2,1,0:T(8,128)(2,1)}), bf16[16,16,384]{2,1,0:T(8,128)(2,1)S(1)}, u32[]{:S(2)}, u32[]{:S(2)}) async-start(bf16[16,16,384]{2,1,0:T(8,128)(2,1)} %partial.1), calls=%async_computation.1 | async-start | bytes 393216 | tf_op jit(solution)/shard_map/all_to_all | solution.py:452
  37.8 17.4 %copy-start.7 = (bf16[512,1024]{1,0:T(8,128)(2,1)S(1)}, bf16[512,1024]{1,0:T(8,128)(2,1)}, u32[]{:S(2)}) copy-start(bf16[512,1024]{1,0:T(8,128)(2,1)} %w_ref.1) | copy-start | bytes 3145732
  39.5 15.7 %copy-start.1 = (bf16[1024,1024]{1,0:T(8,128)(2,1)S(1)}, bf16[1024,1024]{1,0:T(8,128)(2,1)}, u32[]{:S(2)}) copy-start(bf16[1024,1024]{1,0:T(8,128)(2,1)} %x_ref.1) | copy-start | bytes 6291460
  52.3 2.9 %collective-permute-start.1 = (bf16[256,512]{1,0:T(8,128)(2,1)S(1)}, bf16[256,512]{1,0:T(8,128)(2,1)S(1)}, u32[]{:S(2)}, u32[]{:S(2)}) collective-permute-start(bf16[256,512]{1,0:T(8,128)(2,1)S(1)} %bitcast.8), channel_id=1, source_target_pairs={{0,1},{1,0},{2,3},{3,2},{4,5},{5,4},{6,7},{7,6},{8,9},{9,8},{10,11... | collective-permute-start | bytes 786440 | tf_op jit(solution)/shard_map/ppermute | solution.py:495

commit v8 on v7

--- a/solution.py
+++ b/solution.py
@@ -60,16 +60,22 @@
     return pl.CostEstimate(flops=int(flops), bytes_accessed=int(read), transcendentals=int(exps))
 
 
-def ask_kernel(
-    latent_ref, gain_ref, slot_ref, count_ref, need_ref, w_hbm, out_ref, w_ref, sem
-):
-    copy = pltpu.make_async_copy(w_hbm, w_ref, sem)
-    copy.start()
+def ask_kernel(*refs):
+    sources, out_ref, held, sems = refs[:6], refs[6], refs[7:13], refs[13]
+    copies = started(
+        *[
+            pltpu.make_async_copy(source, ref, sems.at[i])
+            for i, (source, ref) in enumerate(zip(sources, held))
+        ]
+    )
+    w_ref, latent_ref, gain_ref, slot_ref, count_ref, need_ref = held
     rows = latent_ref.shape[0]
     width = w_ref.shape[1]
     entries = need_ref.shape[1]
     edges = slot_ref.shape[1]
     per = entries // rows
+    for copy in copies[1:]:
+        copy.wait()
     rows_normed = normed(latent_ref[...], gain_ref[...])
     eye = iota((rows, rows), 0) == iota((rows, rows), 1)
     counts = jnp.sum(jnp.where(eye, count_ref[...], 0), axis=1, keepdims=True)
@@ -84,7 +90,7 @@
         to = iota((entries, LANES), 1) == mod(iota((entries, LANES), 0), per) + 2 * edges + i * per
         spread = jnp.where(own, part.astype(f32), 0.0).astype(bf16)
         extra += dot(spread, to.astype(bf16))
-    copy.wait()
+    copies[0].wait()
     queries = dot(rows_normed, w_ref[...]).astype(bf16)
     half = width // 2
     for p in range(out_ref.shape[0]):
@@ -93,40 +99,34 @@
 
 
 def front_kernel(
-    steps, other_ref, gain_ref, own_hbm, w_hbm, out_hbm, own_ref, w_ref, pairs_ref, sems, out_sems
+    steps, other_ref, gain_hbm, own_hbm, w_hbm, pairs_ref, gain_ref, own_ref, w_ref, sems
 ):
     points = own_ref.shape[0]
     block = points // steps
     half = pairs_ref.shape[1] // 2
     core = lax.axis_index("dom") & 1
     copies = started(
+        pltpu.make_async_copy(gain_hbm, gain_ref, sems.at[0]),
         *[
             pltpu.make_async_copy(
                 w_hbm.at[:, pl.ds(pl.multiple_of((core + 2 * i) * half, half), half)],
                 w_ref.at[:, pl.ds(i * half, half)],
-                sems.at[i],
+                sems.at[1 + i],
             )
             for i in range(2)
         ],
-        pltpu.make_async_copy(own_hbm, own_ref, sems.at[2]),
+        pltpu.make_async_copy(own_hbm, own_ref, sems.at[3]),
     )
+    for copy in copies[:3]:
+        copy.wait()
     gain = gain_ref[...]
-    sends = []
-    for step in range(2 * steps):
-        rows_ref = other_ref if step < steps else own_ref
-        if step == 0:
-            copies[0].wait()
-            copies[1].wait()
-        if step == steps:
-            copies[2].wait()
-        part = pl.ds(step % steps * block, block)
-        place = pl.ds((step + steps) % (2 * steps) * block, block)
-        pairs_ref[place, :] = dot(normed(rows_ref[part, :], gain), w_ref[...]).astype(bf16)
-        sends += started(
-            pltpu.make_async_copy(pairs_ref.at[place], out_hbm.at[place], out_sems.at[step])
-        )
-    for send in sends:
-        send.wait()
+    for start, rows_ref in ((points, other_ref), (0, own_ref)):
+        if start == 0:
+            copies[3].wait()
+        for i in range(steps):
+            rows = normed(rows_ref[pl.ds(i * block, block), :], gain)
+            place = pl.ds(start + i * block, block)
+            pairs_ref[place, :] = dot(rows, w_ref[...]).astype(bf16)
 
 
 def stat_parts(top, total):
@@ -136,9 +136,7 @@
     return top_1, top_2, top - top_1 - top_2, total_1, total - total_1
 
 
-def partial_kernel(cap, edges, asked_ref, pairs_hbm, out_ref, pairs_ref, mixed_ref, sem):
-    copy = pltpu.make_async_copy(pairs_hbm, pairs_ref, sem)
-    copy.start()
+def partial_kernel(cap, edges, asked_ref, pairs_ref, out_ref, mixed_ref):
     me = lax.axis_index("dom")
     points, both = pairs_ref.shape
     points = points // 2
@@ -184,7 +182,6 @@
                     repeat, part, (((1,), (0,)), ((), ())), precision=lax.Precision.HIGHEST
                 )
             biases.append(jnp.where(here, repeated, NEG))
-    copy.wait()
     gathered = [
         dot(chosen[other], pairs_ref[other * points : (other + 1) * points, :]).astype(bf16)
         for other in range(2)
@@ -264,8 +261,8 @@
 
 
 def middle_kernel(
-    steps, cap, rows, gain_ref, need_ref, slot_ref, x_hbm, w_hbm, out_hbm, node_ref,
-    x_ref, w_ref, query_ref, sems, out_sems,
+    steps, cap, rows, gain_ref, need_ref, slot_ref, x_hbm, w_hbm, query_ref, node_ref,
+    x_ref, w_ref, sems,
 ):
     copies = started(
         pltpu.make_async_copy(w_hbm, w_ref, sems.at[0]),
@@ -284,16 +281,10 @@
         node_ref[j : j + 1, :] = div(slots, cap) * rows + found
     for copy in copies:
         copy.wait()
-    sends = []
     for i in range(steps):
         part = pl.ds(i * block, block)
         queries = dot(normed(x_ref[part, :], gain_ref[...]), w_ref[...])
         query_ref[:, part] = queries.T.astype(bf16)
-        sends += started(
-            pltpu.make_async_copy(query_ref.at[:, part], out_hbm.at[:, part], out_sems.at[i])
-        )
-    for send in sends:
-        send.wait()
 
 
 def attend_half(pairs, queries, nodes):
@@ -303,18 +294,19 @@
     size = half // heads
     node = iota((pairs.shape[1], points), 0)
     picks = [(nodes[j : j + 1] == node).astype(bf16) for j in range(edges)]
-    scores = []
+    scores, values = [], []
     for j in range(edges):
-        products = dot(pairs[:half], picks[j]) * queries.astype(f32)
-        score = jnp.sum(products.reshape(heads, size, points), axis=1)
-        scores.append(score * (1.0 / math.sqrt(size)))
+        chosen = dot(pairs, picks[j])
+        products = (chosen[:half] * queries.astype(f32)).reshape(heads, size, points)
+        scores.append(jnp.sum(products, axis=1) * (1.0 / math.sqrt(size)))
+        values.append(chosen[half:].reshape(heads, size, points))
     highest = functools.reduce(jnp.maximum, scores)
     raised = [jnp.exp(score - highest) for score in scores]
     inverse = 1.0 / sum(raised)
     mixed = jnp.zeros((heads, size, points), f32)
     for j in range(edges):
         weight = (raised[j] * inverse).astype(bf16).astype(f32).reshape(heads, 1, points)
-        mixed += dot(pairs[half:], picks[j]).reshape(heads, size, points) * weight
+        mixed += values[j] * weight
     return mixed.reshape(half, points).T.astype(bf16)
 
 
@@ -322,47 +314,44 @@
     return ref.at[pl.ds(pl.multiple_of(first, half), half)]
 
 
-def own_kernel(steps, pairs_ref, node_ref, query_hbm, out_ref, query_ref, sem):
+def own_kernel(steps, pairs_ref, node_ref, query_ref, out_ref):
     points, half = out_ref.shape
     block = points // steps
     core = lax.axis_index("dom") & 1
-    copy = pltpu.make_async_copy(half_of(query_hbm, core * half, half), query_ref, sem)
-    copy.start()
+    queries = half_of(query_ref, core * half, half)
     pairs = pairs_ref[...].T
-    copy.wait()
     for i in range(steps):
         part = pl.ds(i * block, block)
-        out_ref[part, :] = attend_half(pairs, query_ref[:, part], node_ref[:, part])
+        out_ref[part, :] = attend_half(pairs, queries[:, part], node_ref[:, part])
 
 
 def other_kernel(
-    steps, pairs_ref, own_ref, node_ref, x_ref, w_ref, query_hbm, out_hbm,
-    query_ref, out_ref, sem, out_sems,
+    steps, pairs_ref, own_ref, node_ref, query_ref, x_ref, w_ref, out_hbm, out_ref, sems
 ):
     points, half = own_ref.shape
     block = points // steps
     core = lax.axis_index("dom") & 1
-    copy = pltpu.make_async_copy(half_of(query_hbm, (1 - core) * half, half), query_ref, sem)
-    copy.start()
-    pairs = pairs_ref[...].T
+    queries = half_of(query_ref, (1 - core) * half, half)
     own_w = half_of(w_ref, core * half, half)
     other_w = half_of(w_ref, (1 - core) * half, half)
-    copy.wait()
+    pairs = pairs_ref[...].T
     sends = []
     for i in range(steps):
         part = pl.ds(i * block, block)
-        mixed = attend_half(pairs, query_ref[:, part], node_ref[:, part])
+        mixed = attend_half(pairs, queries[:, part], node_ref[:, part])
         update = dot(own_ref[part, :], own_w[...]) + dot(mixed, other_w[...])
         out_ref[part, :] = (x_ref[part, :].astype(f32) + update).astype(bf16)
-        sends += started(
-            pltpu.make_async_copy(out_ref.at[part], out_hbm.at[part], out_sems.at[i])
-        )
+        sends += started(pltpu.make_async_copy(out_ref.at[part], out_hbm.at[part], sems.at[i]))
     for send in sends:
         send.wait()
 
 
 def in_hbm(array):
     return pltpu.with_memory_space_constraint(array, pltpu.HBM)
+
+
+def in_vmem(array):
+    return pltpu.with_memory_space_constraint(array, pltpu.VMEM)
 
 
 def on_device(
@@ -398,56 +387,53 @@
     hbm = pl.BlockSpec(memory_space=pltpu.HBM)
 
     other_grid = lax.ppermute(grid, "dom", swap)
-    asked = pl.pallas_call(
-        ask_kernel,
-        in_specs=[vmem] * 5 + [hbm],
-        out_shape=jax.ShapeDtypeStruct((peers, rows, sent), bf16),
-        scratch_shapes=[pltpu.VMEM((depth, width), bf16), pltpu.SemaphoreType.DMA],
-        compiler_params=params(58),
-        cost_estimate=cost(2 * rows * depth * width, 2 * depth * width),
-        name="ask",
-    )(
+    ask_inputs = (
+        w_q_enc,
         latent_in,
         node_gain.reshape(1, -1),
         enc_slot.T,
         enc_count.reshape(1, -1),
         enc_need,
-        in_hbm(w_q_enc),
     )
+    asked = pl.pallas_call(
+        ask_kernel,
+        in_specs=[hbm] * len(ask_inputs),
+        out_shape=jax.ShapeDtypeStruct((peers, rows, sent), bf16),
+        scratch_shapes=[pltpu.VMEM(one.shape, one.dtype) for one in ask_inputs]
+        + [pltpu.SemaphoreType.DMA((len(ask_inputs),))],
+        compiler_params=params(58),
+        cost_estimate=cost(2 * rows * depth * width, 2 * depth * width),
+        name="ask",
+    )(*map(in_hbm, ask_inputs))
     asked = lax.all_to_all(asked, "dom", split_axis=0, concat_axis=0, tiled=True)
 
     block = math.gcd(points, 256)
     steps = points // block
     pairs = pl.pallas_call(
         functools.partial(front_kernel, steps),
-        in_specs=[vmem, vmem, hbm, hbm],
-        out_specs=hbm,
-        out_shape=pltpu.HBM((2 * points, width), bf16),
+        in_specs=[vmem, hbm, hbm, hbm],
+        out_specs=vmem,
+        out_shape=pltpu.VMEM((2 * points, width), bf16),
         scratch_shapes=[
+            pltpu.VMEM((1, depth), f32),
             pltpu.VMEM((points, depth), bf16),
             pltpu.VMEM((depth, width), bf16),
-            pltpu.VMEM((2 * points, width), bf16),
-            pltpu.SemaphoreType.DMA((3,)),
-            pltpu.SemaphoreType.DMA((2 * steps,)),
+            pltpu.SemaphoreType.DMA((4,)),
         ],
         compiler_params=params(40),
         cost_estimate=cost(4 * points * depth * width, 8 * points * depth),
         name="front",
-    )(other_grid, grid_gain.reshape(1, -1), in_hbm(grid), in_hbm(w_kv_enc))
+    )(other_grid, in_hbm(grid_gain.reshape(1, -1)), in_hbm(grid), in_hbm(w_kv_enc))
 
     parts = pl.pallas_call(
         functools.partial(partial_kernel, cap, edges),
-        in_specs=[vmem, hbm],
+        in_specs=[vmem, vmem],
         out_shape=jax.ShapeDtypeStruct((peers, rows, sent), bf16),
-        scratch_shapes=[
-            pltpu.VMEM((2 * points, width), bf16),
-            pltpu.VMEM((sent, nodes // 2), f32),
-            pltpu.SemaphoreType.DMA,
-        ],
+        scratch_shapes=[pltpu.VMEM((sent, nodes // 2), f32)],
         compiler_params=params(40),
         cost_estimate=cost(4 * entries * points * width, 4 * points * width),
         name="partial",
-    )(asked.reshape(nodes, sent), in_hbm(pairs))
+    )(asked.reshape(nodes, sent), in_vmem(pairs))
     parts, dec_need, dec_slot = lax.optimization_barrier((parts, dec_need, dec_slot))
     parts = lax.all_to_all(parts, "dom", split_axis=0, concat_axis=0, tiled=True)
 
@@ -456,17 +442,15 @@
     queries, node_of = pl.pallas_call(
         functools.partial(middle_kernel, steps, slot_total // peers, rows),
         in_specs=[vmem] * 3 + [hbm] * 2,
-        out_specs=[hbm, vmem],
+        out_specs=[vmem, vmem],
         out_shape=[
-            pltpu.HBM((width, points), bf16),
+            pltpu.VMEM((width, points), bf16),
             jax.ShapeDtypeStruct((edge_count, points), jnp.int32),
         ],
         scratch_shapes=[
             pltpu.VMEM((points, depth), bf16),
             pltpu.VMEM((depth, width), bf16),
-            pltpu.VMEM((width, points), bf16),
             pltpu.SemaphoreType.DMA((2,)),
-            pltpu.SemaphoreType.DMA((steps,)),
         ],
         compiler_params=params(40),
         cost_estimate=cost(2 * points * depth * width, 8 * points * depth),
@@ -494,30 +478,28 @@
     own = own.reshape(nodes, width)
     other = lax.ppermute(own, "dom", swap)
 
+    queries = in_vmem(queries)
     own_mixed = pl.pallas_call(
-        functools.partial(own_kernel, max(steps // 2, 1)),
-        in_specs=[vmem, vmem, hbm],
+        functools.partial(own_kernel, steps),
+        in_specs=[vmem] * 3,
         out_shape=jax.ShapeDtypeStruct((points, half), bf16),
-        scratch_shapes=[pltpu.VMEM((half, points), bf16), pltpu.SemaphoreType.DMA],
         compiler_params=params(48),
         cost_estimate=cost(4 * points * nodes * width, 8 * points * nodes),
         name="own",
-    )(own, node_of, in_hbm(queries))
+    )(own, node_of, queries)
     grid_out = pl.pallas_call(
         functools.partial(other_kernel, steps),
-        in_specs=[vmem] * 5 + [hbm],
+        in_specs=[vmem] * 6,
         out_specs=hbm,
         out_shape=pltpu.HBM((points, depth), bf16),
         scratch_shapes=[
-            pltpu.VMEM((half, points), bf16),
             pltpu.VMEM((points, depth), bf16),
-            pltpu.SemaphoreType.DMA,
             pltpu.SemaphoreType.DMA((steps,)),
         ],
         compiler_params=params(48),
         cost_estimate=cost(4 * points * depth * width, 8 * points * depth),
         name="other",
-    )(other, own_mixed, node_of, grid, w_o_dec, in_hbm(queries))
+    )(other, own_mixed, node_of, queries, grid, w_o_dec)
     return (latent_out, grid_out)
 
 

time: 61.2 us -> 58.3 us (0.953)
  Pallas kernels: 26.6 us -> 20.7 us
  local copies, waits for them, and re-layouts: 0.73 us -> 3.91 us
    unnamed x20 -> x26, local copies, waits for them, and re-layouts: 0.73 us -> 3.91 us
    pallas_call x3, Pallas kernels: 10.6 us -> 8.03 us  [the longest x1 4 us: on_device(): pl.pallas_call(functools.partial(front_kernel, steps), in_specs=[vmem, hb...]
    pallas_call x1, Pallas kernels: 4.78 us -> 3.39 us  [on_device(): pl.pallas_call(functools.partial(partial_kernel, cap, edges), in_specs=[v...]
    pallas_call x1, Pallas kernels: 5.2 us -> 4.09 us  [on_device(): pl.pallas_call(functools.partial(other_kernel, steps), in_specs=[vmem] *...]
    pallas_call x1, Pallas kernels: 4.31 us -> 3.54 us  [on_device(): pl.pallas_call(functools.partial(middle_kernel, steps, slot_total // peer...]
  transfers between devices with their start and end apart: 4 -> 4, of which waited for: 2 -> 2; matrix products, arithmetic and copies ran while one was open for 0% -> 0% of each run, Pallas kernels for 25% -> 20%
where the time goes in v8:
time: 58.3 us; the launch traced here: 57.8 us
  Pallas kernels  20.7 us (36%)
  blocking collectives  12.8 us (22%)
  starting transfers between devices  11.4 us (20%)
  waiting for transfers between devices  8.07 us (14%)
  local copies, waits for them, and re-layouts  3.91 us (7%)
  between operations  0.94 us (2%)
    all_to_all x1, blocking collectives, on_device(): lax.all_to_all(everyone, 'dom', split_axis=0, concat_axis=0, tiled=True)  12.8 us
    all_to_all x1, starting transfers between devices, on_device(): lax.all_to_all(asked, 'dom', split_axis=0, concat_axis=0, tiled=True)  7.06 us
    all_to_all x1, waiting for transfers between devices, on_device(): lax.all_to_all(parts, 'dom', split_axis=0, concat_axis=0, tiled=True)  4.41 us
    pallas_call x1, Pallas kernels, on_device(): pl.pallas_call(functools.partial(other_kernel, steps), in_specs=[vmem] *...  4.09 us
    pallas_call x1, Pallas kernels, on_device(): pl.pallas_call(functools.partial(front_kernel, steps), in_specs=[vmem, hb...  4 us
    unnamed x26, local copies, waits for them, and re-layouts  3.91 us
    all_to_all x1, starting transfers between devices, on_device(): lax.all_to_all(parts, 'dom', split_axis=0, concat_axis=0, tiled=True)  3.8 us
    all_to_all x1, waiting for transfers between devices, on_device(): lax.all_to_all(asked, 'dom', split_axis=0, concat_axis=0, tiled=True)  3.66 us
  transfers between devices with their start and end apart: 4, of which 2 were waited for; matrix products, arithmetic and copies ran while one was open for 0% of the time, Pallas kernels for 20%

profile of v8, /device:TPU:0, one launch (start us, length us, event | category | flops | bytes accessed | tf_op | source)
XLA Modules:
  0.0 57.8 jit_solution(13618756362327787598)
XLA Ops:
  0.6 0.5 collective-permute-start
  1.1 2.4 %ask.1 = bf16[16,16,384]{2,1,0:T(8,128)(2,1)} custom-call(bf16[1024,512]{1,0:T(8,128)(2,1)} %refs_0_.1, bf16[16,1024]{1,0:T(8,128)(2,1)} %latent_ref.1, f32[1,1024]{1,0:T(1,128)} %bitcast.16, s32[16,32]{1,0:T(8,128)} %bitcast.15, s32[1,16]{1,0:T(1,128)} %bitcast.17, s32[1,512]{1,0:T(1,128)} %refs_5_.1), custom_call_target="tpu_custom_call" | custom-call | flops 16777216 | bytes 1048576 | tf_op jit(solution)/shard_map/ask/pallas_call | solution.py:398
  3.5 7.1 %all-to-all-start = ((bf16[16,16,384]{2,1,0:T(8,128)(2,1)}), bf16[16,16,384]{2,1,0:T(8,128)(2,1)S(1)}, u32[]{:S(2)}, u32[]{:S(2)}) async-start(bf16[16,16,384]{2,1,0:T(8,128)(2,1)} %ask.1), calls=%async_computation | async-start | bytes 393216 | tf_op jit(solution)/shard_map/all_to_all | solution.py:408
  10.6 0.0 collective-permute-done.other_ref
  10.6 4.0 %front.1.pairs_ref = bf16[2048,512]{1,0:T(8,128)(2,1)S(1)} custom-call(bf16[1024,1024]{1,0:T(8,128)(2,1)S(1)} %collective-permute-done.other_ref, f32[1,1024]{1,0:T(1,128)} %bitcast.11, bf16[1024,1024]{1,0:T(8,128)(2,1)} %x_ref.1, bf16[1024,1024]{1,0:T(8,128)(2,1)} %w_hbm.2), custom_call_target="tpu_custom_call" | custom-call | flops 2147483648 | bytes 8388608 | tf_op jit(solution)/shard_map/front/pallas_call | solution.py:412
  14.6 0.0 copy-start.2
  14.6 1.3 %copy-done.2 = bf16[2048,512]{1,0:T(8,128)(2,1)} copy-done((bf16[2048,512]{1,0:T(8,128)(2,1)}, bf16[2048,512]{1,0:T(8,128)(2,1)S(1)}, u32[]{:S(2)}) %copy-start.2) | copy-done | bytes 2097176
  15.9 3.7 %all-to-all-done = bf16[16,16,384]{2,1,0:T(8,128)(2,1)S(1)} async-done(((bf16[16,16,384]{2,1,0:T(8,128)(2,1)}), bf16[16,16,384]{2,1,0:T(8,128)(2,1)S(1)}, u32[]{:S(2)}, u32[]{:S(2)}) %all-to-all-start) | async-done | bytes 196640 | tf_op jit(solution)/shard_map/all_to_all | solution.py:408
  19.6 0.0 copy-start.3
  19.6 1.6 %copy-done.3 = bf16[2048,512]{1,0:T(8,128)(2,1)S(1)} copy-done((bf16[2048,512]{1,0:T(8,128)(2,1)S(1)}, bf16[2048,512]{1,0:T(8,128)(2,1)}, u32[]{:S(2)}) %copy-start.3) | copy-done | bytes 2097176
  21.2 0.0 copy-start.6
  21.2 0.0 copy-start.9
  21.2 0.0 copy-start.10
  21.2 3.4 %partial.1 = bf16[16,16,384]{2,1,0:T(8,128)(2,1)} custom-call(bf16[256,384]{1,0:T(8,128)(2,1)S(1)} %bitcast.10, bf16[2048,512]{1,0:T(8,128)(2,1)S(1)} %copy-done.3), custom_call_target="tpu_custom_call" | custom-call | flops 1073741824 | bytes 2097152 | tf_op jit(solution)/shard_map/partial/pallas_call | solution.py:428
  24.6 0.0 copy-start
  24.6 0.0 copy-start.4
  24.6 0.0 copy-start.5
  24.6 0.0 copy-start.7
  24.6 3.8 %all-to-all-start.1 = ((bf16[16,16,384]{2,1,0:T(8,128)(2,1)}), bf16[16,16,384]{2,1,0:T(8,128)(2,1)S(1)}, u32[]{:S(2)}, u32[]{:S(2)}) async-start(bf16[16,16,384]{2,1,0:T(8,128)(2,1)} %partial.1), calls=%async_computation.1 | async-start | bytes 393216 | tf_op jit(solution)/shard_map/all_to_all | solution.py:438
  28.4 0.0 copy-done.6
  28.4 0.0 copy-done.9
  28.4 0.0 copy-done.10
  28.4 3.5 %middle.1 = (bf16[512,1024]{1,0:T(8,128)(2,1)S(1)}, s32[4,1024]{1,0:T(4,128)S(1)}) custom-call(f32[1,1024]{1,0:T(1,128)S(1)} %bitcast.12, s32[32,128]{1,0:T(8,128)S(1)} %bitcast.14, s32[4,1024]{1,0:T(4,128)S(1)} %copy-done.10, bf16[1024,1024]{1,0:T(8,128)(2,1)} %x_ref.1, bf16[1024,512]{1,0:T(8,128)(2,1)} %w_hbm.3), custom_call_target="tpu_custom_call" | custom-call | flops 1073741824 | bytes 8388608 | tf_op jit(solution)/shard_map/middle/pallas_call | solution.py:442
  32.0 0.0 copy-start.11
  32.0 1.0 %copy-done.11 = bf16[512,1024]{1,0:T(8,128)(2,1)} copy-done((bf16[512,1024]{1,0:T(8,128)(2,1)}, bf16[512,1024]{1,0:T(8,128)(2,1)S(1)}, u32[]{:S(2)}) %copy-start.11) | copy-done | bytes 1048600
  33.0 4.4 %all-to-all-done.1.parts_ref = bf16[16,16,384]{2,1,0:T(8,128)(2,1)S(1)} async-done(((bf16[16,16,384]{2,1,0:T(8,128)(2,1)}), bf16[16,16,384]{2,1,0:T(8,128)(2,1)S(1)}, u32[]{:S(2)}, u32[]{:S(2)}) %all-to-all-start.1) | async-done | bytes 196640 | tf_op jit(solution)/shard_map/all_to_all | solution.py:438
  37.4 0.0 copy-start.12
  37.4 0.0 copy-done
  37.4 0.0 copy-done.4
  37.4 0.0 copy-done.5
  37.4 0.0 copy-done.7
  37.4 0.0 copy-start.8
  37.4 1.7 %combine.1 = (bf16[16,1024]{1,0:T(8,128)(2,1)}, bf16[16,16,512]{2,1,0:T(8,128)(2,1)S(1)}) custom-call(bf16[16,16,384]{2,1,0:T(8,128)(2,1)S(1)} %all-to-all-done.1.parts_ref, bf16[16,1024]{1,0:T(8,128)(2,1)S(1)} %copy-done.5, f32[1,1024]{1,0:T(1,128)S(1)} %bitcast.13, bf16[512,1024]{1,0:T(8,128)(2,1)S(1)} %copy-done.4, bf16[1024,1024]{1,0:T(8,128)(2,1)S(1)} %copy-done), custom_call_target="tpu_custom_call" | custom-call | flops 50331648 | bytes 3145728 | tf_op jit(solution)/shard_map/combine/pallas_call | solution.py:467
  39.1 0.0 copy-start.1
  39.1 12.8 %all_to_all.15 = bf16[16,16,512]{2,1,0:T(8,128)(2,1)S(1)} all-to-all(bf16[16,16,512]{2,1,0:T(8,128)(2,1)S(1)} %get-tuple-element.19), channel_id=1, replica_groups=mesh['groups'=2,'dom'=16] {'dom'}, dimensions={0} | all-to-all | bytes 524288 | tf_op jit(solution)/shard_map/all_to_all | solution.py:477
  51.8 0.0 collective-permute-start.1
  51.8 0.0 copy-done.12
  51.8 1.6 %own.1.own_ref = bf16[1024,256]{1,0:T(8,128)(2,1)S(1)} custom-call(bf16[256,512]{1,0:T(8,128)(2,1)S(1)} %bitcast.9, s32[4,1024]{1,0:T(4,128)S(1)} %get-tuple-element.20.node_ref, bf16[512,1024]{1,0:T(8,128)(2,1)S(1)} %copy-done.12), custom_call_target="tpu_custom_call" | custom-call | flops 536870912 | bytes 2097152 | tf_op jit(solution)/shard_map/own/pallas_call | solution.py:482
  53.5 0.0 collective-permute-done.1.pairs_ref
  53.5 0.0 copy-done.8
  53.5 0.0 copy-done.1
  53.5 4.1 %other.1 = bf16[1024,1024]{1,0:T(8,128)(2,1)} custom-call(bf16[256,512]{1,0:T(8,128)(2,1)S(1)} %collective-permute-done.1.pairs_ref, bf16[1024,256]{1,0:T(8,128)(2,1)S(1)} %own.1.own_ref, s32[4,1024]{1,0:T(4,128)S(1)} %get-tuple-element.20.node_ref, bf16[512,1024]{1,0:T(8,128)(2,1)S(1)} %copy-done.12, bf16[1024,1024]{1,0:T(8,128)(2,1)S(1)} %copy-done.1, ...), custom_call_target="tpu_custom_call" | custom-call | flops 2147483648 | bytes 8388608 | tf_op jit(solution)/shard_map/other/pallas_call | solution.py:490
Async XLA Ops:
  0.6 10.0 %collective-permute-start = (bf16[1024,1024]{1,0:T(8,128)(2,1)}, bf16[1024,1024]{1,0:T(8,128)(2,1)S(1)}, u32[]{:S(2)}, u32[]{:S(2)}) collective-permute-start(bf16[1024,1024]{1,0:T(8,128)(2,1)} %x_ref.1), channel_id=1, source_target_pairs={{0,1},{1,0},{2,3},{3,2},{4,5},{5,4},{6,7},{7,6},{8,9},{9,8},{10,11... | collective-permute-start | bytes 6291464 | tf_op jit(solution)/shard_map/ppermute | solution.py:389
  3.5 16.1 %all-to-all-start = ((bf16[16,16,384]{2,1,0:T(8,128)(2,1)}), bf16[16,16,384]{2,1,0:T(8,128)(2,1)S(1)}, u32[]{:S(2)}, u32[]{:S(2)}) async-start(bf16[16,16,384]{2,1,0:T(8,128)(2,1)} %ask.1), calls=%async_computation | async-start | bytes 393216 | tf_op jit(solution)/shard_map/all_to_all | solution.py:408
  14.6 1.3 %copy-start.2 = (bf16[2048,512]{1,0:T(8,128)(2,1)}, bf16[2048,512]{1,0:T(8,128)(2,1)S(1)}, u32[]{:S(2)}) copy-start(bf16[2048,512]{1,0:T(8,128)(2,1)S(1)} %front.1.pairs_ref) | copy-start | bytes 6291460
  19.6 1.6 %copy-start.3 = (bf16[2048,512]{1,0:T(8,128)(2,1)S(1)}, bf16[2048,512]{1,0:T(8,128)(2,1)}, u32[]{:S(2)}) copy-start(bf16[2048,512]{1,0:T(8,128)(2,1)} %copy-done.2) | copy-start | bytes 6291460
  21.2 7.2 %copy-start.6 = (f32[1024]{0:T(1024)S(1)}, f32[1024]{0:T(1024)}, u32[]{:S(2)}) copy-start(f32[1024]{0:T(1024)} %param.18) | copy-start | bytes 12292
  21.2 7.2 %copy-start.9 = (s32[1,4096]{1,0:T(1,128)S(1)}, s32[1,4096]{1,0:T(1,128)}, u32[]{:S(2)}) copy-start(s32[1,4096]{1,0:T(1,128)} %param.30) | copy-start | bytes 49156
  21.2 7.2 %copy-start.10 = (s32[4,1024]{1,0:T(4,128)S(1)}, s32[4,1024]{1,0:T(4,128)}, u32[]{:S(2)}) copy-start(s32[4,1024]{1,0:T(4,128)} %slot_ref) | copy-start | bytes 49156
  24.6 12.8 %copy-start = (bf16[1024,1024]{1,0:T(8,128)(2,1)S(1)}, bf16[1024,1024]{1,0:T(8,128)(2,1)}, u32[]{:S(2)}) copy-start(bf16[1024,1024]{1,0:T(8,128)(2,1)} %w_kv_ref.1) | copy-start | bytes 6291460
  24.6 12.8 %copy-start.4 = (bf16[512,1024]{1,0:T(8,128)(2,1)S(1)}, bf16[512,1024]{1,0:T(8,128)(2,1)}, u32[]{:S(2)}) copy-start(bf16[512,1024]{1,0:T(8,128)(2,1)} %w_o_ref.1) | copy-start | bytes 3145732
  24.6 12.8 %copy-start.5 = (bf16[16,1024]{1,0:T(8,128)(2,1)S(1)}, bf16[16,1024]{1,0:T(8,128)(2,1)}, u32[]{:S(2)}) copy-start(bf16[16,1024]{1,0:T(8,128)(2,1)} %latent_ref.1) | copy-start | bytes 98308
  24.6 12.8 %copy-start.7 = (f32[1024]{0:T(1024)S(1)}, f32[1024]{0:T(1024)}, u32[]{:S(2)}) copy-start(f32[1024]{0:T(1024)} %param.20) | copy-start | bytes 12292
  24.6 12.8 %all-to-all-start.1 = ((bf16[16,16,384]{2,1,0:T(8,128)(2,1)}), bf16[16,16,384]{2,1,0:T(8,128)(2,1)S(1)}, u32[]{:S(2)}, u32[]{:S(2)}) async-start(bf16[16,16,384]{2,1,0:T(8,128)(2,1)} %partial.1), calls=%async_computation.1 | async-start | bytes 393216 | tf_op jit(solution)/shard_map/all_to_all | solution.py:438
  32.0 1.0 %copy-start.11 = (bf16[512,1024]{1,0:T(8,128)(2,1)}, bf16[512,1024]{1,0:T(8,128)(2,1)S(1)}, u32[]{:S(2)}) copy-start(bf16[512,1024]{1,0:T(8,128)(2,1)S(1)} %get-tuple-element.21.query_ref) | copy-start | bytes 3145732
  37.4 14.5 %copy-start.12 = (bf16[512,1024]{1,0:T(8,128)(2,1)S(1)}, bf16[512,1024]{1,0:T(8,128)(2,1)}, u32[]{:S(2)}) copy-start(bf16[512,1024]{1,0:T(8,128)(2,1)} %copy-done.11) | copy-start | bytes 3145732
  37.4 16.1 %copy-start.8 = (bf16[512,1024]{1,0:T(8,128)(2,1)S(1)}, bf16[512,1024]{1,0:T(8,128)(2,1)}, u32[]{:S(2)}) copy-start(bf16[512,1024]{1,0:T(8,128)(2,1)} %w_ref.1) | copy-start | bytes 3145732
  39.1 14.4 %copy-start.1 = (bf16[1024,1024]{1,0:T(8,128)(2,1)S(1)}, bf16[1024,1024]{1,0:T(8,128)(2,1)}, u32[]{:S(2)}) copy-start(bf16[1024,1024]{1,0:T(8,128)(2,1)} %x_ref.1) | copy-start | bytes 6291460
  51.8 1.7 %collective-permute-start.1 = (bf16[256,512]{1,0:T(8,128)(2,1)S(1)}, bf16[256,512]{1,0:T(8,128)(2,1)S(1)}, u32[]{:S(2)}, u32[]{:S(2)}) collective-permute-start(bf16[256,512]{1,0:T(8,128)(2,1)S(1)} %bitcast.8), channel_id=1, source_target_pairs={{0,1},{1,0},{2,3},{3,2},{4,5},{5,4},{6,7},{7,6},{8,9},{9,8},{10,11... | collective-permute-start | bytes 786440 | tf_op jit(solution)/shard_map/ppermute | solution.py:479

commit v9 on v8

--- a/solution.py
+++ b/solution.py
@@ -58,6 +58,10 @@
 
 def cost(flops, read, exps=0):
     return pl.CostEstimate(flops=int(flops), bytes_accessed=int(read), transcendentals=int(exps))
+
+
+def columns_of(ref, where, rows, half):
+    return [ref[where, i * rows : (i + 1) * rows, :] for i in range(half // LANES)]
 
 
 def ask_kernel(*refs):
@@ -73,37 +77,48 @@
     width = w_ref.shape[1]
     entries = need_ref.shape[1]
     edges = slot_ref.shape[1]
-    per = entries // rows
+    peers = out_ref.shape[0]
+    both = 2 * entries // peers
+    tall = rows // 2
     for copy in copies[1:]:
         copy.wait()
     rows_normed = normed(latent_ref[...], gain_ref[...])
-    eye = iota((rows, rows), 0) == iota((rows, rows), 1)
-    counts = jnp.sum(jnp.where(eye, count_ref[...], 0), axis=1, keepdims=True)
-    slots = jnp.where(iota((rows, edges), 1) < counts, slot_ref[...], 65535)
+    live = iota((edges, rows), 0) < count_ref[...]
+    slots = slot_ref[...].astype(f32).T.astype(jnp.int32)
+    slots = jnp.where(live, slots, entries) - entries // 2
+    slots = slots.astype(f32).astype(bf16)
+    tile = jnp.zeros((tall, LANES), f32)
+    for g in range(edges // tall):
+        to = iota((rows, LANES), 1) == iota((rows, LANES), 0) + g * rows
+        tile += dot(slots, to.astype(bf16))[g * tall : (g + 1) * tall]
+    row, lane = iota((tall, LANES), 0), iota((tall, LANES), 1)
+    in_list = (lane >= LANES // 2) & (lane < LANES // 2 + both)
     need = need_ref[...]
-    own = div(iota((rows, entries), 1), per) == iota((rows, entries), 0)
-    extra = jnp.zeros((rows, LANES), f32)
-    for i, part in enumerate((slots & 255, slots >> 8)):
-        to = iota((edges, LANES), 1) == iota((edges, LANES), 0) + i * edges
-        extra += dot(part.astype(f32).astype(bf16), to.astype(bf16))
-    for i, part in enumerate((need & 255, need >> 8)):
-        to = iota((entries, LANES), 1) == mod(iota((entries, LANES), 0), per) + 2 * edges + i * per
-        spread = jnp.where(own, part.astype(f32), 0.0).astype(bf16)
-        extra += dot(spread, to.astype(bf16))
+    tiles = []
+    for chip in range(peers // 2):
+        at = chip * both
+        piece = need[:, at // LANES * LANES : at // LANES * LANES + LANES].astype(f32)
+        piece = pltpu.roll(jnp.broadcast_to(piece, (tall, LANES)), (LANES // 2 - at) % LANES, 1)
+        high = jnp.floor(piece * (1.0 / 256.0))
+        piece = jnp.where(row == 0, piece - high * 256.0, jnp.where(row == 1, high, 0.0))
+        tiles.append((tile + jnp.where(in_list, piece, 0.0)).astype(bf16))
     copies[0].wait()
     queries = dot(rows_normed, w_ref[...]).astype(bf16)
     half = width // 2
-    for p in range(out_ref.shape[0]):
-        out_ref[p, :, :half] = queries[:, p % 2 * half : (p % 2 + 1) * half]
-        out_ref[p, :, half:] = extra.astype(bf16)
+    for p in range(peers):
+        for i in range(half // LANES):
+            at = p % 2 * half + i * LANES
+            out_ref[p, i * rows : (i + 1) * rows, :] = queries[:, at : at + LANES]
+        out_ref[p, half // LANES * rows :, :] = tiles[p // 2]
 
 
 def front_kernel(
-    steps, other_ref, gain_hbm, own_hbm, w_hbm, pairs_ref, gain_ref, own_ref, w_ref, sems
+    steps, gain_hbm, own_hbm, other_hbm, w_hbm, own_out_ref, other_out_ref,
+    gain_ref, own_ref, other_ref, w_ref, sems,
 ):
     points = own_ref.shape[0]
     block = points // steps
-    half = pairs_ref.shape[1] // 2
+    half = own_out_ref.shape[1] // 2
     core = lax.axis_index("dom") & 1
     copies = started(
         pltpu.make_async_copy(gain_hbm, gain_ref, sems.at[0]),
@@ -116,17 +131,19 @@
             for i in range(2)
         ],
         pltpu.make_async_copy(own_hbm, own_ref, sems.at[3]),
+        pltpu.make_async_copy(other_hbm, other_ref, sems.at[4]),
     )
     for copy in copies[:3]:
         copy.wait()
     gain = gain_ref[...]
-    for start, rows_ref in ((points, other_ref), (0, own_ref)):
-        if start == 0:
-            copies[3].wait()
+    for copy, rows_ref, out_ref in (
+        (copies[3], own_ref, own_out_ref),
+        (copies[4], other_ref, other_out_ref),
+    ):
+        copy.wait()
         for i in range(steps):
-            rows = normed(rows_ref[pl.ds(i * block, block), :], gain)
-            place = pl.ds(start + i * block, block)
-            pairs_ref[place, :] = dot(rows, w_ref[...]).astype(bf16)
+            part = pl.ds(i * block, block)
+            out_ref[part, :] = dot(normed(rows_ref[part, :], gain), w_ref[...]).astype(bf16)
 
 
 def stat_parts(top, total):
@@ -136,38 +153,51 @@
     return top_1, top_2, top - top_1 - top_2, total_1, total - total_1
 
 
-def partial_kernel(cap, edges, asked_ref, pairs_ref, out_ref, mixed_ref):
+def partial_kernel(cap, rows, edges, asked_ref, *refs):
+    pairs_refs, out_ref, mixed_ref = refs[:2], refs[2], refs[3]
     me = lax.axis_index("dom")
-    points, both = pairs_ref.shape
-    points = points // 2
-    peers, rows, _ = out_ref.shape
+    points, both = pairs_refs[0].shape
+    peers = out_ref.shape[0]
     width = both // 2
     heads = HEADS // 2
     size = width // heads
-    per = cap * peers // rows
+    tall = rows // 2
+    stack = width // LANES * rows
     scale = math.log2(math.e) / math.sqrt(size)
-    all_nodes = asked_ref.shape[0]
-    all_entries = peers * cap
+    all_nodes, all_entries = peers * rows, peers * cap
     nodes, entries = all_nodes // 2, all_entries // 2
-    pick_shape = (all_entries, all_nodes)
-    pick_row = iota(pick_shape, 1) - div(iota(pick_shape, 0), cap) * rows
-    lane = iota((all_entries, LANES), 1) - mod(iota((all_entries, LANES), 0), cap)
+    tiles = asked_ref[:, stack:, :].astype(f32)
+
+    group, across = div(iota((tall, LANES), 1), rows), LANES // rows
+    slots = []
+    for g in range(edges // tall):
+        line = []
+        for first in range(0, peers, across):
+            merged = jnp.zeros((tall, LANES), f32)
+            for w in range(across):
+                merged = jnp.where(
+                    group == w, pltpu.roll(tiles[first + w], (w - g) * rows % LANES, 1), merged
+                )
+            line.append(merged)
+        slots.append(jnp.concatenate(line, axis=1))
+    all_slots = jnp.concatenate(slots, axis=0).astype(jnp.int32) + all_entries // 2
+
+    tile_rows = peers * tall
+    pick_row = iota((all_entries, tile_rows), 1) - div(iota((all_entries, tile_rows), 0), cap) * tall
+    pick = jnp.where(pick_row == 0, 1.0, jnp.where(pick_row == 1, 256.0, 0.0)).astype(bf16)
+    lists = dot(pick, tiles.reshape(tile_rows, LANES).astype(bf16))
+    lane = iota((all_entries, LANES), 1) - mod(iota((all_entries, LANES), 0), cap) - LANES // 2
     here = div(iota((entries, nodes), 0), cap) == div(iota((entries, nodes), 1), rows)
     listed = -(-cap // 8) * 8
     repeat = iota((entries, listed), 1) == mod(iota((entries, listed), 0), cap)
     repeat = repeat.astype(f32)
-    extra = asked_ref[:, width:]
-    extra_t = extra.astype(f32).T
-    all_slots = (extra_t[:edges] + 256.0 * extra_t[edges : 2 * edges]).astype(jnp.int32)
     chosen, biases = [], []
     for other in range(2):
-        first = (me ^ other) * cap
-        list_row, low_lane = div(first, per), mod(first, per) + 2 * edges
-        weights = jnp.where(lane == low_lane, 1.0, jnp.where(lane == low_lane + per, 256.0, 0.0))
-        lists = dot((pick_row == list_row).astype(bf16), extra)
-        index = jnp.sum(lists * weights, axis=1, keepdims=True).astype(jnp.int32)
+        band = me ^ other
+        mine = lane == (band & 1) * cap
+        index = jnp.sum(jnp.where(mine, lists, 0.0), axis=1, keepdims=True).astype(jnp.int32)
         chosen.append((index == iota((all_entries, points), 1)).astype(bf16))
-        slots = all_slots - first
+        slots = all_slots - band * cap
         uses = jnp.zeros((listed, all_nodes), f32)
         for j in range(edges):
             uses += jnp.where(slots[j : j + 1] == iota((listed, all_nodes), 0), 1.0, 0.0)
@@ -182,16 +212,15 @@
                     repeat, part, (((1,), (0,)), ((), ())), precision=lax.Precision.HIGHEST
                 )
             biases.append(jnp.where(here, repeated, NEG))
-    gathered = [
-        dot(chosen[other], pairs_ref[other * points : (other + 1) * points, :]).astype(bf16)
-        for other in range(2)
-    ]
+    gathered = [dot(one, ref[...]).astype(bf16) for one, ref in zip(chosen, pairs_refs)]
     for half in range(2):
         part = slice(half * entries, (half + 1) * entries)
         pairs = jnp.concatenate([gathered[0][part], gathered[1][part]], axis=0)
         bias = jnp.concatenate([biases[half], biases[2 + half]], axis=0)
         keys, values_t = pairs[:, :width], pairs[:, width:].T
-        queries = asked_ref[half * nodes : (half + 1) * nodes, :width]
+        windows = slice(half * (peers // 2), (half + 1) * (peers // 2))
+        queries = [one.reshape(nodes, LANES) for one in columns_of(asked_ref, windows, rows, width)]
+        queries = jnp.concatenate(queries, axis=1)
         head = div(iota(queries.shape, 1), size)
         queries = jnp.concatenate(
             [jnp.where(head == h, queries, jnp.zeros_like(queries)) for h in range(heads)], axis=0
@@ -214,9 +243,17 @@
         stats = jnp.concatenate(stat_parts(*by_head), axis=0)
         rest = mixed_ref.shape[0] - width - stats.shape[0]
         mixed_ref[width:, :] = jnp.concatenate([stats, jnp.zeros((rest, nodes), f32)], axis=0)
-        result = mixed_ref[...].T.astype(bf16)
+        result = mixed_ref[...].T
+        mixed = result[:, :width].astype(bf16)
         for i in range(peers // 2):
-            out_ref[half * (peers // 2) + i] = result[i * rows : (i + 1) * rows]
+            place = half * (peers // 2) + i
+            for j in range(width // LANES):
+                out_ref[place, j * rows : (j + 1) * rows, :] = mixed[
+                    i * rows : (i + 1) * rows, j * LANES : (j + 1) * LANES
+                ]
+            upper = result[i * rows : i * rows + tall, width:]
+            lower = result[i * rows + tall : (i + 1) * rows, width:]
+            out_ref[place, stack:, :] = (upper + pltpu.roll(lower, LANES // 2, 1)).astype(bf16)
 
 
 def read_stats(stats):
@@ -236,19 +273,25 @@
 
 
 def combine_kernel(parts_ref, latent_ref, gain_ref, w_o_ref, w_kv_ref, latent_out_ref, out_ref):
-    peers, rows, sent = parts_ref.shape
+    peers = parts_ref.shape[0]
+    rows = latent_ref.shape[0]
     width = w_o_ref.shape[0]
     half = width // 2
     chips = (peers // 2, 2, rows)
-    parts = parts_ref[...].reshape(peers * rows, sent)
-    top, total = read_stats(parts[:, half:])
+    parts = [
+        one.reshape(peers * rows, LANES) for one in columns_of(parts_ref, slice(None), rows, half)
+    ]
+    parts = jnp.concatenate(parts, axis=1).astype(f32)
+    tile = parts_ref[:, half // LANES * rows :, :].astype(f32)
+    stats = jnp.concatenate([tile, pltpu.roll(tile, LANES // 2, 2)], axis=1)
+    top, total = read_stats(stats.reshape(peers * rows, LANES).astype(bf16))
     top = top.reshape(*chips, LANES)
     factor = jnp.exp2(top - jnp.max(top, axis=0, keepdims=True))
     total = jnp.sum(total.reshape(*chips, LANES) * factor, axis=0, keepdims=True)
     used = iota((1, 2, rows, LANES), 3) < HEADS // 2
     factor = factor * jnp.where(used, 1.0 / jnp.where(used, total, 1.0), 0.0)
     wide = spread_heads(factor.reshape(peers * rows, LANES), half, width // HEADS)
-    mixed = jnp.sum((parts[:, :half].astype(f32) * wide).reshape(*chips, half), axis=0)
+    mixed = jnp.sum((parts * wide).reshape(*chips, half), axis=0)
     mixed = jnp.concatenate([mixed[0], mixed[1]], axis=1)
     update = dot(mixed.astype(bf16), w_o_ref[...])
     latent_out = (latent_ref[...].astype(f32) + update).astype(bf16)
@@ -381,7 +424,7 @@
     edges = enc_slot.shape[0]
     cap = entries // peers
     half = width // 2
-    sent = half + LANES
+    sent = (peers, half // LANES * rows + rows // 2, LANES)
     swap = [(i, i ^ 1) for i in range(peers)]
     vmem = pl.BlockSpec(memory_space=pltpu.VMEM)
     hbm = pl.BlockSpec(memory_space=pltpu.HBM)
@@ -398,10 +441,10 @@
     asked = pl.pallas_call(
         ask_kernel,
         in_specs=[hbm] * len(ask_inputs),
-        out_shape=jax.ShapeDtypeStruct((peers, rows, sent), bf16),
+        out_shape=jax.ShapeDtypeStruct(sent, bf16),
         scratch_shapes=[pltpu.VMEM(one.shape, one.dtype) for one in ask_inputs]
         + [pltpu.SemaphoreType.DMA((len(ask_inputs),))],
-        compiler_params=params(58),
+        compiler_params=params(63),
         cost_estimate=cost(2 * rows * depth * width, 2 * depth * width),
         name="ask",
     )(*map(in_hbm, ask_inputs))
@@ -411,29 +454,30 @@
     steps = points // block
     pairs = pl.pallas_call(
         functools.partial(front_kernel, steps),
-        in_specs=[vmem, hbm, hbm, hbm],
-        out_specs=vmem,
-        out_shape=pltpu.VMEM((2 * points, width), bf16),
+        in_specs=[hbm] * 4,
+        out_specs=[vmem] * 2,
+        out_shape=[pltpu.VMEM((points, width), bf16)] * 2,
         scratch_shapes=[
             pltpu.VMEM((1, depth), f32),
             pltpu.VMEM((points, depth), bf16),
+            pltpu.VMEM((points, depth), bf16),
             pltpu.VMEM((depth, width), bf16),
-            pltpu.SemaphoreType.DMA((4,)),
+            pltpu.SemaphoreType.DMA((5,)),
         ],
         compiler_params=params(40),
         cost_estimate=cost(4 * points * depth * width, 8 * points * depth),
         name="front",
-    )(other_grid, in_hbm(grid_gain.reshape(1, -1)), in_hbm(grid), in_hbm(w_kv_enc))
+    )(*map(in_hbm, (grid_gain.reshape(1, -1), grid, other_grid, w_kv_enc)))
 
     parts = pl.pallas_call(
-        functools.partial(partial_kernel, cap, edges),
-        in_specs=[vmem, vmem],
-        out_shape=jax.ShapeDtypeStruct((peers, rows, sent), bf16),
-        scratch_shapes=[pltpu.VMEM((sent, nodes // 2), f32)],
+        functools.partial(partial_kernel, cap, rows, edges),
+        in_specs=[vmem] * 3,
+        out_shape=jax.ShapeDtypeStruct(sent, bf16),
+        scratch_shapes=[pltpu.VMEM((half + LANES, nodes // 2), f32)],
         compiler_params=params(40),
         cost_estimate=cost(4 * entries * points * width, 4 * points * width),
         name="partial",
-    )(asked.reshape(nodes, sent), in_vmem(pairs))
+    )(asked, *map(in_vmem, pairs))
     parts, dec_need, dec_slot = lax.optimization_barrier((parts, dec_need, dec_slot))
     parts = lax.all_to_all(parts, "dom", split_axis=0, concat_axis=0, tiled=True)
 

time: 58.3 us -> 55.3 us (0.949)
  local copies, waits for them, and re-layouts: 3.91 us -> 1.01 us
  Pallas kernels: 20.7 us -> 21.4 us
    unnamed x26 -> x22, local copies, waits for them, and re-layouts: 3.91 us -> 1.01 us
    pallas_call x2, Pallas kernels: 7.38 us -> 8.02 us  [the longest x1 4.74 us: on_device(): pl.pallas_call(functools.partial(front_kernel, steps), in_specs=[hbm] * 4...]
  transfers between devices with their start and end apart: 4 -> 4, of which waited for: 2 -> 2; matrix products, arithmetic and copies ran while one was open for 0% -> 0% of each run, Pallas kernels for 20% -> 22%
where the time goes in v9:
time: 55.3 us; the launch traced here: 54.9 us
  Pallas kernels  21.4 us (39%)
  blocking collectives  12.6 us (23%)
  starting transfers between devices  11.4 us (21%)
  waiting for transfers between devices  7.58 us (14%)
  local copies, waits for them, and re-layouts  1.01 us (2%)
  between operations  0.94 us (2%)
    all_to_all x1, blocking collectives, on_device(): lax.all_to_all(everyone, 'dom', split_axis=0, concat_axis=0, tiled=True)  12.6 us
    all_to_all x1, starting transfers between devices, on_device(): lax.all_to_all(asked, 'dom', split_axis=0, concat_axis=0, tiled=True)  7.06 us
    pallas_call x1, Pallas kernels, on_device(): pl.pallas_call(functools.partial(front_kernel, steps), in_specs=[hbm] * 4...  4.74 us
    pallas_call x1, Pallas kernels, on_device(): pl.pallas_call(functools.partial(other_kernel, steps), in_specs=[vmem] *...  4.09 us
    all_to_all x1, waiting for transfers between devices, on_device(): lax.all_to_all(parts, 'dom', split_axis=0, concat_axis=0, tiled=True)  3.87 us
    all_to_all x1, starting transfers between devices, on_device(): lax.all_to_all(parts, 'dom', split_axis=0, concat_axis=0, tiled=True)  3.79 us
    all_to_all x1, waiting for transfers between devices, on_device(): lax.all_to_all(asked, 'dom', split_axis=0, concat_axis=0, tiled=True)  3.7 us
    pallas_call x1, Pallas kernels, on_device(): pl.pallas_call(functools.partial(middle_kernel, steps, slot_total // peer...  3.54 us
  transfers between devices with their start and end apart: 4, of which 2 were waited for; matrix products, arithmetic and copies ran while one was open for 0% of the time, Pallas kernels for 22%

profile of v9, /device:TPU:0, one launch (start us, length us, event | category | flops | bytes accessed | tf_op | source)
XLA Modules:
  0.0 54.9 jit_solution(7813220289911873229)
XLA Ops:
  0.6 0.5 collective-permute-start
  1.1 2.3 %ask.1 = bf16[16,40,128]{2,1,0:T(8,128)(2,1)} custom-call(bf16[1024,512]{1,0:T(8,128)(2,1)} %refs_0_.1, bf16[16,1024]{1,0:T(8,128)(2,1)} %latent_ref.1, f32[1,1024]{1,0:T(1,128)} %bitcast.14, s32[16,32]{1,0:T(8,128)} %bitcast.13, s32[1,16]{1,0:T(1,128)} %bitcast.15, s32[1,512]{1,0:T(1,128)} %refs_5_.1), custom_call_target="tpu_custom_call" | custom-call | flops 16777216 | bytes 1048576 | tf_op jit(solution)/shard_map/ask/pallas_call | solution.py:441
  3.5 7.1 %all-to-all-start = ((bf16[16,40,128]{2,1,0:T(8,128)(2,1)}), bf16[16,40,128]{2,1,0:T(8,128)(2,1)S(1)}, u32[]{:S(2)}, u32[]{:S(2)}) async-start(bf16[16,40,128]{2,1,0:T(8,128)(2,1)} %ask.1), calls=%async_computation | async-start | bytes 327680 | tf_op jit(solution)/shard_map/all_to_all | solution.py:451
  10.5 0.0 collective-permute-done.other_hbm
  10.5 4.7 %front.1 = (bf16[1024,512]{1,0:T(8,128)(2,1)S(1)}, bf16[1024,512]{1,0:T(8,128)(2,1)S(1)}) custom-call(f32[1,1024]{1,0:T(1,128)} %bitcast.11, bf16[1024,1024]{1,0:T(8,128)(2,1)} %x_ref.1, bf16[1024,1024]{1,0:T(8,128)(2,1)} %collective-permute-done.other_hbm, bf16[1024,1024]{1,0:T(8,128)(2,1)} %w_hbm.2), custom_call_target="tpu_custom_call" | custom-call | flops 2147483648 | bytes 8388608 | tf_op jit(solution)/shard_map/front/pallas_call | solution.py:455
  15.3 3.7 %all-to-all-done.asked_ref = bf16[16,40,128]{2,1,0:T(8,128)(2,1)S(1)} async-done(((bf16[16,40,128]{2,1,0:T(8,128)(2,1)}), bf16[16,40,128]{2,1,0:T(8,128)(2,1)S(1)}, u32[]{:S(2)}, u32[]{:S(2)}) %all-to-all-start) | async-done | bytes 163872 | tf_op jit(solution)/shard_map/all_to_all | solution.py:451
  19.0 0.0 copy-start.6
  19.0 0.0 copy-start.7
  19.0 0.0 copy-start.8
  19.0 3.3 %partial.1 = bf16[16,40,128]{2,1,0:T(8,128)(2,1)} custom-call(bf16[16,40,128]{2,1,0:T(8,128)(2,1)S(1)} %all-to-all-done.asked_ref, bf16[1024,512]{1,0:T(8,128)(2,1)S(1)} %get-tuple-element.14.refs_0_, bf16[1024,512]{1,0:T(8,128)(2,1)S(1)} %get-tuple-element.15.refs_1_), custom_call_target="tpu_custom_call" | custom-call | flops 1073741824 | bytes 2097152 | tf_op jit(solution)/shard_map/partial/pallas_call | solution.py:472
  22.3 0.0 copy-start
  22.3 0.0 copy-start.1
  22.3 0.0 copy-start.2
  22.3 0.0 copy-start.3
  22.3 3.8 %all-to-all-start.1 = ((bf16[16,40,128]{2,1,0:T(8,128)(2,1)}), bf16[16,40,128]{2,1,0:T(8,128)(2,1)S(1)}, u32[]{:S(2)}, u32[]{:S(2)}) async-start(bf16[16,40,128]{2,1,0:T(8,128)(2,1)} %partial.1), calls=%async_computation.1 | async-start | bytes 327680 | tf_op jit(solution)/shard_map/all_to_all | solution.py:482
  26.1 0.0 copy-done.6
  26.1 0.0 copy-done.7
  26.1 0.0 copy-done.8
  26.1 3.5 %middle.1 = (bf16[512,1024]{1,0:T(8,128)(2,1)S(1)}, s32[4,1024]{1,0:T(4,128)S(1)}) custom-call(f32[1,1024]{1,0:T(1,128)S(1)} %bitcast.12, s32[32,128]{1,0:T(8,128)S(1)} %bitcast.10, s32[4,1024]{1,0:T(4,128)S(1)} %copy-done.7, bf16[1024,1024]{1,0:T(8,128)(2,1)} %x_ref.1, bf16[1024,512]{1,0:T(8,128)(2,1)} %w_hbm.3), custom_call_target="tpu_custom_call" | custom-call | flops 1073741824 | bytes 8388608 | tf_op jit(solution)/shard_map/middle/pallas_call | solution.py:486
  29.7 0.0 copy-start.9
  29.7 1.0 %copy-done.9 = bf16[512,1024]{1,0:T(8,128)(2,1)} copy-done((bf16[512,1024]{1,0:T(8,128)(2,1)}, bf16[512,1024]{1,0:T(8,128)(2,1)S(1)}, u32[]{:S(2)}) %copy-start.9) | copy-done | bytes 1048600
  30.7 3.9 %all-to-all-done.1.parts_ref = bf16[16,40,128]{2,1,0:T(8,128)(2,1)S(1)} async-done(((bf16[16,40,128]{2,1,0:T(8,128)(2,1)}), bf16[16,40,128]{2,1,0:T(8,128)(2,1)S(1)}, u32[]{:S(2)}, u32[]{:S(2)}) %all-to-all-start.1) | async-done | bytes 163872 | tf_op jit(solution)/shard_map/all_to_all | solution.py:482
  34.5 0.0 copy-start.10
  34.5 0.0 copy-done
  34.5 0.0 copy-done.1
  34.5 0.0 copy-done.2
  34.5 0.0 copy-done.3
  34.5 0.0 copy-start.4
  34.6 0.0 copy-start.5
  34.6 1.7 %combine.1 = (bf16[16,1024]{1,0:T(8,128)(2,1)}, bf16[16,16,512]{2,1,0:T(8,128)(2,1)S(1)}) custom-call(bf16[16,40,128]{2,1,0:T(8,128)(2,1)S(1)} %all-to-all-done.1.parts_ref, bf16[16,1024]{1,0:T(8,128)(2,1)S(1)} %copy-done.2, f32[1,1024]{1,0:T(1,128)S(1)} %bitcast.9, bf16[512,1024]{1,0:T(8,128)(2,1)S(1)} %copy-done.1, bf16[1024,1024]{1,0:T(8,128)(2,1)S(1)} %copy-done), custom_call_target="tpu_custom_call" | custom-call | flops 50331648 | bytes 3145728 | tf_op jit(solution)/shard_map/combine/pallas_call | solution.py:511
  36.3 12.6 %all_to_all.15 = bf16[16,16,512]{2,1,0:T(8,128)(2,1)S(1)} all-to-all(bf16[16,16,512]{2,1,0:T(8,128)(2,1)S(1)} %get-tuple-element.23), channel_id=1, replica_groups=mesh['groups'=2,'dom'=16] {'dom'}, dimensions={0} | all-to-all | bytes 524288 | tf_op jit(solution)/shard_map/all_to_all | solution.py:521
  48.9 0.0 collective-permute-start.1
  48.9 0.0 copy-done.10
  49.0 1.7 %own.1.own_ref = bf16[1024,256]{1,0:T(8,128)(2,1)S(1)} custom-call(bf16[256,512]{1,0:T(8,128)(2,1)S(1)} %bitcast.8, s32[4,1024]{1,0:T(4,128)S(1)} %get-tuple-element.24.node_ref, bf16[512,1024]{1,0:T(8,128)(2,1)S(1)} %copy-done.10), custom_call_target="tpu_custom_call" | custom-call | flops 536870912 | bytes 2097152 | tf_op jit(solution)/shard_map/own/pallas_call | solution.py:526
  50.6 0.0 collective-permute-done.1.pairs_ref
  50.6 0.0 copy-done.4
  50.6 0.0 copy-done.5
  50.6 4.1 %other.1 = bf16[1024,1024]{1,0:T(8,128)(2,1)} custom-call(bf16[256,512]{1,0:T(8,128)(2,1)S(1)} %collective-permute-done.1.pairs_ref, bf16[1024,256]{1,0:T(8,128)(2,1)S(1)} %own.1.own_ref, s32[4,1024]{1,0:T(4,128)S(1)} %get-tuple-element.24.node_ref, bf16[512,1024]{1,0:T(8,128)(2,1)S(1)} %copy-done.10, bf16[1024,1024]{1,0:T(8,128)(2,1)S(1)} %copy-done.4, ...), custom_call_target="tpu_custom_call" | custom-call | flops 2147483648 | bytes 8388608 | tf_op jit(solution)/shard_map/other/pallas_call | solution.py:534
Async XLA Ops:
  0.6 9.9 %collective-permute-start = (bf16[1024,1024]{1,0:T(8,128)(2,1)}, bf16[1024,1024]{1,0:T(8,128)(2,1)}, u32[]{:S(2)}, u32[]{:S(2)}) collective-permute-start(bf16[1024,1024]{1,0:T(8,128)(2,1)} %x_ref.1), channel_id=1, source_target_pairs={{0,1},{1,0},{2,3},{3,2},{4,5},{5,4},{6,7},{7,6},{8,9},{9,8},{10,11... | collective-permute-start | bytes 6291464 | tf_op jit(solution)/shard_map/ppermute | solution.py:432
  3.5 15.5 %all-to-all-start = ((bf16[16,40,128]{2,1,0:T(8,128)(2,1)}), bf16[16,40,128]{2,1,0:T(8,128)(2,1)S(1)}, u32[]{:S(2)}, u32[]{:S(2)}) async-start(bf16[16,40,128]{2,1,0:T(8,128)(2,1)} %ask.1), calls=%async_computation | async-start | bytes 327680 | tf_op jit(solution)/shard_map/all_to_all | solution.py:451
  19.0 7.1 %copy-start.6 = (s32[1,4096]{1,0:T(1,128)S(1)}, s32[1,4096]{1,0:T(1,128)}, u32[]{:S(2)}) copy-start(s32[1,4096]{1,0:T(1,128)} %param.30) | copy-start | bytes 49156
  19.0 7.1 %copy-start.7 = (s32[4,1024]{1,0:T(4,128)S(1)}, s32[4,1024]{1,0:T(4,128)}, u32[]{:S(2)}) copy-start(s32[4,1024]{1,0:T(4,128)} %slot_ref) | copy-start | bytes 49156
  19.0 7.1 %copy-start.8 = (f32[1024]{0:T(1024)S(1)}, f32[1024]{0:T(1024)}, u32[]{:S(2)}) copy-start(f32[1024]{0:T(1024)} %param.18) | copy-start | bytes 12292
  22.3 12.2 %copy-start = (bf16[1024,1024]{1,0:T(8,128)(2,1)S(1)}, bf16[1024,1024]{1,0:T(8,128)(2,1)}, u32[]{:S(2)}) copy-start(bf16[1024,1024]{1,0:T(8,128)(2,1)} %w_kv_ref.1) | copy-start | bytes 6291460
  22.3 12.2 %copy-start.1 = (bf16[512,1024]{1,0:T(8,128)(2,1)S(1)}, bf16[512,1024]{1,0:T(8,128)(2,1)}, u32[]{:S(2)}) copy-start(bf16[512,1024]{1,0:T(8,128)(2,1)} %w_o_ref.1) | copy-start | bytes 3145732
  22.3 12.2 %copy-start.2 = (bf16[16,1024]{1,0:T(8,128)(2,1)S(1)}, bf16[16,1024]{1,0:T(8,128)(2,1)}, u32[]{:S(2)}) copy-start(bf16[16,1024]{1,0:T(8,128)(2,1)} %latent_ref.1) | copy-start | bytes 98308
  22.3 12.2 %copy-start.3 = (f32[1024]{0:T(1024)S(1)}, f32[1024]{0:T(1024)}, u32[]{:S(2)}) copy-start(f32[1024]{0:T(1024)} %param.20) | copy-start | bytes 12292
  22.3 12.2 %all-to-all-start.1 = ((bf16[16,40,128]{2,1,0:T(8,128)(2,1)}), bf16[16,40,128]{2,1,0:T(8,128)(2,1)S(1)}, u32[]{:S(2)}, u32[]{:S(2)}) async-start(bf16[16,40,128]{2,1,0:T(8,128)(2,1)} %partial.1), calls=%async_computation.1 | async-start | bytes 327680 | tf_op jit(solution)/shard_map/all_to_all | solution.py:482
  29.7 1.0 %copy-start.9 = (bf16[512,1024]{1,0:T(8,128)(2,1)}, bf16[512,1024]{1,0:T(8,128)(2,1)S(1)}, u32[]{:S(2)}) copy-start(bf16[512,1024]{1,0:T(8,128)(2,1)S(1)} %get-tuple-element.25.query_ref) | copy-start | bytes 3145732
  34.5 14.4 %copy-start.10 = (bf16[512,1024]{1,0:T(8,128)(2,1)S(1)}, bf16[512,1024]{1,0:T(8,128)(2,1)}, u32[]{:S(2)}) copy-start(bf16[512,1024]{1,0:T(8,128)(2,1)} %copy-done.9) | copy-start | bytes 3145732
  34.5 16.1 %copy-start.4 = (bf16[1024,1024]{1,0:T(8,128)(2,1)S(1)}, bf16[1024,1024]{1,0:T(8,128)(2,1)}, u32[]{:S(2)}) copy-start(bf16[1024,1024]{1,0:T(8,128)(2,1)} %x_ref.1) | copy-start | bytes 6291460
  34.6 16.1 %copy-start.5 = (bf16[512,1024]{1,0:T(8,128)(2,1)S(1)}, bf16[512,1024]{1,0:T(8,128)(2,1)}, u32[]{:S(2)}) copy-start(bf16[512,1024]{1,0:T(8,128)(2,1)} %w_ref.1) | copy-start | bytes 3145732
  48.9 1.7 %collective-permute-start.1 = (bf16[256,512]{1,0:T(8,128)(2,1)S(1)}, bf16[256,512]{1,0:T(8,128)(2,1)S(1)}, u32[]{:S(2)}, u32[]{:S(2)}) collective-permute-start(bf16[256,512]{1,0:T(8,128)(2,1)S(1)} %bitcast.7), channel_id=1, source_target_pairs={{0,1},{1,0},{2,3},{3,2},{4,5},{5,4},{6,7},{7,6},{8,9},{9,8},{10,11... | collective-permute-start | bytes 786440 | tf_op jit(solution)/shard_map/ppermute | solution.py:523

commit v10 on v9

--- a/solution.py
+++ b/solution.py
@@ -58,6 +58,19 @@
 
 def cost(flops, read, exps=0):
     return pl.CostEstimate(flops=int(flops), bytes_accessed=int(read), transcendentals=int(exps))
+
+
+def place_of(index, peers):
+    if isinstance(index, int):
+        return (index + index % 2 * (peers // 2)) % peers
+    return mod(index + (index & 1) * (peers // 2), peers)
+
+
+def exchange(blocks, peers):
+    order = [place_of(i, peers) for i in range(peers)]
+    return lax.all_to_all(
+        blocks, "dom", split_axis=0, concat_axis=0, tiled=True, axis_index_groups=[order]
+    )
 
 
 def columns_of(ref, where, rows, half):
@@ -109,7 +122,7 @@
         for i in range(half // LANES):
             at = p % 2 * half + i * LANES
             out_ref[p, i * rows : (i + 1) * rows, :] = queries[:, at : at + LANES]
-        out_ref[p, half // LANES * rows :, :] = tiles[p // 2]
+        out_ref[p, half // LANES * rows :, :] = tiles[place_of(p, peers) // 2]
 
 
 def front_kernel(
@@ -130,20 +143,23 @@
             )
             for i in range(2)
         ],
-        pltpu.make_async_copy(own_hbm, own_ref, sems.at[3]),
-        pltpu.make_async_copy(other_hbm, other_ref, sems.at[4]),
-    )
-    for copy in copies[:3]:
+    )
+    parts = [pl.ds(i * block, block) for i in range(steps)]
+    sides = ((own_hbm, own_ref, own_out_ref), (other_hbm, other_ref, other_out_ref))
+    rows = started(
+        *[
+            pltpu.make_async_copy(hbm.at[part], ref.at[part], sems.at[3 + side * steps + i])
+            for side, (hbm, ref, _) in enumerate(sides)
+            for i, part in enumerate(parts)
+        ]
+    )
+    for copy in copies:
         copy.wait()
     gain = gain_ref[...]
-    for copy, rows_ref, out_ref in (
-        (copies[3], own_ref, own_out_ref),
-        (copies[4], other_ref, other_out_ref),
-    ):
-        copy.wait()
-        for i in range(steps):
-            part = pl.ds(i * block, block)
-            out_ref[part, :] = dot(normed(rows_ref[part, :], gain), w_ref[...]).astype(bf16)
+    for side, (_, ref, out_ref) in enumerate(sides):
+        for i, part in enumerate(parts):
+            rows[side * steps + i].wait()
+            out_ref[part, :] = dot(normed(ref[part, :], gain), w_ref[...]).astype(bf16)
 
 
 def stat_parts(top, total):
@@ -168,6 +184,18 @@
     nodes, entries = all_nodes // 2, all_entries // 2
     tiles = asked_ref[:, stack:, :].astype(f32)
 
+    tile_rows = peers * tall
+    pick_row = iota((all_entries, tile_rows), 1) - div(iota((all_entries, tile_rows), 0), cap) * tall
+    pick = jnp.where(pick_row == 0, 1.0, jnp.where(pick_row == 1, 256.0, 0.0)).astype(bf16)
+    lists = dot(pick, tiles.reshape(tile_rows, LANES).astype(bf16))
+    lane = iota((all_entries, LANES), 1) - mod(iota((all_entries, LANES), 0), cap) - LANES // 2
+    gathered = []
+    for other, ref in enumerate(pairs_refs):
+        mine = lane == ((me ^ other) & 1) * cap
+        index = jnp.sum(jnp.where(mine, lists, 0.0), axis=1, keepdims=True).astype(jnp.int32)
+        chosen = (index == iota((all_entries, points), 1)).astype(bf16)
+        gathered.append(dot(chosen, ref[...]).astype(bf16))
+
     group, across = div(iota((tall, LANES), 1), rows), LANES // rows
     slots = []
     for g in range(edges // tall):
@@ -182,22 +210,13 @@
         slots.append(jnp.concatenate(line, axis=1))
     all_slots = jnp.concatenate(slots, axis=0).astype(jnp.int32) + all_entries // 2
 
-    tile_rows = peers * tall
-    pick_row = iota((all_entries, tile_rows), 1) - div(iota((all_entries, tile_rows), 0), cap) * tall
-    pick = jnp.where(pick_row == 0, 1.0, jnp.where(pick_row == 1, 256.0, 0.0)).astype(bf16)
-    lists = dot(pick, tiles.reshape(tile_rows, LANES).astype(bf16))
-    lane = iota((all_entries, LANES), 1) - mod(iota((all_entries, LANES), 0), cap) - LANES // 2
     here = div(iota((entries, nodes), 0), cap) == div(iota((entries, nodes), 1), rows)
     listed = -(-cap // 8) * 8
     repeat = iota((entries, listed), 1) == mod(iota((entries, listed), 0), cap)
     repeat = repeat.astype(f32)
-    chosen, biases = [], []
+    biases = []
     for other in range(2):
-        band = me ^ other
-        mine = lane == (band & 1) * cap
-        index = jnp.sum(jnp.where(mine, lists, 0.0), axis=1, keepdims=True).astype(jnp.int32)
-        chosen.append((index == iota((all_entries, points), 1)).astype(bf16))
-        slots = all_slots - band * cap
+        slots = all_slots - (me ^ other) * cap
         uses = jnp.zeros((listed, all_nodes), f32)
         for j in range(edges):
             uses += jnp.where(slots[j : j + 1] == iota((listed, all_nodes), 0), 1.0, 0.0)
@@ -212,7 +231,6 @@
                     repeat, part, (((1,), (0,)), ((), ())), precision=lax.Precision.HIGHEST
                 )
             biases.append(jnp.where(here, repeated, NEG))
-    gathered = [dot(one, ref[...]).astype(bf16) for one, ref in zip(chosen, pairs_refs)]
     for half in range(2):
         part = slice(half * entries, (half + 1) * entries)
         pairs = jnp.concatenate([gathered[0][part], gathered[1][part]], axis=0)
@@ -256,43 +274,36 @@
             out_ref[place, stack:, :] = (upper + pltpu.roll(lower, LANES // 2, 1)).astype(bf16)
 
 
-def read_stats(stats):
-    heads = HEADS // 2
-    col, head = iota((LANES, LANES), 0), iota((LANES, LANES), 1)
-    head_of = mod(col, heads) == head
-    take_top = head_of & (col < 3 * heads)
-    take_sum = head_of & (col >= 3 * heads) & (col < 5 * heads)
-    return dot(stats, take_top.astype(bf16)), dot(stats, take_sum.astype(bf16))
-
-
-def spread_heads(factor, width, size):
-    spread = (div(iota((LANES, width), 1), size) == iota((LANES, width), 0)).astype(bf16)
-    factor_1 = factor.astype(bf16)
-    factor_2 = (factor - factor_1.astype(f32)).astype(bf16)
-    return dot(factor_1, spread) + dot(factor_2, spread)
-
-
 def combine_kernel(parts_ref, latent_ref, gain_ref, w_o_ref, w_kv_ref, latent_out_ref, out_ref):
     peers = parts_ref.shape[0]
     rows = latent_ref.shape[0]
     width = w_o_ref.shape[0]
     half = width // 2
-    chips = (peers // 2, 2, rows)
-    parts = [
-        one.reshape(peers * rows, LANES) for one in columns_of(parts_ref, slice(None), rows, half)
-    ]
-    parts = jnp.concatenate(parts, axis=1).astype(f32)
+    heads, size, tall = HEADS // 2, width // HEADS, rows // 2
+    chips = (peers // 2, 2, tall, LANES)
     tile = parts_ref[:, half // LANES * rows :, :].astype(f32)
-    stats = jnp.concatenate([tile, pltpu.roll(tile, LANES // 2, 2)], axis=1)
-    top, total = read_stats(stats.reshape(peers * rows, LANES).astype(bf16))
-    top = top.reshape(*chips, LANES)
+
+    def moved(columns):
+        return pltpu.roll(tile, LANES - columns, 2)
+
+    top = (tile + moved(heads) + moved(2 * heads)).reshape(chips)
+    total = (moved(3 * heads) + moved(4 * heads)).reshape(chips)
     factor = jnp.exp2(top - jnp.max(top, axis=0, keepdims=True))
-    total = jnp.sum(total.reshape(*chips, LANES) * factor, axis=0, keepdims=True)
-    used = iota((1, 2, rows, LANES), 3) < HEADS // 2
-    factor = factor * jnp.where(used, 1.0 / jnp.where(used, total, 1.0), 0.0)
-    wide = spread_heads(factor.reshape(peers * rows, LANES), half, width // HEADS)
-    mixed = jnp.sum((parts * wide).reshape(*chips, half), axis=0)
-    mixed = jnp.concatenate([mixed[0], mixed[1]], axis=1)
+    factor = factor / jnp.sum(total * factor, axis=0, keepdims=True)
+    head = div(iota(chips, 3), size)
+    blocks = []
+    for i, block in enumerate(columns_of(parts_ref, slice(None), rows, half)):
+        block = block.astype(f32)
+        nodes = []
+        for g in range(2):
+            wide = jnp.zeros(chips, f32)
+            for h in range(LANES // size):
+                at = g * (LANES // 2) + i * (LANES // size) + h
+                wide = jnp.where(head == h, factor[..., at : at + 1], wide)
+            part = block[:, g * tall : (g + 1) * tall].reshape(chips)
+            nodes.append(jnp.sum(part * wide, axis=0))
+        blocks.append(jnp.concatenate(nodes, axis=1))
+    mixed = jnp.concatenate([block[h] for h in range(2) for block in blocks], axis=1)
     update = dot(mixed.astype(bf16), w_o_ref[...])
     latent_out = (latent_ref[...].astype(f32) + update).astype(bf16)
     latent_out_ref[...] = latent_out
@@ -304,7 +315,7 @@
 
 
 def middle_kernel(
-    steps, cap, rows, gain_ref, need_ref, slot_ref, x_hbm, w_hbm, query_ref, node_ref,
+    steps, peers, rows, gain_ref, need_ref, slot_ref, x_hbm, w_hbm, query_ref, node_ref,
     x_ref, w_ref, sems,
 ):
     copies = started(
@@ -314,6 +325,7 @@
     points = x_ref.shape[0]
     block = points // steps
     high_count = need_ref.shape[0]
+    cap = high_count * LANES // peers
     need = need_ref[...].astype(f32).astype(bf16)
     for j in range(slot_ref.shape[0]):
         slots = slot_ref[j : j + 1, :]
@@ -321,7 +333,7 @@
         listed = lax.dot_general(need, row_of, (((0,), (0,)), ((), ())), preferred_element_type=f32)
         own = mod(slots, LANES) == iota((LANES, points), 0)
         found = jnp.sum(jnp.where(own, listed, 0.0), axis=0, keepdims=True).astype(jnp.int32)
-        node_ref[j : j + 1, :] = div(slots, cap) * rows + found
+        node_ref[j : j + 1, :] = place_of(div(slots, cap), peers) * rows + found
     for copy in copies:
         copy.wait()
     for i in range(steps):
@@ -375,14 +387,14 @@
     block = points // steps
     core = lax.axis_index("dom") & 1
     queries = half_of(query_ref, (1 - core) * half, half)
-    own_w = half_of(w_ref, core * half, half)
-    other_w = half_of(w_ref, (1 - core) * half, half)
     pairs = pairs_ref[...].T
     sends = []
     for i in range(steps):
         part = pl.ds(i * block, block)
         mixed = attend_half(pairs, queries[:, part], node_ref[:, part])
-        update = dot(own_ref[part, :], own_w[...]) + dot(mixed, other_w[...])
+        own = own_ref[part, :]
+        both = [jnp.where(core == 0, own, mixed), jnp.where(core == 0, mixed, own)]
+        update = dot(jnp.concatenate(both, axis=1), w_ref[...])
         out_ref[part, :] = (x_ref[part, :].astype(f32) + update).astype(bf16)
         sends += started(pltpu.make_async_copy(out_ref.at[part], out_hbm.at[part], sems.at[i]))
     for send in sends:
@@ -448,7 +460,7 @@
         cost_estimate=cost(2 * rows * depth * width, 2 * depth * width),
         name="ask",
     )(*map(in_hbm, ask_inputs))
-    asked = lax.all_to_all(asked, "dom", split_axis=0, concat_axis=0, tiled=True)
+    asked = exchange(asked, peers)
 
     block = math.gcd(points, 256)
     steps = points // block
@@ -462,7 +474,7 @@
             pltpu.VMEM((points, depth), bf16),
             pltpu.VMEM((points, depth), bf16),
             pltpu.VMEM((depth, width), bf16),
-            pltpu.SemaphoreType.DMA((5,)),
+            pltpu.SemaphoreType.DMA((3 + 2 * steps,)),
         ],
         compiler_params=params(40),
         cost_estimate=cost(4 * points * depth * width, 8 * points * depth),
@@ -479,12 +491,12 @@
         name="partial",
     )(asked, *map(in_vmem, pairs))
     parts, dec_need, dec_slot = lax.optimization_barrier((parts, dec_need, dec_slot))
-    parts = lax.all_to_all(parts, "dom", split_axis=0, concat_axis=0, tiled=True)
+    parts = exchange(parts, peers)
 
     slot_total = dec_need.shape[1]
     edge_count = dec_slot.shape[0]
     queries, node_of = pl.pallas_call(
-        functools.partial(middle_kernel, steps, slot_total // peers, rows),
+        functools.partial(middle_kernel, steps, peers, rows),
         in_specs=[vmem] * 3 + [hbm] * 2,
         out_specs=[vmem, vmem],
         out_shape=[
@@ -518,8 +530,7 @@
         cost_estimate=cost(6 * rows * depth * width, 6 * depth * width),
         name="combine",
     )(parts, latent_in, dec_gain.reshape(1, -1), w_o_enc, w_kv_dec)
-    own = lax.all_to_all(everyone, "dom", split_axis=0, concat_axis=0, tiled=True)
-    own = own.reshape(nodes, width)
+    own = exchange(everyone, peers).reshape(nodes, width)
     other = lax.ppermute(own, "dom", swap)
 
     queries = in_vmem(queries)

time: 55.3 us -> 55.2 us (level)
  waiting for transfers between devices: 7.58 us -> 6.45 us
  Pallas kernels: 21.4 us -> 22.2 us
    all_to_all x2, waiting for transfers between devices: 7.58 us -> 6.44 us  [exchange(): lax.all_to_all(blocks, 'dom', split_axis=0, concat_axis=0, tiled=True, ax...]
    pallas_call x1, Pallas kernels: 4.74 us -> 5.77 us  [on_device(): pl.pallas_call(functools.partial(front_kernel, steps), in_specs=[hbm] * 4...]
  transfers between devices with their start and end apart: 4 -> 4, of which waited for: 2 -> 2; matrix products, arithmetic and copies ran while one was open for 0% -> 0% of each run, Pallas kernels for 22% -> 24%
where the time goes in v10:
time: 55.2 us; the launch traced here: 54.8 us
  Pallas kernels  22.2 us (40%)
  blocking collectives  12.5 us (23%)
  starting transfers between devices  11.7 us (21%)
  waiting for transfers between devices  6.45 us (12%)
  local copies, waits for them, and re-layouts  1.01 us (2%)
  between operations  0.94 us (2%)
    all_to_all x1, blocking collectives, exchange(): lax.all_to_all(blocks, 'dom', split_axis=0, concat_axis=0, tiled=True, ax...  12.5 us
    all_to_all x2, starting transfers between devices, exchange(): lax.all_to_all(blocks, 'dom', split_axis=0, concat_axis=0, tiled=True, ax...  10.9 us
    all_to_all x2, waiting for transfers between devices, exchange(): lax.all_to_all(blocks, 'dom', split_axis=0, concat_axis=0, tiled=True, ax...  6.44 us
    pallas_call x1, Pallas kernels, on_device(): pl.pallas_call(functools.partial(front_kernel, steps), in_specs=[hbm] * 4...  5.77 us
    pallas_call x1, Pallas kernels, on_device(): pl.pallas_call(functools.partial(other_kernel, steps), in_specs=[vmem] *...  4.18 us
    pallas_call x1, Pallas kernels, on_device(): pl.pallas_call(functools.partial(middle_kernel, steps, peers, rows), in_s...  3.54 us
    pallas_call x1, Pallas kernels, on_device(): pl.pallas_call(functools.partial(partial_kernel, cap, rows, edges), in_sp...  3.27 us
    pallas_call x1, Pallas kernels, on_device(): pl.pallas_call(ask_kernel, in_specs=[hbm] * len(ask_inputs), out_shape=ja...  2.31 us
  transfers between devices with their start and end apart: 4, of which 2 were waited for; matrix products, arithmetic and copies ran while one was open for 0% of the time, Pallas kernels for 24%

profile of v10, /device:TPU:0, one launch (start us, length us, event | category | flops | bytes accessed | tf_op | source)
XLA Modules:
  0.0 54.8 jit_solution(15781476891620349611)
XLA Ops:
  0.6 0.5 collective-permute-start
  1.1 2.3 %ask.1 = bf16[16,40,128]{2,1,0:T(8,128)(2,1)} custom-call(bf16[1024,512]{1,0:T(8,128)(2,1)} %refs_0_.1, bf16[16,1024]{1,0:T(8,128)(2,1)} %latent_ref.1, f32[1,1024]{1,0:T(1,128)} %bitcast.14, s32[16,32]{1,0:T(8,128)} %bitcast.13, s32[1,16]{1,0:T(1,128)} %bitcast.15, s32[1,512]{1,0:T(1,128)} %refs_5_.1), custom_call_target="tpu_custom_call" | custom-call | flops 16777216 | bytes 1048576 | tf_op jit(solution)/shard_map/ask/pallas_call | solution.py:453
  3.5 7.1 %all-to-all-start = ((bf16[16,40,128]{2,1,0:T(8,128)(2,1)}), bf16[16,40,128]{2,1,0:T(8,128)(2,1)S(1)}, u32[]{:S(2)}, u32[]{:S(2)}) async-start(bf16[16,40,128]{2,1,0:T(8,128)(2,1)} %ask.1), calls=%async_computation | async-start | bytes 327680 | tf_op jit(solution)/shard_map/all_to_all | solution.py:71
  10.5 0.0 collective-permute-done.other_hbm
  10.5 5.8 %front.1 = (bf16[1024,512]{1,0:T(8,128)(2,1)S(1)}, bf16[1024,512]{1,0:T(8,128)(2,1)S(1)}) custom-call(f32[1,1024]{1,0:T(1,128)} %bitcast.11, bf16[1024,1024]{1,0:T(8,128)(2,1)} %x_ref.1, bf16[1024,1024]{1,0:T(8,128)(2,1)} %collective-permute-done.other_hbm, bf16[1024,1024]{1,0:T(8,128)(2,1)} %w_hbm.2), custom_call_target="tpu_custom_call" | custom-call | flops 2147483648 | bytes 8388608 | tf_op jit(solution)/shard_map/front/pallas_call | solution.py:467
  16.3 2.6 %all-to-all-done.asked_ref = bf16[16,40,128]{2,1,0:T(8,128)(2,1)S(1)} async-done(((bf16[16,40,128]{2,1,0:T(8,128)(2,1)}), bf16[16,40,128]{2,1,0:T(8,128)(2,1)S(1)}, u32[]{:S(2)}, u32[]{:S(2)}) %all-to-all-start) | async-done | bytes 163872 | tf_op jit(solution)/shard_map/all_to_all | solution.py:71
  19.0 0.0 copy-start.6
  19.0 0.0 copy-start.7
  19.0 0.0 copy-start.8
  19.0 3.3 %partial.1 = bf16[16,40,128]{2,1,0:T(8,128)(2,1)} custom-call(bf16[16,40,128]{2,1,0:T(8,128)(2,1)S(1)} %all-to-all-done.asked_ref, bf16[1024,512]{1,0:T(8,128)(2,1)S(1)} %get-tuple-element.14.refs_0_, bf16[1024,512]{1,0:T(8,128)(2,1)S(1)} %get-tuple-element.15.refs_1_), custom_call_target="tpu_custom_call" | custom-call | flops 1073741824 | bytes 2097152 | tf_op jit(solution)/shard_map/partial/pallas_call | solution.py:484
  22.2 0.0 copy-start
  22.2 0.0 copy-start.1
  22.2 0.0 copy-start.2
  22.2 0.0 copy-start.3
  22.2 3.8 %all-to-all-start.1 = ((bf16[16,40,128]{2,1,0:T(8,128)(2,1)}), bf16[16,40,128]{2,1,0:T(8,128)(2,1)S(1)}, u32[]{:S(2)}, u32[]{:S(2)}) async-start(bf16[16,40,128]{2,1,0:T(8,128)(2,1)} %partial.1), calls=%async_computation.1 | async-start | bytes 327680 | tf_op jit(solution)/shard_map/all_to_all | solution.py:71
  26.0 0.0 copy-done.6
  26.1 0.0 copy-done.7
  26.1 0.0 copy-done.8
  26.1 3.5 %middle.1 = (bf16[512,1024]{1,0:T(8,128)(2,1)S(1)}, s32[4,1024]{1,0:T(4,128)S(1)}) custom-call(f32[1,1024]{1,0:T(1,128)S(1)} %bitcast.12, s32[32,128]{1,0:T(8,128)S(1)} %bitcast.10, s32[4,1024]{1,0:T(4,128)S(1)} %copy-done.7, bf16[1024,1024]{1,0:T(8,128)(2,1)} %x_ref.1, bf16[1024,512]{1,0:T(8,128)(2,1)} %w_hbm.3), custom_call_target="tpu_custom_call" | custom-call | flops 1073741824 | bytes 8388608 | tf_op jit(solution)/shard_map/middle/pallas_call | solution.py:498
  29.6 0.0 copy-start.9
  29.6 1.0 %copy-done.9 = bf16[512,1024]{1,0:T(8,128)(2,1)} copy-done((bf16[512,1024]{1,0:T(8,128)(2,1)}, bf16[512,1024]{1,0:T(8,128)(2,1)S(1)}, u32[]{:S(2)}) %copy-start.9) | copy-done | bytes 1048600
  30.6 3.8 %all-to-all-done.1.parts_ref = bf16[16,40,128]{2,1,0:T(8,128)(2,1)S(1)} async-done(((bf16[16,40,128]{2,1,0:T(8,128)(2,1)}), bf16[16,40,128]{2,1,0:T(8,128)(2,1)S(1)}, u32[]{:S(2)}, u32[]{:S(2)}) %all-to-all-start.1) | async-done | bytes 163872 | tf_op jit(solution)/shard_map/all_to_all | solution.py:71
  34.4 0.0 copy-start.10
  34.4 0.0 copy-done
  34.4 0.0 copy-done.1
  34.4 0.0 copy-done.2
  34.4 0.0 copy-done.3
  34.4 0.0 copy-start.4
  34.4 0.0 copy-start.5
  34.5 1.5 %combine.1 = (bf16[16,1024]{1,0:T(8,128)(2,1)}, bf16[16,16,512]{2,1,0:T(8,128)(2,1)S(1)}) custom-call(bf16[16,40,128]{2,1,0:T(8,128)(2,1)S(1)} %all-to-all-done.1.parts_ref, bf16[16,1024]{1,0:T(8,128)(2,1)S(1)} %copy-done.2, f32[1,1024]{1,0:T(1,128)S(1)} %bitcast.9, bf16[512,1024]{1,0:T(8,128)(2,1)S(1)} %copy-done.1, bf16[1024,1024]{1,0:T(8,128)(2,1)S(1)} %copy-done), custom_call_target="tpu_custom_call" | custom-call | flops 50331648 | bytes 3145728 | tf_op jit(solution)/shard_map/combine/pallas_call | solution.py:523
  36.0 12.5 %all_to_all.15 = bf16[16,16,512]{2,1,0:T(8,128)(2,1)S(1)} all-to-all(bf16[16,16,512]{2,1,0:T(8,128)(2,1)S(1)} %get-tuple-element.23), channel_id=1, replica_groups={{0,9,2,11,4,13,6,15,8,1,10,3,12,5,14,7},{16,25,18,27,20,29,22,31,24,17,..., dimensions={0} | all-to-all | bytes 524288 | tf_op jit(solution)/shard_map/all_to_all | solution.py:71
  48.5 0.3 collective-permute-start.1
  48.8 0.0 copy-done.10
  48.8 1.6 %own.1.own_ref = bf16[1024,256]{1,0:T(8,128)(2,1)S(1)} custom-call(bf16[256,512]{1,0:T(8,128)(2,1)S(1)} %bitcast.8, s32[4,1024]{1,0:T(4,128)S(1)} %get-tuple-element.24.node_ref, bf16[512,1024]{1,0:T(8,128)(2,1)S(1)} %copy-done.10), custom_call_target="tpu_custom_call" | custom-call | flops 536870912 | bytes 2097152 | tf_op jit(solution)/shard_map/own/pallas_call | solution.py:537
  50.5 0.0 collective-permute-done.1.pairs_ref
  50.5 0.0 copy-done.4
  50.5 0.0 copy-done.5
  50.5 4.2 %other.1 = bf16[1024,1024]{1,0:T(8,128)(2,1)} custom-call(bf16[256,512]{1,0:T(8,128)(2,1)S(1)} %collective-permute-done.1.pairs_ref, bf16[1024,256]{1,0:T(8,128)(2,1)S(1)} %own.1.own_ref, s32[4,1024]{1,0:T(4,128)S(1)} %get-tuple-element.24.node_ref, bf16[512,1024]{1,0:T(8,128)(2,1)S(1)} %copy-done.10, bf16[1024,1024]{1,0:T(8,128)(2,1)S(1)} %copy-done.4, ...), custom_call_target="tpu_custom_call" | custom-call | flops 2147483648 | bytes 8388608 | tf_op jit(solution)/shard_map/other/pallas_call | solution.py:545
Async XLA Ops:
  0.6 9.9 %collective-permute-start = (bf16[1024,1024]{1,0:T(8,128)(2,1)}, bf16[1024,1024]{1,0:T(8,128)(2,1)}, u32[]{:S(2)}, u32[]{:S(2)}) collective-permute-start(bf16[1024,1024]{1,0:T(8,128)(2,1)} %x_ref.1), channel_id=1, source_target_pairs={{0,1},{1,0},{2,3},{3,2},{4,5},{5,4},{6,7},{7,6},{8,9},{9,8},{10,11... | collective-permute-start | bytes 6291464 | tf_op jit(solution)/shard_map/ppermute | solution.py:444
  3.5 15.5 %all-to-all-start = ((bf16[16,40,128]{2,1,0:T(8,128)(2,1)}), bf16[16,40,128]{2,1,0:T(8,128)(2,1)S(1)}, u32[]{:S(2)}, u32[]{:S(2)}) async-start(bf16[16,40,128]{2,1,0:T(8,128)(2,1)} %ask.1), calls=%async_computation | async-start | bytes 327680 | tf_op jit(solution)/shard_map/all_to_all | solution.py:71
  19.0 7.1 %copy-start.6 = (s32[1,4096]{1,0:T(1,128)S(1)}, s32[1,4096]{1,0:T(1,128)}, u32[]{:S(2)}) copy-start(s32[1,4096]{1,0:T(1,128)} %param.30) | copy-start | bytes 49156
  19.0 7.1 %copy-start.7 = (s32[4,1024]{1,0:T(4,128)S(1)}, s32[4,1024]{1,0:T(4,128)}, u32[]{:S(2)}) copy-start(s32[4,1024]{1,0:T(4,128)} %slot_ref) | copy-start | bytes 49156
  19.0 7.1 %copy-start.8 = (f32[1024]{0:T(1024)S(1)}, f32[1024]{0:T(1024)}, u32[]{:S(2)}) copy-start(f32[1024]{0:T(1024)} %param.18) | copy-start | bytes 12292
  22.2 12.2 %copy-start = (bf16[1024,1024]{1,0:T(8,128)(2,1)S(1)}, bf16[1024,1024]{1,0:T(8,128)(2,1)}, u32[]{:S(2)}) copy-start(bf16[1024,1024]{1,0:T(8,128)(2,1)} %w_kv_ref.1) | copy-start | bytes 6291460
  22.2 12.2 %copy-start.1 = (bf16[512,1024]{1,0:T(8,128)(2,1)S(1)}, bf16[512,1024]{1,0:T(8,128)(2,1)}, u32[]{:S(2)}) copy-start(bf16[512,1024]{1,0:T(8,128)(2,1)} %w_o_ref.1) | copy-start | bytes 3145732
  22.2 12.2 %copy-start.2 = (bf16[16,1024]{1,0:T(8,128)(2,1)S(1)}, bf16[16,1024]{1,0:T(8,128)(2,1)}, u32[]{:S(2)}) copy-start(bf16[16,1024]{1,0:T(8,128)(2,1)} %latent_ref.1) | copy-start | bytes 98308
  22.2 12.2 %copy-start.3 = (f32[1024]{0:T(1024)S(1)}, f32[1024]{0:T(1024)}, u32[]{:S(2)}) copy-start(f32[1024]{0:T(1024)} %param.20) | copy-start | bytes 12292
  22.2 12.2 %all-to-all-start.1 = ((bf16[16,40,128]{2,1,0:T(8,128)(2,1)}), bf16[16,40,128]{2,1,0:T(8,128)(2,1)S(1)}, u32[]{:S(2)}, u32[]{:S(2)}) async-start(bf16[16,40,128]{2,1,0:T(8,128)(2,1)} %partial.1), calls=%async_computation.1 | async-start | bytes 327680 | tf_op jit(solution)/shard_map/all_to_all | solution.py:71
  29.6 1.0 %copy-start.9 = (bf16[512,1024]{1,0:T(8,128)(2,1)}, bf16[512,1024]{1,0:T(8,128)(2,1)S(1)}, u32[]{:S(2)}) copy-start(bf16[512,1024]{1,0:T(8,128)(2,1)S(1)} %get-tuple-element.25.query_ref) | copy-start | bytes 3145732
  34.4 14.4 %copy-start.10 = (bf16[512,1024]{1,0:T(8,128)(2,1)S(1)}, bf16[512,1024]{1,0:T(8,128)(2,1)}, u32[]{:S(2)}) copy-start(bf16[512,1024]{1,0:T(8,128)(2,1)} %copy-done.9) | copy-start | bytes 3145732
  34.4 16.1 %copy-start.4 = (bf16[1024,1024]{1,0:T(8,128)(2,1)S(1)}, bf16[1024,1024]{1,0:T(8,128)(2,1)}, u32[]{:S(2)}) copy-start(bf16[1024,1024]{1,0:T(8,128)(2,1)} %x_ref.1) | copy-start | bytes 6291460
  34.4 16.1 %copy-start.5 = (bf16[512,1024]{1,0:T(8,128)(2,1)S(1)}, bf16[512,1024]{1,0:T(8,128)(2,1)}, u32[]{:S(2)}) copy-start(bf16[512,1024]{1,0:T(8,128)(2,1)} %w_ref.1) | copy-start | bytes 3145732
  48.5 2.0 %collective-permute-start.1 = (bf16[256,512]{1,0:T(8,128)(2,1)S(1)}, bf16[256,512]{1,0:T(8,128)(2,1)S(1)}, u32[]{:S(2)}, u32[]{:S(2)}) collective-permute-start(bf16[256,512]{1,0:T(8,128)(2,1)S(1)} %bitcast.7), channel_id=1, source_target_pairs={{0,1},{1,0},{2,3},{3,2},{4,5},{5,4},{6,7},{7,6},{8,9},{9,8},{10,11... | collective-permute-start | bytes 786440 | tf_op jit(solution)/shard_map/ppermute | solution.py:534

commit v11 on v10

--- a/solution.py
+++ b/solution.py
@@ -135,31 +135,29 @@
     core = lax.axis_index("dom") & 1
     copies = started(
         pltpu.make_async_copy(gain_hbm, gain_ref, sems.at[0]),
+        pltpu.make_async_copy(own_hbm, own_ref, sems.at[1]),
         *[
             pltpu.make_async_copy(
                 w_hbm.at[:, pl.ds(pl.multiple_of((core + 2 * i) * half, half), half)],
                 w_ref.at[:, pl.ds(i * half, half)],
-                sems.at[1 + i],
+                sems.at[2 + i],
             )
             for i in range(2)
         ],
+        pltpu.make_async_copy(other_hbm, other_ref, sems.at[4]),
     )
     parts = [pl.ds(i * block, block) for i in range(steps)]
-    sides = ((own_hbm, own_ref, own_out_ref), (other_hbm, other_ref, other_out_ref))
-    rows = started(
-        *[
-            pltpu.make_async_copy(hbm.at[part], ref.at[part], sems.at[3 + side * steps + i])
-            for side, (hbm, ref, _) in enumerate(sides)
-            for i, part in enumerate(parts)
-        ]
-    )
-    for copy in copies:
-        copy.wait()
+    copies[0].wait()
+    copies[1].wait()
     gain = gain_ref[...]
-    for side, (_, ref, out_ref) in enumerate(sides):
-        for i, part in enumerate(parts):
-            rows[side * steps + i].wait()
-            out_ref[part, :] = dot(normed(ref[part, :], gain), w_ref[...]).astype(bf16)
+    own_rows = [normed(own_ref[part, :], gain) for part in parts]
+    copies[2].wait()
+    copies[3].wait()
+    for part, rows in zip(parts, own_rows):
+        own_out_ref[part, :] = dot(rows, w_ref[...]).astype(bf16)
+    copies[4].wait()
+    for part in parts:
+        other_out_ref[part, :] = dot(normed(other_ref[part, :], gain), w_ref[...]).astype(bf16)
 
 
 def stat_parts(top, total):
@@ -389,14 +387,20 @@
     queries = half_of(query_ref, (1 - core) * half, half)
     pairs = pairs_ref[...].T
     sends = []
-    for i in range(steps):
-        part = pl.ds(i * block, block)
-        mixed = attend_half(pairs, queries[:, part], node_ref[:, part])
+    parts = [pl.ds(i * block, block) for i in range(steps)]
+
+    def attended(part):
+        return attend_half(pairs, queries[:, part], node_ref[:, part])
+
+    mixed = attended(parts[0])
+    for i, part in enumerate(parts):
+        following = attended(parts[i + 1]) if i + 1 < steps else None
         own = own_ref[part, :]
         both = [jnp.where(core == 0, own, mixed), jnp.where(core == 0, mixed, own)]
         update = dot(jnp.concatenate(both, axis=1), w_ref[...])
         out_ref[part, :] = (x_ref[part, :].astype(f32) + update).astype(bf16)
         sends += started(pltpu.make_async_copy(out_ref.at[part], out_hbm.at[part], sems.at[i]))
+        mixed = following
     for send in sends:
         send.wait()
 
@@ -474,7 +478,7 @@
             pltpu.VMEM((points, depth), bf16),
             pltpu.VMEM((points, depth), bf16),
             pltpu.VMEM((depth, width), bf16),
-            pltpu.SemaphoreType.DMA((3 + 2 * steps,)),
+            pltpu.SemaphoreType.DMA((5,)),
         ],
         compiler_params=params(40),
         cost_estimate=cost(4 * points * depth * width, 8 * points * depth),

time: 55.2 us -> 54.6 us (0.989)
  Pallas kernels: 22.2 us -> 21 us
  waiting for transfers between devices: 6.45 us -> 7.12 us
    pallas_call x1, Pallas kernels: 5.77 us -> 5.09 us  [on_device(): pl.pallas_call(functools.partial(front_kernel, steps), in_specs=[hbm] * 4...]
    all_to_all x2, waiting for transfers between devices: 6.44 us -> 7.11 us  [exchange(): lax.all_to_all(blocks, 'dom', split_axis=0, concat_axis=0, tiled=True, ax...]
    pallas_call x1, Pallas kernels: 4.18 us -> 3.59 us  [on_device(): pl.pallas_call(functools.partial(other_kernel, steps), in_specs=[vmem] *...]
  transfers between devices with their start and end apart: 4 -> 4, of which waited for: 2 -> 2; matrix products, arithmetic and copies ran while one was open for 0% -> 0% of each run, Pallas kernels for 24% -> 23%
where the time goes in v11:
time: 54.6 us; the launch traced here: 54.2 us
  Pallas kernels  21 us (38%)
  blocking collectives  12.5 us (23%)
  starting transfers between devices  11.7 us (21%)
  waiting for transfers between devices  7.12 us (13%)
  local copies, waits for them, and re-layouts  1.01 us (2%)
  between operations  0.94 us (2%)
    all_to_all x1, blocking collectives, exchange(): lax.all_to_all(blocks, 'dom', split_axis=0, concat_axis=0, tiled=True, ax...  12.5 us
    all_to_all x2, starting transfers between devices, exchange(): lax.all_to_all(blocks, 'dom', split_axis=0, concat_axis=0, tiled=True, ax...  10.9 us
    all_to_all x2, waiting for transfers between devices, exchange(): lax.all_to_all(blocks, 'dom', split_axis=0, concat_axis=0, tiled=True, ax...  7.11 us
    pallas_call x1, Pallas kernels, on_device(): pl.pallas_call(functools.partial(front_kernel, steps), in_specs=[hbm] * 4...  5.09 us
    pallas_call x1, Pallas kernels, on_device(): pl.pallas_call(functools.partial(other_kernel, steps), in_specs=[vmem] *...  3.59 us
    pallas_call x1, Pallas kernels, on_device(): pl.pallas_call(functools.partial(middle_kernel, steps, peers, rows), in_s...  3.54 us
    pallas_call x1, Pallas kernels, on_device(): pl.pallas_call(functools.partial(partial_kernel, cap, rows, edges), in_sp...  3.27 us
    pallas_call x1, Pallas kernels, on_device(): pl.pallas_call(ask_kernel, in_specs=[hbm] * len(ask_inputs), out_shape=ja...  2.31 us
  transfers between devices with their start and end apart: 4, of which 2 were waited for; matrix products, arithmetic and copies ran while one was open for 0% of the time, Pallas kernels for 23%

profile of v11, /device:TPU:0, one launch (start us, length us, event | category | flops | bytes accessed | tf_op | source)
XLA Modules:
  0.0 54.2 jit_solution(4685807057911587417)
XLA Ops:
  0.6 0.5 collective-permute-start
  1.1 2.3 %ask.1 = bf16[16,40,128]{2,1,0:T(8,128)(2,1)} custom-call(bf16[1024,512]{1,0:T(8,128)(2,1)} %refs_0_.1, bf16[16,1024]{1,0:T(8,128)(2,1)} %latent_ref.1, f32[1,1024]{1,0:T(1,128)} %bitcast.14, s32[16,32]{1,0:T(8,128)} %bitcast.13, s32[1,16]{1,0:T(1,128)} %bitcast.15, s32[1,512]{1,0:T(1,128)} %refs_5_.1), custom_call_target="tpu_custom_call" | custom-call | flops 16777216 | bytes 1048576 | tf_op jit(solution)/shard_map/ask/pallas_call | solution.py:457
  3.5 7.1 %all-to-all-start = ((bf16[16,40,128]{2,1,0:T(8,128)(2,1)}), bf16[16,40,128]{2,1,0:T(8,128)(2,1)S(1)}, u32[]{:S(2)}, u32[]{:S(2)}) async-start(bf16[16,40,128]{2,1,0:T(8,128)(2,1)} %ask.1), calls=%async_computation | async-start | bytes 327680 | tf_op jit(solution)/shard_map/all_to_all | solution.py:71
  10.5 0.0 collective-permute-done.other_hbm
  10.5 5.1 %front.1 = (bf16[1024,512]{1,0:T(8,128)(2,1)S(1)}, bf16[1024,512]{1,0:T(8,128)(2,1)S(1)}) custom-call(f32[1,1024]{1,0:T(1,128)} %bitcast.11, bf16[1024,1024]{1,0:T(8,128)(2,1)} %x_ref.1, bf16[1024,1024]{1,0:T(8,128)(2,1)} %collective-permute-done.other_hbm, bf16[1024,1024]{1,0:T(8,128)(2,1)} %w_hbm.2), custom_call_target="tpu_custom_call" | custom-call | flops 2147483648 | bytes 8388608 | tf_op jit(solution)/shard_map/front/pallas_call | solution.py:471
  15.6 3.3 %all-to-all-done.asked_ref = bf16[16,40,128]{2,1,0:T(8,128)(2,1)S(1)} async-done(((bf16[16,40,128]{2,1,0:T(8,128)(2,1)}), bf16[16,40,128]{2,1,0:T(8,128)(2,1)S(1)}, u32[]{:S(2)}, u32[]{:S(2)}) %all-to-all-start) | async-done | bytes 163872 | tf_op jit(solution)/shard_map/all_to_all | solution.py:71
  19.0 0.0 copy-start.6
  19.0 0.0 copy-start.7
  19.0 0.0 copy-start.8
  19.0 3.3 %partial.1 = bf16[16,40,128]{2,1,0:T(8,128)(2,1)} custom-call(bf16[16,40,128]{2,1,0:T(8,128)(2,1)S(1)} %all-to-all-done.asked_ref, bf16[1024,512]{1,0:T(8,128)(2,1)S(1)} %get-tuple-element.14.refs_0_, bf16[1024,512]{1,0:T(8,128)(2,1)S(1)} %get-tuple-element.15.refs_1_), custom_call_target="tpu_custom_call" | custom-call | flops 1073741824 | bytes 2097152 | tf_op jit(solution)/shard_map/partial/pallas_call | solution.py:488
  22.2 0.0 copy-start
  22.2 0.0 copy-start.1
  22.2 0.0 copy-start.2
  22.2 0.0 copy-start.3
  22.2 3.8 %all-to-all-start.1 = ((bf16[16,40,128]{2,1,0:T(8,128)(2,1)}), bf16[16,40,128]{2,1,0:T(8,128)(2,1)S(1)}, u32[]{:S(2)}, u32[]{:S(2)}) async-start(bf16[16,40,128]{2,1,0:T(8,128)(2,1)} %partial.1), calls=%async_computation.1 | async-start | bytes 327680 | tf_op jit(solution)/shard_map/all_to_all | solution.py:71
  26.0 0.0 copy-done.6
  26.1 0.0 copy-done.7
  26.1 0.0 copy-done.8
  26.1 3.5 %middle.1 = (bf16[512,1024]{1,0:T(8,128)(2,1)S(1)}, s32[4,1024]{1,0:T(4,128)S(1)}) custom-call(f32[1,1024]{1,0:T(1,128)S(1)} %bitcast.12, s32[32,128]{1,0:T(8,128)S(1)} %bitcast.10, s32[4,1024]{1,0:T(4,128)S(1)} %copy-done.7, bf16[1024,1024]{1,0:T(8,128)(2,1)} %x_ref.1, bf16[1024,512]{1,0:T(8,128)(2,1)} %w_hbm.3), custom_call_target="tpu_custom_call" | custom-call | flops 1073741824 | bytes 8388608 | tf_op jit(solution)/shard_map/middle/pallas_call | solution.py:502
  29.6 0.0 copy-start.9
  29.6 1.0 %copy-done.9 = bf16[512,1024]{1,0:T(8,128)(2,1)} copy-done((bf16[512,1024]{1,0:T(8,128)(2,1)}, bf16[512,1024]{1,0:T(8,128)(2,1)S(1)}, u32[]{:S(2)}) %copy-start.9) | copy-done | bytes 1048600
  30.6 3.8 %all-to-all-done.1.parts_ref = bf16[16,40,128]{2,1,0:T(8,128)(2,1)S(1)} async-done(((bf16[16,40,128]{2,1,0:T(8,128)(2,1)}), bf16[16,40,128]{2,1,0:T(8,128)(2,1)S(1)}, u32[]{:S(2)}, u32[]{:S(2)}) %all-to-all-start.1) | async-done | bytes 163872 | tf_op jit(solution)/shard_map/all_to_all | solution.py:71
  34.4 0.0 copy-start.10
  34.4 0.0 copy-done
  34.4 0.0 copy-done.1
  34.4 0.0 copy-done.2
  34.4 0.0 copy-done.3
  34.4 0.0 copy-start.4
  34.4 0.0 copy-start.5
  34.4 1.5 %combine.1 = (bf16[16,1024]{1,0:T(8,128)(2,1)}, bf16[16,16,512]{2,1,0:T(8,128)(2,1)S(1)}) custom-call(bf16[16,40,128]{2,1,0:T(8,128)(2,1)S(1)} %all-to-all-done.1.parts_ref, bf16[16,1024]{1,0:T(8,128)(2,1)S(1)} %copy-done.2, f32[1,1024]{1,0:T(1,128)S(1)} %bitcast.9, bf16[512,1024]{1,0:T(8,128)(2,1)S(1)} %copy-done.1, bf16[1024,1024]{1,0:T(8,128)(2,1)S(1)} %copy-done), custom_call_target="tpu_custom_call" | custom-call | flops 50331648 | bytes 3145728 | tf_op jit(solution)/shard_map/combine/pallas_call | solution.py:527
  36.0 12.5 %all_to_all.15 = bf16[16,16,512]{2,1,0:T(8,128)(2,1)S(1)} all-to-all(bf16[16,16,512]{2,1,0:T(8,128)(2,1)S(1)} %get-tuple-element.23), channel_id=1, replica_groups={{0,9,2,11,4,13,6,15,8,1,10,3,12,5,14,7},{16,25,18,27,20,29,22,31,24,17,..., dimensions={0} | all-to-all | bytes 524288 | tf_op jit(solution)/shard_map/all_to_all | solution.py:71
  48.5 0.3 collective-permute-start.1
  48.8 0.0 copy-done.10
  48.8 1.7 %own.1.own_ref = bf16[1024,256]{1,0:T(8,128)(2,1)S(1)} custom-call(bf16[256,512]{1,0:T(8,128)(2,1)S(1)} %bitcast.8, s32[4,1024]{1,0:T(4,128)S(1)} %get-tuple-element.24.node_ref, bf16[512,1024]{1,0:T(8,128)(2,1)S(1)} %copy-done.10), custom_call_target="tpu_custom_call" | custom-call | flops 536870912 | bytes 2097152 | tf_op jit(solution)/shard_map/own/pallas_call | solution.py:541
  50.5 0.0 collective-permute-done.1.pairs_ref
  50.5 0.0 copy-done.4
  50.5 0.0 copy-done.5
  50.5 3.6 %other.1 = bf16[1024,1024]{1,0:T(8,128)(2,1)} custom-call(bf16[256,512]{1,0:T(8,128)(2,1)S(1)} %collective-permute-done.1.pairs_ref, bf16[1024,256]{1,0:T(8,128)(2,1)S(1)} %own.1.own_ref, s32[4,1024]{1,0:T(4,128)S(1)} %get-tuple-element.24.node_ref, bf16[512,1024]{1,0:T(8,128)(2,1)S(1)} %copy-done.10, bf16[1024,1024]{1,0:T(8,128)(2,1)S(1)} %copy-done.4, ...), custom_call_target="tpu_custom_call" | custom-call | flops 2147483648 | bytes 8388608 | tf_op jit(solution)/shard_map/other/pallas_call | solution.py:549
Async XLA Ops:
  0.6 9.9 %collective-permute-start = (bf16[1024,1024]{1,0:T(8,128)(2,1)}, bf16[1024,1024]{1,0:T(8,128)(2,1)}, u32[]{:S(2)}, u32[]{:S(2)}) collective-permute-start(bf16[1024,1024]{1,0:T(8,128)(2,1)} %x_ref.1), channel_id=1, source_target_pairs={{0,1},{1,0},{2,3},{3,2},{4,5},{5,4},{6,7},{7,6},{8,9},{9,8},{10,11... | collective-permute-start | bytes 6291464 | tf_op jit(solution)/shard_map/ppermute | solution.py:448
  3.5 15.5 %all-to-all-start = ((bf16[16,40,128]{2,1,0:T(8,128)(2,1)}), bf16[16,40,128]{2,1,0:T(8,128)(2,1)S(1)}, u32[]{:S(2)}, u32[]{:S(2)}) async-start(bf16[16,40,128]{2,1,0:T(8,128)(2,1)} %ask.1), calls=%async_computation | async-start | bytes 327680 | tf_op jit(solution)/shard_map/all_to_all | solution.py:71
  19.0 7.1 %copy-start.6 = (s32[1,4096]{1,0:T(1,128)S(1)}, s32[1,4096]{1,0:T(1,128)}, u32[]{:S(2)}) copy-start(s32[1,4096]{1,0:T(1,128)} %param.30) | copy-start | bytes 49156
  19.0 7.1 %copy-start.7 = (s32[4,1024]{1,0:T(4,128)S(1)}, s32[4,1024]{1,0:T(4,128)}, u32[]{:S(2)}) copy-start(s32[4,1024]{1,0:T(4,128)} %slot_ref) | copy-start | bytes 49156
  19.0 7.1 %copy-start.8 = (f32[1024]{0:T(1024)S(1)}, f32[1024]{0:T(1024)}, u32[]{:S(2)}) copy-start(f32[1024]{0:T(1024)} %param.18) | copy-start | bytes 12292
  22.2 12.2 %copy-start = (bf16[1024,1024]{1,0:T(8,128)(2,1)S(1)}, bf16[1024,1024]{1,0:T(8,128)(2,1)}, u32[]{:S(2)}) copy-start(bf16[1024,1024]{1,0:T(8,128)(2,1)} %w_kv_ref.1) | copy-start | bytes 6291460
  22.2 12.2 %copy-start.1 = (bf16[512,1024]{1,0:T(8,128)(2,1)S(1)}, bf16[512,1024]{1,0:T(8,128)(2,1)}, u32[]{:S(2)}) copy-start(bf16[512,1024]{1,0:T(8,128)(2,1)} %w_o_ref.1) | copy-start | bytes 3145732
  22.2 12.2 %copy-start.2 = (bf16[16,1024]{1,0:T(8,128)(2,1)S(1)}, bf16[16,1024]{1,0:T(8,128)(2,1)}, u32[]{:S(2)}) copy-start(bf16[16,1024]{1,0:T(8,128)(2,1)} %latent_ref.1) | copy-start | bytes 98308
  22.2 12.2 %copy-start.3 = (f32[1024]{0:T(1024)S(1)}, f32[1024]{0:T(1024)}, u32[]{:S(2)}) copy-start(f32[1024]{0:T(1024)} %param.20) | copy-start | bytes 12292
  22.2 12.1 %all-to-all-start.1 = ((bf16[16,40,128]{2,1,0:T(8,128)(2,1)}), bf16[16,40,128]{2,1,0:T(8,128)(2,1)S(1)}, u32[]{:S(2)}, u32[]{:S(2)}) async-start(bf16[16,40,128]{2,1,0:T(8,128)(2,1)} %partial.1), calls=%async_computation.1 | async-start | bytes 327680 | tf_op jit(solution)/shard_map/all_to_all | solution.py:71
  29.6 1.0 %copy-start.9 = (bf16[512,1024]{1,0:T(8,128)(2,1)}, bf16[512,1024]{1,0:T(8,128)(2,1)S(1)}, u32[]{:S(2)}) copy-start(bf16[512,1024]{1,0:T(8,128)(2,1)S(1)} %get-tuple-element.25.query_ref) | copy-start | bytes 3145732
  34.4 14.4 %copy-start.10 = (bf16[512,1024]{1,0:T(8,128)(2,1)S(1)}, bf16[512,1024]{1,0:T(8,128)(2,1)}, u32[]{:S(2)}) copy-start(bf16[512,1024]{1,0:T(8,128)(2,1)} %copy-done.9) | copy-start | bytes 3145732
  34.4 16.1 %copy-start.4 = (bf16[1024,1024]{1,0:T(8,128)(2,1)S(1)}, bf16[1024,1024]{1,0:T(8,128)(2,1)}, u32[]{:S(2)}) copy-start(bf16[1024,1024]{1,0:T(8,128)(2,1)} %x_ref.1) | copy-start | bytes 6291460
  34.4 16.1 %copy-start.5 = (bf16[512,1024]{1,0:T(8,128)(2,1)S(1)}, bf16[512,1024]{1,0:T(8,128)(2,1)}, u32[]{:S(2)}) copy-start(bf16[512,1024]{1,0:T(8,128)(2,1)} %w_ref.1) | copy-start | bytes 3145732
  48.5 2.0 %collective-permute-start.1 = (bf16[256,512]{1,0:T(8,128)(2,1)S(1)}, bf16[256,512]{1,0:T(8,128)(2,1)S(1)}, u32[]{:S(2)}, u32[]{:S(2)}) collective-permute-start(bf16[256,512]{1,0:T(8,128)(2,1)S(1)} %bitcast.7), channel_id=1, source_target_pairs={{0,1},{1,0},{2,3},{3,2},{4,5},{5,4},{6,7},{7,6},{8,9},{9,8},{10,11... | collective-permute-start | bytes 786440 | tf_op jit(solution)/shard_map/ppermute | solution.py:538

commit v12 on v11

--- a/solution.py
+++ b/solution.py
@@ -18,6 +18,10 @@
 
 def iota(shape, dim):
     return lax.broadcasted_iota(jnp.int32, shape, dim)
+
+
+def one_hot(places, shape, dim):
+    return (places.astype(jnp.int16) == iota(shape, dim).astype(jnp.int16)).astype(bf16)
 
 
 def div(values, by):
@@ -135,29 +139,26 @@
     core = lax.axis_index("dom") & 1
     copies = started(
         pltpu.make_async_copy(gain_hbm, gain_ref, sems.at[0]),
-        pltpu.make_async_copy(own_hbm, own_ref, sems.at[1]),
         *[
             pltpu.make_async_copy(
                 w_hbm.at[:, pl.ds(pl.multiple_of((core + 2 * i) * half, half), half)],
                 w_ref.at[:, pl.ds(i * half, half)],
-                sems.at[2 + i],
+                sems.at[1 + i],
             )
             for i in range(2)
         ],
+        pltpu.make_async_copy(own_hbm, own_ref, sems.at[3]),
         pltpu.make_async_copy(other_hbm, other_ref, sems.at[4]),
     )
     parts = [pl.ds(i * block, block) for i in range(steps)]
-    copies[0].wait()
-    copies[1].wait()
+    for copy in copies[:3]:
+        copy.wait()
     gain = gain_ref[...]
-    own_rows = [normed(own_ref[part, :], gain) for part in parts]
-    copies[2].wait()
-    copies[3].wait()
-    for part, rows in zip(parts, own_rows):
-        own_out_ref[part, :] = dot(rows, w_ref[...]).astype(bf16)
-    copies[4].wait()
-    for part in parts:
-        other_out_ref[part, :] = dot(normed(other_ref[part, :], gain), w_ref[...]).astype(bf16)
+    sides = ((own_ref, own_out_ref), (other_ref, other_out_ref))
+    for copy, (rows_ref, out_ref) in zip(copies[3:], sides):
+        copy.wait()
+        for part in parts:
+            out_ref[part, :] = dot(normed(rows_ref[part, :], gain), w_ref[...]).astype(bf16)
 
 
 def stat_parts(top, total):
@@ -168,7 +169,7 @@
 
 
 def partial_kernel(cap, rows, edges, asked_ref, *refs):
-    pairs_refs, out_ref, mixed_ref = refs[:2], refs[2], refs[3]
+    pairs_refs, out_ref = refs[:2], refs[2]
     me = lax.axis_index("dom")
     points, both = pairs_refs[0].shape
     peers = out_ref.shape[0]
@@ -179,7 +180,8 @@
     stack = width // LANES * rows
     scale = math.log2(math.e) / math.sqrt(size)
     all_nodes, all_entries = peers * rows, peers * cap
-    nodes, entries = all_nodes // 2, all_entries // 2
+    some = LANES // (heads * rows)
+    nodes, entries = some * rows, some * cap
     tiles = asked_ref[:, stack:, :].astype(f32)
 
     tile_rows = peers * tall
@@ -191,8 +193,7 @@
     for other, ref in enumerate(pairs_refs):
         mine = lane == ((me ^ other) & 1) * cap
         index = jnp.sum(jnp.where(mine, lists, 0.0), axis=1, keepdims=True).astype(jnp.int32)
-        chosen = (index == iota((all_entries, points), 1)).astype(bf16)
-        gathered.append(dot(chosen, ref[...]).astype(bf16))
+        gathered.append(dot(one_hot(index, (all_entries, points), 1), ref[...]))
 
     group, across = div(iota((tall, LANES), 1), rows), LANES // rows
     slots = []
@@ -208,10 +209,7 @@
         slots.append(jnp.concatenate(line, axis=1))
     all_slots = jnp.concatenate(slots, axis=0).astype(jnp.int32) + all_entries // 2
 
-    here = div(iota((entries, nodes), 0), cap) == div(iota((entries, nodes), 1), rows)
     listed = -(-cap // 8) * 8
-    repeat = iota((entries, listed), 1) == mod(iota((entries, listed), 0), cap)
-    repeat = repeat.astype(f32)
     biases = []
     for other in range(2):
         slots = all_slots - (me ^ other) * cap
@@ -219,57 +217,66 @@
         for j in range(edges):
             uses += jnp.where(slots[j : j + 1] == iota((listed, all_nodes), 0), 1.0, 0.0)
         live = uses > 0.5
-        bias = jnp.where(live, jnp.log2(jnp.where(live, uses, 1.0)), NEG)
-        for half in range(2):
-            part = bias[:, half * nodes : (half + 1) * nodes]
-            if cap == listed:
-                repeated = jnp.concatenate([part] * (entries // cap), axis=0)
-            else:
-                repeated = lax.dot_general(
-                    repeat, part, (((1,), (0,)), ((), ())), precision=lax.Precision.HIGHEST
-                )
-            biases.append(jnp.where(here, repeated, NEG))
-    for half in range(2):
-        part = slice(half * entries, (half + 1) * entries)
-        pairs = jnp.concatenate([gathered[0][part], gathered[1][part]], axis=0)
-        bias = jnp.concatenate([biases[half], biases[2 + half]], axis=0)
-        keys, values_t = pairs[:, :width], pairs[:, width:].T
-        windows = slice(half * (peers // 2), (half + 1) * (peers // 2))
+        biases.append(jnp.where(live, jnp.log2(jnp.where(live, uses, 1.0)), NEG))
+
+    window = mod(div(iota((listed, LANES), 1), rows), some)
+    first_nodes = iota((listed, LANES), 1) < nodes
+    first_head = iota((nodes, LANES), 1) < size
+    tops, totals = [], []
+    for start in range(0, peers, some):
+        bias = []
+        for one in biases:
+            at = start * rows
+            one = one[:, at // LANES * LANES : at // LANES * LANES + LANES]
+            one = jnp.where(first_nodes, pltpu.roll(one, -at % LANES, 1), 0.0)
+            spread = nodes
+            while spread < LANES:
+                one += pltpu.roll(one, spread, 1)
+                spread *= 2
+            bias += [jnp.where(window == w, one, NEG)[:cap] for w in range(some)]
+        part = slice(start * cap, start * cap + entries)
+        pairs = jnp.concatenate([one[part] for one in gathered], axis=0).astype(bf16)
+        windows = slice(start, start + some)
         queries = [one.reshape(nodes, LANES) for one in columns_of(asked_ref, windows, rows, width)]
         queries = jnp.concatenate(queries, axis=1)
         head = div(iota(queries.shape, 1), size)
         queries = jnp.concatenate(
             [jnp.where(head == h, queries, jnp.zeros_like(queries)) for h in range(heads)], axis=0
         )
-        scores = dot_t(keys, queries) * scale + jnp.concatenate([bias] * heads, axis=1)
+        scores = dot_t(pairs[:, :width], queries) * scale + jnp.concatenate(bias, axis=0)
         top = jnp.max(scores, axis=0, keepdims=True)
         raised = jnp.exp2(scores - top)
-        total = jnp.sum(raised, axis=0, keepdims=True)
-        raised = raised.astype(bf16)
-        for h in range(0, heads, 2):
-            mixed = dot(
-                values_t[h * size : (h + 2) * size, :], raised[:, h * nodes : (h + 2) * nodes]
-            )
-            mixed_ref[h * size : (h + 1) * size, :] = mixed[:size, :nodes]
-            mixed_ref[(h + 1) * size : (h + 2) * size, :] = mixed[size:, nodes:]
-        by_head = [
-            jnp.concatenate([one[:, h * nodes : (h + 1) * nodes] for h in range(heads)], axis=0)
-            for one in (top, total)
-        ]
-        stats = jnp.concatenate(stat_parts(*by_head), axis=0)
-        rest = mixed_ref.shape[0] - width - stats.shape[0]
-        mixed_ref[width:, :] = jnp.concatenate([stats, jnp.zeros((rest, nodes), f32)], axis=0)
-        result = mixed_ref[...].T
-        mixed = result[:, :width].astype(bf16)
-        for i in range(peers // 2):
-            place = half * (peers // 2) + i
-            for j in range(width // LANES):
-                out_ref[place, j * rows : (j + 1) * rows, :] = mixed[
-                    i * rows : (i + 1) * rows, j * LANES : (j + 1) * LANES
-                ]
-            upper = result[i * rows : i * rows + tall, width:]
-            lower = result[i * rows + tall : (i + 1) * rows, width:]
-            out_ref[place, stack:, :] = (upper + pltpu.roll(lower, LANES // 2, 1)).astype(bf16)
+        tops.append(top)
+        totals.append(jnp.sum(raised, axis=0, keepdims=True))
+        mixed = dot(raised.T.astype(bf16), pairs[:, width:])
+        for j in range(width // LANES):
+            block = mixed[:, j * LANES : (j + 1) * LANES]
+            h = j * (LANES // size)
+            block = jnp.where(
+                first_head, block[h * nodes : (h + 1) * nodes], block[(h + 1) * nodes : (h + 2) * nodes]
+            ).astype(bf16)
+            for w in range(some):
+                out_ref[start + w, j * rows : (j + 1) * rows, :] = block[w * rows : (w + 1) * rows]
+
+    row_lane = iota((tall, LANES), 1)
+    for first in range(0, len(tops), 8):
+        parts = stat_parts(
+            jnp.concatenate(tops[first : first + 8], axis=0),
+            jnp.concatenate(totals[first : first + 8], axis=0),
+        )
+        rest = jnp.zeros((LANES - 8 * len(parts), LANES), f32)
+        columns = jnp.concatenate([*parts, rest], axis=0).T
+        for g in range(8):
+            for w in range(some):
+                tile = jnp.zeros((tall, LANES), f32)
+                for h in range(heads):
+                    for late in range(2):
+                        at = h * nodes + w * rows + late * tall
+                        move = late * (LANES // 2) + h - g
+                        here = (mod(row_lane, 8) == h) & (div(row_lane, LANES // 2) == late)
+                        piece = pltpu.roll(columns[at : at + tall], move % LANES, 1)
+                        tile = jnp.where(here, piece, tile)
+                out_ref[(first + g) * some + w, stack:, :] = tile.astype(bf16)
 
 
 def combine_kernel(parts_ref, latent_ref, gain_ref, w_o_ref, w_kv_ref, latent_out_ref, out_ref):
@@ -277,15 +284,15 @@
     rows = latent_ref.shape[0]
     width = w_o_ref.shape[0]
     half = width // 2
-    heads, size, tall = HEADS // 2, width // HEADS, rows // 2
+    size, tall = width // HEADS, rows // 2
     chips = (peers // 2, 2, tall, LANES)
     tile = parts_ref[:, half // LANES * rows :, :].astype(f32)
 
     def moved(columns):
         return pltpu.roll(tile, LANES - columns, 2)
 
-    top = (tile + moved(heads) + moved(2 * heads)).reshape(chips)
-    total = (moved(3 * heads) + moved(4 * heads)).reshape(chips)
+    top = (tile + moved(8) + moved(16)).reshape(chips)
+    total = (moved(24) + moved(32)).reshape(chips)
     factor = jnp.exp2(top - jnp.max(top, axis=0, keepdims=True))
     factor = factor / jnp.sum(total * factor, axis=0, keepdims=True)
     head = div(iota(chips, 3), size)
@@ -345,8 +352,7 @@
     edges = nodes.shape[0]
     heads = HEADS // 2
     size = half // heads
-    node = iota((pairs.shape[1], points), 0)
-    picks = [(nodes[j : j + 1] == node).astype(bf16) for j in range(edges)]
+    picks = [one_hot(nodes[j : j + 1], (pairs.shape[1], points), 0) for j in range(edges)]
     scores, values = [], []
     for j in range(edges):
         chosen = dot(pairs, picks[j])
@@ -489,7 +495,6 @@
         functools.partial(partial_kernel, cap, rows, edges),
         in_specs=[vmem] * 3,
         out_shape=jax.ShapeDtypeStruct(sent, bf16),
-        scratch_shapes=[pltpu.VMEM((half + LANES, nodes // 2), f32)],
         compiler_params=params(40),
         cost_estimate=cost(4 * entries * points * width, 4 * points * width),
         name="partial",

time: 54.6 us -> 54.7 us (level)
  no operation moved by 1% of the time
where the time goes in v12:
time: 54.7 us; the launch traced here: 54.3 us
  Pallas kernels  20.7 us (38%)
  blocking collectives  12.5 us (23%)
  starting transfers between devices  11.7 us (21%)
  waiting for transfers between devices  7.46 us (14%)
  local copies, waits for them, and re-layouts  1.01 us (2%)
  between operations  0.94 us (2%)
    all_to_all x1, blocking collectives, exchange(): lax.all_to_all(blocks, 'dom', split_axis=0, concat_axis=0, tiled=True, ax...  12.5 us
    all_to_all x2, starting transfers between devices, exchange(): lax.all_to_all(blocks, 'dom', split_axis=0, concat_axis=0, tiled=True, ax...  10.9 us
    all_to_all x2, waiting for transfers between devices, exchange(): lax.all_to_all(blocks, 'dom', split_axis=0, concat_axis=0, tiled=True, ax...  7.46 us
    pallas_call x1, Pallas kernels, on_device(): pl.pallas_call(functools.partial(front_kernel, steps), in_specs=[hbm] * 4...  4.74 us
    pallas_call x1, Pallas kernels, on_device(): pl.pallas_call(functools.partial(other_kernel, steps), in_specs=[vmem] *...  3.8 us
    pallas_call x1, Pallas kernels, on_device(): pl.pallas_call(functools.partial(middle_kernel, steps, peers, rows), in_s...  3.54 us
    pallas_call x1, Pallas kernels, on_device(): pl.pallas_call(functools.partial(partial_kernel, cap, rows, edges), in_sp...  2.97 us
    pallas_call x1, Pallas kernels, on_device(): pl.pallas_call(ask_kernel, in_specs=[hbm] * len(ask_inputs), out_shape=ja...  2.31 us
  transfers between devices with their start and end apart: 4, of which 2 were waited for; matrix products, arithmetic and copies ran while one was open for 0% of the time, Pallas kernels for 23%

profile of v12, /device:TPU:0, one launch (start us, length us, event | category | flops | bytes accessed | tf_op | source)
XLA Modules:
  0.0 54.3 jit_solution(15119370587795109094)
XLA Ops:
  0.6 0.5 collective-permute-start
  1.1 2.3 %ask.1 = bf16[16,40,128]{2,1,0:T(8,128)(2,1)} custom-call(bf16[1024,512]{1,0:T(8,128)(2,1)} %refs_0_.1, bf16[16,1024]{1,0:T(8,128)(2,1)} %latent_ref.1, f32[1,1024]{1,0:T(1,128)} %bitcast.14, s32[16,32]{1,0:T(8,128)} %bitcast.13, s32[1,16]{1,0:T(1,128)} %bitcast.15, s32[1,512]{1,0:T(1,128)} %refs_5_.1), custom_call_target="tpu_custom_call" | custom-call | flops 16777216 | bytes 1048576 | tf_op jit(solution)/shard_map/ask/pallas_call | solution.py:463
  3.5 7.1 %all-to-all-start = ((bf16[16,40,128]{2,1,0:T(8,128)(2,1)}), bf16[16,40,128]{2,1,0:T(8,128)(2,1)S(1)}, u32[]{:S(2)}, u32[]{:S(2)}) async-start(bf16[16,40,128]{2,1,0:T(8,128)(2,1)} %ask.1), calls=%async_computation | async-start | bytes 327680 | tf_op jit(solution)/shard_map/all_to_all | solution.py:75
  10.5 0.0 collective-permute-done.other_hbm
  10.5 4.7 %front.1 = (bf16[1024,512]{1,0:T(8,128)(2,1)S(1)}, bf16[1024,512]{1,0:T(8,128)(2,1)S(1)}) custom-call(f32[1,1024]{1,0:T(1,128)} %bitcast.11, bf16[1024,1024]{1,0:T(8,128)(2,1)} %x_ref.1, bf16[1024,1024]{1,0:T(8,128)(2,1)} %collective-permute-done.other_hbm, bf16[1024,1024]{1,0:T(8,128)(2,1)} %w_hbm.2), custom_call_target="tpu_custom_call" | custom-call | flops 2147483648 | bytes 8388608 | tf_op jit(solution)/shard_map/front/pallas_call | solution.py:477
  15.3 3.7 %all-to-all-done.asked_ref = bf16[16,40,128]{2,1,0:T(8,128)(2,1)S(1)} async-done(((bf16[16,40,128]{2,1,0:T(8,128)(2,1)}), bf16[16,40,128]{2,1,0:T(8,128)(2,1)S(1)}, u32[]{:S(2)}, u32[]{:S(2)}) %all-to-all-start) | async-done | bytes 163872 | tf_op jit(solution)/shard_map/all_to_all | solution.py:75
  19.0 0.0 copy-start.6
  19.0 0.0 copy-start.7
  19.0 0.0 copy-start.8
  19.0 3.0 %partial.1 = bf16[16,40,128]{2,1,0:T(8,128)(2,1)} custom-call(bf16[16,40,128]{2,1,0:T(8,128)(2,1)S(1)} %all-to-all-done.asked_ref, bf16[1024,512]{1,0:T(8,128)(2,1)S(1)} %get-tuple-element.14.refs_0_, bf16[1024,512]{1,0:T(8,128)(2,1)S(1)} %get-tuple-element.15.refs_1_), custom_call_target="tpu_custom_call" | custom-call | flops 1073741824 | bytes 2097152 | tf_op jit(solution)/shard_map/partial/pallas_call | solution.py:494
  21.9 0.0 copy-start
  21.9 0.0 copy-start.1
  21.9 0.0 copy-start.2
  21.9 0.0 copy-start.3
  21.9 3.8 %all-to-all-start.1 = ((bf16[16,40,128]{2,1,0:T(8,128)(2,1)}), bf16[16,40,128]{2,1,0:T(8,128)(2,1)S(1)}, u32[]{:S(2)}, u32[]{:S(2)}) async-start(bf16[16,40,128]{2,1,0:T(8,128)(2,1)} %partial.1), calls=%async_computation.1 | async-start | bytes 327680 | tf_op jit(solution)/shard_map/all_to_all | solution.py:75
  25.7 0.0 copy-done.6
  25.8 0.0 copy-done.7
  25.8 0.0 copy-done.8
  25.8 3.5 %middle.1 = (bf16[512,1024]{1,0:T(8,128)(2,1)S(1)}, s32[4,1024]{1,0:T(4,128)S(1)}) custom-call(f32[1,1024]{1,0:T(1,128)S(1)} %bitcast.12, s32[32,128]{1,0:T(8,128)S(1)} %bitcast.10, s32[4,1024]{1,0:T(4,128)S(1)} %copy-done.7, bf16[1024,1024]{1,0:T(8,128)(2,1)} %x_ref.1, bf16[1024,512]{1,0:T(8,128)(2,1)} %w_hbm.3), custom_call_target="tpu_custom_call" | custom-call | flops 1073741824 | bytes 8388608 | tf_op jit(solution)/shard_map/middle/pallas_call | solution.py:507
  29.3 0.0 copy-start.9
  29.3 1.0 %copy-done.9 = bf16[512,1024]{1,0:T(8,128)(2,1)} copy-done((bf16[512,1024]{1,0:T(8,128)(2,1)}, bf16[512,1024]{1,0:T(8,128)(2,1)S(1)}, u32[]{:S(2)}) %copy-start.9) | copy-done | bytes 1048600
  30.3 3.8 %all-to-all-done.1.parts_ref = bf16[16,40,128]{2,1,0:T(8,128)(2,1)S(1)} async-done(((bf16[16,40,128]{2,1,0:T(8,128)(2,1)}), bf16[16,40,128]{2,1,0:T(8,128)(2,1)S(1)}, u32[]{:S(2)}, u32[]{:S(2)}) %all-to-all-start.1) | async-done | bytes 163872 | tf_op jit(solution)/shard_map/all_to_all | solution.py:75
  34.1 0.0 copy-start.10
  34.1 0.0 copy-done
  34.1 0.0 copy-done.1
  34.1 0.0 copy-done.2
  34.1 0.0 copy-done.3
  34.1 0.0 copy-start.4
  34.1 0.0 copy-start.5
  34.1 1.5 %combine.1 = (bf16[16,1024]{1,0:T(8,128)(2,1)}, bf16[16,16,512]{2,1,0:T(8,128)(2,1)S(1)}) custom-call(bf16[16,40,128]{2,1,0:T(8,128)(2,1)S(1)} %all-to-all-done.1.parts_ref, bf16[16,1024]{1,0:T(8,128)(2,1)S(1)} %copy-done.2, f32[1,1024]{1,0:T(1,128)S(1)} %bitcast.9, bf16[512,1024]{1,0:T(8,128)(2,1)S(1)} %copy-done.1, bf16[1024,1024]{1,0:T(8,128)(2,1)S(1)} %copy-done), custom_call_target="tpu_custom_call" | custom-call | flops 50331648 | bytes 3145728 | tf_op jit(solution)/shard_map/combine/pallas_call | solution.py:532
  35.7 12.5 %all_to_all.15 = bf16[16,16,512]{2,1,0:T(8,128)(2,1)S(1)} all-to-all(bf16[16,16,512]{2,1,0:T(8,128)(2,1)S(1)} %get-tuple-element.23), channel_id=1, replica_groups={{0,9,2,11,4,13,6,15,8,1,10,3,12,5,14,7},{16,25,18,27,20,29,22,31,24,17,..., dimensions={0} | all-to-all | bytes 524288 | tf_op jit(solution)/shard_map/all_to_all | solution.py:75
  48.2 0.3 collective-permute-start.1
  48.5 0.0 copy-done.10
  48.5 1.8 %own.1.own_ref = bf16[1024,256]{1,0:T(8,128)(2,1)S(1)} custom-call(bf16[256,512]{1,0:T(8,128)(2,1)S(1)} %bitcast.8, s32[4,1024]{1,0:T(4,128)S(1)} %get-tuple-element.24.node_ref, bf16[512,1024]{1,0:T(8,128)(2,1)S(1)} %copy-done.10), custom_call_target="tpu_custom_call" | custom-call | flops 536870912 | bytes 2097152 | tf_op jit(solution)/shard_map/own/pallas_call | solution.py:546
  50.3 0.0 collective-permute-done.1.pairs_ref
  50.3 0.0 copy-done.4
  50.3 0.0 copy-done.5
  50.3 3.8 %other.1 = bf16[1024,1024]{1,0:T(8,128)(2,1)} custom-call(bf16[256,512]{1,0:T(8,128)(2,1)S(1)} %collective-permute-done.1.pairs_ref, bf16[1024,256]{1,0:T(8,128)(2,1)S(1)} %own.1.own_ref, s32[4,1024]{1,0:T(4,128)S(1)} %get-tuple-element.24.node_ref, bf16[512,1024]{1,0:T(8,128)(2,1)S(1)} %copy-done.10, bf16[1024,1024]{1,0:T(8,128)(2,1)S(1)} %copy-done.4, ...), custom_call_target="tpu_custom_call" | custom-call | flops 2147483648 | bytes 8388608 | tf_op jit(solution)/shard_map/other/pallas_call | solution.py:554
Async XLA Ops:
  0.6 9.9 %collective-permute-start = (bf16[1024,1024]{1,0:T(8,128)(2,1)}, bf16[1024,1024]{1,0:T(8,128)(2,1)}, u32[]{:S(2)}, u32[]{:S(2)}) collective-permute-start(bf16[1024,1024]{1,0:T(8,128)(2,1)} %x_ref.1), channel_id=1, source_target_pairs={{0,1},{1,0},{2,3},{3,2},{4,5},{5,4},{6,7},{7,6},{8,9},{9,8},{10,11... | collective-permute-start | bytes 6291464 | tf_op jit(solution)/shard_map/ppermute | solution.py:454
  3.5 15.5 %all-to-all-start = ((bf16[16,40,128]{2,1,0:T(8,128)(2,1)}), bf16[16,40,128]{2,1,0:T(8,128)(2,1)S(1)}, u32[]{:S(2)}, u32[]{:S(2)}) async-start(bf16[16,40,128]{2,1,0:T(8,128)(2,1)} %ask.1), calls=%async_computation | async-start | bytes 327680 | tf_op jit(solution)/shard_map/all_to_all | solution.py:75
  19.0 6.8 %copy-start.6 = (s32[1,4096]{1,0:T(1,128)S(1)}, s32[1,4096]{1,0:T(1,128)}, u32[]{:S(2)}) copy-start(s32[1,4096]{1,0:T(1,128)} %param.30) | copy-start | bytes 49156
  19.0 6.8 %copy-start.7 = (s32[4,1024]{1,0:T(4,128)S(1)}, s32[4,1024]{1,0:T(4,128)}, u32[]{:S(2)}) copy-start(s32[4,1024]{1,0:T(4,128)} %slot_ref) | copy-start | bytes 49156
  19.0 6.8 %copy-start.8 = (f32[1024]{0:T(1024)S(1)}, f32[1024]{0:T(1024)}, u32[]{:S(2)}) copy-start(f32[1024]{0:T(1024)} %param.18) | copy-start | bytes 12292
  21.9 12.2 %copy-start = (bf16[1024,1024]{1,0:T(8,128)(2,1)S(1)}, bf16[1024,1024]{1,0:T(8,128)(2,1)}, u32[]{:S(2)}) copy-start(bf16[1024,1024]{1,0:T(8,128)(2,1)} %w_kv_ref.1) | copy-start | bytes 6291460
  21.9 12.2 %copy-start.1 = (bf16[512,1024]{1,0:T(8,128)(2,1)S(1)}, bf16[512,1024]{1,0:T(8,128)(2,1)}, u32[]{:S(2)}) copy-start(bf16[512,1024]{1,0:T(8,128)(2,1)} %w_o_ref.1) | copy-start | bytes 3145732
  21.9 12.2 %copy-start.2 = (bf16[16,1024]{1,0:T(8,128)(2,1)S(1)}, bf16[16,1024]{1,0:T(8,128)(2,1)}, u32[]{:S(2)}) copy-start(bf16[16,1024]{1,0:T(8,128)(2,1)} %latent_ref.1) | copy-start | bytes 98308
  21.9 12.2 %copy-start.3 = (f32[1024]{0:T(1024)S(1)}, f32[1024]{0:T(1024)}, u32[]{:S(2)}) copy-start(f32[1024]{0:T(1024)} %param.20) | copy-start | bytes 12292
  21.9 12.1 %all-to-all-start.1 = ((bf16[16,40,128]{2,1,0:T(8,128)(2,1)}), bf16[16,40,128]{2,1,0:T(8,128)(2,1)S(1)}, u32[]{:S(2)}, u32[]{:S(2)}) async-start(bf16[16,40,128]{2,1,0:T(8,128)(2,1)} %partial.1), calls=%async_computation.1 | async-start | bytes 327680 | tf_op jit(solution)/shard_map/all_to_all | solution.py:75
  29.3 1.0 %copy-start.9 = (bf16[512,1024]{1,0:T(8,128)(2,1)}, bf16[512,1024]{1,0:T(8,128)(2,1)S(1)}, u32[]{:S(2)}) copy-start(bf16[512,1024]{1,0:T(8,128)(2,1)S(1)} %get-tuple-element.25.query_ref) | copy-start | bytes 3145732
  34.1 14.4 %copy-start.10 = (bf16[512,1024]{1,0:T(8,128)(2,1)S(1)}, bf16[512,1024]{1,0:T(8,128)(2,1)}, u32[]{:S(2)}) copy-start(bf16[512,1024]{1,0:T(8,128)(2,1)} %copy-done.9) | copy-start | bytes 3145732
  34.1 16.2 %copy-start.4 = (bf16[1024,1024]{1,0:T(8,128)(2,1)S(1)}, bf16[1024,1024]{1,0:T(8,128)(2,1)}, u32[]{:S(2)}) copy-start(bf16[1024,1024]{1,0:T(8,128)(2,1)} %x_ref.1) | copy-start | bytes 6291460
  34.1 16.2 %copy-start.5 = (bf16[512,1024]{1,0:T(8,128)(2,1)S(1)}, bf16[512,1024]{1,0:T(8,128)(2,1)}, u32[]{:S(2)}) copy-start(bf16[512,1024]{1,0:T(8,128)(2,1)} %w_ref.1) | copy-start | bytes 3145732
  48.2 2.1 %collective-permute-start.1 = (bf16[256,512]{1,0:T(8,128)(2,1)S(1)}, bf16[256,512]{1,0:T(8,128)(2,1)S(1)}, u32[]{:S(2)}, u32[]{:S(2)}) collective-permute-start(bf16[256,512]{1,0:T(8,128)(2,1)S(1)} %bitcast.7), channel_id=1, source_target_pairs={{0,1},{1,0},{2,3},{3,2},{4,5},{5,4},{6,7},{7,6},{8,9},{9,8},{10,11... | collective-permute-start | bytes 786440 | tf_op jit(solution)/shard_map/ppermute | solution.py:543

commit v13 on v12

--- a/solution.py
+++ b/solution.py
@@ -21,7 +21,7 @@
 
 
 def one_hot(places, shape, dim):
-    return (places.astype(jnp.int16) == iota(shape, dim).astype(jnp.int16)).astype(bf16)
+    return (places == iota(shape, dim)).astype(bf16)
 
 
 def div(values, by):
@@ -70,10 +70,9 @@
     return mod(index + (index & 1) * (peers // 2), peers)
 
 
-def exchange(blocks, peers):
-    order = [place_of(i, peers) for i in range(peers)]
+def exchange(blocks, order=None):
     return lax.all_to_all(
-        blocks, "dom", split_axis=0, concat_axis=0, tiled=True, axis_index_groups=[order]
+        blocks, "dom", split_axis=0, concat_axis=0, tiled=True, axis_index_groups=order
     )
 
 
@@ -126,7 +125,7 @@
         for i in range(half // LANES):
             at = p % 2 * half + i * LANES
             out_ref[p, i * rows : (i + 1) * rows, :] = queries[:, at : at + LANES]
-        out_ref[p, half // LANES * rows :, :] = tiles[place_of(p, peers) // 2]
+        out_ref[p, half // LANES * rows :, :] = tiles[p // 2]
 
 
 def front_kernel(
@@ -256,7 +255,7 @@
                 first_head, block[h * nodes : (h + 1) * nodes], block[(h + 1) * nodes : (h + 2) * nodes]
             ).astype(bf16)
             for w in range(some):
-                out_ref[start + w, j * rows : (j + 1) * rows, :] = block[w * rows : (w + 1) * rows]
+                out_ref[place_of(start + w, peers), j * rows : (j + 1) * rows, :] = block[w * rows : (w + 1) * rows]
 
     row_lane = iota((tall, LANES), 1)
     for first in range(0, len(tops), 8):
@@ -276,7 +275,7 @@
                         here = (mod(row_lane, 8) == h) & (div(row_lane, LANES // 2) == late)
                         piece = pltpu.roll(columns[at : at + tall], move % LANES, 1)
                         tile = jnp.where(here, piece, tile)
-                out_ref[(first + g) * some + w, stack:, :] = tile.astype(bf16)
+                out_ref[place_of((first + g) * some + w, peers), stack:, :] = tile.astype(bf16)
 
 
 def combine_kernel(parts_ref, latent_ref, gain_ref, w_o_ref, w_kv_ref, latent_out_ref, out_ref):
@@ -470,7 +469,7 @@
         cost_estimate=cost(2 * rows * depth * width, 2 * depth * width),
         name="ask",
     )(*map(in_hbm, ask_inputs))
-    asked = exchange(asked, peers)
+    asked = exchange(asked)
 
     block = math.gcd(points, 256)
     steps = points // block
@@ -500,7 +499,8 @@
         name="partial",
     )(asked, *map(in_vmem, pairs))
     parts, dec_need, dec_slot = lax.optimization_barrier((parts, dec_need, dec_slot))
-    parts = exchange(parts, peers)
+    order = [[place_of(i, peers) for i in range(peers)]]
+    parts = exchange(parts, order)
 
     slot_total = dec_need.shape[1]
     edge_count = dec_slot.shape[0]
@@ -532,14 +532,14 @@
     latent_out, everyone = pl.pallas_call(
         combine_kernel,
         out_shape=[
-            jax.ShapeDtypeStruct((rows, depth), bf16),
+            pltpu.VMEM((rows, depth), bf16),
             jax.ShapeDtypeStruct((peers, rows, width), bf16),
         ],
         compiler_params=params(24),
         cost_estimate=cost(6 * rows * depth * width, 6 * depth * width),
         name="combine",
     )(parts, latent_in, dec_gain.reshape(1, -1), w_o_enc, w_kv_dec)
-    own = exchange(everyone, peers).reshape(nodes, width)
+    own = exchange(everyone, order).reshape(nodes, width)
     other = lax.ppermute(own, "dom", swap)
 
     queries = in_vmem(queries)

time: 54.7 us -> 54.5 us (level)
  Pallas kernels: 20.7 us -> 19.7 us
  local copies, waits for them, and re-layouts: 1.01 us -> 1.62 us
    unnamed x22 -> x23, local copies, waits for them, and re-layouts: 1.01 us -> 1.62 us
  transfers between devices with their start and end apart: 4 -> 4, of which waited for: 2 -> 2; matrix products, arithmetic and copies ran while one was open for 0% -> 1% of each run, Pallas kernels for 23% -> 23%
where the time goes in v13:
time: 54.5 us; the launch traced here: 54.1 us
  Pallas kernels  19.7 us (36%)
  blocking collectives  12.7 us (23%)
  starting transfers between devices  11.7 us (21%)
  waiting for transfers between devices  7.51 us (14%)
  local copies, waits for them, and re-layouts  1.62 us (3%)
  between operations  0.95 us (2%)
    all_to_all x1, blocking collectives, exchange(): lax.all_to_all(blocks, 'dom', split_axis=0, concat_axis=0, tiled=True, ax...  12.7 us
    all_to_all x2, starting transfers between devices, exchange(): lax.all_to_all(blocks, 'dom', split_axis=0, concat_axis=0, tiled=True, ax...  10.9 us
    all_to_all x2, waiting for transfers between devices, exchange(): lax.all_to_all(blocks, 'dom', split_axis=0, concat_axis=0, tiled=True, ax...  7.5 us
    pallas_call x1, Pallas kernels, on_device(): pl.pallas_call(functools.partial(front_kernel, steps), in_specs=[hbm] * 4...  4.74 us
    pallas_call x1, Pallas kernels, on_device(): pl.pallas_call(functools.partial(other_kernel, steps), in_specs=[vmem] *...  3.59 us
    pallas_call x1, Pallas kernels, on_device(): pl.pallas_call(functools.partial(middle_kernel, steps, peers, rows), in_s...  3.54 us
    pallas_call x1, Pallas kernels, on_device(): pl.pallas_call(functools.partial(partial_kernel, cap, rows, edges), in_sp...  2.86 us
    pallas_call x1, Pallas kernels, on_device(): pl.pallas_call(ask_kernel, in_specs=[hbm] * len(ask_inputs), out_shape=ja...  2.31 us
  transfers between devices with their start and end apart: 4, of which 2 were waited for; matrix products, arithmetic and copies ran while one was open for 1% of the time, Pallas kernels for 23%

profile of v13, /device:TPU:0, one launch (start us, length us, event | category | flops | bytes accessed | tf_op | source)
XLA Modules:
  0.0 54.1 jit_solution(15799956534307482162)
XLA Ops:
  0.6 0.5 collective-permute-start
  1.1 2.3 %ask.1 = bf16[16,40,128]{2,1,0:T(8,128)(2,1)} custom-call(bf16[1024,512]{1,0:T(8,128)(2,1)} %refs_0_.1, bf16[16,1024]{1,0:T(8,128)(2,1)} %latent_ref.1, f32[1,1024]{1,0:T(1,128)} %bitcast.14, s32[16,32]{1,0:T(8,128)} %bitcast.13, s32[1,16]{1,0:T(1,128)} %bitcast.15, s32[1,512]{1,0:T(1,128)} %refs_5_.1), custom_call_target="tpu_custom_call" | custom-call | flops 16777216 | bytes 1048576 | tf_op jit(solution)/shard_map/ask/pallas_call | solution.py:462
  3.5 7.1 %all-to-all-start = ((bf16[16,40,128]{2,1,0:T(8,128)(2,1)}), bf16[16,40,128]{2,1,0:T(8,128)(2,1)S(1)}, u32[]{:S(2)}, u32[]{:S(2)}) async-start(bf16[16,40,128]{2,1,0:T(8,128)(2,1)} %ask.1), calls=%async_computation | async-start | bytes 327680 | tf_op jit(solution)/shard_map/all_to_all | solution.py:74
  10.5 0.0 collective-permute-done.other_hbm
  10.5 4.7 %front.1 = (bf16[1024,512]{1,0:T(8,128)(2,1)S(1)}, bf16[1024,512]{1,0:T(8,128)(2,1)S(1)}) custom-call(f32[1,1024]{1,0:T(1,128)} %bitcast.11, bf16[1024,1024]{1,0:T(8,128)(2,1)} %x_ref.1, bf16[1024,1024]{1,0:T(8,128)(2,1)} %collective-permute-done.other_hbm, bf16[1024,1024]{1,0:T(8,128)(2,1)} %w_hbm.2), custom_call_target="tpu_custom_call" | custom-call | flops 2147483648 | bytes 8388608 | tf_op jit(solution)/shard_map/front/pallas_call | solution.py:476
  15.3 3.7 %all-to-all-done.asked_ref = bf16[16,40,128]{2,1,0:T(8,128)(2,1)S(1)} async-done(((bf16[16,40,128]{2,1,0:T(8,128)(2,1)}), bf16[16,40,128]{2,1,0:T(8,128)(2,1)S(1)}, u32[]{:S(2)}, u32[]{:S(2)}) %all-to-all-start) | async-done | bytes 163872 | tf_op jit(solution)/shard_map/all_to_all | solution.py:74
  19.0 0.0 copy-start.6
  19.0 0.0 copy-start.7
  19.0 0.0 copy-start.8
  19.0 2.9 %partial.1 = bf16[16,40,128]{2,1,0:T(8,128)(2,1)} custom-call(bf16[16,40,128]{2,1,0:T(8,128)(2,1)S(1)} %all-to-all-done.asked_ref, bf16[1024,512]{1,0:T(8,128)(2,1)S(1)} %get-tuple-element.14.refs_0_, bf16[1024,512]{1,0:T(8,128)(2,1)S(1)} %get-tuple-element.15.refs_1_), custom_call_target="tpu_custom_call" | custom-call | flops 1073741824 | bytes 2097152 | tf_op jit(solution)/shard_map/partial/pallas_call | solution.py:493
  21.9 0.0 copy-start
  21.9 0.0 copy-start.1
  21.9 0.0 copy-start.2
  21.9 0.0 copy-start.3
  21.9 3.8 %all-to-all-start.1 = ((bf16[16,40,128]{2,1,0:T(8,128)(2,1)}), bf16[16,40,128]{2,1,0:T(8,128)(2,1)S(1)}, u32[]{:S(2)}, u32[]{:S(2)}) async-start(bf16[16,40,128]{2,1,0:T(8,128)(2,1)} %partial.1), calls=%async_computation.1 | async-start | bytes 327680 | tf_op jit(solution)/shard_map/all_to_all | solution.py:74
  25.7 0.0 copy-done.6
  25.7 0.0 copy-done.7
  25.7 0.0 copy-done.8
  25.7 3.5 %middle.1 = (bf16[512,1024]{1,0:T(8,128)(2,1)S(1)}, s32[4,1024]{1,0:T(4,128)S(1)}) custom-call(f32[1,1024]{1,0:T(1,128)S(1)} %bitcast.12, s32[32,128]{1,0:T(8,128)S(1)} %bitcast.10, s32[4,1024]{1,0:T(4,128)S(1)} %copy-done.7, bf16[1024,1024]{1,0:T(8,128)(2,1)} %x_ref.1, bf16[1024,512]{1,0:T(8,128)(2,1)} %w_hbm.3), custom_call_target="tpu_custom_call" | custom-call | flops 1073741824 | bytes 8388608 | tf_op jit(solution)/shard_map/middle/pallas_call | solution.py:507
  29.2 0.0 copy-start.9
  29.3 1.0 %copy-done.9 = bf16[512,1024]{1,0:T(8,128)(2,1)} copy-done((bf16[512,1024]{1,0:T(8,128)(2,1)}, bf16[512,1024]{1,0:T(8,128)(2,1)S(1)}, u32[]{:S(2)}) %copy-start.9) | copy-done | bytes 1048600
  30.2 3.8 %all-to-all-done.1.parts_ref = bf16[16,40,128]{2,1,0:T(8,128)(2,1)S(1)} async-done(((bf16[16,40,128]{2,1,0:T(8,128)(2,1)}), bf16[16,40,128]{2,1,0:T(8,128)(2,1)S(1)}, u32[]{:S(2)}, u32[]{:S(2)}) %all-to-all-start.1) | async-done | bytes 163872 | tf_op jit(solution)/shard_map/all_to_all | solution.py:74
  34.0 0.0 copy-start.10
  34.0 0.0 copy-done
  34.0 0.0 copy-done.1
  34.0 0.0 copy-done.2
  34.0 0.0 copy-done.3
  34.0 0.0 copy-start.5
  34.1 1.0 %combine.1 = (bf16[16,1024]{1,0:T(8,128)(2,1)S(1)}, bf16[16,16,512]{2,1,0:T(8,128)(2,1)S(1)}) custom-call(bf16[16,40,128]{2,1,0:T(8,128)(2,1)S(1)} %all-to-all-done.1.parts_ref, bf16[16,1024]{1,0:T(8,128)(2,1)S(1)} %copy-done.2, f32[1,1024]{1,0:T(1,128)S(1)} %bitcast.9, bf16[512,1024]{1,0:T(8,128)(2,1)S(1)} %copy-done.1, bf16[1024,1024]{1,0:T(8,128)(2,1)S(1)} %copy-done), custom_call_target="tpu_custom_call" | custom-call | flops 50331648 | bytes 3145728 | tf_op jit(solution)/shard_map/combine/pallas_call | solution.py:532
  35.1 0.0 copy-start.4
  35.1 12.7 %all_to_all.15 = bf16[16,16,512]{2,1,0:T(8,128)(2,1)S(1)} all-to-all(bf16[16,16,512]{2,1,0:T(8,128)(2,1)S(1)} %get-tuple-element.23), channel_id=1, replica_groups={{0,9,2,11,4,13,6,15,8,1,10,3,12,5,14,7},{16,25,18,27,20,29,22,31,24,17,..., dimensions={0} | all-to-all | bytes 524288 | tf_op jit(solution)/shard_map/all_to_all | solution.py:74
  47.8 0.3 collective-permute-start.1
  48.1 0.6 %copy.18 = bf16[16,1024]{1,0:T(8,128)(2,1)} copy(bf16[16,1024]{1,0:T(8,128)(2,1)S(1)} %get-tuple-element.26) | data formatting | bytes 65536
  48.7 0.0 copy-done.10
  48.7 1.6 %own.1.own_ref = bf16[1024,256]{1,0:T(8,128)(2,1)S(1)} custom-call(bf16[256,512]{1,0:T(8,128)(2,1)S(1)} %bitcast.8, s32[4,1024]{1,0:T(4,128)S(1)} %get-tuple-element.24.node_ref, bf16[512,1024]{1,0:T(8,128)(2,1)S(1)} %copy-done.10), custom_call_target="tpu_custom_call" | custom-call | flops 536870912 | bytes 2097152 | tf_op jit(solution)/shard_map/own/pallas_call | solution.py:546
  50.4 0.0 collective-permute-done.1.pairs_ref
  50.4 0.0 copy-done.5
  50.4 0.0 copy-done.4
  50.4 3.6 %other.1 = bf16[1024,1024]{1,0:T(8,128)(2,1)} custom-call(bf16[256,512]{1,0:T(8,128)(2,1)S(1)} %collective-permute-done.1.pairs_ref, bf16[1024,256]{1,0:T(8,128)(2,1)S(1)} %own.1.own_ref, s32[4,1024]{1,0:T(4,128)S(1)} %get-tuple-element.24.node_ref, bf16[512,1024]{1,0:T(8,128)(2,1)S(1)} %copy-done.10, bf16[1024,1024]{1,0:T(8,128)(2,1)S(1)} %copy-done.4, ...), custom_call_target="tpu_custom_call" | custom-call | flops 2147483648 | bytes 8388608 | tf_op jit(solution)/shard_map/other/pallas_call | solution.py:554
Async XLA Ops:
  0.6 9.9 %collective-permute-start = (bf16[1024,1024]{1,0:T(8,128)(2,1)}, bf16[1024,1024]{1,0:T(8,128)(2,1)}, u32[]{:S(2)}, u32[]{:S(2)}) collective-permute-start(bf16[1024,1024]{1,0:T(8,128)(2,1)} %x_ref.1), channel_id=1, source_target_pairs={{0,1},{1,0},{2,3},{3,2},{4,5},{5,4},{6,7},{7,6},{8,9},{9,8},{10,11... | collective-permute-start | bytes 6291464 | tf_op jit(solution)/shard_map/ppermute | solution.py:453
  3.5 15.5 %all-to-all-start = ((bf16[16,40,128]{2,1,0:T(8,128)(2,1)}), bf16[16,40,128]{2,1,0:T(8,128)(2,1)S(1)}, u32[]{:S(2)}, u32[]{:S(2)}) async-start(bf16[16,40,128]{2,1,0:T(8,128)(2,1)} %ask.1), calls=%async_computation | async-start | bytes 327680 | tf_op jit(solution)/shard_map/all_to_all | solution.py:74
  19.0 6.7 %copy-start.6 = (s32[1,4096]{1,0:T(1,128)S(1)}, s32[1,4096]{1,0:T(1,128)}, u32[]{:S(2)}) copy-start(s32[1,4096]{1,0:T(1,128)} %param.30) | copy-start | bytes 49156
  19.0 6.7 %copy-start.7 = (s32[4,1024]{1,0:T(4,128)S(1)}, s32[4,1024]{1,0:T(4,128)}, u32[]{:S(2)}) copy-start(s32[4,1024]{1,0:T(4,128)} %slot_ref) | copy-start | bytes 49156
  19.0 6.7 %copy-start.8 = (f32[1024]{0:T(1024)S(1)}, f32[1024]{0:T(1024)}, u32[]{:S(2)}) copy-start(f32[1024]{0:T(1024)} %param.18) | copy-start | bytes 12292
  21.9 12.2 %copy-start = (bf16[1024,1024]{1,0:T(8,128)(2,1)S(1)}, bf16[1024,1024]{1,0:T(8,128)(2,1)}, u32[]{:S(2)}) copy-start(bf16[1024,1024]{1,0:T(8,128)(2,1)} %w_kv_ref.1) | copy-start | bytes 6291460
  21.9 12.2 %copy-start.1 = (bf16[512,1024]{1,0:T(8,128)(2,1)S(1)}, bf16[512,1024]{1,0:T(8,128)(2,1)}, u32[]{:S(2)}) copy-start(bf16[512,1024]{1,0:T(8,128)(2,1)} %w_o_ref.1) | copy-start | bytes 3145732
  21.9 12.2 %copy-start.2 = (bf16[16,1024]{1,0:T(8,128)(2,1)S(1)}, bf16[16,1024]{1,0:T(8,128)(2,1)}, u32[]{:S(2)}) copy-start(bf16[16,1024]{1,0:T(8,128)(2,1)} %latent_ref.1) | copy-start | bytes 98308
  21.9 12.2 %copy-start.3 = (f32[1024]{0:T(1024)S(1)}, f32[1024]{0:T(1024)}, u32[]{:S(2)}) copy-start(f32[1024]{0:T(1024)} %param.20) | copy-start | bytes 12292
  21.9 12.1 %all-to-all-start.1 = ((bf16[16,40,128]{2,1,0:T(8,128)(2,1)}), bf16[16,40,128]{2,1,0:T(8,128)(2,1)S(1)}, u32[]{:S(2)}, u32[]{:S(2)}) async-start(bf16[16,40,128]{2,1,0:T(8,128)(2,1)} %partial.1), calls=%async_computation.1 | async-start | bytes 327680 | tf_op jit(solution)/shard_map/all_to_all | solution.py:74
  29.2 1.0 %copy-start.9 = (bf16[512,1024]{1,0:T(8,128)(2,1)}, bf16[512,1024]{1,0:T(8,128)(2,1)S(1)}, u32[]{:S(2)}) copy-start(bf16[512,1024]{1,0:T(8,128)(2,1)S(1)} %get-tuple-element.25.query_ref) | copy-start | bytes 3145732
  34.0 14.7 %copy-start.10 = (bf16[512,1024]{1,0:T(8,128)(2,1)S(1)}, bf16[512,1024]{1,0:T(8,128)(2,1)}, u32[]{:S(2)}) copy-start(bf16[512,1024]{1,0:T(8,128)(2,1)} %copy-done.9) | copy-start | bytes 3145732
  34.0 16.3 %copy-start.5 = (bf16[512,1024]{1,0:T(8,128)(2,1)S(1)}, bf16[512,1024]{1,0:T(8,128)(2,1)}, u32[]{:S(2)}) copy-start(bf16[512,1024]{1,0:T(8,128)(2,1)} %w_ref.1) | copy-start | bytes 3145732
  35.1 15.3 %copy-start.4 = (bf16[1024,1024]{1,0:T(8,128)(2,1)S(1)}, bf16[1024,1024]{1,0:T(8,128)(2,1)}, u32[]{:S(2)}) copy-start(bf16[1024,1024]{1,0:T(8,128)(2,1)} %x_ref.1) | copy-start | bytes 6291460
  47.8 2.6 %collective-permute-start.1 = (bf16[256,512]{1,0:T(8,128)(2,1)S(1)}, bf16[256,512]{1,0:T(8,128)(2,1)S(1)}, u32[]{:S(2)}, u32[]{:S(2)}) collective-permute-start(bf16[256,512]{1,0:T(8,128)(2,1)S(1)} %bitcast.7), channel_id=1, source_target_pairs={{0,1},{1,0},{2,3},{3,2},{4,5},{5,4},{6,7},{7,6},{8,9},{9,8},{10,11... | collective-permute-start | bytes 786440 | tf_op jit(solution)/shard_map/ppermute | solution.py:543

commit v14 on v13

--- a/solution.py
+++ b/solution.py
@@ -76,8 +76,8 @@
     )
 
 
-def columns_of(ref, where, rows, half):
-    return [ref[where, i * rows : (i + 1) * rows, :] for i in range(half // LANES)]
+def slab(values, i, late, tall):
+    return values[late * tall : (late + 1) * tall, i * LANES : (i + 1) * LANES]
 
 
 def ask_kernel(*refs):
@@ -119,13 +119,15 @@
         piece = jnp.where(row == 0, piece - high * 256.0, jnp.where(row == 1, high, 0.0))
         tiles.append((tile + jnp.where(in_list, piece, 0.0)).astype(bf16))
     copies[0].wait()
-    queries = dot(rows_normed, w_ref[...]).astype(bf16)
-    half = width // 2
+    queries = dot(rows_normed, w_ref[...])
+    blocks = width // 2 // LANES
+    slabs = [
+        slab(queries, i, late, tall).astype(bf16) for i in range(2 * blocks) for late in range(2)
+    ]
     for p in range(peers):
-        for i in range(half // LANES):
-            at = p % 2 * half + i * LANES
-            out_ref[p, i * rows : (i + 1) * rows, :] = queries[:, at : at + LANES]
-        out_ref[p, half // LANES * rows :, :] = tiles[p // 2]
+        for i in range(2 * blocks):
+            out_ref[p, i] = slabs[p % 2 * 2 * blocks + i]
+        out_ref[p, 2 * blocks] = tiles[p // 2]
 
 
 def front_kernel(
@@ -176,12 +178,12 @@
     heads = HEADS // 2
     size = width // heads
     tall = rows // 2
-    stack = width // LANES * rows
+    blocks = width // LANES
     scale = math.log2(math.e) / math.sqrt(size)
     all_nodes, all_entries = peers * rows, peers * cap
     some = LANES // (heads * rows)
     nodes, entries = some * rows, some * cap
-    tiles = asked_ref[:, stack:, :].astype(f32)
+    tiles = asked_ref[:, 2 * blocks].astype(f32)
 
     tile_rows = peers * tall
     pick_row = iota((all_entries, tile_rows), 1) - div(iota((all_entries, tile_rows), 0), cap) * tall
@@ -235,9 +237,13 @@
             bias += [jnp.where(window == w, one, NEG)[:cap] for w in range(some)]
         part = slice(start * cap, start * cap + entries)
         pairs = jnp.concatenate([one[part] for one in gathered], axis=0).astype(bf16)
-        windows = slice(start, start + some)
-        queries = [one.reshape(nodes, LANES) for one in columns_of(asked_ref, windows, rows, width)]
-        queries = jnp.concatenate(queries, axis=1)
+        queries = [
+            jnp.concatenate(
+                [asked_ref[start + n // 2, 2 * i + n % 2].astype(f32) for n in range(2 * some)], axis=0
+            )
+            for i in range(blocks)
+        ]
+        queries = jnp.concatenate(queries, axis=1).astype(bf16)
         head = div(iota(queries.shape, 1), size)
         queries = jnp.concatenate(
             [jnp.where(head == h, queries, jnp.zeros_like(queries)) for h in range(heads)], axis=0
@@ -248,14 +254,15 @@
         tops.append(top)
         totals.append(jnp.sum(raised, axis=0, keepdims=True))
         mixed = dot(raised.T.astype(bf16), pairs[:, width:])
-        for j in range(width // LANES):
-            block = mixed[:, j * LANES : (j + 1) * LANES]
-            h = j * (LANES // size)
+        for i in range(blocks):
+            block = mixed[:, i * LANES : (i + 1) * LANES]
+            h = i * (LANES // size)
             block = jnp.where(
                 first_head, block[h * nodes : (h + 1) * nodes], block[(h + 1) * nodes : (h + 2) * nodes]
-            ).astype(bf16)
-            for w in range(some):
-                out_ref[place_of(start + w, peers), j * rows : (j + 1) * rows, :] = block[w * rows : (w + 1) * rows]
+            )
+            for n in range(2 * some):
+                place = place_of(start + n // 2, peers)
+                out_ref[place, 2 * i + n % 2] = slab(block, 0, n, tall).astype(bf16)
 
     row_lane = iota((tall, LANES), 1)
     for first in range(0, len(tops), 8):
@@ -275,17 +282,19 @@
                         here = (mod(row_lane, 8) == h) & (div(row_lane, LANES // 2) == late)
                         piece = pltpu.roll(columns[at : at + tall], move % LANES, 1)
                         tile = jnp.where(here, piece, tile)
-                out_ref[place_of((first + g) * some + w, peers), stack:, :] = tile.astype(bf16)
-
-
-def combine_kernel(parts_ref, latent_ref, gain_ref, w_o_ref, w_kv_ref, latent_out_ref, out_ref):
+                out_ref[place_of((first + g) * some + w, peers), 2 * blocks] = tile.astype(bf16)
+
+
+def combine_kernel(
+    parts_ref, latent_ref, gain_ref, w_o_ref, w_kv_ref, latent_hbm, out_ref, latent_out_ref, sem
+):
     peers = parts_ref.shape[0]
     rows = latent_ref.shape[0]
     width = w_o_ref.shape[0]
     half = width // 2
     size, tall = width // HEADS, rows // 2
     chips = (peers // 2, 2, tall, LANES)
-    tile = parts_ref[:, half // LANES * rows :, :].astype(f32)
+    tile = parts_ref[:, 2 * (half // LANES)].astype(f32)
 
     def moved(columns):
         return pltpu.roll(tile, LANES - columns, 2)
@@ -296,26 +305,28 @@
     factor = factor / jnp.sum(total * factor, axis=0, keepdims=True)
     head = div(iota(chips, 3), size)
     blocks = []
-    for i, block in enumerate(columns_of(parts_ref, slice(None), rows, half)):
-        block = block.astype(f32)
+    for i in range(half // LANES):
         nodes = []
-        for g in range(2):
+        for late in range(2):
             wide = jnp.zeros(chips, f32)
             for h in range(LANES // size):
-                at = g * (LANES // 2) + i * (LANES // size) + h
+                at = late * (LANES // 2) + i * (LANES // size) + h
                 wide = jnp.where(head == h, factor[..., at : at + 1], wide)
-            part = block[:, g * tall : (g + 1) * tall].reshape(chips)
+            part = parts_ref[:, 2 * i + late].astype(f32).reshape(chips)
             nodes.append(jnp.sum(part * wide, axis=0))
         blocks.append(jnp.concatenate(nodes, axis=1))
     mixed = jnp.concatenate([block[h] for h in range(2) for block in blocks], axis=1)
     update = dot(mixed.astype(bf16), w_o_ref[...])
     latent_out = (latent_ref[...].astype(f32) + update).astype(bf16)
     latent_out_ref[...] = latent_out
+    copy = pltpu.make_async_copy(latent_out_ref, latent_hbm, sem)
+    copy.start()
     pairs = dot(normed(latent_out, gain_ref[...]), w_kv_ref[...]).astype(bf16)
     for p in range(peers):
         at = p % 2 * half
         out_ref[p, :, :half] = pairs[:, at : at + half]
         out_ref[p, :, half:] = pairs[:, width + at : width + at + half]
+    copy.wait()
 
 
 def middle_kernel(
@@ -445,7 +456,7 @@
     edges = enc_slot.shape[0]
     cap = entries // peers
     half = width // 2
-    sent = (peers, half // LANES * rows + rows // 2, LANES)
+    sent = (peers, 2 * (half // LANES) + 1, rows // 2, LANES)
     swap = [(i, i ^ 1) for i in range(peers)]
     vmem = pl.BlockSpec(memory_space=pltpu.VMEM)
     hbm = pl.BlockSpec(memory_space=pltpu.HBM)
@@ -531,10 +542,13 @@
 
     latent_out, everyone = pl.pallas_call(
         combine_kernel,
+        in_specs=[vmem] * 5,
+        out_specs=[hbm, vmem],
         out_shape=[
-            pltpu.VMEM((rows, depth), bf16),
+            pltpu.HBM((rows, depth), bf16),
             jax.ShapeDtypeStruct((peers, rows, width), bf16),
         ],
+        scratch_shapes=[pltpu.VMEM((rows, depth), bf16), pltpu.SemaphoreType.DMA],
         compiler_params=params(24),
         cost_estimate=cost(6 * rows * depth * width, 6 * depth * width),
         name="combine",

time: 54.5 us -> 54.3 us (level)
  local copies, waits for them, and re-layouts: 1.62 us -> 1.01 us
    unnamed x23 -> x22, local copies, waits for them, and re-layouts: 1.62 us -> 1.01 us
  transfers between devices with their start and end apart: 4 -> 4, of which waited for: 2 -> 2; matrix products, arithmetic and copies ran while one was open for 1% -> 0% of each run, Pallas kernels for 23% -> 23%
where the time goes in v14:
time: 54.3 us; the launch traced here: 53.9 us
  Pallas kernels  20.2 us (37%)
  blocking collectives  12.6 us (23%)
  starting transfers between devices  11.7 us (22%)
  waiting for transfers between devices  7.51 us (14%)
  local copies, waits for them, and re-layouts  1.01 us (2%)
  between operations  0.95 us (2%)
    all_to_all x1, blocking collectives, exchange(): lax.all_to_all(blocks, 'dom', split_axis=0, concat_axis=0, tiled=True, ax...  12.6 us
    all_to_all x2, starting transfers between devices, exchange(): lax.all_to_all(blocks, 'dom', split_axis=0, concat_axis=0, tiled=True, ax...  10.9 us
    all_to_all x2, waiting for transfers between devices, exchange(): lax.all_to_all(blocks, 'dom', split_axis=0, concat_axis=0, tiled=True, ax...  7.5 us
    pallas_call x1, Pallas kernels, on_device(): pl.pallas_call(functools.partial(front_kernel, steps), in_specs=[hbm] * 4...  4.74 us
    pallas_call x1, Pallas kernels, on_device(): pl.pallas_call(functools.partial(other_kernel, steps), in_specs=[vmem] *...  3.59 us
    pallas_call x1, Pallas kernels, on_device(): pl.pallas_call(functools.partial(middle_kernel, steps, peers, rows), in_s...  3.54 us
    pallas_call x1, Pallas kernels, on_device(): pl.pallas_call(functools.partial(partial_kernel, cap, rows, edges), in_sp...  2.86 us
    pallas_call x1, Pallas kernels, on_device(): pl.pallas_call(ask_kernel, in_specs=[hbm] * len(ask_inputs), out_shape=ja...  2.31 us
  transfers between devices with their start and end apart: 4, of which 2 were waited for; matrix products, arithmetic and copies ran while one was open for 0% of the time, Pallas kernels for 23%

profile of v14, /device:TPU:0, one launch (start us, length us, event | category | flops | bytes accessed | tf_op | source)
XLA Modules:
  0.0 53.9 jit_solution(15803253892770266739)
XLA Ops:
  0.6 0.5 collective-permute-start
  1.1 2.3 %ask.1 = bf16[16,5,8,128]{3,2,1,0:T(8,128)(2,1)} custom-call(bf16[1024,512]{1,0:T(8,128)(2,1)} %refs_0_.1, bf16[16,1024]{1,0:T(8,128)(2,1)} %latent_ref.1, f32[1,1024]{1,0:T(1,128)} %bitcast.14, s32[16,32]{1,0:T(8,128)} %bitcast.13, s32[1,16]{1,0:T(1,128)} %bitcast.15, s32[1,512]{1,0:T(1,128)} %refs_5_.1), custom_call_target="tpu_custom_call" | custom-call | flops 16777216 | bytes 1048576 | tf_op jit(solution)/shard_map/ask/pallas_call | solution.py:473
  3.5 7.1 %all-to-all-start = ((bf16[16,5,8,128]{3,2,1,0:T(8,128)(2,1)}), bf16[16,5,8,128]{3,2,1,0:T(8,128)(2,1)S(1)}, u32[]{:S(2)}, u32[]{:S(2)}) async-start(bf16[16,5,8,128]{3,2,1,0:T(8,128)(2,1)} %ask.1), calls=%async_computation | async-start | bytes 327680 | tf_op jit(solution)/shard_map/all_to_all | solution.py:74
  10.5 0.0 collective-permute-done.other_hbm
  10.5 4.7 %front.1 = (bf16[1024,512]{1,0:T(8,128)(2,1)S(1)}, bf16[1024,512]{1,0:T(8,128)(2,1)S(1)}) custom-call(f32[1,1024]{1,0:T(1,128)} %bitcast.11, bf16[1024,1024]{1,0:T(8,128)(2,1)} %x_ref.1, bf16[1024,1024]{1,0:T(8,128)(2,1)} %collective-permute-done.other_hbm, bf16[1024,1024]{1,0:T(8,128)(2,1)} %w_hbm.2), custom_call_target="tpu_custom_call" | custom-call | flops 2147483648 | bytes 8388608 | tf_op jit(solution)/shard_map/front/pallas_call | solution.py:487
  15.3 3.7 %all-to-all-done.asked_ref = bf16[16,5,8,128]{3,2,1,0:T(8,128)(2,1)S(1)} async-done(((bf16[16,5,8,128]{3,2,1,0:T(8,128)(2,1)}), bf16[16,5,8,128]{3,2,1,0:T(8,128)(2,1)S(1)}, u32[]{:S(2)}, u32[]{:S(2)}) %all-to-all-start) | async-done | bytes 163872 | tf_op jit(solution)/shard_map/all_to_all | solution.py:74
  19.0 0.0 copy-start.6
  19.0 0.0 copy-start.7
  19.0 0.0 copy-start.8
  19.0 2.9 %partial.1 = bf16[16,5,8,128]{3,2,1,0:T(8,128)(2,1)} custom-call(bf16[16,5,8,128]{3,2,1,0:T(8,128)(2,1)S(1)} %all-to-all-done.asked_ref, bf16[1024,512]{1,0:T(8,128)(2,1)S(1)} %get-tuple-element.14.refs_0_, bf16[1024,512]{1,0:T(8,128)(2,1)S(1)} %get-tuple-element.15.refs_1_), custom_call_target="tpu_custom_call" | custom-call | flops 1073741824 | bytes 2097152 | tf_op jit(solution)/shard_map/partial/pallas_call | solution.py:504
  21.9 0.0 copy-start
  21.9 0.0 copy-start.1
  21.9 0.0 copy-start.2
  21.9 0.0 copy-start.3
  21.9 3.8 %all-to-all-start.1 = ((bf16[16,5,8,128]{3,2,1,0:T(8,128)(2,1)}), bf16[16,5,8,128]{3,2,1,0:T(8,128)(2,1)S(1)}, u32[]{:S(2)}, u32[]{:S(2)}) async-start(bf16[16,5,8,128]{3,2,1,0:T(8,128)(2,1)} %partial.1), calls=%async_computation.1 | async-start | bytes 327680 | tf_op jit(solution)/shard_map/all_to_all | solution.py:74
  25.7 0.0 copy-done.6
  25.7 0.0 copy-done.7
  25.7 0.0 copy-done.8
  25.7 3.5 %middle.1 = (bf16[512,1024]{1,0:T(8,128)(2,1)S(1)}, s32[4,1024]{1,0:T(4,128)S(1)}) custom-call(f32[1,1024]{1,0:T(1,128)S(1)} %bitcast.12, s32[32,128]{1,0:T(8,128)S(1)} %bitcast.10, s32[4,1024]{1,0:T(4,128)S(1)} %copy-done.7, bf16[1024,1024]{1,0:T(8,128)(2,1)} %x_ref.1, bf16[1024,512]{1,0:T(8,128)(2,1)} %w_hbm.3), custom_call_target="tpu_custom_call" | custom-call | flops 1073741824 | bytes 8388608 | tf_op jit(solution)/shard_map/middle/pallas_call | solution.py:518
  29.2 0.0 copy-start.9
  29.3 1.0 %copy-done.9 = bf16[512,1024]{1,0:T(8,128)(2,1)} copy-done((bf16[512,1024]{1,0:T(8,128)(2,1)}, bf16[512,1024]{1,0:T(8,128)(2,1)S(1)}, u32[]{:S(2)}) %copy-start.9) | copy-done | bytes 1048600
  30.2 3.8 %all-to-all-done.1.parts_ref = bf16[16,5,8,128]{3,2,1,0:T(8,128)(2,1)S(1)} async-done(((bf16[16,5,8,128]{3,2,1,0:T(8,128)(2,1)}), bf16[16,5,8,128]{3,2,1,0:T(8,128)(2,1)S(1)}, u32[]{:S(2)}, u32[]{:S(2)}) %all-to-all-start.1) | async-done | bytes 163872 | tf_op jit(solution)/shard_map/all_to_all | solution.py:74
  34.0 0.0 copy-start.10
  34.0 0.0 copy-done
  34.0 0.0 copy-done.1
  34.0 0.0 copy-done.2
  34.0 0.0 copy-done.3
  34.0 0.0 copy-start.4
  34.1 0.0 copy-start.5
  34.1 1.5 %combine.1 = (bf16[16,1024]{1,0:T(8,128)(2,1)}, bf16[16,16,512]{2,1,0:T(8,128)(2,1)S(1)}) custom-call(bf16[16,5,8,128]{3,2,1,0:T(8,128)(2,1)S(1)} %all-to-all-done.1.parts_ref, bf16[16,1024]{1,0:T(8,128)(2,1)S(1)} %copy-done.2, f32[1,1024]{1,0:T(1,128)S(1)} %bitcast.9, bf16[512,1024]{1,0:T(8,128)(2,1)S(1)} %copy-done.1, bf16[1024,1024]{1,0:T(8,128)(2,1)S(1)} %copy-done), custom_call_target="tpu_custom_call" | custom-call | flops 50331648 | bytes 3145728 | tf_op jit(solution)/shard_map/combine/pallas_call | solution.py:543
  35.6 12.6 %all_to_all.15 = bf16[16,16,512]{2,1,0:T(8,128)(2,1)S(1)} all-to-all(bf16[16,16,512]{2,1,0:T(8,128)(2,1)S(1)} %get-tuple-element.23), channel_id=1, replica_groups={{0,9,2,11,4,13,6,15,8,1,10,3,12,5,14,7},{16,25,18,27,20,29,22,31,24,17,..., dimensions={0} | all-to-all | bytes 524288 | tf_op jit(solution)/shard_map/all_to_all | solution.py:74
  48.2 0.3 collective-permute-start.1
  48.5 0.0 copy-done.10
  48.5 1.6 %own.1.own_ref = bf16[1024,256]{1,0:T(8,128)(2,1)S(1)} custom-call(bf16[256,512]{1,0:T(8,128)(2,1)S(1)} %bitcast.8, s32[4,1024]{1,0:T(4,128)S(1)} %get-tuple-element.24.node_ref, bf16[512,1024]{1,0:T(8,128)(2,1)S(1)} %copy-done.10), custom_call_target="tpu_custom_call" | custom-call | flops 536870912 | bytes 2097152 | tf_op jit(solution)/shard_map/own/pallas_call | solution.py:560
  50.1 0.0 collective-permute-done.1.pairs_ref
  50.1 0.0 copy-done.4
  50.1 0.0 copy-done.5
  50.1 3.6 %other.1 = bf16[1024,1024]{1,0:T(8,128)(2,1)} custom-call(bf16[256,512]{1,0:T(8,128)(2,1)S(1)} %collective-permute-done.1.pairs_ref, bf16[1024,256]{1,0:T(8,128)(2,1)S(1)} %own.1.own_ref, s32[4,1024]{1,0:T(4,128)S(1)} %get-tuple-element.24.node_ref, bf16[512,1024]{1,0:T(8,128)(2,1)S(1)} %copy-done.10, bf16[1024,1024]{1,0:T(8,128)(2,1)S(1)} %copy-done.4, ...), custom_call_target="tpu_custom_call" | custom-call | flops 2147483648 | bytes 8388608 | tf_op jit(solution)/shard_map/other/pallas_call | solution.py:568
Async XLA Ops:
  0.6 9.9 %collective-permute-start = (bf16[1024,1024]{1,0:T(8,128)(2,1)}, bf16[1024,1024]{1,0:T(8,128)(2,1)}, u32[]{:S(2)}, u32[]{:S(2)}) collective-permute-start(bf16[1024,1024]{1,0:T(8,128)(2,1)} %x_ref.1), channel_id=1, source_target_pairs={{0,1},{1,0},{2,3},{3,2},{4,5},{5,4},{6,7},{7,6},{8,9},{9,8},{10,11... | collective-permute-start | bytes 6291464 | tf_op jit(solution)/shard_map/ppermute | solution.py:464
  3.5 15.5 %all-to-all-start = ((bf16[16,5,8,128]{3,2,1,0:T(8,128)(2,1)}), bf16[16,5,8,128]{3,2,1,0:T(8,128)(2,1)S(1)}, u32[]{:S(2)}, u32[]{:S(2)}) async-start(bf16[16,5,8,128]{3,2,1,0:T(8,128)(2,1)} %ask.1), calls=%async_computation | async-start | bytes 327680 | tf_op jit(solution)/shard_map/all_to_all | solution.py:74
  19.0 6.7 %copy-start.6 = (s32[1,4096]{1,0:T(1,128)S(1)}, s32[1,4096]{1,0:T(1,128)}, u32[]{:S(2)}) copy-start(s32[1,4096]{1,0:T(1,128)} %param.30) | copy-start | bytes 49156
  19.0 6.7 %copy-start.7 = (s32[4,1024]{1,0:T(4,128)S(1)}, s32[4,1024]{1,0:T(4,128)}, u32[]{:S(2)}) copy-start(s32[4,1024]{1,0:T(4,128)} %slot_ref) | copy-start | bytes 49156
  19.0 6.7 %copy-start.8 = (f32[1024]{0:T(1024)S(1)}, f32[1024]{0:T(1024)}, u32[]{:S(2)}) copy-start(f32[1024]{0:T(1024)} %param.18) | copy-start | bytes 12292
  21.9 12.2 %copy-start = (bf16[1024,1024]{1,0:T(8,128)(2,1)S(1)}, bf16[1024,1024]{1,0:T(8,128)(2,1)}, u32[]{:S(2)}) copy-start(bf16[1024,1024]{1,0:T(8,128)(2,1)} %w_kv_ref.1) | copy-start | bytes 6291460
  21.9 12.2 %copy-start.1 = (bf16[512,1024]{1,0:T(8,128)(2,1)S(1)}, bf16[512,1024]{1,0:T(8,128)(2,1)}, u32[]{:S(2)}) copy-start(bf16[512,1024]{1,0:T(8,128)(2,1)} %w_o_ref.1) | copy-start | bytes 3145732
  21.9 12.2 %copy-start.2 = (bf16[16,1024]{1,0:T(8,128)(2,1)S(1)}, bf16[16,1024]{1,0:T(8,128)(2,1)}, u32[]{:S(2)}) copy-start(bf16[16,1024]{1,0:T(8,128)(2,1)} %latent_ref.1) | copy-start | bytes 98308
  21.9 12.2 %copy-start.3 = (f32[1024]{0:T(1024)S(1)}, f32[1024]{0:T(1024)}, u32[]{:S(2)}) copy-start(f32[1024]{0:T(1024)} %param.20) | copy-start | bytes 12292
  21.9 12.1 %all-to-all-start.1 = ((bf16[16,5,8,128]{3,2,1,0:T(8,128)(2,1)}), bf16[16,5,8,128]{3,2,1,0:T(8,128)(2,1)S(1)}, u32[]{:S(2)}, u32[]{:S(2)}) async-start(bf16[16,5,8,128]{3,2,1,0:T(8,128)(2,1)} %partial.1), calls=%async_computation.1 | async-start | bytes 327680 | tf_op jit(solution)/shard_map/all_to_all | solution.py:74
  29.2 1.0 %copy-start.9 = (bf16[512,1024]{1,0:T(8,128)(2,1)}, bf16[512,1024]{1,0:T(8,128)(2,1)S(1)}, u32[]{:S(2)}) copy-start(bf16[512,1024]{1,0:T(8,128)(2,1)S(1)} %get-tuple-element.25.query_ref) | copy-start | bytes 3145732
  34.0 14.4 %copy-start.10 = (bf16[512,1024]{1,0:T(8,128)(2,1)S(1)}, bf16[512,1024]{1,0:T(8,128)(2,1)}, u32[]{:S(2)}) copy-start(bf16[512,1024]{1,0:T(8,128)(2,1)} %copy-done.9) | copy-start | bytes 3145732
  34.0 16.1 %copy-start.4 = (bf16[1024,1024]{1,0:T(8,128)(2,1)S(1)}, bf16[1024,1024]{1,0:T(8,128)(2,1)}, u32[]{:S(2)}) copy-start(bf16[1024,1024]{1,0:T(8,128)(2,1)} %x_ref.1) | copy-start | bytes 6291460
  34.1 16.1 %copy-start.5 = (bf16[512,1024]{1,0:T(8,128)(2,1)S(1)}, bf16[512,1024]{1,0:T(8,128)(2,1)}, u32[]{:S(2)}) copy-start(bf16[512,1024]{1,0:T(8,128)(2,1)} %w_ref.1) | copy-start | bytes 3145732
  48.2 2.0 %collective-permute-start.1 = (bf16[256,512]{1,0:T(8,128)(2,1)S(1)}, bf16[256,512]{1,0:T(8,128)(2,1)S(1)}, u32[]{:S(2)}, u32[]{:S(2)}) collective-permute-start(bf16[256,512]{1,0:T(8,128)(2,1)S(1)} %bitcast.7), channel_id=1, source_target_pairs={{0,1},{1,0},{2,3},{3,2},{4,5},{5,4},{6,7},{7,6},{8,9},{9,8},{10,11... | collective-permute-start | bytes 786440 | tf_op jit(solution)/shard_map/ppermute | solution.py:557

commit v15 on v14

--- a/solution.py
+++ b/solution.py
@@ -285,9 +285,7 @@
                 out_ref[place_of((first + g) * some + w, peers), 2 * blocks] = tile.astype(bf16)
 
 
-def combine_kernel(
-    parts_ref, latent_ref, gain_ref, w_o_ref, w_kv_ref, latent_hbm, out_ref, latent_out_ref, sem
-):
+def combine_kernel(parts_ref, latent_ref, gain_ref, w_o_ref, w_kv_ref, latent_out_ref, out_ref):
     peers = parts_ref.shape[0]
     rows = latent_ref.shape[0]
     width = w_o_ref.shape[0]
@@ -319,14 +317,11 @@
     update = dot(mixed.astype(bf16), w_o_ref[...])
     latent_out = (latent_ref[...].astype(f32) + update).astype(bf16)
     latent_out_ref[...] = latent_out
-    copy = pltpu.make_async_copy(latent_out_ref, latent_hbm, sem)
-    copy.start()
     pairs = dot(normed(latent_out, gain_ref[...]), w_kv_ref[...]).astype(bf16)
     for p in range(peers):
         at = p % 2 * half
         out_ref[p, :, :half] = pairs[:, at : at + half]
         out_ref[p, :, half:] = pairs[:, width + at : width + at + half]
-    copy.wait()
 
 
 def middle_kernel(
@@ -395,8 +390,11 @@
 
 
 def other_kernel(
-    steps, pairs_ref, own_ref, node_ref, query_ref, x_ref, w_ref, out_hbm, out_ref, sems
+    steps, pairs_ref, own_ref, node_ref, query_ref, x_ref, w_ref, latent_ref,
+    out_hbm, latent_hbm, out_ref, sems,
 ):
+    latent_copy = pltpu.make_async_copy(latent_ref, latent_hbm, sems.at[steps])
+    latent_copy.start()
     points, half = own_ref.shape
     block = points // steps
     core = lax.axis_index("dom") & 1
@@ -419,6 +417,7 @@
         mixed = following
     for send in sends:
         send.wait()
+    latent_copy.wait()
 
 
 def in_hbm(array):
@@ -543,12 +542,11 @@
     latent_out, everyone = pl.pallas_call(
         combine_kernel,
         in_specs=[vmem] * 5,
-        out_specs=[hbm, vmem],
+        out_specs=[vmem] * 2,
         out_shape=[
-            pltpu.HBM((rows, depth), bf16),
+            pltpu.VMEM((rows, depth), bf16),
             jax.ShapeDtypeStruct((peers, rows, width), bf16),
         ],
-        scratch_shapes=[pltpu.VMEM((rows, depth), bf16), pltpu.SemaphoreType.DMA],
         compiler_params=params(24),
         cost_estimate=cost(6 * rows * depth * width, 6 * depth * width),
         name="combine",
@@ -565,19 +563,19 @@
         cost_estimate=cost(4 * points * nodes * width, 8 * points * nodes),
         name="own",
     )(own, node_of, queries)
-    grid_out = pl.pallas_call(
+    grid_out, latent_out = pl.pallas_call(
         functools.partial(other_kernel, steps),
-        in_specs=[vmem] * 6,
-        out_specs=hbm,
-        out_shape=pltpu.HBM((points, depth), bf16),
+        in_specs=[vmem] * 7,
+        out_specs=[hbm] * 2,
+        out_shape=[pltpu.HBM((points, depth), bf16), pltpu.HBM((rows, depth), bf16)],
         scratch_shapes=[
             pltpu.VMEM((points, depth), bf16),
-            pltpu.SemaphoreType.DMA((steps,)),
+            pltpu.SemaphoreType.DMA((steps + 1,)),
         ],
         compiler_params=params(48),
         cost_estimate=cost(4 * points * depth * width, 8 * points * depth),
         name="other",
-    )(other, own_mixed, node_of, queries, grid, w_o_dec)
+    )(other, own_mixed, node_of, queries, grid, w_o_dec, in_vmem(latent_out))
     return (latent_out, grid_out)
 
 

time: 54.3 us -> 54 us (level)
  no operation moved by 1% of the time
where the time goes in v15:
time: 54 us; the launch traced here: 53.6 us
  Pallas kernels  19.7 us (36%)
  blocking collectives  12.7 us (24%)
  starting transfers between devices  11.7 us (22%)
  waiting for transfers between devices  7.5 us (14%)
  local copies, waits for them, and re-layouts  1.01 us (2%)
  between operations  0.95 us (2%)
    all_to_all x1, blocking collectives, exchange(): lax.all_to_all(blocks, 'dom', split_axis=0, concat_axis=0, tiled=True, ax...  12.7 us
    all_to_all x2, starting transfers between devices, exchange(): lax.all_to_all(blocks, 'dom', split_axis=0, concat_axis=0, tiled=True, ax...  10.9 us
    all_to_all x2, waiting for transfers between devices, exchange(): lax.all_to_all(blocks, 'dom', split_axis=0, concat_axis=0, tiled=True, ax...  7.5 us
    pallas_call x1, Pallas kernels, on_device(): pl.pallas_call(functools.partial(front_kernel, steps), in_specs=[hbm] * 4...  4.74 us
    pallas_call x1, Pallas kernels, on_device(): pl.pallas_call(functools.partial(other_kernel, steps), in_specs=[vmem] *...  3.61 us
    pallas_call x1, Pallas kernels, on_device(): pl.pallas_call(functools.partial(middle_kernel, steps, peers, rows), in_s...  3.54 us
    pallas_call x1, Pallas kernels, on_device(): pl.pallas_call(functools.partial(partial_kernel, cap, rows, edges), in_sp...  2.86 us
    pallas_call x1, Pallas kernels, on_device(): pl.pallas_call(ask_kernel, in_specs=[hbm] * len(ask_inputs), out_shape=ja...  2.31 us
  transfers between devices with their start and end apart: 4, of which 2 were waited for; matrix products, arithmetic and copies ran while one was open for 0% of the time, Pallas kernels for 23%

profile of v15, /device:TPU:0, one launch (start us, length us, event | category | flops | bytes accessed | tf_op | source)
XLA Modules:
  0.0 53.6 jit_solution(1736207046970792904)
XLA Ops:
  0.6 0.5 collective-permute-start
  1.1 2.3 %ask.1 = bf16[16,5,8,128]{3,2,1,0:T(8,128)(2,1)} custom-call(bf16[1024,512]{1,0:T(8,128)(2,1)} %refs_0_.1, bf16[16,1024]{1,0:T(8,128)(2,1)} %latent_ref.1, f32[1,1024]{1,0:T(1,128)} %bitcast.14, s32[16,32]{1,0:T(8,128)} %bitcast.13, s32[1,16]{1,0:T(1,128)} %bitcast.15, s32[1,512]{1,0:T(1,128)} %refs_5_.1), custom_call_target="tpu_custom_call" | custom-call | flops 16777216 | bytes 1048576 | tf_op jit(solution)/shard_map/ask/pallas_call | solution.py:472
  3.5 7.1 %all-to-all-start = ((bf16[16,5,8,128]{3,2,1,0:T(8,128)(2,1)}), bf16[16,5,8,128]{3,2,1,0:T(8,128)(2,1)S(1)}, u32[]{:S(2)}, u32[]{:S(2)}) async-start(bf16[16,5,8,128]{3,2,1,0:T(8,128)(2,1)} %ask.1), calls=%async_computation | async-start | bytes 327680 | tf_op jit(solution)/shard_map/all_to_all | solution.py:74
  10.5 0.0 collective-permute-done.other_hbm
  10.5 4.7 %front.1 = (bf16[1024,512]{1,0:T(8,128)(2,1)S(1)}, bf16[1024,512]{1,0:T(8,128)(2,1)S(1)}) custom-call(f32[1,1024]{1,0:T(1,128)} %bitcast.11, bf16[1024,1024]{1,0:T(8,128)(2,1)} %x_ref.1, bf16[1024,1024]{1,0:T(8,128)(2,1)} %collective-permute-done.other_hbm, bf16[1024,1024]{1,0:T(8,128)(2,1)} %w_hbm.2), custom_call_target="tpu_custom_call" | custom-call | flops 2147483648 | bytes 8388608 | tf_op jit(solution)/shard_map/front/pallas_call | solution.py:486
  15.3 3.7 %all-to-all-done.asked_ref = bf16[16,5,8,128]{3,2,1,0:T(8,128)(2,1)S(1)} async-done(((bf16[16,5,8,128]{3,2,1,0:T(8,128)(2,1)}), bf16[16,5,8,128]{3,2,1,0:T(8,128)(2,1)S(1)}, u32[]{:S(2)}, u32[]{:S(2)}) %all-to-all-start) | async-done | bytes 163872 | tf_op jit(solution)/shard_map/all_to_all | solution.py:74
  19.0 0.0 copy-start.6
  19.0 0.0 copy-start.7
  19.0 0.0 copy-start.8
  19.0 2.9 %partial.1 = bf16[16,5,8,128]{3,2,1,0:T(8,128)(2,1)} custom-call(bf16[16,5,8,128]{3,2,1,0:T(8,128)(2,1)S(1)} %all-to-all-done.asked_ref, bf16[1024,512]{1,0:T(8,128)(2,1)S(1)} %get-tuple-element.16.refs_0_, bf16[1024,512]{1,0:T(8,128)(2,1)S(1)} %get-tuple-element.17.refs_1_), custom_call_target="tpu_custom_call" | custom-call | flops 1073741824 | bytes 2097152 | tf_op jit(solution)/shard_map/partial/pallas_call | solution.py:503
  21.9 0.0 copy-start
  21.9 0.0 copy-start.1
  21.9 0.0 copy-start.2
  21.9 0.0 copy-start.3
  21.9 3.8 %all-to-all-start.1 = ((bf16[16,5,8,128]{3,2,1,0:T(8,128)(2,1)}), bf16[16,5,8,128]{3,2,1,0:T(8,128)(2,1)S(1)}, u32[]{:S(2)}, u32[]{:S(2)}) async-start(bf16[16,5,8,128]{3,2,1,0:T(8,128)(2,1)} %partial.1), calls=%async_computation.1 | async-start | bytes 327680 | tf_op jit(solution)/shard_map/all_to_all | solution.py:74
  25.7 0.0 copy-done.6
  25.7 0.0 copy-done.7
  25.7 0.0 copy-done.8
  25.7 3.5 %middle.1 = (bf16[512,1024]{1,0:T(8,128)(2,1)S(1)}, s32[4,1024]{1,0:T(4,128)S(1)}) custom-call(f32[1,1024]{1,0:T(1,128)S(1)} %bitcast.12, s32[32,128]{1,0:T(8,128)S(1)} %bitcast.10, s32[4,1024]{1,0:T(4,128)S(1)} %copy-done.7, bf16[1024,1024]{1,0:T(8,128)(2,1)} %x_ref.1, bf16[1024,512]{1,0:T(8,128)(2,1)} %w_hbm.3), custom_call_target="tpu_custom_call" | custom-call | flops 1073741824 | bytes 8388608 | tf_op jit(solution)/shard_map/middle/pallas_call | solution.py:517
  29.3 0.0 copy-start.9
  29.3 1.0 %copy-done.9 = bf16[512,1024]{1,0:T(8,128)(2,1)} copy-done((bf16[512,1024]{1,0:T(8,128)(2,1)}, bf16[512,1024]{1,0:T(8,128)(2,1)S(1)}, u32[]{:S(2)}) %copy-start.9) | copy-done | bytes 1048600
  30.2 3.8 %all-to-all-done.1.parts_ref = bf16[16,5,8,128]{3,2,1,0:T(8,128)(2,1)S(1)} async-done(((bf16[16,5,8,128]{3,2,1,0:T(8,128)(2,1)}), bf16[16,5,8,128]{3,2,1,0:T(8,128)(2,1)S(1)}, u32[]{:S(2)}, u32[]{:S(2)}) %all-to-all-start.1) | async-done | bytes 163872 | tf_op jit(solution)/shard_map/all_to_all | solution.py:74
  34.0 0.0 copy-start.10
  34.0 0.0 copy-done
  34.0 0.0 copy-done.1
  34.0 0.0 copy-done.2
  34.0 0.0 copy-done.3
  34.0 0.0 copy-start.4
  34.1 0.0 copy-start.5
  34.1 1.0 %combine.1 = (bf16[16,1024]{1,0:T(8,128)(2,1)S(1)}, bf16[16,16,512]{2,1,0:T(8,128)(2,1)S(1)}) custom-call(bf16[16,5,8,128]{3,2,1,0:T(8,128)(2,1)S(1)} %all-to-all-done.1.parts_ref, bf16[16,1024]{1,0:T(8,128)(2,1)S(1)} %copy-done.2, f32[1,1024]{1,0:T(1,128)S(1)} %bitcast.9, bf16[512,1024]{1,0:T(8,128)(2,1)S(1)} %copy-done.1, bf16[1024,1024]{1,0:T(8,128)(2,1)S(1)} %copy-done), custom_call_target="tpu_custom_call" | custom-call | flops 50331648 | bytes 3145728 | tf_op jit(solution)/shard_map/combine/pallas_call | solution.py:542
  35.1 12.7 %all_to_all.15 = bf16[16,16,512]{2,1,0:T(8,128)(2,1)S(1)} all-to-all(bf16[16,16,512]{2,1,0:T(8,128)(2,1)S(1)} %get-tuple-element.24), channel_id=1, replica_groups={{0,9,2,11,4,13,6,15,8,1,10,3,12,5,14,7},{16,25,18,27,20,29,22,31,24,17,..., dimensions={0} | all-to-all | bytes 524288 | tf_op jit(solution)/shard_map/all_to_all | solution.py:74
  47.8 0.3 collective-permute-start.1
  48.1 0.0 copy-done.10
  48.1 1.6 %own.1.own_ref = bf16[1024,256]{1,0:T(8,128)(2,1)S(1)} custom-call(bf16[256,512]{1,0:T(8,128)(2,1)S(1)} %bitcast.8, s32[4,1024]{1,0:T(4,128)S(1)} %get-tuple-element.25.node_ref, bf16[512,1024]{1,0:T(8,128)(2,1)S(1)} %copy-done.10), custom_call_target="tpu_custom_call" | custom-call | flops 536870912 | bytes 2097152 | tf_op jit(solution)/shard_map/own/pallas_call | solution.py:558
  49.8 0.0 collective-permute-done.1.pairs_ref
  49.8 0.0 copy-done.4
  49.8 0.0 copy-done.5
  49.8 3.6 %other.1 = (bf16[1024,1024]{1,0:T(8,128)(2,1)}, bf16[16,1024]{1,0:T(8,128)(2,1)}) custom-call(bf16[256,512]{1,0:T(8,128)(2,1)S(1)} %collective-permute-done.1.pairs_ref, bf16[1024,256]{1,0:T(8,128)(2,1)S(1)} %own.1.own_ref, s32[4,1024]{1,0:T(4,128)S(1)} %get-tuple-element.25.node_ref, bf16[512,1024]{1,0:T(8,128)(2,1)S(1)} %copy-done.10, ...), custom_call_target="tpu_custom_call" | custom-call | flops 2147483648 | bytes 8388608 | tf_op jit(solution)/shard_map/other/pallas_call | solution.py:566
Async XLA Ops:
  0.6 9.9 %collective-permute-start = (bf16[1024,1024]{1,0:T(8,128)(2,1)}, bf16[1024,1024]{1,0:T(8,128)(2,1)}, u32[]{:S(2)}, u32[]{:S(2)}) collective-permute-start(bf16[1024,1024]{1,0:T(8,128)(2,1)} %x_ref.1), channel_id=1, source_target_pairs={{0,1},{1,0},{2,3},{3,2},{4,5},{5,4},{6,7},{7,6},{8,9},{9,8},{10,11... | collective-permute-start | bytes 6291464 | tf_op jit(solution)/shard_map/ppermute | solution.py:463
  3.5 15.5 %all-to-all-start = ((bf16[16,5,8,128]{3,2,1,0:T(8,128)(2,1)}), bf16[16,5,8,128]{3,2,1,0:T(8,128)(2,1)S(1)}, u32[]{:S(2)}, u32[]{:S(2)}) async-start(bf16[16,5,8,128]{3,2,1,0:T(8,128)(2,1)} %ask.1), calls=%async_computation | async-start | bytes 327680 | tf_op jit(solution)/shard_map/all_to_all | solution.py:74
  19.0 6.7 %copy-start.6 = (s32[1,4096]{1,0:T(1,128)S(1)}, s32[1,4096]{1,0:T(1,128)}, u32[]{:S(2)}) copy-start(s32[1,4096]{1,0:T(1,128)} %param.30) | copy-start | bytes 49156
  19.0 6.7 %copy-start.7 = (s32[4,1024]{1,0:T(4,128)S(1)}, s32[4,1024]{1,0:T(4,128)}, u32[]{:S(2)}) copy-start(s32[4,1024]{1,0:T(4,128)} %slot_ref) | copy-start | bytes 49156
  19.0 6.7 %copy-start.8 = (f32[1024]{0:T(1024)S(1)}, f32[1024]{0:T(1024)}, u32[]{:S(2)}) copy-start(f32[1024]{0:T(1024)} %param.18) | copy-start | bytes 12292
  21.9 12.2 %copy-start = (bf16[1024,1024]{1,0:T(8,128)(2,1)S(1)}, bf16[1024,1024]{1,0:T(8,128)(2,1)}, u32[]{:S(2)}) copy-start(bf16[1024,1024]{1,0:T(8,128)(2,1)} %w_kv_ref.1) | copy-start | bytes 6291460
  21.9 12.2 %copy-start.1 = (bf16[512,1024]{1,0:T(8,128)(2,1)S(1)}, bf16[512,1024]{1,0:T(8,128)(2,1)}, u32[]{:S(2)}) copy-start(bf16[512,1024]{1,0:T(8,128)(2,1)} %w_o_ref.1) | copy-start | bytes 3145732
  21.9 12.2 %copy-start.2 = (bf16[16,1024]{1,0:T(8,128)(2,1)S(1)}, bf16[16,1024]{1,0:T(8,128)(2,1)}, u32[]{:S(2)}) copy-start(bf16[16,1024]{1,0:T(8,128)(2,1)} %latent_ref.1) | copy-start | bytes 98308
  21.9 12.2 %copy-start.3 = (f32[1024]{0:T(1024)S(1)}, f32[1024]{0:T(1024)}, u32[]{:S(2)}) copy-start(f32[1024]{0:T(1024)} %param.20) | copy-start | bytes 12292
  21.9 12.1 %all-to-all-start.1 = ((bf16[16,5,8,128]{3,2,1,0:T(8,128)(2,1)}), bf16[16,5,8,128]{3,2,1,0:T(8,128)(2,1)S(1)}, u32[]{:S(2)}, u32[]{:S(2)}) async-start(bf16[16,5,8,128]{3,2,1,0:T(8,128)(2,1)} %partial.1), calls=%async_computation.1 | async-start | bytes 327680 | tf_op jit(solution)/shard_map/all_to_all | solution.py:74
  29.3 1.0 %copy-start.9 = (bf16[512,1024]{1,0:T(8,128)(2,1)}, bf16[512,1024]{1,0:T(8,128)(2,1)S(1)}, u32[]{:S(2)}) copy-start(bf16[512,1024]{1,0:T(8,128)(2,1)S(1)} %get-tuple-element.26.query_ref) | copy-start | bytes 3145732
  34.0 14.1 %copy-start.10 = (bf16[512,1024]{1,0:T(8,128)(2,1)S(1)}, bf16[512,1024]{1,0:T(8,128)(2,1)}, u32[]{:S(2)}) copy-start(bf16[512,1024]{1,0:T(8,128)(2,1)} %copy-done.9) | copy-start | bytes 3145732
  34.0 15.7 %copy-start.4 = (bf16[1024,1024]{1,0:T(8,128)(2,1)S(1)}, bf16[1024,1024]{1,0:T(8,128)(2,1)}, u32[]{:S(2)}) copy-start(bf16[1024,1024]{1,0:T(8,128)(2,1)} %x_ref.1) | copy-start | bytes 6291460
  34.1 15.7 %copy-start.5 = (bf16[512,1024]{1,0:T(8,128)(2,1)S(1)}, bf16[512,1024]{1,0:T(8,128)(2,1)}, u32[]{:S(2)}) copy-start(bf16[512,1024]{1,0:T(8,128)(2,1)} %w_ref.1) | copy-start | bytes 3145732
  47.8 2.0 %collective-permute-start.1 = (bf16[256,512]{1,0:T(8,128)(2,1)S(1)}, bf16[256,512]{1,0:T(8,128)(2,1)S(1)}, u32[]{:S(2)}, u32[]{:S(2)}) collective-permute-start(bf16[256,512]{1,0:T(8,128)(2,1)S(1)} %bitcast.7), channel_id=1, source_target_pairs={{0,1},{1,0},{2,3},{3,2},{4,5},{5,4},{6,7},{7,6},{8,9},{9,8},{10,11... | collective-permute-start | bytes 786440 | tf_op jit(solution)/shard_map/ppermute | solution.py:555

commit v16 on v15

--- a/solution.py
+++ b/solution.py
@@ -472,10 +472,11 @@
     asked = pl.pallas_call(
         ask_kernel,
         in_specs=[hbm] * len(ask_inputs),
-        out_shape=jax.ShapeDtypeStruct(sent, bf16),
+        out_specs=vmem,
+        out_shape=pltpu.VMEM(sent, bf16),
         scratch_shapes=[pltpu.VMEM(one.shape, one.dtype) for one in ask_inputs]
         + [pltpu.SemaphoreType.DMA((len(ask_inputs),))],
-        compiler_params=params(63),
+        compiler_params=params(62),
         cost_estimate=cost(2 * rows * depth * width, 2 * depth * width),
         name="ask",
     )(*map(in_hbm, ask_inputs))
@@ -503,7 +504,8 @@
     parts = pl.pallas_call(
         functools.partial(partial_kernel, cap, rows, edges),
         in_specs=[vmem] * 3,
-        out_shape=jax.ShapeDtypeStruct(sent, bf16),
+        out_specs=vmem,
+        out_shape=pltpu.VMEM(sent, bf16),
         compiler_params=params(40),
         cost_estimate=cost(4 * entries * points * width, 4 * points * width),
         name="partial",

time: 54 us -> 54 us (level)
  no operation moved by 1% of the time
where the time goes in v16:
time: 54 us; the launch traced here: 53.6 us
  Pallas kernels  19.7 us (36%)
  blocking collectives  12.7 us (24%)
  starting transfers between devices  11.7 us (22%)
  waiting for transfers between devices  7.5 us (14%)
  local copies, waits for them, and re-layouts  1.01 us (2%)
  between operations  0.95 us (2%)
    all_to_all x1, blocking collectives, exchange(): lax.all_to_all(blocks, 'dom', split_axis=0, concat_axis=0, tiled=True, ax...  12.7 us
    all_to_all x2, starting transfers between devices, exchange(): lax.all_to_all(blocks, 'dom', split_axis=0, concat_axis=0, tiled=True, ax...  10.9 us
    all_to_all x2, waiting for transfers between devices, exchange(): lax.all_to_all(blocks, 'dom', split_axis=0, concat_axis=0, tiled=True, ax...  7.5 us
    pallas_call x1, Pallas kernels, on_device(): pl.pallas_call(functools.partial(front_kernel, steps), in_specs=[hbm] * 4...  4.74 us
    pallas_call x1, Pallas kernels, on_device(): pl.pallas_call(functools.partial(other_kernel, steps), in_specs=[vmem] *...  3.61 us
    pallas_call x1, Pallas kernels, on_device(): pl.pallas_call(functools.partial(middle_kernel, steps, peers, rows), in_s...  3.54 us
    pallas_call x1, Pallas kernels, on_device(): pl.pallas_call(functools.partial(partial_kernel, cap, rows, edges), in_sp...  2.86 us
    pallas_call x1, Pallas kernels, on_device(): pl.pallas_call(ask_kernel, in_specs=[hbm] * len(ask_inputs), out_specs=vm...  2.31 us
  transfers between devices with their start and end apart: 4, of which 2 were waited for; matrix products, arithmetic and copies ran while one was open for 0% of the time, Pallas kernels for 23%

profile of v16, /device:TPU:0, one launch (start us, length us, event | category | flops | bytes accessed | tf_op | source)
XLA Modules:
  0.0 53.6 jit_solution(7112010934833521613)
XLA Ops:
  0.6 0.5 collective-permute-start
  1.1 2.3 %ask.1 = bf16[16,5,8,128]{3,2,1,0:T(8,128)(2,1)} custom-call(bf16[1024,512]{1,0:T(8,128)(2,1)} %refs_0_.1, bf16[16,1024]{1,0:T(8,128)(2,1)} %latent_ref.1, f32[1,1024]{1,0:T(1,128)} %bitcast.14, s32[16,32]{1,0:T(8,128)} %bitcast.13, s32[1,16]{1,0:T(1,128)} %bitcast.15, s32[1,512]{1,0:T(1,128)} %refs_5_.1), custom_call_target="tpu_custom_call" | custom-call | flops 16777216 | bytes 1048576 | tf_op jit(solution)/shard_map/ask/pallas_call | solution.py:472
  3.5 7.1 %all-to-all-start = ((bf16[16,5,8,128]{3,2,1,0:T(8,128)(2,1)}), bf16[16,5,8,128]{3,2,1,0:T(8,128)(2,1)S(1)}, u32[]{:S(2)}, u32[]{:S(2)}) async-start(bf16[16,5,8,128]{3,2,1,0:T(8,128)(2,1)} %ask.1), calls=%async_computation | async-start | bytes 327680 | tf_op jit(solution)/shard_map/all_to_all | solution.py:74
  10.5 0.0 collective-permute-done.other_hbm
  10.5 4.7 %front.1 = (bf16[1024,512]{1,0:T(8,128)(2,1)S(1)}, bf16[1024,512]{1,0:T(8,128)(2,1)S(1)}) custom-call(f32[1,1024]{1,0:T(1,128)} %bitcast.11, bf16[1024,1024]{1,0:T(8,128)(2,1)} %x_ref.1, bf16[1024,1024]{1,0:T(8,128)(2,1)} %collective-permute-done.other_hbm, bf16[1024,1024]{1,0:T(8,128)(2,1)} %w_hbm.2), custom_call_target="tpu_custom_call" | custom-call | flops 2147483648 | bytes 8388608 | tf_op jit(solution)/shard_map/front/pallas_call | solution.py:487
  15.3 3.7 %all-to-all-done.asked_ref = bf16[16,5,8,128]{3,2,1,0:T(8,128)(2,1)S(1)} async-done(((bf16[16,5,8,128]{3,2,1,0:T(8,128)(2,1)}), bf16[16,5,8,128]{3,2,1,0:T(8,128)(2,1)S(1)}, u32[]{:S(2)}, u32[]{:S(2)}) %all-to-all-start) | async-done | bytes 163872 | tf_op jit(solution)/shard_map/all_to_all | solution.py:74
  19.0 0.0 copy-start.6
  19.0 0.0 copy-start.7
  19.0 0.0 copy-start.8
  19.0 2.9 %partial.1 = bf16[16,5,8,128]{3,2,1,0:T(8,128)(2,1)} custom-call(bf16[16,5,8,128]{3,2,1,0:T(8,128)(2,1)S(1)} %all-to-all-done.asked_ref, bf16[1024,512]{1,0:T(8,128)(2,1)S(1)} %get-tuple-element.16.refs_0_, bf16[1024,512]{1,0:T(8,128)(2,1)S(1)} %get-tuple-element.17.refs_1_), custom_call_target="tpu_custom_call" | custom-call | flops 1073741824 | bytes 2097152 | tf_op jit(solution)/shard_map/partial/pallas_call | solution.py:504
  21.9 0.0 copy-start
  21.9 0.0 copy-start.1
  21.9 0.0 copy-start.2
  21.9 0.0 copy-start.3
  21.9 3.8 %all-to-all-start.1 = ((bf16[16,5,8,128]{3,2,1,0:T(8,128)(2,1)}), bf16[16,5,8,128]{3,2,1,0:T(8,128)(2,1)S(1)}, u32[]{:S(2)}, u32[]{:S(2)}) async-start(bf16[16,5,8,128]{3,2,1,0:T(8,128)(2,1)} %partial.1), calls=%async_computation.1 | async-start | bytes 327680 | tf_op jit(solution)/shard_map/all_to_all | solution.py:74
  25.7 0.0 copy-done.6
  25.7 0.0 copy-done.7
  25.7 0.0 copy-done.8
  25.7 3.5 %middle.1 = (bf16[512,1024]{1,0:T(8,128)(2,1)S(1)}, s32[4,1024]{1,0:T(4,128)S(1)}) custom-call(f32[1,1024]{1,0:T(1,128)S(1)} %bitcast.12, s32[32,128]{1,0:T(8,128)S(1)} %bitcast.10, s32[4,1024]{1,0:T(4,128)S(1)} %copy-done.7, bf16[1024,1024]{1,0:T(8,128)(2,1)} %x_ref.1, bf16[1024,512]{1,0:T(8,128)(2,1)} %w_hbm.3), custom_call_target="tpu_custom_call" | custom-call | flops 1073741824 | bytes 8388608 | tf_op jit(solution)/shard_map/middle/pallas_call | solution.py:519
  29.3 0.0 copy-start.9
  29.3 1.0 %copy-done.9 = bf16[512,1024]{1,0:T(8,128)(2,1)} copy-done((bf16[512,1024]{1,0:T(8,128)(2,1)}, bf16[512,1024]{1,0:T(8,128)(2,1)S(1)}, u32[]{:S(2)}) %copy-start.9) | copy-done | bytes 1048600
  30.2 3.8 %all-to-all-done.1.parts_ref = bf16[16,5,8,128]{3,2,1,0:T(8,128)(2,1)S(1)} async-done(((bf16[16,5,8,128]{3,2,1,0:T(8,128)(2,1)}), bf16[16,5,8,128]{3,2,1,0:T(8,128)(2,1)S(1)}, u32[]{:S(2)}, u32[]{:S(2)}) %all-to-all-start.1) | async-done | bytes 163872 | tf_op jit(solution)/shard_map/all_to_all | solution.py:74
  34.0 0.0 copy-start.10
  34.0 0.0 copy-done
  34.0 0.0 copy-done.1
  34.0 0.0 copy-done.2
  34.0 0.0 copy-done.3
  34.0 0.0 copy-start.4
  34.1 0.0 copy-start.5
  34.1 1.0 %combine.1 = (bf16[16,1024]{1,0:T(8,128)(2,1)S(1)}, bf16[16,16,512]{2,1,0:T(8,128)(2,1)S(1)}) custom-call(bf16[16,5,8,128]{3,2,1,0:T(8,128)(2,1)S(1)} %all-to-all-done.1.parts_ref, bf16[16,1024]{1,0:T(8,128)(2,1)S(1)} %copy-done.2, f32[1,1024]{1,0:T(1,128)S(1)} %bitcast.9, bf16[512,1024]{1,0:T(8,128)(2,1)S(1)} %copy-done.1, bf16[1024,1024]{1,0:T(8,128)(2,1)S(1)} %copy-done), custom_call_target="tpu_custom_call" | custom-call | flops 50331648 | bytes 3145728 | tf_op jit(solution)/shard_map/combine/pallas_call | solution.py:544
  35.1 12.7 %all_to_all.15 = bf16[16,16,512]{2,1,0:T(8,128)(2,1)S(1)} all-to-all(bf16[16,16,512]{2,1,0:T(8,128)(2,1)S(1)} %get-tuple-element.24), channel_id=1, replica_groups={{0,9,2,11,4,13,6,15,8,1,10,3,12,5,14,7},{16,25,18,27,20,29,22,31,24,17,..., dimensions={0} | all-to-all | bytes 524288 | tf_op jit(solution)/shard_map/all_to_all | solution.py:74
  47.8 0.3 collective-permute-start.1
  48.1 0.0 copy-done.10
  48.1 1.6 %own.1.own_ref = bf16[1024,256]{1,0:T(8,128)(2,1)S(1)} custom-call(bf16[256,512]{1,0:T(8,128)(2,1)S(1)} %bitcast.8, s32[4,1024]{1,0:T(4,128)S(1)} %get-tuple-element.25.node_ref, bf16[512,1024]{1,0:T(8,128)(2,1)S(1)} %copy-done.10), custom_call_target="tpu_custom_call" | custom-call | flops 536870912 | bytes 2097152 | tf_op jit(solution)/shard_map/own/pallas_call | solution.py:560
  49.8 0.0 collective-permute-done.1.pairs_ref
  49.8 0.0 copy-done.4
  49.8 0.0 copy-done.5
  49.8 3.6 %other.1 = (bf16[1024,1024]{1,0:T(8,128)(2,1)}, bf16[16,1024]{1,0:T(8,128)(2,1)}) custom-call(bf16[256,512]{1,0:T(8,128)(2,1)S(1)} %collective-permute-done.1.pairs_ref, bf16[1024,256]{1,0:T(8,128)(2,1)S(1)} %own.1.own_ref, s32[4,1024]{1,0:T(4,128)S(1)} %get-tuple-element.25.node_ref, bf16[512,1024]{1,0:T(8,128)(2,1)S(1)} %copy-done.10, ...), custom_call_target="tpu_custom_call" | custom-call | flops 2147483648 | bytes 8388608 | tf_op jit(solution)/shard_map/other/pallas_call | solution.py:568
Async XLA Ops:
  0.6 9.9 %collective-permute-start = (bf16[1024,1024]{1,0:T(8,128)(2,1)}, bf16[1024,1024]{1,0:T(8,128)(2,1)}, u32[]{:S(2)}, u32[]{:S(2)}) collective-permute-start(bf16[1024,1024]{1,0:T(8,128)(2,1)} %x_ref.1), channel_id=1, source_target_pairs={{0,1},{1,0},{2,3},{3,2},{4,5},{5,4},{6,7},{7,6},{8,9},{9,8},{10,11... | collective-permute-start | bytes 6291464 | tf_op jit(solution)/shard_map/ppermute | solution.py:463
  3.5 15.5 %all-to-all-start = ((bf16[16,5,8,128]{3,2,1,0:T(8,128)(2,1)}), bf16[16,5,8,128]{3,2,1,0:T(8,128)(2,1)S(1)}, u32[]{:S(2)}, u32[]{:S(2)}) async-start(bf16[16,5,8,128]{3,2,1,0:T(8,128)(2,1)} %ask.1), calls=%async_computation | async-start | bytes 327680 | tf_op jit(solution)/shard_map/all_to_all | solution.py:74
  19.0 6.7 %copy-start.6 = (s32[1,4096]{1,0:T(1,128)S(1)}, s32[1,4096]{1,0:T(1,128)}, u32[]{:S(2)}) copy-start(s32[1,4096]{1,0:T(1,128)} %param.30) | copy-start | bytes 49156
  19.0 6.7 %copy-start.7 = (s32[4,1024]{1,0:T(4,128)S(1)}, s32[4,1024]{1,0:T(4,128)}, u32[]{:S(2)}) copy-start(s32[4,1024]{1,0:T(4,128)} %slot_ref) | copy-start | bytes 49156
  19.0 6.7 %copy-start.8 = (f32[1024]{0:T(1024)S(1)}, f32[1024]{0:T(1024)}, u32[]{:S(2)}) copy-start(f32[1024]{0:T(1024)} %param.18) | copy-start | bytes 12292
  21.9 12.2 %copy-start = (bf16[1024,1024]{1,0:T(8,128)(2,1)S(1)}, bf16[1024,1024]{1,0:T(8,128)(2,1)}, u32[]{:S(2)}) copy-start(bf16[1024,1024]{1,0:T(8,128)(2,1)} %w_kv_ref.1) | copy-start | bytes 6291460
  21.9 12.2 %copy-start.1 = (bf16[512,1024]{1,0:T(8,128)(2,1)S(1)}, bf16[512,1024]{1,0:T(8,128)(2,1)}, u32[]{:S(2)}) copy-start(bf16[512,1024]{1,0:T(8,128)(2,1)} %w_o_ref.1) | copy-start | bytes 3145732
  21.9 12.2 %copy-start.2 = (bf16[16,1024]{1,0:T(8,128)(2,1)S(1)}, bf16[16,1024]{1,0:T(8,128)(2,1)}, u32[]{:S(2)}) copy-start(bf16[16,1024]{1,0:T(8,128)(2,1)} %latent_ref.1) | copy-start | bytes 98308
  21.9 12.2 %copy-start.3 = (f32[1024]{0:T(1024)S(1)}, f32[1024]{0:T(1024)}, u32[]{:S(2)}) copy-start(f32[1024]{0:T(1024)} %param.20) | copy-start | bytes 12292
  21.9 12.1 %all-to-all-start.1 = ((bf16[16,5,8,128]{3,2,1,0:T(8,128)(2,1)}), bf16[16,5,8,128]{3,2,1,0:T(8,128)(2,1)S(1)}, u32[]{:S(2)}, u32[]{:S(2)}) async-start(bf16[16,5,8,128]{3,2,1,0:T(8,128)(2,1)} %partial.1), calls=%async_computation.1 | async-start | bytes 327680 | tf_op jit(solution)/shard_map/all_to_all | solution.py:74
  29.3 1.0 %copy-start.9 = (bf16[512,1024]{1,0:T(8,128)(2,1)}, bf16[512,1024]{1,0:T(8,128)(2,1)S(1)}, u32[]{:S(2)}) copy-start(bf16[512,1024]{1,0:T(8,128)(2,1)S(1)} %get-tuple-element.26.query_ref) | copy-start | bytes 3145732
  34.0 14.1 %copy-start.10 = (bf16[512,1024]{1,0:T(8,128)(2,1)S(1)}, bf16[512,1024]{1,0:T(8,128)(2,1)}, u32[]{:S(2)}) copy-start(bf16[512,1024]{1,0:T(8,128)(2,1)} %copy-done.9) | copy-start | bytes 3145732
  34.0 15.7 %copy-start.4 = (bf16[1024,1024]{1,0:T(8,128)(2,1)S(1)}, bf16[1024,1024]{1,0:T(8,128)(2,1)}, u32[]{:S(2)}) copy-start(bf16[1024,1024]{1,0:T(8,128)(2,1)} %x_ref.1) | copy-start | bytes 6291460
  34.1 15.7 %copy-start.5 = (bf16[512,1024]{1,0:T(8,128)(2,1)S(1)}, bf16[512,1024]{1,0:T(8,128)(2,1)}, u32[]{:S(2)}) copy-start(bf16[512,1024]{1,0:T(8,128)(2,1)} %w_ref.1) | copy-start | bytes 3145732
  47.8 2.0 %collective-permute-start.1 = (bf16[256,512]{1,0:T(8,128)(2,1)S(1)}, bf16[256,512]{1,0:T(8,128)(2,1)S(1)}, u32[]{:S(2)}, u32[]{:S(2)}) collective-permute-start(bf16[256,512]{1,0:T(8,128)(2,1)S(1)} %bitcast.7), channel_id=1, source_target_pairs={{0,1},{1,0},{2,3},{3,2},{4,5},{5,4},{6,7},{7,6},{8,9},{9,8},{10,11... | collective-permute-start | bytes 786440 | tf_op jit(solution)/shard_map/ppermute | solution.py:557

commit v17 on v16

--- a/solution.py
+++ b/solution.py
@@ -60,6 +60,15 @@
     return copies
 
 
+def split_copy(source, target, sems, count=4):
+    rows = target.shape[0] // count
+    parts = [pl.ds(i * rows, rows) for i in range(count)]
+    return [
+        pltpu.make_async_copy(source.at[part], target.at[part], sems.at[i])
+        for i, part in enumerate(parts)
+    ]
+
+
 def cost(flops, read, exps=0):
     return pl.CostEstimate(flops=int(flops), bytes_accessed=int(read), transcendentals=int(exps))
 
@@ -82,10 +91,11 @@
 
 def ask_kernel(*refs):
     sources, out_ref, held, sems = refs[:6], refs[6], refs[7:13], refs[13]
+    weights = started(*split_copy(sources[0], held[0], sems.at[pl.ds(0, 4)]))
     copies = started(
         *[
-            pltpu.make_async_copy(source, ref, sems.at[i])
-            for i, (source, ref) in enumerate(zip(sources, held))
+            pltpu.make_async_copy(source, ref, sems.at[4 + i])
+            for i, (source, ref) in enumerate(zip(sources[1:], held[1:]))
         ]
     )
     w_ref, latent_ref, gain_ref, slot_ref, count_ref, need_ref = held
@@ -96,7 +106,7 @@
     peers = out_ref.shape[0]
     both = 2 * entries // peers
     tall = rows // 2
-    for copy in copies[1:]:
+    for copy in copies:
         copy.wait()
     rows_normed = normed(latent_ref[...], gain_ref[...])
     live = iota((edges, rows), 0) < count_ref[...]
@@ -118,7 +128,8 @@
         high = jnp.floor(piece * (1.0 / 256.0))
         piece = jnp.where(row == 0, piece - high * 256.0, jnp.where(row == 1, high, 0.0))
         tiles.append((tile + jnp.where(in_list, piece, 0.0)).astype(bf16))
-    copies[0].wait()
+    for copy in weights:
+        copy.wait()
     queries = dot(rows_normed, w_ref[...])
     blocks = width // 2 // LANES
     slabs = [
@@ -138,26 +149,22 @@
     block = points // steps
     half = own_out_ref.shape[1] // 2
     core = lax.axis_index("dom") & 1
-    copies = started(
-        pltpu.make_async_copy(gain_hbm, gain_ref, sems.at[0]),
-        *[
-            pltpu.make_async_copy(
-                w_hbm.at[:, pl.ds(pl.multiple_of((core + 2 * i) * half, half), half)],
-                w_ref.at[:, pl.ds(i * half, half)],
-                sems.at[1 + i],
-            )
-            for i in range(2)
-        ],
-        pltpu.make_async_copy(own_hbm, own_ref, sems.at[3]),
-        pltpu.make_async_copy(other_hbm, other_ref, sems.at[4]),
-    )
+    first = [pltpu.make_async_copy(gain_hbm, gain_ref, sems.at[0])]
+    for i in range(2):
+        source = w_hbm.at[:, pl.ds(pl.multiple_of((core + 2 * i) * half, half), half)]
+        target = w_ref.at[:, pl.ds(i * half, half)]
+        first += split_copy(source, target, sems.at[pl.ds(1 + 4 * i, 4)])
+    first += split_copy(own_hbm, own_ref, sems.at[pl.ds(9, 4)])
+    second = split_copy(other_hbm, other_ref, sems.at[pl.ds(13, 4)])
+    started(*first, *second)
     parts = [pl.ds(i * block, block) for i in range(steps)]
-    for copy in copies[:3]:
-        copy.wait()
-    gain = gain_ref[...]
-    sides = ((own_ref, own_out_ref), (other_ref, other_out_ref))
-    for copy, (rows_ref, out_ref) in zip(copies[3:], sides):
-        copy.wait()
+    for copies, rows_ref, out_ref in (
+        (first, own_ref, own_out_ref),
+        (second, other_ref, other_out_ref),
+    ):
+        for copy in copies:
+            copy.wait()
+        gain = gain_ref[...]
         for part in parts:
             out_ref[part, :] = dot(normed(rows_ref[part, :], gain), w_ref[...]).astype(bf16)
 
@@ -329,8 +336,8 @@
     x_ref, w_ref, sems,
 ):
     copies = started(
-        pltpu.make_async_copy(w_hbm, w_ref, sems.at[0]),
-        pltpu.make_async_copy(x_hbm, x_ref, sems.at[1]),
+        *split_copy(w_hbm, w_ref, sems.at[pl.ds(0, 4)]),
+        *split_copy(x_hbm, x_ref, sems.at[pl.ds(4, 4)]),
     )
     points = x_ref.shape[0]
     block = points // steps
@@ -475,7 +482,7 @@
         out_specs=vmem,
         out_shape=pltpu.VMEM(sent, bf16),
         scratch_shapes=[pltpu.VMEM(one.shape, one.dtype) for one in ask_inputs]
-        + [pltpu.SemaphoreType.DMA((len(ask_inputs),))],
+        + [pltpu.SemaphoreType.DMA((len(ask_inputs) + 3,))],
         compiler_params=params(62),
         cost_estimate=cost(2 * rows * depth * width, 2 * depth * width),
         name="ask",
@@ -494,7 +501,7 @@
             pltpu.VMEM((points, depth), bf16),
             pltpu.VMEM((points, depth), bf16),
             pltpu.VMEM((depth, width), bf16),
-            pltpu.SemaphoreType.DMA((5,)),
+            pltpu.SemaphoreType.DMA((17,)),
         ],
         compiler_params=params(40),
         cost_estimate=cost(4 * points * depth * width, 8 * points * depth),
@@ -527,7 +534,7 @@
         scratch_shapes=[
             pltpu.VMEM((points, depth), bf16),
             pltpu.VMEM((depth, width), bf16),
-            pltpu.SemaphoreType.DMA((2,)),
+            pltpu.SemaphoreType.DMA((8,)),
         ],
         compiler_params=params(40),
         cost_estimate=cost(2 * points * depth * width, 8 * points * depth),
@@ -558,7 +565,7 @@
 
     queries = in_vmem(queries)
     own_mixed = pl.pallas_call(
-        functools.partial(own_kernel, steps),
+        functools.partial(own_kernel, max(steps // 2, 1)),
         in_specs=[vmem] * 3,
         out_shape=jax.ShapeDtypeStruct((points, half), bf16),
         compiler_params=params(48),

time: 54 us -> 54.2 us (level)
  no operation moved by 1% of the time
where the time goes in v17:
time: 54.2 us; the launch traced here: 53.8 us
  Pallas kernels  20.1 us (37%)
  blocking collectives  12.7 us (23%)
  starting transfers between devices  11.7 us (22%)
  waiting for transfers between devices  7.41 us (14%)
  local copies, waits for them, and re-layouts  1.01 us (2%)
  between operations  0.95 us (2%)
    all_to_all x1, blocking collectives, exchange(): lax.all_to_all(blocks, 'dom', split_axis=0, concat_axis=0, tiled=True, ax...  12.7 us
    all_to_all x2, starting transfers between devices, exchange(): lax.all_to_all(blocks, 'dom', split_axis=0, concat_axis=0, tiled=True, ax...  10.9 us
    all_to_all x2, waiting for transfers between devices, exchange(): lax.all_to_all(blocks, 'dom', split_axis=0, concat_axis=0, tiled=True, ax...  7.4 us
    pallas_call x1, Pallas kernels, on_device(): pl.pallas_call(functools.partial(front_kernel, steps), in_specs=[hbm] * 4...  4.86 us
    pallas_call x1, Pallas kernels, on_device(): pl.pallas_call(functools.partial(other_kernel, steps), in_specs=[vmem] *...  3.6 us
    pallas_call x1, Pallas kernels, on_device(): pl.pallas_call(functools.partial(middle_kernel, steps, peers, rows), in_s...  3.51 us
    pallas_call x1, Pallas kernels, on_device(): pl.pallas_call(functools.partial(partial_kernel, cap, rows, edges), in_sp...  2.86 us
    pallas_call x1, Pallas kernels, on_device(): pl.pallas_call(ask_kernel, in_specs=[hbm] * len(ask_inputs), out_specs=vm...  2.34 us
  transfers between devices with their start and end apart: 4, of which 2 were waited for; matrix products, arithmetic and copies ran while one was open for 0% of the time, Pallas kernels for 23%

profile of v17, /device:TPU:0, one launch (start us, length us, event | category | flops | bytes accessed | tf_op | source)
XLA Modules:
  0.0 53.8 jit_solution(6326776989177720918)
XLA Ops:
  0.6 0.5 collective-permute-start
  1.1 2.3 %ask.1 = bf16[16,5,8,128]{3,2,1,0:T(8,128)(2,1)} custom-call(bf16[1024,512]{1,0:T(8,128)(2,1)} %refs_0_.1, bf16[16,1024]{1,0:T(8,128)(2,1)} %latent_ref.1, f32[1,1024]{1,0:T(1,128)} %bitcast.14, s32[16,32]{1,0:T(8,128)} %bitcast.13, s32[1,16]{1,0:T(1,128)} %bitcast.15, s32[1,512]{1,0:T(1,128)} %refs_5_.1), custom_call_target="tpu_custom_call" | custom-call | flops 16777216 | bytes 1048576 | tf_op jit(solution)/shard_map/ask/pallas_call | solution.py:479
  3.5 7.1 %all-to-all-start = ((bf16[16,5,8,128]{3,2,1,0:T(8,128)(2,1)}), bf16[16,5,8,128]{3,2,1,0:T(8,128)(2,1)S(1)}, u32[]{:S(2)}, u32[]{:S(2)}) async-start(bf16[16,5,8,128]{3,2,1,0:T(8,128)(2,1)} %ask.1), calls=%async_computation | async-start | bytes 327680 | tf_op jit(solution)/shard_map/all_to_all | solution.py:83
  10.6 0.0 collective-permute-done.other_hbm
  10.6 4.9 %front.1 = (bf16[1024,512]{1,0:T(8,128)(2,1)S(1)}, bf16[1024,512]{1,0:T(8,128)(2,1)S(1)}) custom-call(f32[1,1024]{1,0:T(1,128)} %bitcast.11, bf16[1024,1024]{1,0:T(8,128)(2,1)} %x_ref.1, bf16[1024,1024]{1,0:T(8,128)(2,1)} %collective-permute-done.other_hbm, bf16[1024,1024]{1,0:T(8,128)(2,1)} %w_hbm.2), custom_call_target="tpu_custom_call" | custom-call | flops 2147483648 | bytes 8388608 | tf_op jit(solution)/shard_map/front/pallas_call | solution.py:494
  15.5 3.6 %all-to-all-done.asked_ref = bf16[16,5,8,128]{3,2,1,0:T(8,128)(2,1)S(1)} async-done(((bf16[16,5,8,128]{3,2,1,0:T(8,128)(2,1)}), bf16[16,5,8,128]{3,2,1,0:T(8,128)(2,1)S(1)}, u32[]{:S(2)}, u32[]{:S(2)}) %all-to-all-start) | async-done | bytes 163872 | tf_op jit(solution)/shard_map/all_to_all | solution.py:83
  19.0 0.0 copy-start.6
  19.0 0.0 copy-start.7
  19.0 0.0 copy-start.8
  19.0 2.9 %partial.1 = bf16[16,5,8,128]{3,2,1,0:T(8,128)(2,1)} custom-call(bf16[16,5,8,128]{3,2,1,0:T(8,128)(2,1)S(1)} %all-to-all-done.asked_ref, bf16[1024,512]{1,0:T(8,128)(2,1)S(1)} %get-tuple-element.16.refs_0_, bf16[1024,512]{1,0:T(8,128)(2,1)S(1)} %get-tuple-element.17.refs_1_), custom_call_target="tpu_custom_call" | custom-call | flops 1073741824 | bytes 2097152 | tf_op jit(solution)/shard_map/partial/pallas_call | solution.py:511
  21.9 0.0 copy-start
  21.9 0.0 copy-start.1
  21.9 0.0 copy-start.2
  21.9 0.0 copy-start.3
  21.9 3.8 %all-to-all-start.1 = ((bf16[16,5,8,128]{3,2,1,0:T(8,128)(2,1)}), bf16[16,5,8,128]{3,2,1,0:T(8,128)(2,1)S(1)}, u32[]{:S(2)}, u32[]{:S(2)}) async-start(bf16[16,5,8,128]{3,2,1,0:T(8,128)(2,1)} %partial.1), calls=%async_computation.1 | async-start | bytes 327680 | tf_op jit(solution)/shard_map/all_to_all | solution.py:83
  25.7 0.0 copy-done.6
  25.7 0.0 copy-done.7
  25.7 0.0 copy-done.8
  25.7 3.5 %middle.1 = (bf16[512,1024]{1,0:T(8,128)(2,1)S(1)}, s32[4,1024]{1,0:T(4,128)S(1)}) custom-call(f32[1,1024]{1,0:T(1,128)S(1)} %bitcast.12, s32[32,128]{1,0:T(8,128)S(1)} %bitcast.10, s32[4,1024]{1,0:T(4,128)S(1)} %copy-done.7, bf16[1024,1024]{1,0:T(8,128)(2,1)} %x_ref.1, bf16[1024,512]{1,0:T(8,128)(2,1)} %w_hbm.3), custom_call_target="tpu_custom_call" | custom-call | flops 1073741824 | bytes 8388608 | tf_op jit(solution)/shard_map/middle/pallas_call | solution.py:526
  29.3 0.0 copy-start.9
  29.3 1.0 %copy-done.9 = bf16[512,1024]{1,0:T(8,128)(2,1)} copy-done((bf16[512,1024]{1,0:T(8,128)(2,1)}, bf16[512,1024]{1,0:T(8,128)(2,1)S(1)}, u32[]{:S(2)}) %copy-start.9) | copy-done | bytes 1048600
  30.2 3.8 %all-to-all-done.1.parts_ref = bf16[16,5,8,128]{3,2,1,0:T(8,128)(2,1)S(1)} async-done(((bf16[16,5,8,128]{3,2,1,0:T(8,128)(2,1)}), bf16[16,5,8,128]{3,2,1,0:T(8,128)(2,1)S(1)}, u32[]{:S(2)}, u32[]{:S(2)}) %all-to-all-start.1) | async-done | bytes 163872 | tf_op jit(solution)/shard_map/all_to_all | solution.py:83
  34.1 0.0 copy-start.10
  34.1 0.0 copy-done
  34.1 0.0 copy-done.1
  34.1 0.0 copy-done.2
  34.1 0.0 copy-done.3
  34.1 0.0 copy-start.4
  34.1 0.0 copy-start.5
  34.1 1.0 %combine.1 = (bf16[16,1024]{1,0:T(8,128)(2,1)S(1)}, bf16[16,16,512]{2,1,0:T(8,128)(2,1)S(1)}) custom-call(bf16[16,5,8,128]{3,2,1,0:T(8,128)(2,1)S(1)} %all-to-all-done.1.parts_ref, bf16[16,1024]{1,0:T(8,128)(2,1)S(1)} %copy-done.2, f32[1,1024]{1,0:T(1,128)S(1)} %bitcast.9, bf16[512,1024]{1,0:T(8,128)(2,1)S(1)} %copy-done.1, bf16[1024,1024]{1,0:T(8,128)(2,1)S(1)} %copy-done), custom_call_target="tpu_custom_call" | custom-call | flops 50331648 | bytes 3145728 | tf_op jit(solution)/shard_map/combine/pallas_call | solution.py:551
  35.1 12.7 %all_to_all.15 = bf16[16,16,512]{2,1,0:T(8,128)(2,1)S(1)} all-to-all(bf16[16,16,512]{2,1,0:T(8,128)(2,1)S(1)} %get-tuple-element.24), channel_id=1, replica_groups={{0,9,2,11,4,13,6,15,8,1,10,3,12,5,14,7},{16,25,18,27,20,29,22,31,24,17,..., dimensions={0} | all-to-all | bytes 524288 | tf_op jit(solution)/shard_map/all_to_all | solution.py:83
  47.8 0.3 collective-permute-start.1
  48.1 0.0 copy-done.10
  48.1 1.9 %own.1.own_ref = bf16[1024,256]{1,0:T(8,128)(2,1)S(1)} custom-call(bf16[256,512]{1,0:T(8,128)(2,1)S(1)} %bitcast.8, s32[4,1024]{1,0:T(4,128)S(1)} %get-tuple-element.25.node_ref, bf16[512,1024]{1,0:T(8,128)(2,1)S(1)} %copy-done.10), custom_call_target="tpu_custom_call" | custom-call | flops 536870912 | bytes 2097152 | tf_op jit(solution)/shard_map/own/pallas_call | solution.py:567
  50.0 0.0 collective-permute-done.1.pairs_ref
  50.1 0.0 copy-done.4
  50.1 0.0 copy-done.5
  50.1 3.6 %other.1 = (bf16[1024,1024]{1,0:T(8,128)(2,1)}, bf16[16,1024]{1,0:T(8,128)(2,1)}) custom-call(bf16[256,512]{1,0:T(8,128)(2,1)S(1)} %collective-permute-done.1.pairs_ref, bf16[1024,256]{1,0:T(8,128)(2,1)S(1)} %own.1.own_ref, s32[4,1024]{1,0:T(4,128)S(1)} %get-tuple-element.25.node_ref, bf16[512,1024]{1,0:T(8,128)(2,1)S(1)} %copy-done.10, ...), custom_call_target="tpu_custom_call" | custom-call | flops 2147483648 | bytes 8388608 | tf_op jit(solution)/shard_map/other/pallas_call | solution.py:575
Async XLA Ops:
  0.6 9.9 %collective-permute-start = (bf16[1024,1024]{1,0:T(8,128)(2,1)}, bf16[1024,1024]{1,0:T(8,128)(2,1)}, u32[]{:S(2)}, u32[]{:S(2)}) collective-permute-start(bf16[1024,1024]{1,0:T(8,128)(2,1)} %x_ref.1), channel_id=1, source_target_pairs={{0,1},{1,0},{2,3},{3,2},{4,5},{5,4},{6,7},{7,6},{8,9},{9,8},{10,11... | collective-permute-start | bytes 6291464 | tf_op jit(solution)/shard_map/ppermute | solution.py:470
  3.5 15.5 %all-to-all-start = ((bf16[16,5,8,128]{3,2,1,0:T(8,128)(2,1)}), bf16[16,5,8,128]{3,2,1,0:T(8,128)(2,1)S(1)}, u32[]{:S(2)}, u32[]{:S(2)}) async-start(bf16[16,5,8,128]{3,2,1,0:T(8,128)(2,1)} %ask.1), calls=%async_computation | async-start | bytes 327680 | tf_op jit(solution)/shard_map/all_to_all | solution.py:83
  19.0 6.7 %copy-start.6 = (s32[1,4096]{1,0:T(1,128)S(1)}, s32[1,4096]{1,0:T(1,128)}, u32[]{:S(2)}) copy-start(s32[1,4096]{1,0:T(1,128)} %param.30) | copy-start | bytes 49156
  19.0 6.7 %copy-start.7 = (s32[4,1024]{1,0:T(4,128)S(1)}, s32[4,1024]{1,0:T(4,128)}, u32[]{:S(2)}) copy-start(s32[4,1024]{1,0:T(4,128)} %slot_ref) | copy-start | bytes 49156
  19.0 6.7 %copy-start.8 = (f32[1024]{0:T(1024)S(1)}, f32[1024]{0:T(1024)}, u32[]{:S(2)}) copy-start(f32[1024]{0:T(1024)} %param.18) | copy-start | bytes 12292
  21.9 12.2 %copy-start = (bf16[1024,1024]{1,0:T(8,128)(2,1)S(1)}, bf16[1024,1024]{1,0:T(8,128)(2,1)}, u32[]{:S(2)}) copy-start(bf16[1024,1024]{1,0:T(8,128)(2,1)} %w_kv_ref.1) | copy-start | bytes 6291460
  21.9 12.2 %copy-start.1 = (bf16[512,1024]{1,0:T(8,128)(2,1)S(1)}, bf16[512,1024]{1,0:T(8,128)(2,1)}, u32[]{:S(2)}) copy-start(bf16[512,1024]{1,0:T(8,128)(2,1)} %w_o_ref.1) | copy-start | bytes 3145732
  21.9 12.2 %copy-start.2 = (bf16[16,1024]{1,0:T(8,128)(2,1)S(1)}, bf16[16,1024]{1,0:T(8,128)(2,1)}, u32[]{:S(2)}) copy-start(bf16[16,1024]{1,0:T(8,128)(2,1)} %latent_ref.1) | copy-start | bytes 98308
  21.9 12.2 %copy-start.3 = (f32[1024]{0:T(1024)S(1)}, f32[1024]{0:T(1024)}, u32[]{:S(2)}) copy-start(f32[1024]{0:T(1024)} %param.20) | copy-start | bytes 12292
  21.9 12.1 %all-to-all-start.1 = ((bf16[16,5,8,128]{3,2,1,0:T(8,128)(2,1)}), bf16[16,5,8,128]{3,2,1,0:T(8,128)(2,1)S(1)}, u32[]{:S(2)}, u32[]{:S(2)}) async-start(bf16[16,5,8,128]{3,2,1,0:T(8,128)(2,1)} %partial.1), calls=%async_computation.1 | async-start | bytes 327680 | tf_op jit(solution)/shard_map/all_to_all | solution.py:83
  29.3 1.0 %copy-start.9 = (bf16[512,1024]{1,0:T(8,128)(2,1)}, bf16[512,1024]{1,0:T(8,128)(2,1)S(1)}, u32[]{:S(2)}) copy-start(bf16[512,1024]{1,0:T(8,128)(2,1)S(1)} %get-tuple-element.26.query_ref) | copy-start | bytes 3145732
  34.1 14.1 %copy-start.10 = (bf16[512,1024]{1,0:T(8,128)(2,1)S(1)}, bf16[512,1024]{1,0:T(8,128)(2,1)}, u32[]{:S(2)}) copy-start(bf16[512,1024]{1,0:T(8,128)(2,1)} %copy-done.9) | copy-start | bytes 3145732
  34.1 16.0 %copy-start.4 = (bf16[1024,1024]{1,0:T(8,128)(2,1)S(1)}, bf16[1024,1024]{1,0:T(8,128)(2,1)}, u32[]{:S(2)}) copy-start(bf16[1024,1024]{1,0:T(8,128)(2,1)} %x_ref.1) | copy-start | bytes 6291460
  34.1 16.0 %copy-start.5 = (bf16[512,1024]{1,0:T(8,128)(2,1)S(1)}, bf16[512,1024]{1,0:T(8,128)(2,1)}, u32[]{:S(2)}) copy-start(bf16[512,1024]{1,0:T(8,128)(2,1)} %w_ref.1) | copy-start | bytes 3145732
  47.8 2.2 %collective-permute-start.1 = (bf16[256,512]{1,0:T(8,128)(2,1)S(1)}, bf16[256,512]{1,0:T(8,128)(2,1)S(1)}, u32[]{:S(2)}, u32[]{:S(2)}) collective-permute-start(bf16[256,512]{1,0:T(8,128)(2,1)S(1)} %bitcast.7), channel_id=1, source_target_pairs={{0,1},{1,0},{2,3},{3,2},{4,5},{5,4},{6,7},{7,6},{8,9},{9,8},{10,11... | collective-permute-start | bytes 786440 | tf_op jit(solution)/shard_map/ppermute | solution.py:564

commit v18 on v16

--- a/solution.py
+++ b/solution.py
@@ -64,15 +64,9 @@
     return pl.CostEstimate(flops=int(flops), bytes_accessed=int(read), transcendentals=int(exps))
 
 
-def place_of(index, peers):
-    if isinstance(index, int):
-        return (index + index % 2 * (peers // 2)) % peers
-    return mod(index + (index & 1) * (peers // 2), peers)
-
-
-def exchange(blocks, order=None):
+def exchange(blocks, groups=None):
     return lax.all_to_all(
-        blocks, "dom", split_axis=0, concat_axis=0, tiled=True, axis_index_groups=order
+        blocks, "dom", split_axis=0, concat_axis=0, tiled=True, axis_index_groups=groups
     )
 
 
@@ -261,7 +255,7 @@
                 first_head, block[h * nodes : (h + 1) * nodes], block[(h + 1) * nodes : (h + 2) * nodes]
             )
             for n in range(2 * some):
-                place = place_of(start + n // 2, peers)
+                place = start + n // 2
                 out_ref[place, 2 * i + n % 2] = slab(block, 0, n, tall).astype(bf16)
 
     row_lane = iota((tall, LANES), 1)
@@ -282,46 +276,65 @@
                         here = (mod(row_lane, 8) == h) & (div(row_lane, LANES // 2) == late)
                         piece = pltpu.roll(columns[at : at + tall], move % LANES, 1)
                         tile = jnp.where(here, piece, tile)
-                out_ref[place_of((first + g) * some + w, peers), 2 * blocks] = tile.astype(bf16)
-
-
-def combine_kernel(parts_ref, latent_ref, gain_ref, w_o_ref, w_kv_ref, latent_out_ref, out_ref):
-    peers = parts_ref.shape[0]
-    rows = latent_ref.shape[0]
-    width = w_o_ref.shape[0]
-    half = width // 2
-    size, tall = width // HEADS, rows // 2
-    chips = (peers // 2, 2, tall, LANES)
-    tile = parts_ref[:, 2 * (half // LANES)].astype(f32)
+                out_ref[(first + g) * some + w, 2 * blocks] = tile.astype(bf16)
+
+
+def merge_kernel(parts_ref, out_ref):
+    chips, windows, slabs, tall, _ = parts_ref.shape
+    half = out_ref.shape[1]
+    size = half // (HEADS // 2)
+    tile = parts_ref[:, :, slabs - 1].astype(f32)
 
     def moved(columns):
-        return pltpu.roll(tile, LANES - columns, 2)
-
-    top = (tile + moved(8) + moved(16)).reshape(chips)
-    total = (moved(24) + moved(32)).reshape(chips)
+        return pltpu.roll(tile, LANES - columns, 3)
+
+    top = tile + moved(8) + moved(16)
     factor = jnp.exp2(top - jnp.max(top, axis=0, keepdims=True))
-    factor = factor / jnp.sum(total * factor, axis=0, keepdims=True)
-    head = div(iota(chips, 3), size)
+    factor = factor / jnp.sum((moved(24) + moved(32)) * factor, axis=0, keepdims=True)
+    head = div(iota(tile.shape, 3), size)
     blocks = []
     for i in range(half // LANES):
         nodes = []
         for late in range(2):
-            wide = jnp.zeros(chips, f32)
+            wide = jnp.zeros(tile.shape, f32)
             for h in range(LANES // size):
                 at = late * (LANES // 2) + i * (LANES // size) + h
                 wide = jnp.where(head == h, factor[..., at : at + 1], wide)
-            part = parts_ref[:, 2 * i + late].astype(f32).reshape(chips)
+            part = parts_ref[:, :, 2 * i + late].astype(f32)
             nodes.append(jnp.sum(part * wide, axis=0))
         blocks.append(jnp.concatenate(nodes, axis=1))
-    mixed = jnp.concatenate([block[h] for h in range(2) for block in blocks], axis=1)
-    update = dot(mixed.astype(bf16), w_o_ref[...])
-    latent_out = (latent_ref[...].astype(f32) + update).astype(bf16)
-    latent_out_ref[...] = latent_out
-    pairs = dot(normed(latent_out, gain_ref[...]), w_kv_ref[...]).astype(bf16)
-    for p in range(peers):
-        at = p % 2 * half
-        out_ref[p, :, :half] = pairs[:, at : at + half]
-        out_ref[p, :, half:] = pairs[:, width + at : width + at + half]
+    mixed = jnp.concatenate(blocks, axis=2)
+    out_ref[...] = mixed.reshape(windows * 2 * tall, half).astype(bf16)
+
+
+def combine_kernel(
+    mixed_ref, other_mixed_ref, latent_ref, other_latent_ref, gain_ref, w_o_ref, w_kv_ref,
+    latent_out_ref, out_ref,
+):
+    chips = out_ref.shape[0]
+    rows = latent_ref.shape[0]
+    width, half = w_o_ref.shape[0], w_o_ref.shape[0] // 2
+    core = lax.axis_index("dom") & 1
+
+    def in_order(own_ref, other_ref, axis):
+        own, other = own_ref[...], other_ref[...]
+        both = [jnp.where(core == 0, own, other), jnp.where(core == 0, other, own)]
+        return jnp.concatenate(both, axis=axis)
+
+    update = dot(in_order(mixed_ref, other_mixed_ref, 1), w_o_ref[...])
+    latent_in = in_order(latent_ref, other_latent_ref, 0)
+    latent_out = (latent_in.astype(f32) + update).astype(bf16)
+    latent_out_ref[...] = jnp.where(core == 0, latent_out[:rows], latent_out[rows:])
+    latent_rows = normed(latent_out, gain_ref[...])
+    for c in range(2):
+
+        @pl.when(core == c)
+        def _():
+            for i in range(2):
+                at = i * width + c * half
+                pairs = dot(latent_rows, w_kv_ref[:, at : at + half]).astype(bf16)
+                for k in range(chips):
+                    out_ref[k, :, i * half : (i + 1) * half] = pairs
 
 
 def middle_kernel(
@@ -343,7 +356,7 @@
         listed = lax.dot_general(need, row_of, (((0,), (0,)), ((), ())), preferred_element_type=f32)
         own = mod(slots, LANES) == iota((LANES, points), 0)
         found = jnp.sum(jnp.where(own, listed, 0.0), axis=0, keepdims=True).astype(jnp.int32)
-        node_ref[j : j + 1, :] = place_of(div(slots, cap), peers) * rows + found
+        node_ref[j : j + 1, :] = div(slots, cap) * rows + found
     for copy in copies:
         copy.wait()
     for i in range(steps):
@@ -461,6 +474,7 @@
     hbm = pl.BlockSpec(memory_space=pltpu.HBM)
 
     other_grid = lax.ppermute(grid, "dom", swap)
+    other_latent = lax.ppermute(latent_in, "dom", swap)
     ask_inputs = (
         w_q_enc,
         latent_in,
@@ -511,8 +525,9 @@
         name="partial",
     )(asked, *map(in_vmem, pairs))
     parts, dec_need, dec_slot = lax.optimization_barrier((parts, dec_need, dec_slot))
-    order = [[place_of(i, peers) for i in range(peers)]]
-    parts = exchange(parts, order)
+    same_core = [list(range(c, peers, 2)) for c in range(2)]
+    parts = parts.reshape(peers // 2, 2 * sent[1], *sent[2:])
+    parts = exchange(parts, same_core).reshape(peers // 2, 2, *sent[1:])
 
     slot_total = dec_need.shape[1]
     edge_count = dec_slot.shape[0]
@@ -541,19 +556,36 @@
     )
     parts, queries, node_of = lax.optimization_barrier((parts, queries, node_of))
 
+    mixed = pl.pallas_call(
+        merge_kernel,
+        in_specs=[vmem],
+        out_specs=vmem,
+        out_shape=jax.ShapeDtypeStruct((2 * rows, half), bf16),
+        compiler_params=params(24),
+        cost_estimate=cost(8 * nodes * half, 8 * nodes * half),
+        name="merge",
+    )(parts)
     latent_out, everyone = pl.pallas_call(
         combine_kernel,
-        in_specs=[vmem] * 5,
+        in_specs=[vmem] * 7,
         out_specs=[vmem] * 2,
         out_shape=[
             pltpu.VMEM((rows, depth), bf16),
-            jax.ShapeDtypeStruct((peers, rows, width), bf16),
+            jax.ShapeDtypeStruct((peers // 2, 2 * rows, width), bf16),
         ],
         compiler_params=params(24),
         cost_estimate=cost(6 * rows * depth * width, 6 * depth * width),
         name="combine",
-    )(parts, latent_in, dec_gain.reshape(1, -1), w_o_enc, w_kv_dec)
-    own = exchange(everyone, order).reshape(nodes, width)
+    )(
+        mixed,
+        lax.ppermute(mixed, "dom", swap),
+        latent_in,
+        other_latent,
+        dec_gain.reshape(1, -1),
+        w_o_enc,
+        w_kv_dec,
+    )
+    own = exchange(everyone, same_core).reshape(nodes, width)
     other = lax.ppermute(own, "dom", swap)
 
     queries = in_vmem(queries)

time: 54 us -> 53.5 us (level)
  starting transfers between devices: 11.7 us -> 11.1 us
    ppermute x0 -> x2, waiting for transfers between devices: none -> 1.16 us  [the longest x1 1.16 us: on_device(): lax.ppermute(mixed, 'dom', swap)]
    all_to_all x2, waiting for transfers between devices: 7.5 us -> 6.4 us  [exchange(): lax.all_to_all(blocks, 'dom', split_axis=0, concat_axis=0, tiled=True, ax...]
  transfers between devices with their start and end apart: 4 -> 6, of which waited for: 2 -> 3; matrix products, arithmetic and copies ran while one was open for 0% -> 0% of each run, Pallas kernels for 23% -> 24%
where the time goes in v18:
time: 53.5 us; the launch traced here: 53.1 us
  Pallas kernels  19.9 us (37%)
  blocking collectives  12.6 us (24%)
  starting transfers between devices  11.1 us (21%)
  waiting for transfers between devices  7.56 us (14%)
  local copies, waits for them, and re-layouts  1.01 us (2%)
  between operations  1 us (2%)
    all_to_all x1, blocking collectives, exchange(): lax.all_to_all(blocks, 'dom', split_axis=0, concat_axis=0, tiled=True, ax...  12.6 us
    all_to_all x2, starting transfers between devices, exchange(): lax.all_to_all(blocks, 'dom', split_axis=0, concat_axis=0, tiled=True, ax...  10.4 us
    all_to_all x2, waiting for transfers between devices, exchange(): lax.all_to_all(blocks, 'dom', split_axis=0, concat_axis=0, tiled=True, ax...  6.4 us
    pallas_call x1, Pallas kernels, on_device(): pl.pallas_call(functools.partial(front_kernel, steps), in_specs=[hbm] * 4...  4.74 us
    pallas_call x1, Pallas kernels, on_device(): pl.pallas_call(functools.partial(middle_kernel, steps, peers, rows), in_s...  3.67 us
    pallas_call x1, Pallas kernels, on_device(): pl.pallas_call(functools.partial(other_kernel, steps), in_specs=[vmem] *...  3.6 us
    pallas_call x1, Pallas kernels, on_device(): pl.pallas_call(functools.partial(partial_kernel, cap, rows, edges), in_sp...  2.86 us
    pallas_call x1, Pallas kernels, on_device(): pl.pallas_call(ask_kernel, in_specs=[hbm] * len(ask_inputs), out_specs=vm...  2.31 us
  transfers between devices with their start and end apart: 6, of which 3 were waited for; matrix products, arithmetic and copies ran while one was open for 0% of the time, Pallas kernels for 24%

profile of v18, /device:TPU:0, one launch (start us, length us, event | category | flops | bytes accessed | tf_op | source)
XLA Modules:
  0.0 53.1 jit_solution(14791498868758461766)
XLA Ops:
  0.6 0.5 collective-permute-start
  1.1 2.3 %ask.1 = bf16[16,5,8,128]{3,2,1,0:T(8,128)(2,1)} custom-call(bf16[1024,512]{1,0:T(8,128)(2,1)} %refs_0_.1, bf16[16,1024]{1,0:T(8,128)(2,1)} %latent_ref.1, f32[1,1024]{1,0:T(1,128)} %bitcast.17, s32[16,32]{1,0:T(8,128)} %bitcast.16, s32[1,16]{1,0:T(1,128)} %bitcast.18, s32[1,512]{1,0:T(1,128)} %refs_5_.1), custom_call_target="tpu_custom_call" | custom-call | flops 16777216 | bytes 1048576 | tf_op jit(solution)/shard_map/ask/pallas_call | solution.py:486
  3.5 7.1 %all-to-all-start = ((bf16[16,5,8,128]{3,2,1,0:T(8,128)(2,1)}), bf16[16,5,8,128]{3,2,1,0:T(8,128)(2,1)S(1)}, u32[]{:S(2)}, u32[]{:S(2)}) async-start(bf16[16,5,8,128]{3,2,1,0:T(8,128)(2,1)} %ask.1), calls=%async_computation | async-start | bytes 327680 | tf_op jit(solution)/shard_map/all_to_all | solution.py:68
  10.5 0.0 collective-permute-done.other_hbm
  10.5 4.7 %front.1 = (bf16[1024,512]{1,0:T(8,128)(2,1)S(1)}, bf16[1024,512]{1,0:T(8,128)(2,1)S(1)}) custom-call(f32[1,1024]{1,0:T(1,128)} %bitcast.14, bf16[1024,1024]{1,0:T(8,128)(2,1)} %x_ref.1, bf16[1024,1024]{1,0:T(8,128)(2,1)} %collective-permute-done.other_hbm, bf16[1024,1024]{1,0:T(8,128)(2,1)} %w_hbm.2), custom_call_target="tpu_custom_call" | custom-call | flops 2147483648 | bytes 8388608 | tf_op jit(solution)/shard_map/front/pallas_call | solution.py:501
  15.3 3.7 %all-to-all-done.asked_ref = bf16[16,5,8,128]{3,2,1,0:T(8,128)(2,1)S(1)} async-done(((bf16[16,5,8,128]{3,2,1,0:T(8,128)(2,1)}), bf16[16,5,8,128]{3,2,1,0:T(8,128)(2,1)S(1)}, u32[]{:S(2)}, u32[]{:S(2)}) %all-to-all-start) | async-done | bytes 163872 | tf_op jit(solution)/shard_map/all_to_all | solution.py:68
  19.0 0.0 copy-start.2
  19.0 0.0 copy-start.6
  19.0 0.0 copy-start.7
  19.0 0.0 copy-start.8
  19.0 2.9 %partial.1 = bf16[16,5,8,128]{3,2,1,0:T(8,128)(2,1)} custom-call(bf16[16,5,8,128]{3,2,1,0:T(8,128)(2,1)S(1)} %all-to-all-done.asked_ref, bf16[1024,512]{1,0:T(8,128)(2,1)S(1)} %get-tuple-element.16.refs_0_, bf16[1024,512]{1,0:T(8,128)(2,1)S(1)} %get-tuple-element.17.refs_1_), custom_call_target="tpu_custom_call" | custom-call | flops 1073741824 | bytes 2097152 | tf_op jit(solution)/shard_map/partial/pallas_call | solution.py:518
  21.9 3.4 %all-to-all-start.1 = ((bf16[8,10,8,128]{3,2,1,0:T(8,128)(2,1)}), bf16[8,10,8,128]{3,2,1,0:T(8,128)(2,1)S(1)}, u32[]{:S(2)}, u32[]{:S(2)}) async-start(bf16[8,10,8,128]{3,2,1,0:T(8,128)(2,1)} %bitcast.4), calls=%async_computation.1 | async-start | bytes 327680 | tf_op jit(solution)/shard_map/all_to_all | solution.py:68
  25.3 0.0 copy-done.2
  25.3 0.0 copy-start
  25.3 0.0 copy-start.1
  25.3 0.0 copy-start.3
  25.3 0.1 collective-permute-start.2
  25.4 0.0 copy-done.6
  25.4 0.0 copy-done.7
  25.4 0.0 copy-done.8
  25.4 3.7 %middle.1 = (bf16[512,1024]{1,0:T(8,128)(2,1)S(1)}, s32[4,1024]{1,0:T(4,128)S(1)}) custom-call(f32[1,1024]{1,0:T(1,128)S(1)} %bitcast.15, s32[32,128]{1,0:T(8,128)S(1)} %bitcast.13, s32[4,1024]{1,0:T(4,128)S(1)} %copy-done.7, bf16[1024,1024]{1,0:T(8,128)(2,1)} %x_ref.1, bf16[1024,512]{1,0:T(8,128)(2,1)} %w_hbm.3), custom_call_target="tpu_custom_call" | custom-call | flops 1073741824 | bytes 8388608 | tf_op jit(solution)/shard_map/middle/pallas_call | solution.py:534
  29.1 0.0 copy-start.9
  29.1 1.0 %copy-done.9 = bf16[512,1024]{1,0:T(8,128)(2,1)} copy-done((bf16[512,1024]{1,0:T(8,128)(2,1)}, bf16[512,1024]{1,0:T(8,128)(2,1)S(1)}, u32[]{:S(2)}) %copy-start.9) | copy-done | bytes 1048600
  30.1 2.7 %all-to-all-done.1 = bf16[8,10,8,128]{3,2,1,0:T(8,128)(2,1)S(1)} async-done(((bf16[8,10,8,128]{3,2,1,0:T(8,128)(2,1)}), bf16[8,10,8,128]{3,2,1,0:T(8,128)(2,1)S(1)}, u32[]{:S(2)}, u32[]{:S(2)}) %all-to-all-start.1) | async-done | bytes 163872 | tf_op jit(solution)/shard_map/all_to_all | solution.py:68
  32.8 0.0 copy-start.10
  32.8 0.3 merge.1.mixed_ref
  33.1 0.1 collective-permute-start.1
  33.2 0.0 collective-permute-done.2.other_latent_ref
  33.2 1.2 %collective-permute-done.1.other_mixed_ref = bf16[32,256]{1,0:T(8,128)(2,1)S(1)} collective-permute-done((bf16[32,256]{1,0:T(8,128)(2,1)S(1)}, bf16[32,256]{1,0:T(8,128)(2,1)S(1)}, u32[]{:S(2)}, u32[]{:S(2)}) %collective-permute-start.1) | collective-permute-done | bytes 16416 | tf_op jit(solution)/shard_map/ppermute | solution.py:581
  34.4 0.0 copy-done
  34.4 0.0 copy-done.1
  34.4 0.0 copy-done.3
  34.4 0.0 copy-start.4
  34.4 0.0 copy-start.5
  34.4 0.7 %combine.1 = (bf16[16,1024]{1,0:T(8,128)(2,1)S(1)}, bf16[8,32,512]{2,1,0:T(8,128)(2,1)S(1)}) custom-call(bf16[32,256]{1,0:T(8,128)(2,1)S(1)} %merge.1.mixed_ref, bf16[32,256]{1,0:T(8,128)(2,1)S(1)} %collective-permute-done.1.other_mixed_ref, bf16[16,1024]{1,0:T(8,128)(2,1)S(1)} %copy-done.2, bf16[16,1024]{1,0:T(8,128)(2,1)S(1)} %collective-permute-done.2.other_latent_ref, ...), custom_call_target="tpu_custom_call" | custom-call | flops 50331648 | bytes 3145728 | tf_op jit(solution)/shard_map/combine/pallas_call | solution.py:568
  35.1 12.6 %all_to_all.15 = bf16[8,32,512]{2,1,0:T(8,128)(2,1)S(1)} all-to-all(bf16[8,32,512]{2,1,0:T(8,128)(2,1)S(1)} %get-tuple-element.24), channel_id=1, replica_groups={{0,2,4,6,8,10,12,14},{1,3,5,7,9,11,13,15},{16,18,20,22,24,26,28,30},{17..., dimensions={0} | all-to-all | bytes 524288 | tf_op jit(solution)/shard_map/all_to_all | solution.py:68
  47.7 0.0 collective-permute-start.3
  47.7 0.0 copy-done.10
  47.7 1.7 %own.1.own_ref = bf16[1024,256]{1,0:T(8,128)(2,1)S(1)} custom-call(bf16[256,512]{1,0:T(8,128)(2,1)S(1)} %bitcast.11, s32[4,1024]{1,0:T(4,128)S(1)} %get-tuple-element.25.node_ref, bf16[512,1024]{1,0:T(8,128)(2,1)S(1)} %copy-done.10), custom_call_target="tpu_custom_call" | custom-call | flops 536870912 | bytes 2097152 | tf_op jit(solution)/shard_map/own/pallas_call | solution.py:592
  49.3 0.0 collective-permute-done.3.pairs_ref
  49.3 0.0 copy-done.4
  49.4 0.0 copy-done.5
  49.4 3.6 %other.1 = (bf16[1024,1024]{1,0:T(8,128)(2,1)}, bf16[16,1024]{1,0:T(8,128)(2,1)}) custom-call(bf16[256,512]{1,0:T(8,128)(2,1)S(1)} %collective-permute-done.3.pairs_ref, bf16[1024,256]{1,0:T(8,128)(2,1)S(1)} %own.1.own_ref, s32[4,1024]{1,0:T(4,128)S(1)} %get-tuple-element.25.node_ref, bf16[512,1024]{1,0:T(8,128)(2,1)S(1)} %copy-done.10, ...), custom_call_target="tpu_custom_call" | custom-call | flops 2147483648 | bytes 8388608 | tf_op jit(solution)/shard_map/other/pallas_call | solution.py:600
Async XLA Ops:
  0.6 9.9 %collective-permute-start = (bf16[1024,1024]{1,0:T(8,128)(2,1)}, bf16[1024,1024]{1,0:T(8,128)(2,1)}, u32[]{:S(2)}, u32[]{:S(2)}) collective-permute-start(bf16[1024,1024]{1,0:T(8,128)(2,1)} %x_ref.1), channel_id=1, source_target_pairs={{0,1},{1,0},{2,3},{3,2},{4,5},{5,4},{6,7},{7,6},{8,9},{9,8},{10,11... | collective-permute-start | bytes 6291464 | tf_op jit(solution)/shard_map/ppermute | solution.py:476
  3.5 15.5 %all-to-all-start = ((bf16[16,5,8,128]{3,2,1,0:T(8,128)(2,1)}), bf16[16,5,8,128]{3,2,1,0:T(8,128)(2,1)S(1)}, u32[]{:S(2)}, u32[]{:S(2)}) async-start(bf16[16,5,8,128]{3,2,1,0:T(8,128)(2,1)} %ask.1), calls=%async_computation | async-start | bytes 327680 | tf_op jit(solution)/shard_map/all_to_all | solution.py:68
  19.0 6.3 %copy-start.2 = (bf16[16,1024]{1,0:T(8,128)(2,1)S(1)}, bf16[16,1024]{1,0:T(8,128)(2,1)}, u32[]{:S(2)}) copy-start(bf16[16,1024]{1,0:T(8,128)(2,1)} %latent_ref.1) | copy-start | bytes 98308
  19.0 6.4 %copy-start.6 = (s32[1,4096]{1,0:T(1,128)S(1)}, s32[1,4096]{1,0:T(1,128)}, u32[]{:S(2)}) copy-start(s32[1,4096]{1,0:T(1,128)} %param.30) | copy-start | bytes 49156
  19.0 6.4 %copy-start.7 = (s32[4,1024]{1,0:T(4,128)S(1)}, s32[4,1024]{1,0:T(4,128)}, u32[]{:S(2)}) copy-start(s32[4,1024]{1,0:T(4,128)} %slot_ref) | copy-start | bytes 49156
  19.0 6.4 %copy-start.8 = (f32[1024]{0:T(1024)S(1)}, f32[1024]{0:T(1024)}, u32[]{:S(2)}) copy-start(f32[1024]{0:T(1024)} %param.18) | copy-start | bytes 12292
  21.9 10.9 %all-to-all-start.1 = ((bf16[8,10,8,128]{3,2,1,0:T(8,128)(2,1)}), bf16[8,10,8,128]{3,2,1,0:T(8,128)(2,1)S(1)}, u32[]{:S(2)}, u32[]{:S(2)}) async-start(bf16[8,10,8,128]{3,2,1,0:T(8,128)(2,1)} %bitcast.4), calls=%async_computation.1 | async-start | bytes 327680 | tf_op jit(solution)/shard_map/all_to_all | solution.py:68
  25.3 9.1 %copy-start = (bf16[1024,1024]{1,0:T(8,128)(2,1)S(1)}, bf16[1024,1024]{1,0:T(8,128)(2,1)}, u32[]{:S(2)}) copy-start(bf16[1024,1024]{1,0:T(8,128)(2,1)} %w_kv_ref.1) | copy-start | bytes 6291460
  25.3 9.1 %copy-start.1 = (bf16[512,1024]{1,0:T(8,128)(2,1)S(1)}, bf16[512,1024]{1,0:T(8,128)(2,1)}, u32[]{:S(2)}) copy-start(bf16[512,1024]{1,0:T(8,128)(2,1)} %w_o_ref.1) | copy-start | bytes 3145732
  25.3 9.1 %copy-start.3 = (f32[1024]{0:T(1024)S(1)}, f32[1024]{0:T(1024)}, u32[]{:S(2)}) copy-start(f32[1024]{0:T(1024)} %param.20) | copy-start | bytes 12292
  25.3 7.9 %collective-permute-start.2 = (bf16[16,1024]{1,0:T(8,128)(2,1)S(1)}, bf16[16,1024]{1,0:T(8,128)(2,1)S(1)}, u32[]{:S(2)}, u32[]{:S(2)}) collective-permute-start(bf16[16,1024]{1,0:T(8,128)(2,1)S(1)} %copy-done.2), channel_id=1, source_target_pairs={{0,1},{1,0},{2,3},{3,2},{4,5},{5,4},{6,7},{7,6},{8,9},{9,8},{10,11... | collective-permute-start | bytes 98312 | tf_op jit(solution)/shard_map/ppermute | solution.py:477
  29.1 1.0 %copy-start.9 = (bf16[512,1024]{1,0:T(8,128)(2,1)}, bf16[512,1024]{1,0:T(8,128)(2,1)S(1)}, u32[]{:S(2)}) copy-start(bf16[512,1024]{1,0:T(8,128)(2,1)S(1)} %get-tuple-element.26.query_ref) | copy-start | bytes 3145732
  32.8 14.9 %copy-start.10 = (bf16[512,1024]{1,0:T(8,128)(2,1)S(1)}, bf16[512,1024]{1,0:T(8,128)(2,1)}, u32[]{:S(2)}) copy-start(bf16[512,1024]{1,0:T(8,128)(2,1)} %copy-done.9) | copy-start | bytes 3145732
  33.1 1.2 %collective-permute-start.1 = (bf16[32,256]{1,0:T(8,128)(2,1)S(1)}, bf16[32,256]{1,0:T(8,128)(2,1)S(1)}, u32[]{:S(2)}, u32[]{:S(2)}) collective-permute-start(bf16[32,256]{1,0:T(8,128)(2,1)S(1)} %merge.1.mixed_ref), channel_id=1, source_target_pairs={{0,1},{1,0},{2,3},{3,2},{4,5},{5,4},{6,7},{7,6},{8,9},{9,8},{10,11... | collective-permute-start | bytes 49160 | tf_op jit(solution)/shard_map/ppermute | solution.py:581
  34.4 15.0 %copy-start.4 = (bf16[1024,1024]{1,0:T(8,128)(2,1)S(1)}, bf16[1024,1024]{1,0:T(8,128)(2,1)}, u32[]{:S(2)}) copy-start(bf16[1024,1024]{1,0:T(8,128)(2,1)} %x_ref.1) | copy-start | bytes 6291460
  34.4 15.0 %copy-start.5 = (bf16[512,1024]{1,0:T(8,128)(2,1)S(1)}, bf16[512,1024]{1,0:T(8,128)(2,1)}, u32[]{:S(2)}) copy-start(bf16[512,1024]{1,0:T(8,128)(2,1)} %w_ref.1) | copy-start | bytes 3145732
  47.7 1.7 %collective-permute-start.3 = (bf16[256,512]{1,0:T(8,128)(2,1)S(1)}, bf16[256,512]{1,0:T(8,128)(2,1)S(1)}, u32[]{:S(2)}, u32[]{:S(2)}) collective-permute-start(bf16[256,512]{1,0:T(8,128)(2,1)S(1)} %bitcast.10), channel_id=1, source_target_pairs={{0,1},{1,0},{2,3},{3,2},{4,5},{5,4},{6,7},{7,6},{8,9},{9,8},{10,11... | collective-permute-start | bytes 786440 | tf_op jit(solution)/shard_map/ppermute | solution.py:589

commit v19 on v18

--- a/solution.py
+++ b/solution.py
@@ -311,9 +311,7 @@
     mixed_ref, other_mixed_ref, latent_ref, other_latent_ref, gain_ref, w_o_ref, w_kv_ref,
     latent_out_ref, out_ref,
 ):
-    chips = out_ref.shape[0]
     rows = latent_ref.shape[0]
-    width, half = w_o_ref.shape[0], w_o_ref.shape[0] // 2
     core = lax.axis_index("dom") & 1
 
     def in_order(own_ref, other_ref, axis):
@@ -326,24 +324,30 @@
     latent_out = (latent_in.astype(f32) + update).astype(bf16)
     latent_out_ref[...] = jnp.where(core == 0, latent_out[:rows], latent_out[rows:])
     latent_rows = normed(latent_out, gain_ref[...])
-    for c in range(2):
-
-        @pl.when(core == c)
-        def _():
-            for i in range(2):
-                at = i * width + c * half
-                pairs = dot(latent_rows, w_kv_ref[:, at : at + half]).astype(bf16)
-                for k in range(chips):
-                    out_ref[k, :, i * half : (i + 1) * half] = pairs
+    pairs = dot(latent_rows, w_kv_ref[...]).astype(bf16)
+    for k in range(out_ref.shape[0]):
+        out_ref[k] = pairs
 
 
 def middle_kernel(
-    steps, peers, rows, gain_ref, need_ref, slot_ref, x_hbm, w_hbm, query_ref, node_ref,
-    x_ref, w_ref, sems,
+    steps, peers, rows, gain_ref, need_ref, slot_ref, x_hbm, w_hbm, w_kv_hbm,
+    query_ref, node_ref, w_kv_ref, x_ref, w_ref, sems,
 ):
     copies = started(
         pltpu.make_async_copy(w_hbm, w_ref, sems.at[0]),
         pltpu.make_async_copy(x_hbm, x_ref, sems.at[1]),
+    )
+    half = w_kv_ref.shape[1] // 2
+    core = lax.axis_index("dom") & 1
+    later = started(
+        *[
+            pltpu.make_async_copy(
+                w_kv_hbm.at[:, pl.ds(pl.multiple_of((core + 2 * i) * half, half), half)],
+                w_kv_ref.at[:, pl.ds(i * half, half)],
+                sems.at[2 + i],
+            )
+            for i in range(2)
+        ]
     )
     points = x_ref.shape[0]
     block = points // steps
@@ -363,6 +367,8 @@
         part = pl.ds(i * block, block)
         queries = dot(normed(x_ref[part, :], gain_ref[...]), w_ref[...])
         query_ref[:, part] = queries.T.astype(bf16)
+    for copy in later:
+        copy.wait()
 
 
 def attend_half(pairs, queries, nodes):
@@ -531,18 +537,19 @@
 
     slot_total = dec_need.shape[1]
     edge_count = dec_slot.shape[0]
-    queries, node_of = pl.pallas_call(
+    queries, node_of, w_kv_half = pl.pallas_call(
         functools.partial(middle_kernel, steps, peers, rows),
-        in_specs=[vmem] * 3 + [hbm] * 2,
-        out_specs=[vmem, vmem],
+        in_specs=[vmem] * 3 + [hbm] * 3,
+        out_specs=[vmem] * 3,
         out_shape=[
             pltpu.VMEM((width, points), bf16),
             jax.ShapeDtypeStruct((edge_count, points), jnp.int32),
+            pltpu.VMEM((depth, width), bf16),
         ],
         scratch_shapes=[
             pltpu.VMEM((points, depth), bf16),
             pltpu.VMEM((depth, width), bf16),
-            pltpu.SemaphoreType.DMA((2,)),
+            pltpu.SemaphoreType.DMA((4,)),
         ],
         compiler_params=params(40),
         cost_estimate=cost(2 * points * depth * width, 8 * points * depth),
@@ -553,6 +560,7 @@
         dec_slot,
         in_hbm(grid),
         in_hbm(w_q_dec),
+        in_hbm(w_kv_dec),
     )
     parts, queries, node_of = lax.optimization_barrier((parts, queries, node_of))
 
@@ -583,7 +591,7 @@
         other_latent,
         dec_gain.reshape(1, -1),
         w_o_enc,
-        w_kv_dec,
+        in_vmem(w_kv_half),
     )
     own = exchange(everyone, same_core).reshape(nodes, width)
     other = lax.ppermute(own, "dom", swap)

time: 53.5 us -> 53 us (level)
  waiting for transfers between devices: 7.56 us -> 8.59 us
  local copies, waits for them, and re-layouts: 1.01 us -> 0.03 us
    all_to_all x2, waiting for transfers between devices: 6.4 us -> 7.42 us  [exchange(): lax.all_to_all(blocks, 'dom', split_axis=0, concat_axis=0, tiled=True, ax...]
    unnamed x22 -> x16, local copies, waits for them, and re-layouts: 1.01 us -> 0.03 us
where the time goes in v19:
time: 53 us; the launch traced here: 52.6 us
  Pallas kernels  19.8 us (37%)
  blocking collectives  12.1 us (23%)
  starting transfers between devices  11.1 us (21%)
  waiting for transfers between devices  8.59 us (16%)
  between operations  0.97 us (2%)
    all_to_all x1, blocking collectives, exchange(): lax.all_to_all(blocks, 'dom', split_axis=0, concat_axis=0, tiled=True, ax...  12.1 us
    all_to_all x2, starting transfers between devices, exchange(): lax.all_to_all(blocks, 'dom', split_axis=0, concat_axis=0, tiled=True, ax...  10.4 us
    all_to_all x2, waiting for transfers between devices, exchange(): lax.all_to_all(blocks, 'dom', split_axis=0, concat_axis=0, tiled=True, ax...  7.42 us
    pallas_call x1, Pallas kernels, on_device(): pl.pallas_call(functools.partial(front_kernel, steps), in_specs=[hbm] * 4...  4.74 us
    pallas_call x1, Pallas kernels, on_device(): pl.pallas_call(functools.partial(middle_kernel, steps, peers, rows), in_s...  3.63 us
    pallas_call x1, Pallas kernels, on_device(): pl.pallas_call(functools.partial(other_kernel, steps), in_specs=[vmem] *...  3.61 us
    pallas_call x1, Pallas kernels, on_device(): pl.pallas_call(functools.partial(partial_kernel, cap, rows, edges), in_sp...  2.87 us
    pallas_call x1, Pallas kernels, on_device(): pl.pallas_call(ask_kernel, in_specs=[hbm] * len(ask_inputs), out_specs=vm...  2.31 us
  transfers between devices with their start and end apart: 6, of which 3 were waited for; matrix products, arithmetic and copies ran while one was open for 0% of the time, Pallas kernels for 24%

profile of v19, /device:TPU:0, one launch (start us, length us, event | category | flops | bytes accessed | tf_op | source)
XLA Modules:
  0.0 52.6 jit_solution(7642265535076630147)
XLA Ops:
  0.6 0.5 collective-permute-start
  1.1 2.3 %ask.1 = bf16[16,5,8,128]{3,2,1,0:T(8,128)(2,1)} custom-call(bf16[1024,512]{1,0:T(8,128)(2,1)} %refs_0_.1, bf16[16,1024]{1,0:T(8,128)(2,1)} %latent_ref.1, f32[1,1024]{1,0:T(1,128)} %bitcast.17, s32[16,32]{1,0:T(8,128)} %bitcast.16, s32[1,16]{1,0:T(1,128)} %bitcast.18, s32[1,512]{1,0:T(1,128)} %refs_5_.1), custom_call_target="tpu_custom_call" | custom-call | flops 16777216 | bytes 1048576 | tf_op jit(solution)/shard_map/ask/pallas_call | solution.py:492
  3.5 7.1 %all-to-all-start = ((bf16[16,5,8,128]{3,2,1,0:T(8,128)(2,1)}), bf16[16,5,8,128]{3,2,1,0:T(8,128)(2,1)S(1)}, u32[]{:S(2)}, u32[]{:S(2)}) async-start(bf16[16,5,8,128]{3,2,1,0:T(8,128)(2,1)} %ask.1), calls=%async_computation | async-start | bytes 327680 | tf_op jit(solution)/shard_map/all_to_all | solution.py:68
  10.5 0.0 collective-permute-done.other_hbm
  10.5 4.7 %front.1 = (bf16[1024,512]{1,0:T(8,128)(2,1)S(1)}, bf16[1024,512]{1,0:T(8,128)(2,1)S(1)}) custom-call(f32[1,1024]{1,0:T(1,128)} %bitcast.14, bf16[1024,1024]{1,0:T(8,128)(2,1)} %x_ref.1, bf16[1024,1024]{1,0:T(8,128)(2,1)} %collective-permute-done.other_hbm, bf16[1024,1024]{1,0:T(8,128)(2,1)} %w_hbm.2), custom_call_target="tpu_custom_call" | custom-call | flops 2147483648 | bytes 8388608 | tf_op jit(solution)/shard_map/front/pallas_call | solution.py:507
  15.3 3.7 %all-to-all-done.asked_ref = bf16[16,5,8,128]{3,2,1,0:T(8,128)(2,1)S(1)} async-done(((bf16[16,5,8,128]{3,2,1,0:T(8,128)(2,1)}), bf16[16,5,8,128]{3,2,1,0:T(8,128)(2,1)S(1)}, u32[]{:S(2)}, u32[]{:S(2)}) %all-to-all-start) | async-done | bytes 163872 | tf_op jit(solution)/shard_map/all_to_all | solution.py:68
  19.0 0.0 copy-start.2
  19.0 0.0 copy-start.3
  19.0 0.0 copy-start.4
  19.0 0.0 copy-start.6
  19.0 2.9 %partial.1 = bf16[16,5,8,128]{3,2,1,0:T(8,128)(2,1)} custom-call(bf16[16,5,8,128]{3,2,1,0:T(8,128)(2,1)S(1)} %all-to-all-done.asked_ref, bf16[1024,512]{1,0:T(8,128)(2,1)S(1)} %get-tuple-element.17.refs_0_, bf16[1024,512]{1,0:T(8,128)(2,1)S(1)} %get-tuple-element.18.refs_1_), custom_call_target="tpu_custom_call" | custom-call | flops 1073741824 | bytes 2097152 | tf_op jit(solution)/shard_map/partial/pallas_call | solution.py:524
  21.9 3.4 %all-to-all-start.1 = ((bf16[8,10,8,128]{3,2,1,0:T(8,128)(2,1)}), bf16[8,10,8,128]{3,2,1,0:T(8,128)(2,1)S(1)}, u32[]{:S(2)}, u32[]{:S(2)}) async-start(bf16[8,10,8,128]{3,2,1,0:T(8,128)(2,1)} %bitcast.4), calls=%async_computation.1 | async-start | bytes 327680 | tf_op jit(solution)/shard_map/all_to_all | solution.py:68
  25.3 0.0 copy-done.2
  25.3 0.1 collective-permute-start.2
  25.4 0.0 copy-done.3
  25.4 0.0 copy-done.4
  25.4 0.0 copy-done.6
  25.4 0.0 copy-start.1
  25.4 0.0 copy-start.5
  25.4 3.6 %middle.1 = (bf16[512,1024]{1,0:T(8,128)(2,1)S(1)}, s32[4,1024]{1,0:T(4,128)S(1)}, bf16[1024,512]{1,0:T(8,128)(2,1)S(1)}) custom-call(f32[1,1024]{1,0:T(1,128)S(1)} %bitcast.15, s32[32,128]{1,0:T(8,128)S(1)} %bitcast.12, s32[4,1024]{1,0:T(4,128)S(1)} %copy-done.4, bf16[1024,1024]{1,0:T(8,128)(2,1)} %x_ref.1, bf16[1024,512]{1,0:T(8,128)(2,1)} %w_hbm.3, ...), custom_call_target="tpu_custom_call" | custom-call | flops 1073741824 | bytes 8388608 | tf_op jit(solution)/shard_map/middle/pallas_call | solution.py:540
  29.1 3.7 %all-to-all-done.1 = bf16[8,10,8,128]{3,2,1,0:T(8,128)(2,1)S(1)} async-done(((bf16[8,10,8,128]{3,2,1,0:T(8,128)(2,1)}), bf16[8,10,8,128]{3,2,1,0:T(8,128)(2,1)S(1)}, u32[]{:S(2)}, u32[]{:S(2)}) %all-to-all-start.1) | async-done | bytes 163872 | tf_op jit(solution)/shard_map/all_to_all | solution.py:68
  32.8 0.3 merge.1.mixed_ref
  33.1 0.1 collective-permute-start.1
  33.2 0.0 collective-permute-done.2.other_latent_ref
  33.2 1.2 %collective-permute-done.1.other_mixed_ref = bf16[32,256]{1,0:T(8,128)(2,1)S(1)} collective-permute-done((bf16[32,256]{1,0:T(8,128)(2,1)S(1)}, bf16[32,256]{1,0:T(8,128)(2,1)S(1)}, u32[]{:S(2)}, u32[]{:S(2)}) %collective-permute-start.1) | collective-permute-done | bytes 16416 | tf_op jit(solution)/shard_map/ppermute | solution.py:589
  34.4 0.0 copy-done.1
  34.4 0.0 copy-done.5
  34.4 0.0 copy-start
  34.4 0.0 copy-start.7
  34.4 0.6 %combine.1 = (bf16[16,1024]{1,0:T(8,128)(2,1)S(1)}, bf16[8,32,512]{2,1,0:T(8,128)(2,1)S(1)}) custom-call(bf16[32,256]{1,0:T(8,128)(2,1)S(1)} %merge.1.mixed_ref, bf16[32,256]{1,0:T(8,128)(2,1)S(1)} %collective-permute-done.1.other_mixed_ref, bf16[16,1024]{1,0:T(8,128)(2,1)S(1)} %copy-done.2, bf16[16,1024]{1,0:T(8,128)(2,1)S(1)} %collective-permute-done.2.other_latent_ref, ...), custom_call_target="tpu_custom_call" | custom-call | flops 50331648 | bytes 3145728 | tf_op jit(solution)/shard_map/combine/pallas_call | solution.py:576
  35.0 12.1 %all_to_all.15 = bf16[8,32,512]{2,1,0:T(8,128)(2,1)S(1)} all-to-all(bf16[8,32,512]{2,1,0:T(8,128)(2,1)S(1)} %get-tuple-element.26), channel_id=1, replica_groups={{0,2,4,6,8,10,12,14},{1,3,5,7,9,11,13,15},{16,18,20,22,24,26,28,30},{17..., dimensions={0} | all-to-all | bytes 524288 | tf_op jit(solution)/shard_map/all_to_all | solution.py:68
  47.1 0.0 collective-permute-start.3
  47.1 1.7 %own.1.own_ref = bf16[1024,256]{1,0:T(8,128)(2,1)S(1)} custom-call(bf16[256,512]{1,0:T(8,128)(2,1)S(1)} %bitcast.11, s32[4,1024]{1,0:T(4,128)S(1)} %get-tuple-element.27.node_ref, bf16[512,1024]{1,0:T(8,128)(2,1)S(1)} %get-tuple-element.28.query_ref), custom_call_target="tpu_custom_call" | custom-call | flops 536870912 | bytes 2097152 | tf_op jit(solution)/shard_map/own/pallas_call | solution.py:600
  48.8 0.0 collective-permute-done.3.pairs_ref
  48.8 0.0 copy-done
  48.8 0.0 copy-done.7
  48.8 3.6 %other.1 = (bf16[1024,1024]{1,0:T(8,128)(2,1)}, bf16[16,1024]{1,0:T(8,128)(2,1)}) custom-call(bf16[256,512]{1,0:T(8,128)(2,1)S(1)} %collective-permute-done.3.pairs_ref, bf16[1024,256]{1,0:T(8,128)(2,1)S(1)} %own.1.own_ref, s32[4,1024]{1,0:T(4,128)S(1)} %get-tuple-element.27.node_ref, bf16[512,1024]{1,0:T(8,128)(2,1)S(1)} %get-tuple-element.28.query_ref, ...), custom_call_target="tpu_custom_call" | custom-call | flops 2147483648 | bytes 8388608 | tf_op jit(solution)/shard_map/other/pallas_call | solution.py:608
Async XLA Ops:
  0.6 9.9 %collective-permute-start = (bf16[1024,1024]{1,0:T(8,128)(2,1)}, bf16[1024,1024]{1,0:T(8,128)(2,1)}, u32[]{:S(2)}, u32[]{:S(2)}) collective-permute-start(bf16[1024,1024]{1,0:T(8,128)(2,1)} %x_ref.1), channel_id=1, source_target_pairs={{0,1},{1,0},{2,3},{3,2},{4,5},{5,4},{6,7},{7,6},{8,9},{9,8},{10,11... | collective-permute-start | bytes 6291464 | tf_op jit(solution)/shard_map/ppermute | solution.py:482
  3.5 15.5 %all-to-all-start = ((bf16[16,5,8,128]{3,2,1,0:T(8,128)(2,1)}), bf16[16,5,8,128]{3,2,1,0:T(8,128)(2,1)S(1)}, u32[]{:S(2)}, u32[]{:S(2)}) async-start(bf16[16,5,8,128]{3,2,1,0:T(8,128)(2,1)} %ask.1), calls=%async_computation | async-start | bytes 327680 | tf_op jit(solution)/shard_map/all_to_all | solution.py:68
  19.0 6.3 %copy-start.2 = (bf16[16,1024]{1,0:T(8,128)(2,1)S(1)}, bf16[16,1024]{1,0:T(8,128)(2,1)}, u32[]{:S(2)}) copy-start(bf16[16,1024]{1,0:T(8,128)(2,1)} %latent_ref.1) | copy-start | bytes 98308
  19.0 6.4 %copy-start.3 = (s32[1,4096]{1,0:T(1,128)S(1)}, s32[1,4096]{1,0:T(1,128)}, u32[]{:S(2)}) copy-start(s32[1,4096]{1,0:T(1,128)} %param.30) | copy-start | bytes 49156
  19.0 6.4 %copy-start.4 = (s32[4,1024]{1,0:T(4,128)S(1)}, s32[4,1024]{1,0:T(4,128)}, u32[]{:S(2)}) copy-start(s32[4,1024]{1,0:T(4,128)} %slot_ref) | copy-start | bytes 49156
  19.0 6.4 %copy-start.6 = (f32[1024]{0:T(1024)S(1)}, f32[1024]{0:T(1024)}, u32[]{:S(2)}) copy-start(f32[1024]{0:T(1024)} %param.18) | copy-start | bytes 12292
  21.9 10.9 %all-to-all-start.1 = ((bf16[8,10,8,128]{3,2,1,0:T(8,128)(2,1)}), bf16[8,10,8,128]{3,2,1,0:T(8,128)(2,1)S(1)}, u32[]{:S(2)}, u32[]{:S(2)}) async-start(bf16[8,10,8,128]{3,2,1,0:T(8,128)(2,1)} %bitcast.4), calls=%async_computation.1 | async-start | bytes 327680 | tf_op jit(solution)/shard_map/all_to_all | solution.py:68
  25.3 7.9 %collective-permute-start.2 = (bf16[16,1024]{1,0:T(8,128)(2,1)S(1)}, bf16[16,1024]{1,0:T(8,128)(2,1)S(1)}, u32[]{:S(2)}, u32[]{:S(2)}) collective-permute-start(bf16[16,1024]{1,0:T(8,128)(2,1)S(1)} %copy-done.2), channel_id=1, source_target_pairs={{0,1},{1,0},{2,3},{3,2},{4,5},{5,4},{6,7},{7,6},{8,9},{9,8},{10,11... | collective-permute-start | bytes 98312 | tf_op jit(solution)/shard_map/ppermute | solution.py:483
  25.4 9.0 %copy-start.1 = (bf16[512,1024]{1,0:T(8,128)(2,1)S(1)}, bf16[512,1024]{1,0:T(8,128)(2,1)}, u32[]{:S(2)}) copy-start(bf16[512,1024]{1,0:T(8,128)(2,1)} %w_o_ref.1) | copy-start | bytes 3145732
  25.4 9.0 %copy-start.5 = (f32[1024]{0:T(1024)S(1)}, f32[1024]{0:T(1024)}, u32[]{:S(2)}) copy-start(f32[1024]{0:T(1024)} %param.20) | copy-start | bytes 12292
  33.1 1.2 %collective-permute-start.1 = (bf16[32,256]{1,0:T(8,128)(2,1)S(1)}, bf16[32,256]{1,0:T(8,128)(2,1)S(1)}, u32[]{:S(2)}, u32[]{:S(2)}) collective-permute-start(bf16[32,256]{1,0:T(8,128)(2,1)S(1)} %merge.1.mixed_ref), channel_id=1, source_target_pairs={{0,1},{1,0},{2,3},{3,2},{4,5},{5,4},{6,7},{7,6},{8,9},{9,8},{10,11... | collective-permute-start | bytes 49160 | tf_op jit(solution)/shard_map/ppermute | solution.py:589
  34.4 14.4 %copy-start = (bf16[1024,1024]{1,0:T(8,128)(2,1)S(1)}, bf16[1024,1024]{1,0:T(8,128)(2,1)}, u32[]{:S(2)}) copy-start(bf16[1024,1024]{1,0:T(8,128)(2,1)} %x_ref.1) | copy-start | bytes 6291460
  34.4 14.4 %copy-start.7 = (bf16[512,1024]{1,0:T(8,128)(2,1)S(1)}, bf16[512,1024]{1,0:T(8,128)(2,1)}, u32[]{:S(2)}) copy-start(bf16[512,1024]{1,0:T(8,128)(2,1)} %w_ref.1) | copy-start | bytes 3145732
  47.1 1.7 %collective-permute-start.3 = (bf16[256,512]{1,0:T(8,128)(2,1)S(1)}, bf16[256,512]{1,0:T(8,128)(2,1)S(1)}, u32[]{:S(2)}, u32[]{:S(2)}) collective-permute-start(bf16[256,512]{1,0:T(8,128)(2,1)S(1)} %bitcast.10), channel_id=1, source_target_pairs={{0,1},{1,0},{2,3},{3,2},{4,5},{5,4},{6,7},{7,6},{8,9},{9,8},{10,11... | collective-permute-start | bytes 786440 | tf_op jit(solution)/shard_map/ppermute | solution.py:597

commit v20 on v19

--- a/solution.py
+++ b/solution.py
@@ -167,7 +167,8 @@
     pairs_refs, out_ref = refs[:2], refs[2]
     me = lax.axis_index("dom")
     points, both = pairs_refs[0].shape
-    peers = out_ref.shape[0]
+    chips = out_ref.shape[0]
+    peers = 2 * chips
     width = both // 2
     heads = HEADS // 2
     size = width // heads
@@ -255,8 +256,8 @@
                 first_head, block[h * nodes : (h + 1) * nodes], block[(h + 1) * nodes : (h + 2) * nodes]
             )
             for n in range(2 * some):
-                place = start + n // 2
-                out_ref[place, 2 * i + n % 2] = slab(block, 0, n, tall).astype(bf16)
+                place = n // 2 * 2 * blocks + 2 * i + n % 2
+                out_ref[start // some, place] = slab(block, 0, n, tall).astype(bf16)
 
     row_lane = iota((tall, LANES), 1)
     for first in range(0, len(tops), 8):
@@ -267,44 +268,45 @@
         rest = jnp.zeros((LANES - 8 * len(parts), LANES), f32)
         columns = jnp.concatenate([*parts, rest], axis=0).T
         for g in range(8):
+            tile = jnp.zeros((tall, LANES), f32)
             for w in range(some):
-                tile = jnp.zeros((tall, LANES), f32)
                 for h in range(heads):
                     for late in range(2):
                         at = h * nodes + w * rows + late * tall
-                        move = late * (LANES // 2) + h - g
-                        here = (mod(row_lane, 8) == h) & (div(row_lane, LANES // 2) == late)
+                        to = w * heads + h
+                        here = (mod(row_lane, 8) == to) & (div(row_lane, LANES // 2) == late)
+                        move = late * (LANES // 2) + to - g
                         piece = pltpu.roll(columns[at : at + tall], move % LANES, 1)
                         tile = jnp.where(here, piece, tile)
-                out_ref[(first + g) * some + w, 2 * blocks] = tile.astype(bf16)
+            out_ref[first + g, some * 2 * blocks] = tile.astype(bf16)
 
 
 def merge_kernel(parts_ref, out_ref):
-    chips, windows, slabs, tall, _ = parts_ref.shape
-    half = out_ref.shape[1]
-    size = half // (HEADS // 2)
-    tile = parts_ref[:, :, slabs - 1].astype(f32)
+    heads, half = HEADS // 2, out_ref.shape[1]
+    size, blocks = half // heads, half // LANES
+    windows = (parts_ref.shape[1] - 1) // (2 * blocks)
+    tile = parts_ref[:, windows * 2 * blocks].astype(f32)
 
     def moved(columns):
-        return pltpu.roll(tile, LANES - columns, 3)
+        return pltpu.roll(tile, LANES - columns, 2)
 
     top = tile + moved(8) + moved(16)
     factor = jnp.exp2(top - jnp.max(top, axis=0, keepdims=True))
     factor = factor / jnp.sum((moved(24) + moved(32)) * factor, axis=0, keepdims=True)
-    head = div(iota(tile.shape, 3), size)
-    blocks = []
-    for i in range(half // LANES):
-        nodes = []
+    head = div(iota(tile.shape, 2), size)
+    nodes = []
+    for w in range(windows):
         for late in range(2):
-            wide = jnp.zeros(tile.shape, f32)
-            for h in range(LANES // size):
-                at = late * (LANES // 2) + i * (LANES // size) + h
-                wide = jnp.where(head == h, factor[..., at : at + 1], wide)
-            part = parts_ref[:, :, 2 * i + late].astype(f32)
-            nodes.append(jnp.sum(part * wide, axis=0))
-        blocks.append(jnp.concatenate(nodes, axis=1))
-    mixed = jnp.concatenate(blocks, axis=2)
-    out_ref[...] = mixed.reshape(windows * 2 * tall, half).astype(bf16)
+            line = []
+            for i in range(blocks):
+                wide = jnp.zeros(tile.shape, f32)
+                for h in range(LANES // size):
+                    at = late * (LANES // 2) + w * heads + i * (LANES // size) + h
+                    wide = jnp.where(head == h, factor[..., at : at + 1], wide)
+                part = parts_ref[:, w * 2 * blocks + 2 * i + late].astype(f32)
+                line.append(jnp.sum(part * wide, axis=0))
+            nodes.append(jnp.concatenate(line, axis=1))
+    out_ref[...] = jnp.concatenate(nodes, axis=0).astype(bf16)
 
 
 def combine_kernel(
@@ -525,15 +527,14 @@
         functools.partial(partial_kernel, cap, rows, edges),
         in_specs=[vmem] * 3,
         out_specs=vmem,
-        out_shape=pltpu.VMEM(sent, bf16),
+        out_shape=pltpu.VMEM((peers // 2, 2 * sent[1] - 1, *sent[2:]), bf16),
         compiler_params=params(40),
         cost_estimate=cost(4 * entries * points * width, 4 * points * width),
         name="partial",
     )(asked, *map(in_vmem, pairs))
     parts, dec_need, dec_slot = lax.optimization_barrier((parts, dec_need, dec_slot))
     same_core = [list(range(c, peers, 2)) for c in range(2)]
-    parts = parts.reshape(peers // 2, 2 * sent[1], *sent[2:])
-    parts = exchange(parts, same_core).reshape(peers // 2, 2, *sent[1:])
+    parts = exchange(parts, same_core)
 
     slot_total = dec_need.shape[1]
     edge_count = dec_slot.shape[0]

time: 53 us -> 52.9 us (level)
  no operation moved by 1% of the time
where the time goes in v20:
time: 52.9 us; the launch traced here: 52.5 us
  Pallas kernels  19.8 us (37%)
  blocking collectives  12.1 us (23%)
  starting transfers between devices  11.1 us (21%)
  waiting for transfers between devices  8.48 us (16%)
  between operations  0.97 us (2%)
    all_to_all x1, blocking collectives, exchange(): lax.all_to_all(blocks, 'dom', split_axis=0, concat_axis=0, tiled=True, ax...  12.1 us
    all_to_all x2, starting transfers between devices, exchange(): lax.all_to_all(blocks, 'dom', split_axis=0, concat_axis=0, tiled=True, ax...  10.4 us
    all_to_all x2, waiting for transfers between devices, exchange(): lax.all_to_all(blocks, 'dom', split_axis=0, concat_axis=0, tiled=True, ax...  7.31 us
    pallas_call x1, Pallas kernels, on_device(): pl.pallas_call(functools.partial(front_kernel, steps), in_specs=[hbm] * 4...  4.74 us
    pallas_call x1, Pallas kernels, on_device(): pl.pallas_call(functools.partial(middle_kernel, steps, peers, rows), in_s...  3.63 us
    pallas_call x1, Pallas kernels, on_device(): pl.pallas_call(functools.partial(other_kernel, steps), in_specs=[vmem] *...  3.61 us
    pallas_call x1, Pallas kernels, on_device(): pl.pallas_call(functools.partial(partial_kernel, cap, rows, edges), in_sp...  2.86 us
    pallas_call x1, Pallas kernels, on_device(): pl.pallas_call(ask_kernel, in_specs=[hbm] * len(ask_inputs), out_specs=vm...  2.31 us
  transfers between devices with their start and end apart: 6, of which 3 were waited for; matrix products, arithmetic and copies ran while one was open for 0% of the time, Pallas kernels for 24%

profile of v20, /device:TPU:0, one launch (start us, length us, event | category | flops | bytes accessed | tf_op | source)
XLA Modules:
  0.0 52.5 jit_solution(12291885471822301311)
XLA Ops:
  0.6 0.5 collective-permute-start
  1.1 2.3 %ask.1 = bf16[16,5,8,128]{3,2,1,0:T(8,128)(2,1)} custom-call(bf16[1024,512]{1,0:T(8,128)(2,1)} %refs_0_.1, bf16[16,1024]{1,0:T(8,128)(2,1)} %latent_ref.1, f32[1,1024]{1,0:T(1,128)} %bitcast.14, s32[16,32]{1,0:T(8,128)} %bitcast.13, s32[1,16]{1,0:T(1,128)} %bitcast.15, s32[1,512]{1,0:T(1,128)} %refs_5_.1), custom_call_target="tpu_custom_call" | custom-call | flops 16777216 | bytes 1048576 | tf_op jit(solution)/shard_map/ask/pallas_call | solution.py:494
  3.5 7.1 %all-to-all-start = ((bf16[16,5,8,128]{3,2,1,0:T(8,128)(2,1)}), bf16[16,5,8,128]{3,2,1,0:T(8,128)(2,1)S(1)}, u32[]{:S(2)}, u32[]{:S(2)}) async-start(bf16[16,5,8,128]{3,2,1,0:T(8,128)(2,1)} %ask.1), calls=%async_computation | async-start | bytes 327680 | tf_op jit(solution)/shard_map/all_to_all | solution.py:68
  10.5 0.0 collective-permute-done.other_hbm
  10.5 4.7 %front.1 = (bf16[1024,512]{1,0:T(8,128)(2,1)S(1)}, bf16[1024,512]{1,0:T(8,128)(2,1)S(1)}) custom-call(f32[1,1024]{1,0:T(1,128)} %bitcast.11, bf16[1024,1024]{1,0:T(8,128)(2,1)} %x_ref.1, bf16[1024,1024]{1,0:T(8,128)(2,1)} %collective-permute-done.other_hbm, bf16[1024,1024]{1,0:T(8,128)(2,1)} %w_hbm.2), custom_call_target="tpu_custom_call" | custom-call | flops 2147483648 | bytes 8388608 | tf_op jit(solution)/shard_map/front/pallas_call | solution.py:509
  15.3 3.7 %all-to-all-done.asked_ref = bf16[16,5,8,128]{3,2,1,0:T(8,128)(2,1)S(1)} async-done(((bf16[16,5,8,128]{3,2,1,0:T(8,128)(2,1)}), bf16[16,5,8,128]{3,2,1,0:T(8,128)(2,1)S(1)}, u32[]{:S(2)}, u32[]{:S(2)}) %all-to-all-start) | async-done | bytes 163872 | tf_op jit(solution)/shard_map/all_to_all | solution.py:68
  19.0 0.0 copy-start.2
  19.0 0.0 copy-start.3
  19.0 0.0 copy-start.4
  19.0 0.0 copy-start.6
  19.0 2.9 %partial.1 = bf16[8,9,8,128]{3,2,1,0:T(8,128)(2,1)} custom-call(bf16[16,5,8,128]{3,2,1,0:T(8,128)(2,1)S(1)} %all-to-all-done.asked_ref, bf16[1024,512]{1,0:T(8,128)(2,1)S(1)} %get-tuple-element.17.refs_0_, bf16[1024,512]{1,0:T(8,128)(2,1)S(1)} %get-tuple-element.18.refs_1_), custom_call_target="tpu_custom_call" | custom-call | flops 1073741824 | bytes 2097152 | tf_op jit(solution)/shard_map/partial/pallas_call | solution.py:526
  21.9 3.4 %all-to-all-start.1 = ((bf16[8,9,8,128]{3,2,1,0:T(8,128)(2,1)}), bf16[8,9,8,128]{3,2,1,0:T(8,128)(2,1)S(1)}, u32[]{:S(2)}, u32[]{:S(2)}) async-start(bf16[8,9,8,128]{3,2,1,0:T(8,128)(2,1)} %partial.1), calls=%async_computation.1 | async-start | bytes 294912 | tf_op jit(solution)/shard_map/all_to_all | solution.py:68
  25.3 0.0 copy-done.2
  25.3 0.1 collective-permute-start.2
  25.3 0.0 copy-done.3
  25.4 0.0 copy-done.4
  25.4 0.0 copy-done.6
  25.4 0.0 copy-start.1
  25.4 0.0 copy-start.5
  25.4 3.6 %middle.1 = (bf16[512,1024]{1,0:T(8,128)(2,1)S(1)}, s32[4,1024]{1,0:T(4,128)S(1)}, bf16[1024,512]{1,0:T(8,128)(2,1)S(1)}) custom-call(f32[1,1024]{1,0:T(1,128)S(1)} %bitcast.12, s32[32,128]{1,0:T(8,128)S(1)} %bitcast.9, s32[4,1024]{1,0:T(4,128)S(1)} %copy-done.4, bf16[1024,1024]{1,0:T(8,128)(2,1)} %x_ref.1, bf16[1024,512]{1,0:T(8,128)(2,1)} %w_hbm.3, ...), custom_call_target="tpu_custom_call" | custom-call | flops 1073741824 | bytes 8388608 | tf_op jit(solution)/shard_map/middle/pallas_call | solution.py:541
  29.0 3.6 %all-to-all-done.1.parts_ref = bf16[8,9,8,128]{3,2,1,0:T(8,128)(2,1)S(1)} async-done(((bf16[8,9,8,128]{3,2,1,0:T(8,128)(2,1)}), bf16[8,9,8,128]{3,2,1,0:T(8,128)(2,1)S(1)}, u32[]{:S(2)}, u32[]{:S(2)}) %all-to-all-start.1) | async-done | bytes 147488 | tf_op jit(solution)/shard_map/all_to_all | solution.py:68
  32.7 0.3 merge.1.mixed_ref
  33.0 0.1 collective-permute-start.1
  33.1 0.0 collective-permute-done.2.other_latent_ref
  33.1 1.2 %collective-permute-done.1.other_mixed_ref = bf16[32,256]{1,0:T(8,128)(2,1)S(1)} collective-permute-done((bf16[32,256]{1,0:T(8,128)(2,1)S(1)}, bf16[32,256]{1,0:T(8,128)(2,1)S(1)}, u32[]{:S(2)}, u32[]{:S(2)}) %collective-permute-start.1) | collective-permute-done | bytes 16416 | tf_op jit(solution)/shard_map/ppermute | solution.py:590
  34.2 0.0 copy-done.1
  34.2 0.0 copy-done.5
  34.2 0.0 copy-start
  34.2 0.0 copy-start.7
  34.3 0.6 %combine.1 = (bf16[16,1024]{1,0:T(8,128)(2,1)S(1)}, bf16[8,32,512]{2,1,0:T(8,128)(2,1)S(1)}) custom-call(bf16[32,256]{1,0:T(8,128)(2,1)S(1)} %merge.1.mixed_ref, bf16[32,256]{1,0:T(8,128)(2,1)S(1)} %collective-permute-done.1.other_mixed_ref, bf16[16,1024]{1,0:T(8,128)(2,1)S(1)} %copy-done.2, bf16[16,1024]{1,0:T(8,128)(2,1)S(1)} %collective-permute-done.2.other_latent_ref, ...), custom_call_target="tpu_custom_call" | custom-call | flops 50331648 | bytes 3145728 | tf_op jit(solution)/shard_map/combine/pallas_call | solution.py:577
  34.9 12.1 %all_to_all.15 = bf16[8,32,512]{2,1,0:T(8,128)(2,1)S(1)} all-to-all(bf16[8,32,512]{2,1,0:T(8,128)(2,1)S(1)} %get-tuple-element.26), channel_id=1, replica_groups={{0,2,4,6,8,10,12,14},{1,3,5,7,9,11,13,15},{16,18,20,22,24,26,28,30},{17..., dimensions={0} | all-to-all | bytes 524288 | tf_op jit(solution)/shard_map/all_to_all | solution.py:68
  47.0 0.0 collective-permute-start.3
  47.0 1.7 %own.1.own_ref = bf16[1024,256]{1,0:T(8,128)(2,1)S(1)} custom-call(bf16[256,512]{1,0:T(8,128)(2,1)S(1)} %bitcast.8, s32[4,1024]{1,0:T(4,128)S(1)} %get-tuple-element.27.node_ref, bf16[512,1024]{1,0:T(8,128)(2,1)S(1)} %get-tuple-element.28.query_ref), custom_call_target="tpu_custom_call" | custom-call | flops 536870912 | bytes 2097152 | tf_op jit(solution)/shard_map/own/pallas_call | solution.py:601
  48.6 0.0 collective-permute-done.3.pairs_ref
  48.7 0.0 copy-done
  48.7 0.0 copy-done.7
  48.7 3.6 %other.1 = (bf16[1024,1024]{1,0:T(8,128)(2,1)}, bf16[16,1024]{1,0:T(8,128)(2,1)}) custom-call(bf16[256,512]{1,0:T(8,128)(2,1)S(1)} %collective-permute-done.3.pairs_ref, bf16[1024,256]{1,0:T(8,128)(2,1)S(1)} %own.1.own_ref, s32[4,1024]{1,0:T(4,128)S(1)} %get-tuple-element.27.node_ref, bf16[512,1024]{1,0:T(8,128)(2,1)S(1)} %get-tuple-element.28.query_ref, ...), custom_call_target="tpu_custom_call" | custom-call | flops 2147483648 | bytes 8388608 | tf_op jit(solution)/shard_map/other/pallas_call | solution.py:609
Async XLA Ops:
  0.6 9.9 %collective-permute-start = (bf16[1024,1024]{1,0:T(8,128)(2,1)}, bf16[1024,1024]{1,0:T(8,128)(2,1)}, u32[]{:S(2)}, u32[]{:S(2)}) collective-permute-start(bf16[1024,1024]{1,0:T(8,128)(2,1)} %x_ref.1), channel_id=1, source_target_pairs={{0,1},{1,0},{2,3},{3,2},{4,5},{5,4},{6,7},{7,6},{8,9},{9,8},{10,11... | collective-permute-start | bytes 6291464 | tf_op jit(solution)/shard_map/ppermute | solution.py:484
  3.5 15.5 %all-to-all-start = ((bf16[16,5,8,128]{3,2,1,0:T(8,128)(2,1)}), bf16[16,5,8,128]{3,2,1,0:T(8,128)(2,1)S(1)}, u32[]{:S(2)}, u32[]{:S(2)}) async-start(bf16[16,5,8,128]{3,2,1,0:T(8,128)(2,1)} %ask.1), calls=%async_computation | async-start | bytes 327680 | tf_op jit(solution)/shard_map/all_to_all | solution.py:68
  19.0 6.3 %copy-start.2 = (bf16[16,1024]{1,0:T(8,128)(2,1)S(1)}, bf16[16,1024]{1,0:T(8,128)(2,1)}, u32[]{:S(2)}) copy-start(bf16[16,1024]{1,0:T(8,128)(2,1)} %latent_ref.1) | copy-start | bytes 98308
  19.0 6.3 %copy-start.3 = (s32[1,4096]{1,0:T(1,128)S(1)}, s32[1,4096]{1,0:T(1,128)}, u32[]{:S(2)}) copy-start(s32[1,4096]{1,0:T(1,128)} %param.30) | copy-start | bytes 49156
  19.0 6.4 %copy-start.4 = (s32[4,1024]{1,0:T(4,128)S(1)}, s32[4,1024]{1,0:T(4,128)}, u32[]{:S(2)}) copy-start(s32[4,1024]{1,0:T(4,128)} %slot_ref) | copy-start | bytes 49156
  19.0 6.4 %copy-start.6 = (f32[1024]{0:T(1024)S(1)}, f32[1024]{0:T(1024)}, u32[]{:S(2)}) copy-start(f32[1024]{0:T(1024)} %param.18) | copy-start | bytes 12292
  21.9 10.8 %all-to-all-start.1 = ((bf16[8,9,8,128]{3,2,1,0:T(8,128)(2,1)}), bf16[8,9,8,128]{3,2,1,0:T(8,128)(2,1)S(1)}, u32[]{:S(2)}, u32[]{:S(2)}) async-start(bf16[8,9,8,128]{3,2,1,0:T(8,128)(2,1)} %partial.1), calls=%async_computation.1 | async-start | bytes 294912 | tf_op jit(solution)/shard_map/all_to_all | solution.py:68
  25.3 7.8 %collective-permute-start.2 = (bf16[16,1024]{1,0:T(8,128)(2,1)S(1)}, bf16[16,1024]{1,0:T(8,128)(2,1)S(1)}, u32[]{:S(2)}, u32[]{:S(2)}) collective-permute-start(bf16[16,1024]{1,0:T(8,128)(2,1)S(1)} %copy-done.2), channel_id=1, source_target_pairs={{0,1},{1,0},{2,3},{3,2},{4,5},{5,4},{6,7},{7,6},{8,9},{9,8},{10,11... | collective-permute-start | bytes 98312 | tf_op jit(solution)/shard_map/ppermute | solution.py:485
  25.4 8.9 %copy-start.1 = (bf16[512,1024]{1,0:T(8,128)(2,1)S(1)}, bf16[512,1024]{1,0:T(8,128)(2,1)}, u32[]{:S(2)}) copy-start(bf16[512,1024]{1,0:T(8,128)(2,1)} %w_o_ref.1) | copy-start | bytes 3145732
  25.4 8.9 %copy-start.5 = (f32[1024]{0:T(1024)S(1)}, f32[1024]{0:T(1024)}, u32[]{:S(2)}) copy-start(f32[1024]{0:T(1024)} %param.20) | copy-start | bytes 12292
  33.0 1.2 %collective-permute-start.1 = (bf16[32,256]{1,0:T(8,128)(2,1)S(1)}, bf16[32,256]{1,0:T(8,128)(2,1)S(1)}, u32[]{:S(2)}, u32[]{:S(2)}) collective-permute-start(bf16[32,256]{1,0:T(8,128)(2,1)S(1)} %merge.1.mixed_ref), channel_id=1, source_target_pairs={{0,1},{1,0},{2,3},{3,2},{4,5},{5,4},{6,7},{7,6},{8,9},{9,8},{10,11... | collective-permute-start | bytes 49160 | tf_op jit(solution)/shard_map/ppermute | solution.py:590
  34.2 14.4 %copy-start = (bf16[1024,1024]{1,0:T(8,128)(2,1)S(1)}, bf16[1024,1024]{1,0:T(8,128)(2,1)}, u32[]{:S(2)}) copy-start(bf16[1024,1024]{1,0:T(8,128)(2,1)} %x_ref.1) | copy-start | bytes 6291460
  34.2 14.4 %copy-start.7 = (bf16[512,1024]{1,0:T(8,128)(2,1)S(1)}, bf16[512,1024]{1,0:T(8,128)(2,1)}, u32[]{:S(2)}) copy-start(bf16[512,1024]{1,0:T(8,128)(2,1)} %w_ref.1) | copy-start | bytes 3145732
  47.0 1.7 %collective-permute-start.3 = (bf16[256,512]{1,0:T(8,128)(2,1)S(1)}, bf16[256,512]{1,0:T(8,128)(2,1)S(1)}, u32[]{:S(2)}, u32[]{:S(2)}) collective-permute-start(bf16[256,512]{1,0:T(8,128)(2,1)S(1)} %bitcast.7), channel_id=1, source_target_pairs={{0,1},{1,0},{2,3},{3,2},{4,5},{5,4},{6,7},{7,6},{8,9},{9,8},{10,11... | collective-permute-start | bytes 786440 | tf_op jit(solution)/shard_map/ppermute | solution.py:598

commit v21 on v20

--- a/solution.py
+++ b/solution.py
@@ -58,6 +58,15 @@
     for copy in copies:
         copy.start()
     return copies
+
+
+def split_copy(source, target, sems, count):
+    rows = target.shape[0] // count
+    parts = [pl.ds(i * rows, rows) for i in range(count)]
+    return [
+        pltpu.make_async_copy(source.at[part], target.at[part], sems.at[i])
+        for i, part in enumerate(parts)
+    ]
 
 
 def cost(flops, read, exps=0):
@@ -337,7 +346,7 @@
 ):
     copies = started(
         pltpu.make_async_copy(w_hbm, w_ref, sems.at[0]),
-        pltpu.make_async_copy(x_hbm, x_ref, sems.at[1]),
+        *split_copy(x_hbm, x_ref, sems.at[pl.ds(4, 2)], 2),
     )
     half = w_kv_ref.shape[1] // 2
     core = lax.axis_index("dom") & 1
@@ -363,9 +372,10 @@
         own = mod(slots, LANES) == iota((LANES, points), 0)
         found = jnp.sum(jnp.where(own, listed, 0.0), axis=0, keepdims=True).astype(jnp.int32)
         node_ref[j : j + 1, :] = div(slots, cap) * rows + found
-    for copy in copies:
-        copy.wait()
+    copies[0].wait()
     for i in range(steps):
+        if i * 2 % steps == 0:
+            copies[1 + i * 2 // steps].wait()
         part = pl.ds(i * block, block)
         queries = dot(normed(x_ref[part, :], gain_ref[...]), w_ref[...])
         query_ref[:, part] = queries.T.astype(bf16)
@@ -550,7 +560,7 @@
         scratch_shapes=[
             pltpu.VMEM((points, depth), bf16),
             pltpu.VMEM((depth, width), bf16),
-            pltpu.SemaphoreType.DMA((4,)),
+            pltpu.SemaphoreType.DMA((6,)),
         ],
         compiler_params=params(40),
         cost_estimate=cost(2 * points * depth * width, 8 * points * depth),

time: 52.9 us -> 52.9 us (level)
  no operation moved by 1% of the time
where the time goes in v21:
time: 52.9 us; the launch traced here: 52.5 us
  Pallas kernels  19.6 us (37%)
  blocking collectives  12.1 us (23%)
  starting transfers between devices  11.1 us (21%)
  waiting for transfers between devices  8.64 us (16%)
  between operations  0.97 us (2%)
    all_to_all x1, blocking collectives, exchange(): lax.all_to_all(blocks, 'dom', split_axis=0, concat_axis=0, tiled=True, ax...  12.1 us
    all_to_all x2, starting transfers between devices, exchange(): lax.all_to_all(blocks, 'dom', split_axis=0, concat_axis=0, tiled=True, ax...  10.4 us
    all_to_all x2, waiting for transfers between devices, exchange(): lax.all_to_all(blocks, 'dom', split_axis=0, concat_axis=0, tiled=True, ax...  7.47 us
    pallas_call x1, Pallas kernels, on_device(): pl.pallas_call(functools.partial(front_kernel, steps), in_specs=[hbm] * 4...  4.74 us
    pallas_call x1, Pallas kernels, on_device(): pl.pallas_call(functools.partial(other_kernel, steps), in_specs=[vmem] *...  3.61 us
    pallas_call x1, Pallas kernels, on_device(): pl.pallas_call(functools.partial(middle_kernel, steps, peers, rows), in_s...  3.47 us
    pallas_call x1, Pallas kernels, on_device(): pl.pallas_call(functools.partial(partial_kernel, cap, rows, edges), in_sp...  2.86 us
    pallas_call x1, Pallas kernels, on_device(): pl.pallas_call(ask_kernel, in_specs=[hbm] * len(ask_inputs), out_specs=vm...  2.31 us
  transfers between devices with their start and end apart: 6, of which 3 were waited for; matrix products, arithmetic and copies ran while one was open for 0% of the time, Pallas kernels for 24%

profile of v21, /device:TPU:0, one launch (start us, length us, event | category | flops | bytes accessed | tf_op | source)
XLA Modules:
  0.0 52.5 jit_solution(8041741746229024337)
XLA Ops:
  0.6 0.5 collective-permute-start
  1.1 2.3 %ask.1 = bf16[16,5,8,128]{3,2,1,0:T(8,128)(2,1)} custom-call(bf16[1024,512]{1,0:T(8,128)(2,1)} %refs_0_.1, bf16[16,1024]{1,0:T(8,128)(2,1)} %latent_ref.1, f32[1,1024]{1,0:T(1,128)} %bitcast.14, s32[16,32]{1,0:T(8,128)} %bitcast.13, s32[1,16]{1,0:T(1,128)} %bitcast.15, s32[1,512]{1,0:T(1,128)} %refs_5_.1), custom_call_target="tpu_custom_call" | custom-call | flops 16777216 | bytes 1048576 | tf_op jit(solution)/shard_map/ask/pallas_call | solution.py:504
  3.5 7.1 %all-to-all-start = ((bf16[16,5,8,128]{3,2,1,0:T(8,128)(2,1)}), bf16[16,5,8,128]{3,2,1,0:T(8,128)(2,1)S(1)}, u32[]{:S(2)}, u32[]{:S(2)}) async-start(bf16[16,5,8,128]{3,2,1,0:T(8,128)(2,1)} %ask.1), calls=%async_computation | async-start | bytes 327680 | tf_op jit(solution)/shard_map/all_to_all | solution.py:77
  10.5 0.0 collective-permute-done.other_hbm
  10.5 4.7 %front.1 = (bf16[1024,512]{1,0:T(8,128)(2,1)S(1)}, bf16[1024,512]{1,0:T(8,128)(2,1)S(1)}) custom-call(f32[1,1024]{1,0:T(1,128)} %bitcast.11, bf16[1024,1024]{1,0:T(8,128)(2,1)} %x_ref.1, bf16[1024,1024]{1,0:T(8,128)(2,1)} %collective-permute-done.other_hbm, bf16[1024,1024]{1,0:T(8,128)(2,1)} %w_hbm.2), custom_call_target="tpu_custom_call" | custom-call | flops 2147483648 | bytes 8388608 | tf_op jit(solution)/shard_map/front/pallas_call | solution.py:519
  15.3 3.7 %all-to-all-done.asked_ref = bf16[16,5,8,128]{3,2,1,0:T(8,128)(2,1)S(1)} async-done(((bf16[16,5,8,128]{3,2,1,0:T(8,128)(2,1)}), bf16[16,5,8,128]{3,2,1,0:T(8,128)(2,1)S(1)}, u32[]{:S(2)}, u32[]{:S(2)}) %all-to-all-start) | async-done | bytes 163872 | tf_op jit(solution)/shard_map/all_to_all | solution.py:77
  19.0 0.0 copy-start.2
  19.0 0.0 copy-start.3
  19.0 0.0 copy-start.4
  19.0 0.0 copy-start.6
  19.0 2.9 %partial.1 = bf16[8,9,8,128]{3,2,1,0:T(8,128)(2,1)} custom-call(bf16[16,5,8,128]{3,2,1,0:T(8,128)(2,1)S(1)} %all-to-all-done.asked_ref, bf16[1024,512]{1,0:T(8,128)(2,1)S(1)} %get-tuple-element.17.refs_0_, bf16[1024,512]{1,0:T(8,128)(2,1)S(1)} %get-tuple-element.18.refs_1_), custom_call_target="tpu_custom_call" | custom-call | flops 1073741824 | bytes 2097152 | tf_op jit(solution)/shard_map/partial/pallas_call | solution.py:536
  21.9 3.4 %all-to-all-start.1 = ((bf16[8,9,8,128]{3,2,1,0:T(8,128)(2,1)}), bf16[8,9,8,128]{3,2,1,0:T(8,128)(2,1)S(1)}, u32[]{:S(2)}, u32[]{:S(2)}) async-start(bf16[8,9,8,128]{3,2,1,0:T(8,128)(2,1)} %partial.1), calls=%async_computation.1 | async-start | bytes 294912 | tf_op jit(solution)/shard_map/all_to_all | solution.py:77
  25.3 0.0 copy-done.2
  25.3 0.1 collective-permute-start.2
  25.3 0.0 copy-done.3
  25.4 0.0 copy-done.4
  25.4 0.0 copy-done.6
  25.4 0.0 copy-start.1
  25.4 0.0 copy-start.5
  25.4 3.5 %middle.1 = (bf16[512,1024]{1,0:T(8,128)(2,1)S(1)}, s32[4,1024]{1,0:T(4,128)S(1)}, bf16[1024,512]{1,0:T(8,128)(2,1)S(1)}) custom-call(f32[1,1024]{1,0:T(1,128)S(1)} %bitcast.12, s32[32,128]{1,0:T(8,128)S(1)} %bitcast.9, s32[4,1024]{1,0:T(4,128)S(1)} %copy-done.4, bf16[1024,1024]{1,0:T(8,128)(2,1)} %x_ref.1, bf16[1024,512]{1,0:T(8,128)(2,1)} %w_hbm.3, ...), custom_call_target="tpu_custom_call" | custom-call | flops 1073741824 | bytes 8388608 | tf_op jit(solution)/shard_map/middle/pallas_call | solution.py:551
  28.9 3.8 %all-to-all-done.1.parts_ref = bf16[8,9,8,128]{3,2,1,0:T(8,128)(2,1)S(1)} async-done(((bf16[8,9,8,128]{3,2,1,0:T(8,128)(2,1)}), bf16[8,9,8,128]{3,2,1,0:T(8,128)(2,1)S(1)}, u32[]{:S(2)}, u32[]{:S(2)}) %all-to-all-start.1) | async-done | bytes 147488 | tf_op jit(solution)/shard_map/all_to_all | solution.py:77
  32.7 0.3 merge.1.mixed_ref
  33.0 0.1 collective-permute-start.1
  33.1 0.0 collective-permute-done.2.other_latent_ref
  33.1 1.2 %collective-permute-done.1.other_mixed_ref = bf16[32,256]{1,0:T(8,128)(2,1)S(1)} collective-permute-done((bf16[32,256]{1,0:T(8,128)(2,1)S(1)}, bf16[32,256]{1,0:T(8,128)(2,1)S(1)}, u32[]{:S(2)}, u32[]{:S(2)}) %collective-permute-start.1) | collective-permute-done | bytes 16416 | tf_op jit(solution)/shard_map/ppermute | solution.py:600
  34.2 0.0 copy-done.1
  34.2 0.0 copy-done.5
  34.2 0.0 copy-start
  34.2 0.0 copy-start.7
  34.3 0.6 %combine.1 = (bf16[16,1024]{1,0:T(8,128)(2,1)S(1)}, bf16[8,32,512]{2,1,0:T(8,128)(2,1)S(1)}) custom-call(bf16[32,256]{1,0:T(8,128)(2,1)S(1)} %merge.1.mixed_ref, bf16[32,256]{1,0:T(8,128)(2,1)S(1)} %collective-permute-done.1.other_mixed_ref, bf16[16,1024]{1,0:T(8,128)(2,1)S(1)} %copy-done.2, bf16[16,1024]{1,0:T(8,128)(2,1)S(1)} %collective-permute-done.2.other_latent_ref, ...), custom_call_target="tpu_custom_call" | custom-call | flops 50331648 | bytes 3145728 | tf_op jit(solution)/shard_map/combine/pallas_call | solution.py:587
  34.9 12.1 %all_to_all.15 = bf16[8,32,512]{2,1,0:T(8,128)(2,1)S(1)} all-to-all(bf16[8,32,512]{2,1,0:T(8,128)(2,1)S(1)} %get-tuple-element.26), channel_id=1, replica_groups={{0,2,4,6,8,10,12,14},{1,3,5,7,9,11,13,15},{16,18,20,22,24,26,28,30},{17..., dimensions={0} | all-to-all | bytes 524288 | tf_op jit(solution)/shard_map/all_to_all | solution.py:77
  47.0 0.0 collective-permute-start.3
  47.0 1.7 %own.1.own_ref = bf16[1024,256]{1,0:T(8,128)(2,1)S(1)} custom-call(bf16[256,512]{1,0:T(8,128)(2,1)S(1)} %bitcast.8, s32[4,1024]{1,0:T(4,128)S(1)} %get-tuple-element.27.node_ref, bf16[512,1024]{1,0:T(8,128)(2,1)S(1)} %get-tuple-element.28.query_ref), custom_call_target="tpu_custom_call" | custom-call | flops 536870912 | bytes 2097152 | tf_op jit(solution)/shard_map/own/pallas_call | solution.py:611
  48.6 0.0 collective-permute-done.3.pairs_ref
  48.7 0.0 copy-done
  48.7 0.0 copy-done.7
  48.7 3.6 %other.1 = (bf16[1024,1024]{1,0:T(8,128)(2,1)}, bf16[16,1024]{1,0:T(8,128)(2,1)}) custom-call(bf16[256,512]{1,0:T(8,128)(2,1)S(1)} %collective-permute-done.3.pairs_ref, bf16[1024,256]{1,0:T(8,128)(2,1)S(1)} %own.1.own_ref, s32[4,1024]{1,0:T(4,128)S(1)} %get-tuple-element.27.node_ref, bf16[512,1024]{1,0:T(8,128)(2,1)S(1)} %get-tuple-element.28.query_ref, ...), custom_call_target="tpu_custom_call" | custom-call | flops 2147483648 | bytes 8388608 | tf_op jit(solution)/shard_map/other/pallas_call | solution.py:619
Async XLA Ops:
  0.6 9.9 %collective-permute-start = (bf16[1024,1024]{1,0:T(8,128)(2,1)}, bf16[1024,1024]{1,0:T(8,128)(2,1)}, u32[]{:S(2)}, u32[]{:S(2)}) collective-permute-start(bf16[1024,1024]{1,0:T(8,128)(2,1)} %x_ref.1), channel_id=1, source_target_pairs={{0,1},{1,0},{2,3},{3,2},{4,5},{5,4},{6,7},{7,6},{8,9},{9,8},{10,11... | collective-permute-start | bytes 6291464 | tf_op jit(solution)/shard_map/ppermute | solution.py:494
  3.5 15.5 %all-to-all-start = ((bf16[16,5,8,128]{3,2,1,0:T(8,128)(2,1)}), bf16[16,5,8,128]{3,2,1,0:T(8,128)(2,1)S(1)}, u32[]{:S(2)}, u32[]{:S(2)}) async-start(bf16[16,5,8,128]{3,2,1,0:T(8,128)(2,1)} %ask.1), calls=%async_computation | async-start | bytes 327680 | tf_op jit(solution)/shard_map/all_to_all | solution.py:77
  19.0 6.3 %copy-start.2 = (bf16[16,1024]{1,0:T(8,128)(2,1)S(1)}, bf16[16,1024]{1,0:T(8,128)(2,1)}, u32[]{:S(2)}) copy-start(bf16[16,1024]{1,0:T(8,128)(2,1)} %latent_ref.1) | copy-start | bytes 98308
  19.0 6.3 %copy-start.3 = (s32[1,4096]{1,0:T(1,128)S(1)}, s32[1,4096]{1,0:T(1,128)}, u32[]{:S(2)}) copy-start(s32[1,4096]{1,0:T(1,128)} %param.30) | copy-start | bytes 49156
  19.0 6.4 %copy-start.4 = (s32[4,1024]{1,0:T(4,128)S(1)}, s32[4,1024]{1,0:T(4,128)}, u32[]{:S(2)}) copy-start(s32[4,1024]{1,0:T(4,128)} %slot_ref) | copy-start | bytes 49156
  19.0 6.4 %copy-start.6 = (f32[1024]{0:T(1024)S(1)}, f32[1024]{0:T(1024)}, u32[]{:S(2)}) copy-start(f32[1024]{0:T(1024)} %param.18) | copy-start | bytes 12292
  21.9 10.8 %all-to-all-start.1 = ((bf16[8,9,8,128]{3,2,1,0:T(8,128)(2,1)}), bf16[8,9,8,128]{3,2,1,0:T(8,128)(2,1)S(1)}, u32[]{:S(2)}, u32[]{:S(2)}) async-start(bf16[8,9,8,128]{3,2,1,0:T(8,128)(2,1)} %partial.1), calls=%async_computation.1 | async-start | bytes 294912 | tf_op jit(solution)/shard_map/all_to_all | solution.py:77
  25.3 7.8 %collective-permute-start.2 = (bf16[16,1024]{1,0:T(8,128)(2,1)S(1)}, bf16[16,1024]{1,0:T(8,128)(2,1)S(1)}, u32[]{:S(2)}, u32[]{:S(2)}) collective-permute-start(bf16[16,1024]{1,0:T(8,128)(2,1)S(1)} %copy-done.2), channel_id=1, source_target_pairs={{0,1},{1,0},{2,3},{3,2},{4,5},{5,4},{6,7},{7,6},{8,9},{9,8},{10,11... | collective-permute-start | bytes 98312 | tf_op jit(solution)/shard_map/ppermute | solution.py:495
  25.4 8.9 %copy-start.1 = (bf16[512,1024]{1,0:T(8,128)(2,1)S(1)}, bf16[512,1024]{1,0:T(8,128)(2,1)}, u32[]{:S(2)}) copy-start(bf16[512,1024]{1,0:T(8,128)(2,1)} %w_o_ref.1) | copy-start | bytes 3145732
  25.4 8.9 %copy-start.5 = (f32[1024]{0:T(1024)S(1)}, f32[1024]{0:T(1024)}, u32[]{:S(2)}) copy-start(f32[1024]{0:T(1024)} %param.20) | copy-start | bytes 12292
  33.0 1.2 %collective-permute-start.1 = (bf16[32,256]{1,0:T(8,128)(2,1)S(1)}, bf16[32,256]{1,0:T(8,128)(2,1)S(1)}, u32[]{:S(2)}, u32[]{:S(2)}) collective-permute-start(bf16[32,256]{1,0:T(8,128)(2,1)S(1)} %merge.1.mixed_ref), channel_id=1, source_target_pairs={{0,1},{1,0},{2,3},{3,2},{4,5},{5,4},{6,7},{7,6},{8,9},{9,8},{10,11... | collective-permute-start | bytes 49160 | tf_op jit(solution)/shard_map/ppermute | solution.py:600
  34.2 14.4 %copy-start = (bf16[1024,1024]{1,0:T(8,128)(2,1)S(1)}, bf16[1024,1024]{1,0:T(8,128)(2,1)}, u32[]{:S(2)}) copy-start(bf16[1024,1024]{1,0:T(8,128)(2,1)} %x_ref.1) | copy-start | bytes 6291460
  34.2 14.4 %copy-start.7 = (bf16[512,1024]{1,0:T(8,128)(2,1)S(1)}, bf16[512,1024]{1,0:T(8,128)(2,1)}, u32[]{:S(2)}) copy-start(bf16[512,1024]{1,0:T(8,128)(2,1)} %w_ref.1) | copy-start | bytes 3145732
  47.0 1.7 %collective-permute-start.3 = (bf16[256,512]{1,0:T(8,128)(2,1)S(1)}, bf16[256,512]{1,0:T(8,128)(2,1)S(1)}, u32[]{:S(2)}, u32[]{:S(2)}) collective-permute-start(bf16[256,512]{1,0:T(8,128)(2,1)S(1)} %bitcast.7), channel_id=1, source_target_pairs={{0,1},{1,0},{2,3},{3,2},{4,5},{5,4},{6,7},{7,6},{8,9},{9,8},{10,11... | collective-permute-start | bytes 786440 | tf_op jit(solution)/shard_map/ppermute | solution.py:608

commit v22 on v21

--- a/solution.py
+++ b/solution.py
@@ -609,7 +609,7 @@
 
     queries = in_vmem(queries)
     own_mixed = pl.pallas_call(
-        functools.partial(own_kernel, steps),
+        functools.partial(own_kernel, 2 * steps),
         in_specs=[vmem] * 3,
         out_shape=jax.ShapeDtypeStruct((points, half), bf16),
         compiler_params=params(48),

time: 52.9 us -> 53.6 us (1.013)
  Pallas kernels: 19.6 us -> 20.4 us
    pallas_call x1, Pallas kernels: 1.66 us -> 2.46 us  [on_device(): pl.pallas_call(functools.partial(own_kernel, 2 * steps), in_specs=[vmem]...]
  transfers between devices with their start and end apart: 6 -> 6, of which waited for: 3 -> 3; matrix products, arithmetic and copies ran while one was open for 0% -> 0% of each run, Pallas kernels for 24% -> 25%
where the time goes in v22:
time: 53.6 us; the launch traced here: 53.2 us
  Pallas kernels  20.4 us (38%)
  blocking collectives  12.1 us (23%)
  starting transfers between devices  11.1 us (21%)
  waiting for transfers between devices  8.64 us (16%)
  between operations  0.97 us (2%)
    all_to_all x1, blocking collectives, exchange(): lax.all_to_all(blocks, 'dom', split_axis=0, concat_axis=0, tiled=True, ax...  12.1 us
    all_to_all x2, starting transfers between devices, exchange(): lax.all_to_all(blocks, 'dom', split_axis=0, concat_axis=0, tiled=True, ax...  10.4 us
    all_to_all x2, waiting for transfers between devices, exchange(): lax.all_to_all(blocks, 'dom', split_axis=0, concat_axis=0, tiled=True, ax...  7.47 us
    pallas_call x1, Pallas kernels, on_device(): pl.pallas_call(functools.partial(front_kernel, steps), in_specs=[hbm] * 4...  4.74 us
    pallas_call x1, Pallas kernels, on_device(): pl.pallas_call(functools.partial(other_kernel, steps), in_specs=[vmem] *...  3.61 us
    pallas_call x1, Pallas kernels, on_device(): pl.pallas_call(functools.partial(middle_kernel, steps, peers, rows), in_s...  3.47 us
    pallas_call x1, Pallas kernels, on_device(): pl.pallas_call(functools.partial(partial_kernel, cap, rows, edges), in_sp...  2.86 us
    pallas_call x1, Pallas kernels, on_device(): pl.pallas_call(functools.partial(own_kernel, 2 * steps), in_specs=[vmem]...  2.46 us
  transfers between devices with their start and end apart: 6, of which 3 were waited for; matrix products, arithmetic and copies ran while one was open for 0% of the time, Pallas kernels for 25%

profile of v22, /device:TPU:0, one launch (start us, length us, event | category | flops | bytes accessed | tf_op | source)
XLA Modules:
  0.0 53.2 jit_solution(11972140557353978121)
XLA Ops:
  0.6 0.5 collective-permute-start
  1.1 2.3 %ask.1 = bf16[16,5,8,128]{3,2,1,0:T(8,128)(2,1)} custom-call(bf16[1024,512]{1,0:T(8,128)(2,1)} %refs_0_.1, bf16[16,1024]{1,0:T(8,128)(2,1)} %latent_ref.1, f32[1,1024]{1,0:T(1,128)} %bitcast.14, s32[16,32]{1,0:T(8,128)} %bitcast.13, s32[1,16]{1,0:T(1,128)} %bitcast.15, s32[1,512]{1,0:T(1,128)} %refs_5_.1), custom_call_target="tpu_custom_call" | custom-call | flops 16777216 | bytes 1048576 | tf_op jit(solution)/shard_map/ask/pallas_call | solution.py:504
  3.5 7.1 %all-to-all-start = ((bf16[16,5,8,128]{3,2,1,0:T(8,128)(2,1)}), bf16[16,5,8,128]{3,2,1,0:T(8,128)(2,1)S(1)}, u32[]{:S(2)}, u32[]{:S(2)}) async-start(bf16[16,5,8,128]{3,2,1,0:T(8,128)(2,1)} %ask.1), calls=%async_computation | async-start | bytes 327680 | tf_op jit(solution)/shard_map/all_to_all | solution.py:77
  10.5 0.0 collective-permute-done.other_hbm
  10.5 4.7 %front.1 = (bf16[1024,512]{1,0:T(8,128)(2,1)S(1)}, bf16[1024,512]{1,0:T(8,128)(2,1)S(1)}) custom-call(f32[1,1024]{1,0:T(1,128)} %bitcast.11, bf16[1024,1024]{1,0:T(8,128)(2,1)} %x_ref.1, bf16[1024,1024]{1,0:T(8,128)(2,1)} %collective-permute-done.other_hbm, bf16[1024,1024]{1,0:T(8,128)(2,1)} %w_hbm.2), custom_call_target="tpu_custom_call" | custom-call | flops 2147483648 | bytes 8388608 | tf_op jit(solution)/shard_map/front/pallas_call | solution.py:519
  15.3 3.7 %all-to-all-done.asked_ref = bf16[16,5,8,128]{3,2,1,0:T(8,128)(2,1)S(1)} async-done(((bf16[16,5,8,128]{3,2,1,0:T(8,128)(2,1)}), bf16[16,5,8,128]{3,2,1,0:T(8,128)(2,1)S(1)}, u32[]{:S(2)}, u32[]{:S(2)}) %all-to-all-start) | async-done | bytes 163872 | tf_op jit(solution)/shard_map/all_to_all | solution.py:77
  19.0 0.0 copy-start.2
  19.0 0.0 copy-start.3
  19.0 0.0 copy-start.4
  19.0 0.0 copy-start.6
  19.0 2.9 %partial.1 = bf16[8,9,8,128]{3,2,1,0:T(8,128)(2,1)} custom-call(bf16[16,5,8,128]{3,2,1,0:T(8,128)(2,1)S(1)} %all-to-all-done.asked_ref, bf16[1024,512]{1,0:T(8,128)(2,1)S(1)} %get-tuple-element.17.refs_0_, bf16[1024,512]{1,0:T(8,128)(2,1)S(1)} %get-tuple-element.18.refs_1_), custom_call_target="tpu_custom_call" | custom-call | flops 1073741824 | bytes 2097152 | tf_op jit(solution)/shard_map/partial/pallas_call | solution.py:536
  21.9 3.4 %all-to-all-start.1 = ((bf16[8,9,8,128]{3,2,1,0:T(8,128)(2,1)}), bf16[8,9,8,128]{3,2,1,0:T(8,128)(2,1)S(1)}, u32[]{:S(2)}, u32[]{:S(2)}) async-start(bf16[8,9,8,128]{3,2,1,0:T(8,128)(2,1)} %partial.1), calls=%async_computation.1 | async-start | bytes 294912 | tf_op jit(solution)/shard_map/all_to_all | solution.py:77
  25.3 0.0 copy-done.2
  25.3 0.1 collective-permute-start.2
  25.3 0.0 copy-done.3
  25.4 0.0 copy-done.4
  25.4 0.0 copy-done.6
  25.4 0.0 copy-start.1
  25.4 0.0 copy-start.5
  25.4 3.5 %middle.1 = (bf16[512,1024]{1,0:T(8,128)(2,1)S(1)}, s32[4,1024]{1,0:T(4,128)S(1)}, bf16[1024,512]{1,0:T(8,128)(2,1)S(1)}) custom-call(f32[1,1024]{1,0:T(1,128)S(1)} %bitcast.12, s32[32,128]{1,0:T(8,128)S(1)} %bitcast.9, s32[4,1024]{1,0:T(4,128)S(1)} %copy-done.4, bf16[1024,1024]{1,0:T(8,128)(2,1)} %x_ref.1, bf16[1024,512]{1,0:T(8,128)(2,1)} %w_hbm.3, ...), custom_call_target="tpu_custom_call" | custom-call | flops 1073741824 | bytes 8388608 | tf_op jit(solution)/shard_map/middle/pallas_call | solution.py:551
  28.9 3.8 %all-to-all-done.1.parts_ref = bf16[8,9,8,128]{3,2,1,0:T(8,128)(2,1)S(1)} async-done(((bf16[8,9,8,128]{3,2,1,0:T(8,128)(2,1)}), bf16[8,9,8,128]{3,2,1,0:T(8,128)(2,1)S(1)}, u32[]{:S(2)}, u32[]{:S(2)}) %all-to-all-start.1) | async-done | bytes 147488 | tf_op jit(solution)/shard_map/all_to_all | solution.py:77
  32.7 0.3 merge.1.mixed_ref
  33.0 0.1 collective-permute-start.1
  33.1 0.0 collective-permute-done.2.other_latent_ref
  33.1 1.2 %collective-permute-done.1.other_mixed_ref = bf16[32,256]{1,0:T(8,128)(2,1)S(1)} collective-permute-done((bf16[32,256]{1,0:T(8,128)(2,1)S(1)}, bf16[32,256]{1,0:T(8,128)(2,1)S(1)}, u32[]{:S(2)}, u32[]{:S(2)}) %collective-permute-start.1) | collective-permute-done | bytes 16416 | tf_op jit(solution)/shard_map/ppermute | solution.py:600
  34.2 0.0 copy-done.1
  34.2 0.0 copy-done.5
  34.2 0.0 copy-start
  34.2 0.0 copy-start.7
  34.3 0.6 %combine.1 = (bf16[16,1024]{1,0:T(8,128)(2,1)S(1)}, bf16[8,32,512]{2,1,0:T(8,128)(2,1)S(1)}) custom-call(bf16[32,256]{1,0:T(8,128)(2,1)S(1)} %merge.1.mixed_ref, bf16[32,256]{1,0:T(8,128)(2,1)S(1)} %collective-permute-done.1.other_mixed_ref, bf16[16,1024]{1,0:T(8,128)(2,1)S(1)} %copy-done.2, bf16[16,1024]{1,0:T(8,128)(2,1)S(1)} %collective-permute-done.2.other_latent_ref, ...), custom_call_target="tpu_custom_call" | custom-call | flops 50331648 | bytes 3145728 | tf_op jit(solution)/shard_map/combine/pallas_call | solution.py:587
  34.9 12.1 %all_to_all.15 = bf16[8,32,512]{2,1,0:T(8,128)(2,1)S(1)} all-to-all(bf16[8,32,512]{2,1,0:T(8,128)(2,1)S(1)} %get-tuple-element.26), channel_id=1, replica_groups={{0,2,4,6,8,10,12,14},{1,3,5,7,9,11,13,15},{16,18,20,22,24,26,28,30},{17..., dimensions={0} | all-to-all | bytes 524288 | tf_op jit(solution)/shard_map/all_to_all | solution.py:77
  47.0 0.0 collective-permute-start.3
  47.0 2.5 %own.1.own_ref = bf16[1024,256]{1,0:T(8,128)(2,1)S(1)} custom-call(bf16[256,512]{1,0:T(8,128)(2,1)S(1)} %bitcast.8, s32[4,1024]{1,0:T(4,128)S(1)} %get-tuple-element.27.node_ref, bf16[512,1024]{1,0:T(8,128)(2,1)S(1)} %get-tuple-element.28.query_ref), custom_call_target="tpu_custom_call" | custom-call | flops 536870912 | bytes 2097152 | tf_op jit(solution)/shard_map/own/pallas_call | solution.py:611
  49.4 0.0 collective-permute-done.3.pairs_ref
  49.5 0.0 copy-done
  49.5 0.0 copy-done.7
  49.5 3.6 %other.1 = (bf16[1024,1024]{1,0:T(8,128)(2,1)}, bf16[16,1024]{1,0:T(8,128)(2,1)}) custom-call(bf16[256,512]{1,0:T(8,128)(2,1)S(1)} %collective-permute-done.3.pairs_ref, bf16[1024,256]{1,0:T(8,128)(2,1)S(1)} %own.1.own_ref, s32[4,1024]{1,0:T(4,128)S(1)} %get-tuple-element.27.node_ref, bf16[512,1024]{1,0:T(8,128)(2,1)S(1)} %get-tuple-element.28.query_ref, ...), custom_call_target="tpu_custom_call" | custom-call | flops 2147483648 | bytes 8388608 | tf_op jit(solution)/shard_map/other/pallas_call | solution.py:619
Async XLA Ops:
  0.6 9.9 %collective-permute-start = (bf16[1024,1024]{1,0:T(8,128)(2,1)}, bf16[1024,1024]{1,0:T(8,128)(2,1)}, u32[]{:S(2)}, u32[]{:S(2)}) collective-permute-start(bf16[1024,1024]{1,0:T(8,128)(2,1)} %x_ref.1), channel_id=1, source_target_pairs={{0,1},{1,0},{2,3},{3,2},{4,5},{5,4},{6,7},{7,6},{8,9},{9,8},{10,11... | collective-permute-start | bytes 6291464 | tf_op jit(solution)/shard_map/ppermute | solution.py:494
  3.5 15.5 %all-to-all-start = ((bf16[16,5,8,128]{3,2,1,0:T(8,128)(2,1)}), bf16[16,5,8,128]{3,2,1,0:T(8,128)(2,1)S(1)}, u32[]{:S(2)}, u32[]{:S(2)}) async-start(bf16[16,5,8,128]{3,2,1,0:T(8,128)(2,1)} %ask.1), calls=%async_computation | async-start | bytes 327680 | tf_op jit(solution)/shard_map/all_to_all | solution.py:77
  19.0 6.3 %copy-start.2 = (bf16[16,1024]{1,0:T(8,128)(2,1)S(1)}, bf16[16,1024]{1,0:T(8,128)(2,1)}, u32[]{:S(2)}) copy-start(bf16[16,1024]{1,0:T(8,128)(2,1)} %latent_ref.1) | copy-start | bytes 98308
  19.0 6.3 %copy-start.3 = (s32[1,4096]{1,0:T(1,128)S(1)}, s32[1,4096]{1,0:T(1,128)}, u32[]{:S(2)}) copy-start(s32[1,4096]{1,0:T(1,128)} %param.30) | copy-start | bytes 49156
  19.0 6.4 %copy-start.4 = (s32[4,1024]{1,0:T(4,128)S(1)}, s32[4,1024]{1,0:T(4,128)}, u32[]{:S(2)}) copy-start(s32[4,1024]{1,0:T(4,128)} %slot_ref) | copy-start | bytes 49156
  19.0 6.4 %copy-start.6 = (f32[1024]{0:T(1024)S(1)}, f32[1024]{0:T(1024)}, u32[]{:S(2)}) copy-start(f32[1024]{0:T(1024)} %param.18) | copy-start | bytes 12292
  21.9 10.8 %all-to-all-start.1 = ((bf16[8,9,8,128]{3,2,1,0:T(8,128)(2,1)}), bf16[8,9,8,128]{3,2,1,0:T(8,128)(2,1)S(1)}, u32[]{:S(2)}, u32[]{:S(2)}) async-start(bf16[8,9,8,128]{3,2,1,0:T(8,128)(2,1)} %partial.1), calls=%async_computation.1 | async-start | bytes 294912 | tf_op jit(solution)/shard_map/all_to_all | solution.py:77
  25.3 7.8 %collective-permute-start.2 = (bf16[16,1024]{1,0:T(8,128)(2,1)S(1)}, bf16[16,1024]{1,0:T(8,128)(2,1)S(1)}, u32[]{:S(2)}, u32[]{:S(2)}) collective-permute-start(bf16[16,1024]{1,0:T(8,128)(2,1)S(1)} %copy-done.2), channel_id=1, source_target_pairs={{0,1},{1,0},{2,3},{3,2},{4,5},{5,4},{6,7},{7,6},{8,9},{9,8},{10,11... | collective-permute-start | bytes 98312 | tf_op jit(solution)/shard_map/ppermute | solution.py:495
  25.4 8.9 %copy-start.1 = (bf16[512,1024]{1,0:T(8,128)(2,1)S(1)}, bf16[512,1024]{1,0:T(8,128)(2,1)}, u32[]{:S(2)}) copy-start(bf16[512,1024]{1,0:T(8,128)(2,1)} %w_o_ref.1) | copy-start | bytes 3145732
  25.4 8.9 %copy-start.5 = (f32[1024]{0:T(1024)S(1)}, f32[1024]{0:T(1024)}, u32[]{:S(2)}) copy-start(f32[1024]{0:T(1024)} %param.20) | copy-start | bytes 12292
  33.0 1.2 %collective-permute-start.1 = (bf16[32,256]{1,0:T(8,128)(2,1)S(1)}, bf16[32,256]{1,0:T(8,128)(2,1)S(1)}, u32[]{:S(2)}, u32[]{:S(2)}) collective-permute-start(bf16[32,256]{1,0:T(8,128)(2,1)S(1)} %merge.1.mixed_ref), channel_id=1, source_target_pairs={{0,1},{1,0},{2,3},{3,2},{4,5},{5,4},{6,7},{7,6},{8,9},{9,8},{10,11... | collective-permute-start | bytes 49160 | tf_op jit(solution)/shard_map/ppermute | solution.py:600
  34.2 15.2 %copy-start = (bf16[1024,1024]{1,0:T(8,128)(2,1)S(1)}, bf16[1024,1024]{1,0:T(8,128)(2,1)}, u32[]{:S(2)}) copy-start(bf16[1024,1024]{1,0:T(8,128)(2,1)} %x_ref.1) | copy-start | bytes 6291460
  34.2 15.2 %copy-start.7 = (bf16[512,1024]{1,0:T(8,128)(2,1)S(1)}, bf16[512,1024]{1,0:T(8,128)(2,1)}, u32[]{:S(2)}) copy-start(bf16[512,1024]{1,0:T(8,128)(2,1)} %w_ref.1) | copy-start | bytes 3145732
  47.0 2.5 %collective-permute-start.3 = (bf16[256,512]{1,0:T(8,128)(2,1)S(1)}, bf16[256,512]{1,0:T(8,128)(2,1)S(1)}, u32[]{:S(2)}, u32[]{:S(2)}) collective-permute-start(bf16[256,512]{1,0:T(8,128)(2,1)S(1)} %bitcast.7), channel_id=1, source_target_pairs={{0,1},{1,0},{2,3},{3,2},{4,5},{5,4},{6,7},{7,6},{8,9},{9,8},{10,11... | collective-permute-start | bytes 786440 | tf_op jit(solution)/shard_map/ppermute | solution.py:608
